TPU v7x, 32 devices: a whole 2x2x4 slice. The times are simulated.
32 devices in a mesh: grp: 4 (over x, core), tile: 8 (over z, y).
Axes of the slice: x: 2, y: 2, z: 4, core: 2. Of those that a mesh axis runs over, the one named last changes fastest.
Arguments:
- nodes: bfloat16 [32768, 192], P(('grp', 'tile')), may hold values from -6 to 6
- node_ids: int32 [32768], P(('grp', 'tile')), may hold values from 0 to 262143
- node_count: int32 [32], P(('grp', 'tile')), may hold values from 256 to 1024
- pos_weight: float32 [3, 192], replicated, may hold values from -6 to 6
- gain_one: float32 [192], replicated, may hold values from 0.25 to 1.75
- qkv_one: bfloat16 [192, 576], replicated, may hold values from -0.4375 to 0.4375
- out_one: bfloat16 [192, 192], replicated, may hold values from -0.4375 to 0.4375
- gain_two: float32 [192], replicated, may hold values from 0.25 to 1.75
- qkv_two: bfloat16 [192, 576], replicated, may hold values from -0.4375 to 0.4375
- out_two: bfloat16 [192, 192], replicated, may hold values from -0.4375 to 0.4375
- gain_three: float32 [192], replicated, may hold values from 0.25 to 1.75
- w_up: bfloat16 [192, 768], replicated, may hold values from -0.4375 to 0.4375
- w_down: bfloat16 [768, 192], replicated, may hold values from -0.21875 to 0.21875
- vote_slot: int32 [16384], P(('grp', 'tile')), may hold values from 0 to 1023
- vote_owner: int32 [16384, 1], P(('grp', 'tile')), may hold values from 0 to 7; in each aligned block of 512 rows (0 to 511, 512 to 1023, ...) at most 128 rows name the same one
- vote_voxel: int32 [16384], P(('grp', 'tile')), may hold values from 0 to 255
Outputs:
- features_out: float32 [32768, 192], P(('grp', 'tile'))
- voxel_sums: float32 [8192, 192], P(('grp', 'tile'))
Inputs may be any that keep to these rules, and one draw needn't show every extreme that they name: `vote_owner`: among the votes of one shard, at most 128 name any one owner; some owner is named by exactly 128.
All inputs are finite; a program needn't handle non-finite values.
Results may differ from a plain program's by a relative error of at most 0.017.
Values may be sent and summed in bfloat16 or wider, within the bound.
No kernel may reach another device: no remote copies, remote signals or barrier semaphores. Data moves between devices by JAX's collectives and lax.ppermute only.
A program may use at most 64 MiB of HBM per device.

v0:
```python
import jax
import jax.numpy as jnp
from jax import lax
from jax.sharding import PartitionSpec as P

HEADS = 12
WIN = 32
VOX_DEV = 256


def position(node_ids, pos_weight):
    rows = []
    for axis in range(3):
        total = jnp.zeros(node_ids.shape, jnp.int32)
        for level in range(6):
            bit = jnp.bitwise_and(jnp.right_shift(node_ids, 3 * level + axis), 1)
            total = total + bit * 2**level
        rows.append(total.astype(jnp.float32) / 64.0 - 0.5)
    coords = jnp.stack(rows, 0)
    return jnp.einsum("an,ac->nc", coords, pos_weight, precision=lax.Precision.HIGHEST)


def normed(x, gain):
    mean = jnp.mean(x, -1, keepdims=True)
    var = jnp.mean((x - mean) ** 2, -1, keepdims=True)
    return ((x - mean) * lax.rsqrt(var + 1e-05) * gain).astype(jnp.bfloat16)


def attend(windows, keep, gain, w_qkv, w_out):
    xf = windows.astype(jnp.float32)
    count, width, chans = windows.shape
    head_dim = chans // HEADS
    inner = normed(xf, gain)
    qkv = jnp.einsum("nwc,cd->nwd", inner, w_qkv, preferred_element_type=jnp.float32).astype(
        jnp.bfloat16
    )
    qkv = qkv.reshape(count, width, 3, HEADS, head_dim)
    query, keys, values = (qkv[:, :, 0], qkv[:, :, 1], qkv[:, :, 2])
    scores = jnp.einsum(
        "nqhd,nkhd->nhqk", query, keys, preferred_element_type=jnp.float32
    ) * head_dim ** (-0.5)
    scores = scores + ((keep - 1.0) * 1000000000.0)[:, None, None, :]
    probs = jax.nn.softmax(scores, -1).astype(jnp.bfloat16)
    context = jnp.einsum("nhqk,nkhd->nqhd", probs, values, preferred_element_type=jnp.float32)
    context = context.reshape(count, width, chans).astype(jnp.bfloat16)
    return xf + jnp.einsum("nwc,cd->nwd", context, w_out, preferred_element_type=jnp.float32)


def feed(x, gain, w_up, w_down):
    inner = normed(x, gain)
    hidden = jax.nn.gelu(
        jnp.einsum("nwc,cd->nwd", inner, w_up, preferred_element_type=jnp.float32)
    ).astype(jnp.bfloat16)
    return x + jnp.einsum("nwd,dc->nwc", hidden, w_down, preferred_element_type=jnp.float32)


def body(
    nodes,
    node_ids,
    node_count,
    pos_weight,
    gain_one,
    qkv_one,
    out_one,
    gain_two,
    qkv_two,
    out_two,
    gain_three,
    w_up,
    w_down,
    vote_slot,
    vote_owner,
    vote_voxel,
):
    n_local, width = nodes.shape
    groups = lax.axis_size("grp")
    block = n_local // groups
    run = WIN // groups
    keep = (jnp.arange(n_local, dtype=jnp.int32) < node_count[0]).astype(jnp.float32)
    start = (nodes.astype(jnp.float32) + position(node_ids, pos_weight)).astype(jnp.bfloat16)
    first = attend(
        start.reshape(n_local // WIN, WIN, width),
        keep.reshape(n_local // WIN, WIN),
        gain_one,
        qkv_one,
        out_one,
    )
    first = first.astype(jnp.bfloat16).reshape(groups, block, width)
    arrived, arrived_keep = (
        lax.all_to_all(first, "grp", split_axis=0, concat_axis=0, tiled=True),
        lax.all_to_all(
            keep.astype(jnp.bfloat16).reshape(groups, block),
            "grp",
            split_axis=0,
            concat_axis=0,
            tiled=True,
        ),
    )
    windows = (
        arrived.reshape(groups, block // run, run, width)
        .transpose(1, 0, 2, 3)
        .reshape(block // run, WIN, width)
    )
    window_keep = (
        arrived_keep.reshape(groups, block // run, run)
        .transpose(1, 0, 2)
        .reshape(block // run, WIN)
    )
    second = attend(windows, window_keep.astype(jnp.float32), gain_two, qkv_two, out_two)
    third = feed(second, gain_three, w_up, w_down)
    outgoing = (
        third.reshape(block // run, groups, run, width)
        .transpose(1, 0, 2, 3)
        .reshape(groups, block, width)
    )
    returned = (
        lax.all_to_all(
            outgoing.astype(jnp.bfloat16), "grp", split_axis=0, concat_axis=0, tiled=True
        )
        .astype(outgoing.dtype)
        .reshape(n_local, width)
    )
    features_out = returned * keep[:, None]
    picked = features_out[vote_slot].astype(jnp.bfloat16)
    owner = vote_owner[:, 0]
    tiles = lax.axis_size("tile")
    capacity = 2 * vote_slot.shape[0] // tiles
    owner_hot = (owner[:, None] == jnp.arange(tiles, dtype=jnp.int32)[None, :]).astype(jnp.int32)
    rank = jnp.sum(jnp.cumsum(owner_hot, 0) * owner_hot, 1) - 1
    code = owner * capacity + rank
    buffer = jnp.zeros((tiles * capacity, width), jnp.bfloat16).at[code].set(picked)
    labels = jnp.full((tiles * capacity,), -1, jnp.int32).at[code].set(vote_voxel)
    got_rows, got_labels = (
        lax.all_to_all(
            buffer.reshape(tiles, capacity, width), "tile", split_axis=0, concat_axis=0, tiled=True
        ),
        lax.all_to_all(
            labels.reshape(tiles, capacity), "tile", split_axis=0, concat_axis=0, tiled=True
        ),
    )
    onehot = (
        jnp.arange(VOX_DEV, dtype=jnp.int32)[:, None] == got_labels.reshape(-1)[None, :]
    ).astype(jnp.bfloat16)
    voxel_sums = jnp.dot(onehot, got_rows.reshape(-1, width), preferred_element_type=jnp.float32)
    return (features_out, voxel_sums)


def solution(mesh):
    in_specs = (
        P(("grp", "tile"), None),
        P(("grp", "tile")),
        P(("grp", "tile")),
        P(),
        P(),
        P(),
        P(),
        P(),
        P(),
        P(),
        P(),
        P(),
        P(),
        P(("grp", "tile")),
        P(("grp", "tile"), None),
        P(("grp", "tile")),
    )
    out_specs = (P(("grp", "tile"), None), P(("grp", "tile"), None))
    return jax.shard_map(body, mesh=mesh, in_specs=in_specs, out_specs=out_specs, check_vma=False)
```

profile of v0, /device:TPU:0, one launch (start us, length us, event | category | flops | bytes accessed | tf_op | source)
XLA Modules:
  0.0 105.5 jit_solution(6148482116680986118)
XLA Ops:
  1.9 0.7 reduce.8
  3.1 4.2 %all-to-all-start.1 = ((bf16[4,2,128]{2,1,0:T(2,128)(2,1)}), bf16[4,2,128]{2,1,0:T(2,128)(2,1)S(1)}, u32[]{:S(2)}, u32[]{:S(2)}) async-start(bf16[4,2,128]{2,1,0:T(2,128)(2,1)} %reshape.275), calls=%async_computation.1 | async-start | bytes 4096 | tf_op jit(solution)/shard_map/all_to_all | solution.py:91
  7.3 0.7 multiply_add_fusion.10
  8.0 1.9 %fusion.80 = (f32[1024]{0:T(1024)S(1)}, f32[1024,192]{0,1:T(8,128)S(1)}) fusion(f32[3,192]{1,0:T(4,128)} %param.19, f32[1,1024]{1,0:T(1,128)S(1)} %bitcast.149, f32[1,1024]{1,0:T(1,128)S(1)} %bitcast.150, f32[1,1024]{1,0:T(1,128)S(1)} %bitcast.148, bf16[1024,192]{0,1:T(8,128)(2,1)} %param.16), kind=kOutput, calls=%fused_computation.128 | convolution fusion | flops 8066048 | bytes 1198336 | tf_op jit(solution)/shard_map/an,ac->nc/dot_general | solution.py:20
  10.5 1.7 %convolution_convert_fusion.1 = bf16[32,32,576]{2,1,0:T(8,128)(2,1)S(1)} fusion(f32[32,32,192]{2,1,0:T(8,128)S(1)} %bitcast.137, f32[192]{0:T(256)} %param.20, f32[32,32]{1,0:T(8,128)S(1)} %rsqrt.31, f32[32,32]{1,0:T(8,128)S(1)} %div.51, bf16[192,576]{1,0:T(8,128)(2,1)} %param.21), kind=kOutput, calls=%fused_computation.31 | convolution fusion | flops 227868672 | bytes 2196224 | tf_op jit(solution)/shard_map/nwc,cd->nwd/dot_general | solution.py:34
  12.2 3.4 %copy.142 = bf16[32,32,576]{1,2,0:T(8,128)(2,1)} copy(bf16[32,32,576]{2,1,0:T(8,128)(2,1)S(1)} %convolution_convert_fusion.1) | data formatting | bytes 2359296 | tf_op jit(solution)/shard_map/convert_element_type | solution.py:34
  15.6 5.7 %fusion.21 = f32[32,12,32,32]{2,3,1,0:T(8,128)} fusion(bf16[32,32,3,12,16]{1,4,3,2,0:T(8,128)(2,1)} %bitcast.133), kind=kOutput, calls=%fused_computation.37 | convolution fusion | flops 12582912 | bytes 4718592 | tf_op jit(solution)/shard_map/nqhd,nkhd->nhqk/dot_general | solution.py:39
  21.4 1.1 %reduce-window.6 = s32[8,4,128]{2,0,1:T(8,128)S(1)} reduce-window(s32[8,4,128]{2,0,1:T(8,128)S(1)} %fusion.66, s32[]{:T(128)} %constant.37.clone.1), window={size=1x1x128 pad=0_0x0_0x127_0}, to_apply=%region_10.0 | reduce-window | flops 520192 | bytes 32772 | tf_op jit(solution)/shard_map/reduce-window
  22.8 7.4 %fusion.81 = (f32[32,12,32]{2,1,0:T(8,128)S(1)}, f32[32,12,32,32]{2,3,1,0:T(8,128)S(1)}) fusion(f32[32,12,32,32]{2,3,1,0:T(8,128)} %fusion.21, f32[32,32]{1,0:T(8,128)S(1)} %add_multiply_fusion), kind=kOutput, calls=%fused_computation.129 | output fusion | flops 2359327 | bytes 3198976 | tf_op jit(solution)/shard_map/sub | solution.py:43
  30.2 2.5 %fusion.19 = bf16[32,12,16,32]{3,2,1,0:T(8,128)(2,1)S(1)} fusion(f32[32,12,32,32]{2,3,1,0:T(8,128)S(1)} %get-tuple-element.22, f32[32,12,32]{2,1,0:T(8,128)S(1)} %get-tuple-element.21, bf16[32,32,3,12,16]{1,4,3,2,0:T(8,128)(2,1)} %bitcast.134), kind=kOutput, calls=%fused_computation.29 | convolution fusion | flops 13565952 | bytes 3588096 | tf_op jit(solution)/shard_map/nhqk,nkhd->nqhd/dot_general | solution.py:44
  33.5 1.0 copy.148
  34.4 3.5 %all-to-all-start = ((bf16[4,256,192]{1,2,0:T(8,128)(2,1)}), bf16[4,256,192]{1,2,0:T(8,128)(2,1)S(1)}, u32[]{:S(2)}, u32[]{:S(2)}) async-start(bf16[4,256,192]{1,2,0:T(8,128)(2,1)} %copy.148), calls=%async_computation | async-start | bytes 786432 | tf_op jit(solution)/shard_map/all_to_all | solution.py:90
  37.9 3.2 %scatter_custom_fusion = s32[1024]{0:T(1024)} fusion(s32[512]{0:T(512)S(1)} %bitcast.153, s32[512]{0:T(512)} %param.31, s32[]{:T(128)} %constant.100.clone.1), kind=kCustom, calls=%fused_computation.115 | custom fusion | bytes 4608 | tf_op jit(solution)/shard_map/scatter | solution.py:132
  41.4 3.9 %all-to-all-done = bf16[4,256,192]{1,2,0:T(8,128)(2,1)S(1)} async-done(((bf16[4,256,192]{1,2,0:T(8,128)(2,1)}), bf16[4,256,192]{1,2,0:T(8,128)(2,1)S(1)}, u32[]{:S(2)}, u32[]{:S(2)}) %all-to-all-start) | async-done | bytes 393248 | tf_op jit(solution)/shard_map/all_to_all | solution.py:90
  46.5 0.7 convolution_convert_fusion
  47.3 3.3 %copy.158 = bf16[32,32,576]{1,2,0:T(8,128)(2,1)} copy(bf16[32,32,576]{2,1,0:T(8,128)(2,1)S(1)} %convolution_convert_fusion) | data formatting | bytes 2359296 | tf_op jit(solution)/shard_map/convert_element_type | solution.py:34
  50.6 3.0 %fusion.20 = f32[32,12,32,32]{2,3,1,0:T(8,128)S(1)} fusion(bf16[32,32,3,12,16]{1,4,3,2,0:T(8,128)(2,1)} %bitcast.135), kind=kOutput, calls=%fused_computation.33 | convolution fusion | flops 12582912 | bytes 4718592 | tf_op jit(solution)/shard_map/nqhd,nkhd->nhqk/dot_general | solution.py:39
  53.7 5.2 %fusion.82 = (f32[32,12,32]{2,1,0:T(8,128)S(1)}, f32[32,12,32,32]{2,3,1,0:T(8,128)S(1)}) fusion(f32[32,12,32,32]{2,3,1,0:T(8,128)S(1)} %fusion.20, f32[32,32]{1,0:T(8,128)S(1)} %copy.163), kind=kOutput, calls=%fused_computation.130 | output fusion | flops 2359327 | bytes 3198976 | tf_op jit(solution)/shard_map/sub | solution.py:43
  58.9 2.5 %fusion.18 = bf16[32,12,16,32]{3,2,1,0:T(8,128)(2,1)S(1)} fusion(f32[32,12,32,32]{2,3,1,0:T(8,128)S(1)} %get-tuple-element.24, f32[32,12,32]{2,1,0:T(8,128)S(1)} %get-tuple-element.23, bf16[32,32,3,12,16]{1,4,3,2,0:T(8,128)(2,1)} %bitcast.136), kind=kOutput, calls=%fused_computation.28 | convolution fusion | flops 13565952 | bytes 3588096 | tf_op jit(solution)/shard_map/nhqk,nkhd->nqhd/dot_general | solution.py:44
  61.4 0.7 fusion.83
  62.6 1.5 %fusion.28 = bf16[32,4,8,192]{3,2,1,0:T(8,128)(2,1)S(1)} fusion(f32[32,32,192]{2,1,0:T(8,128)S(1)} %get-tuple-element.26, f32[192]{0:T(256)S(1)} %copy-done.9, f32[32,32]{1,0:T(8,128)S(1)} %add_rsqrt_fusion, f32[32,32]{1,0:T(8,128)S(1)} %broadcast_multiply_fusion, bf16[768,192]{0,1:T(8,128)(2,1)S(1)} %copy-done, bf16[192,768]{1,0:T(8,128)(2,1)S(1)} %copy-done.6), kind=kOutput, calls=%fused_computation.49 | convolution fusion | flops 612237312 | bytes 1778432 | tf_op jit(solution)/shard_map/nwd,dc->nwc/dot_general | solution.py:54
  64.1 1.0 copy.167
  65.1 3.5 %all-to-all-start.2 = ((bf16[4,256,192]{1,2,0:T(8,128)(2,1)}), bf16[4,256,192]{1,2,0:T(8,128)(2,1)S(1)}, u32[]{:S(2)}, u32[]{:S(2)}) async-start(bf16[4,256,192]{1,2,0:T(8,128)(2,1)} %copy.167), calls=%async_computation.2 | async-start | bytes 786432 | tf_op jit(solution)/shard_map/all_to_all | solution.py:117
  68.6 7.4 %all-to-all-done.2 = bf16[4,256,192]{1,2,0:T(8,128)(2,1)S(1)} async-done(((bf16[4,256,192]{1,2,0:T(8,128)(2,1)}), bf16[4,256,192]{1,2,0:T(8,128)(2,1)S(1)}, u32[]{:S(2)}, u32[]{:S(2)}) %all-to-all-start.2) | async-done | bytes 393248 | tf_op jit(solution)/shard_map/all_to_all | solution.py:117
  76.0 6.2 %all-to-all-start.3 = ((s32[8,1,128]{2,1,0:T(1,128)}), s32[8,1,128]{2,1,0:T(1,128)S(1)}, u32[]{:S(2)}, u32[]{:S(2)}) async-start(s32[8,1,128]{2,1,0:T(1,128)} %bitcast.42), calls=%async_computation.3 | async-start | bytes 8192 | tf_op jit(solution)/shard_map/all_to_all | solution.py:137
  82.6 4.0 %scatter_custom_fusion.1 = bf16[1024,192]{1,0:T(8,128)(2,1)S(1)} fusion(s32[512]{0:T(512)S(1)} %bitcast.154, bf16[]{:T(256)} %constant.103.clone.1, f32[1024,192]{1,0:T(8,128)S(1)} %bitcast_multiply_fusion, s32[1024]{0:T(1024)S(1)} %pad_clamp_fusion), kind=kCustom, calls=%fused_computation.79 | custom fusion | bytes 393218 | tf_op jit(solution)/shard_map/scatter | solution.py:131
  86.6 0.9 copy.170
  87.6 1.0 all-to-all-done.3
  88.6 5.0 %all-to-all-start.4 = ((bf16[8,128,192]{1,2,0:T(8,128)(2,1)}), bf16[8,128,192]{1,2,0:T(8,128)(2,1)S(1)}, u32[]{:S(2)}, u32[]{:S(2)}) async-start(bf16[8,128,192]{1,2,0:T(8,128)(2,1)} %copy.170), calls=%async_computation.4 | async-start | bytes 786432 | tf_op jit(solution)/shard_map/all_to_all | solution.py:134
  93.6 1.2 %copy.172 = f32[1024,192]{0,1:T(8,128)} copy(f32[1024,192]{1,0:T(8,128)S(1)} %bitcast_multiply_fusion) | data formatting | bytes 1572864
  94.8 9.7 %all-to-all-done.4 = bf16[8,128,192]{1,2,0:T(8,128)(2,1)S(1)} async-done(((bf16[8,128,192]{1,2,0:T(8,128)(2,1)}), bf16[8,128,192]{1,2,0:T(8,128)(2,1)S(1)}, u32[]{:S(2)}, u32[]{:S(2)}) %all-to-all-start.4) | async-done | bytes 393248 | tf_op jit(solution)/shard_map/all_to_all | solution.py:134
  104.5 1.0 fusion.32
  (64 shorter events, 5.0 us)
Async XLA Ops:
  0.6 61.9 %copy-start = (bf16[768,192]{0,1:T(8,128)(2,1)S(1)}, bf16[768,192]{0,1:T(8,128)(2,1)}, u32[]{:S(2)}) copy-start(bf16[768,192]{0,1:T(8,128)(2,1)} %param.28) | copy-start | bytes 884740
  3.1 31.3 %all-to-all-start.1 = ((bf16[4,2,128]{2,1,0:T(2,128)(2,1)}), bf16[4,2,128]{2,1,0:T(2,128)(2,1)S(1)}, u32[]{:S(2)}, u32[]{:S(2)}) async-start(bf16[4,2,128]{2,1,0:T(2,128)(2,1)} %reshape.275), calls=%async_computation.1 | async-start | bytes 4096 | tf_op jit(solution)/shard_map/all_to_all | solution.py:91
  15.6 5.7 %copy-start.3 = (s32[512,1]{0,1:T(1,128)S(1)}, s32[512,1]{0,1:T(1,128)}, u32[]{:S(2)}) copy-start(s32[512,1]{0,1:T(1,128)} %param.30) | copy-start | bytes 6148
  22.8 7.4 %copy-start.4 = (s32[8,5]{0,1:T(8,128)}, s32[8,5]{0,1:T(8,128)S(1)}, u32[]{:S(2)}) copy-start(s32[8,5]{0,1:T(8,128)S(1)} %reduce-window.9) | copy-start | bytes 484
  30.2 2.6 %copy-start.1 = (bf16[192,192]{1,0:T(8,128)(2,1)S(1)}, bf16[192,192]{1,0:T(8,128)(2,1)}, u32[]{:S(2)}) copy-start(bf16[192,192]{1,0:T(8,128)(2,1)} %param.22) | copy-start | bytes 221188
  30.2 3.1 %slice-start = ((s32[8,5]{0,1:T(8,128)}), s32[8,4]{0,1:T(4,128)S(1)}, s32[]{:S(2)}) async-start(s32[8,5]{0,1:T(8,128)} %copy-done.4), calls=%async_computation.5 | async-start | bytes 4096 | tf_op jit(solution)/shard_map/slice.1
  32.8 13.8 %copy-start.7 = (bf16[192,576]{1,0:T(8,128)(2,1)S(1)}, bf16[192,576]{1,0:T(8,128)(2,1)}, u32[]{:S(2)}) copy-start(bf16[192,576]{1,0:T(8,128)(2,1)} %param.24) | copy-start | bytes 663556
  32.8 13.8 %copy-start.8 = (f32[192]{0:T(256)S(1)}, f32[192]{0:T(256)}, u32[]{:S(2)}) copy-start(f32[192]{0:T(256)} %param.23) | copy-start | bytes 2308
  34.4 10.9 %all-to-all-start = ((bf16[4,256,192]{1,2,0:T(8,128)(2,1)}), bf16[4,256,192]{1,2,0:T(8,128)(2,1)S(1)}, u32[]{:S(2)}, u32[]{:S(2)}) async-start(bf16[4,256,192]{1,2,0:T(8,128)(2,1)} %copy.148), calls=%async_computation | async-start | bytes 786432 | tf_op jit(solution)/shard_map/all_to_all | solution.py:90
  58.8 2.6 %copy-start.2 = (bf16[192,192]{1,0:T(8,128)(2,1)S(1)}, bf16[192,192]{1,0:T(8,128)(2,1)}, u32[]{:S(2)}) copy-start(bf16[192,192]{1,0:T(8,128)(2,1)} %param.25) | copy-start | bytes 221188
  58.9 3.7 %copy-start.6 = (bf16[192,768]{1,0:T(8,128)(2,1)S(1)}, bf16[192,768]{1,0:T(8,128)(2,1)}, u32[]{:S(2)}) copy-start(bf16[192,768]{1,0:T(8,128)(2,1)} %param.27) | copy-start | bytes 884740
  58.9 3.7 %copy-start.9 = (f32[192]{0:T(256)S(1)}, f32[192]{0:T(256)}, u32[]{:S(2)}) copy-start(f32[192]{0:T(256)} %param.26) | copy-start | bytes 2308
  62.6 5.9 %copy-start.5 = (s32[512]{0:T(512)S(1)}, s32[512]{0:T(512)}, u32[]{:S(2)}) copy-start(s32[512]{0:T(512)} %param.29) | copy-start | bytes 6148
  65.1 10.9 %all-to-all-start.2 = ((bf16[4,256,192]{1,2,0:T(8,128)(2,1)}), bf16[4,256,192]{1,2,0:T(8,128)(2,1)S(1)}, u32[]{:S(2)}, u32[]{:S(2)}) async-start(bf16[4,256,192]{1,2,0:T(8,128)(2,1)} %copy.167), calls=%async_computation.2 | async-start | bytes 786432 | tf_op jit(solution)/shard_map/all_to_all | solution.py:117
  76.0 12.6 %all-to-all-start.3 = ((s32[8,1,128]{2,1,0:T(1,128)}), s32[8,1,128]{2,1,0:T(1,128)S(1)}, u32[]{:S(2)}, u32[]{:S(2)}) async-start(s32[8,1,128]{2,1,0:T(1,128)} %bitcast.42), calls=%async_computation.3 | async-start | bytes 8192 | tf_op jit(solution)/shard_map/all_to_all | solution.py:137
  88.6 15.9 %all-to-all-start.4 = ((bf16[8,128,192]{1,2,0:T(8,128)(2,1)}), bf16[8,128,192]{1,2,0:T(8,128)(2,1)S(1)}, u32[]{:S(2)}, u32[]{:S(2)}) async-start(bf16[8,128,192]{1,2,0:T(8,128)(2,1)} %copy.170), calls=%async_computation.4 | async-start | bytes 786432 | tf_op jit(solution)/shard_map/all_to_all | solution.py:134
where the time goes:
time: 106 us
  starting transfers between devices  22.4 us (21%)
  waiting for transfers between devices  22 us (21%)
  matrix products  21.9 us (21%)
  local copies, waits for them, and re-layouts  20.9 us (20%)
  other arithmetic  16.6 us (16%)
  between operations  1.72 us (2%)
    sub x2, other arithmetic, attend(): probs = jax.nn.softmax(scores, -1).astype(jnp.bfloat16)  12.6 us
    all_to_all x1, waiting for transfers between devices, body(): lax.all_to_all(buffer.reshape(tiles, capacity, width), 'tile', split_axis...  9.72 us
    dot_general x2, matrix products, attend(): jnp.einsum('nqhd,nkhd->nhqk', query, keys, preferred_element_type=jnp.flo...  8.76 us
    all_to_all x1, waiting for transfers between devices, body(): lax.all_to_all(outgoing.astype(jnp.bfloat16), 'grp', split_axis=0, concat...  7.37 us
    convert_element_type x2, local copies, waits for them, and re-layouts, attend(): jnp.einsum('nwc,cd->nwd', inner, w_qkv, preferred_element_type=jnp.float32)  6.71 us
    all_to_all x1, starting transfers between devices, body(): lax.all_to_all(labels.reshape(tiles, capacity), 'tile', split_axis=0, con...  6.22 us
    dot_general x2, matrix products, attend(): jnp.einsum('nhqk,nkhd->nqhd', probs, values, preferred_element_type=jnp.f...  5.04 us
    all_to_all x1, starting transfers between devices, body(): lax.all_to_all(buffer.reshape(tiles, capacity, width), 'tile', split_axis...  5.02 us
  transfers between devices with their start and end apart: 5, of which 4 were waited for; matrix products, arithmetic and copies ran while one was open for 35% of the time, Pallas kernels for 0%

commit v1 on v0

v1 whole, which is shorter than its diff:
```python
import functools
import math

import jax
import jax.numpy as jnp
from jax import lax
from jax.experimental import pallas as pl
from jax.experimental.pallas import tpu as pltpu
from jax.sharding import PartitionSpec as P

HEADS = 12
WIN = 32
VOX_DEV = 256
LANES = 128
FLAG = 16384.0
VMEM = 48 * 1024 * 1024
F32 = jnp.float32
BF16 = jnp.bfloat16


def iota(shape, dim):
    return lax.broadcasted_iota(jnp.int32, shape, dim)


def dot(a, b):
    return jnp.dot(a, b, preferred_element_type=F32)


def dot_t(a, b):
    return lax.dot_general(a, b, (((1,), (1,)), ((), ())), preferred_element_type=F32)


def head_order(j, chans):
    size = chans // HEADS
    cut = 8 * size
    high = j - cut
    low_src = (j % 8) * size + j // 8
    high_src = (8 + high % 4) * size + high // 8 + (size // 2) * ((high % 8) // 4)
    return jnp.where(j < cut, low_src, high_src)


def permutation(parts, chans):
    n = parts * chans
    row = iota((n, n), 0)
    src = (row // chans) * chans + head_order(row % chans, chans)
    return (src == iota((n, n), 1)).astype(BF16)


def project_weights(w_qkv, w_out):
    chans = w_out.shape[0]
    qkv_t = dot_t(permutation(3, chans), w_qkv).astype(BF16)
    out_t = dot(permutation(1, chans), w_out).T.astype(BF16)
    return qkv_t, out_t


def norm_t(x, gain):
    inv = 1.0 / x.shape[0]
    mean = jnp.sum(x, 0, keepdims=True) * inv
    cent = x - mean
    var = jnp.sum(cent * cent, 0, keepdims=True) * inv
    return cent * lax.rsqrt(var + 1e-05) * gain


def attend_tiles(q_s, k_s, v_s, s_s, tiles, mask_of, write):
    cut = 2 * q_s.shape[1] // 3

    def one(t, _):
        query = q_s[t]

        def score(key, top):
            prod = query * k_s[key]
            a = jnp.sum(prod[:cut], 0)
            b = jnp.sum(prod[cut:], 0)
            b = b + pltpu.roll(b, 4, 0)
            mask = mask_of(key)
            a = a + mask
            b = b + mask
            s_s[key, 0] = a
            s_s[key, 1] = b
            return jnp.maximum(top[0], a), jnp.maximum(top[1], b)

        low = jnp.full((8, LANES), -3e38, F32)
        top_a, top_b = lax.fori_loop(0, WIN, score, (low, low), unroll=4)

        def gather(key, carry):
            sum_a, sum_b, acc_a, acc_b = carry
            pa = jnp.exp2(s_s[key, 0] - top_a)
            pb = jnp.exp2(s_s[key, 1] - top_b)
            value = v_s[key]
            return (
                sum_a + pa,
                sum_b + pb,
                acc_a + pa[None] * value[:cut],
                acc_b + pb[None] * value[cut:],
            )

        zero = jnp.zeros((8, LANES), F32)
        sum_a, sum_b, acc_a, acc_b = lax.fori_loop(
            0,
            WIN,
            gather,
            (
                zero,
                zero,
                jnp.zeros((cut, 8, LANES), F32),
                jnp.zeros((q_s.shape[1] - cut, 8, LANES), F32),
            ),
            unroll=4,
        )
        ctx = jnp.concatenate([acc_a / sum_a[None], acc_b / sum_b[None]], 0)
        write(t, ctx.reshape(-1, LANES).astype(BF16))
        return 0

    lax.fori_loop(0, tiles, one, 0)


def slot_base(run, unit, r):
    lane = iota((8, LANES), 1)
    rep_at = lane // WIN
    return (lane % 8) * LANES + ((lane // 8) % 4) * WIN + (4 * unit + rep_at) * run + r


def first_kernel(
    run, count_ref, nodes_ref, ids_ref, pos_ref, gain_one_ref, gain_two_ref, qkv_ref, out_ref,
    first_ref, sent_ref, x_s, start_s, n_s, q_s, k_s, v_s, s_s, ctx_s
):
    slots, chans = nodes_ref.shape
    tiles = slots // LANES
    units = tiles // run
    rows8 = chans // 8
    count = count_ref[0]
    qkv_t, out_t = project_weights(qkv_ref[...], out_ref[...])
    cols = jnp.concatenate(
        [pos_ref[...], gain_one_ref[...], gain_two_ref[...], jnp.zeros((3, chans), F32)], 0
    ).T
    left = nodes_ref[...].astype(F32)
    x_s[0] = left[:, :LANES]
    x_s[1, :, : chans - LANES] = left[:, LANES:]
    ids = ids_ref[...]
    ids = jnp.concatenate([ids[:, w * WIN : (w + 1) * WIN] for w in range(4)], 0).T
    ids = jnp.concatenate(
        [
            jnp.concatenate(
                [ids[(4 * u + i) * run : (4 * u + i + 1) * run] for i in range(4)], 1
            )
            for u in range(units)
        ],
        0,
    )
    coords = []
    for axis in range(3):
        total = jnp.zeros(ids.shape, jnp.int32)
        for level in range(6):
            bit = jnp.bitwise_and(jnp.right_shift(ids, 3 * level + axis), 1)
            total = total + bit * 2**level
        coords.append(total.astype(F32) / 64.0 - 0.5)
    eye = (iota((chans, chans), 0) == iota((chans, chans), 1)).astype(BF16)
    for q in range(tiles):
        u, r = q // run, q % run
        halves = [
            jnp.concatenate(
                [
                    x_s[half, pl.ds(w * WIN + (4 * u + i) * run + r, 8, stride=LANES), :]
                    for i in range(4)
                    for w in range(4)
                ],
                0,
            )
            for half in range(2)
        ]
        rows = jnp.concatenate([halves[0], halves[1][:, : chans - LANES]], 1).astype(BF16)
        at = cols[:, 0:1] * coords[0][q : q + 1]
        at = at + cols[:, 1:2] * coords[1][q : q + 1]
        at = at + cols[:, 2:3] * coords[2][q : q + 1]
        start = (dot_t(eye, rows) + at).astype(BF16)
        start_s[:, q * LANES : (q + 1) * LANES] = start
        n_s[:, q * LANES : (q + 1) * LANES] = norm_t(start.astype(F32), cols[:, 3:4]).astype(BF16)
    spread = (
        iota((LANES, 4 * LANES), 0)
        == (iota((LANES, 4 * LANES), 1) // LANES) * WIN + iota((LANES, 4 * LANES), 1) % WIN
    ).astype(BF16)
    scale = (chans // HEADS) ** -0.5 * math.log2(math.e)
    for q in range(tiles):
        u, r = q // run, q % run
        qkv = dot(qkv_t, n_s[:, q * LANES : (q + 1) * LANES])
        q_s[q] = (qkv[:chans] * scale).reshape(rows8, 8, LANES)
        wide = dot(qkv[chans:].astype(BF16), spread)
        for i in range(4):
            p = (4 * u + i) * run + r
            piece = wide[:, i * LANES : (i + 1) * LANES]
            k_s[p] = piece[:chans].reshape(rows8, 8, LANES)
            v_s[p] = piece[chans:].reshape(rows8, 8, LANES)

    lane = iota((8, LANES), 1)
    base = (lane % 8) * LANES + ((lane // 8) % 4) * WIN

    def mask_of(key):
        return jnp.where(base + key < count, 0.0, -1e9).astype(F32)

    def write(t, ctx):
        ctx_s[t] = ctx

    attend_tiles(q_s, k_s, v_s, s_s, tiles, mask_of, write)
    for q in range(tiles):
        u, r = q // run, q % run
        at = slice(q * LANES, (q + 1) * LANES)
        first = (start_s[:, at].astype(F32) + dot(out_t, ctx_s[q])).astype(BF16)
        first_ref[:, at] = first
        normed = norm_t(first.astype(F32), cols[:, 4:5])
        kept = slot_base(run, u, r)[0:1] < count
        head = jnp.where((iota((16, LANES), 0) > 0) | kept, normed[:16], FLAG)
        sent_ref[:, at] = jnp.concatenate([head, normed[16:]], 0).astype(BF16)


def tables_kernel(
    run, cap, qkv_ref, out_ref, up_ref, down_ref, slot_ref, owner_ref, voxel_ref,
    qkv_t_ref, out_t_ref, up_t_ref, down_t_ref, token_ref, label_ref
):
    votes = slot_ref.shape[1]
    codes = token_ref.shape[1]
    owners = codes // cap
    qkv_t_ref[...], out_t_ref[...] = project_weights(qkv_ref[...], out_ref[...])
    up_t_ref[...] = up_ref[...].astype(F32).T.astype(BF16)
    down_t_ref[...] = down_ref[...].astype(F32).T.astype(BF16)
    owner = owner_ref[...]
    hot = owner == iota((owners, votes), 0)
    upto = (iota((votes, votes), 0) <= iota((votes, votes), 1)).astype(BF16)
    rank = jnp.sum(jnp.where(hot, dot(hot.astype(BF16), upto), 0.0), 0, keepdims=True)
    code = owner * cap + rank.astype(jnp.int32) - 1
    member = (code == iota((codes, votes), 0)).astype(BF16)
    slot = slot_ref[...]
    p = slot % WIN
    i = p // run
    token = (
        ((i // 4) * run + p % run) * LANES
        + (i % 4) * WIN
        + ((slot // WIN) % 4) * 8
        + slot // LANES
    )
    row = iota((16, votes), 0)
    facts = jnp.where(
        row == 0,
        token // 32,
        jnp.where(row == 1, token % 32, jnp.where(row == 2, voxel_ref[...], 1)),
    )
    listed = dot_t(facts.astype(F32).astype(BF16), member)
    held = listed[3:4] > 0.5
    token_of = listed[0:1] * 32.0 + listed[1:2]
    token_ref[...] = jnp.where(held, token_of, -1.0).astype(jnp.int32)
    label = jnp.where(held, listed[2:3], -1.0)
    label_ref[...] = jnp.broadcast_to(label, label_ref.shape).astype(BF16)


def second_kernel(
    run, cap, count_ref, all_ref, own_ref, first_ref, gain_ref, qkv_t_ref, out_t_ref, up_t_ref,
    down_t_ref, token_ref, label_ref, feat_ref, votes_ref, q_s, k_s, v_s, m_s, s_s, ctx_s, bf_s, x_s
):
    groups, chans, slots = all_ref.shape
    tiles = slots // LANES
    units = tiles // run
    rows8 = chans // 8
    count = count_ref[0]
    gain = jnp.concatenate([gain_ref[...], jnp.zeros((7, chans), F32)], 0).T[:, 0:1]
    scale = (chans // HEADS) ** -0.5 * math.log2(math.e)

    def clean(block):
        head = block[:16].astype(F32)
        gone = head[0:1] > 0.5 * FLAG
        head = jnp.where((iota(head.shape, 0) == 0) & gone, 0.0, head)
        return jnp.concatenate([head.astype(BF16), block[16:]], 0), gone

    q_t = qkv_t_ref[:chans, :]
    kv_t = qkv_t_ref[chans:, :]
    for u in range(units):
        for r in range(run):
            t = u * run + r
            at = slice(t * LANES, (t + 1) * LANES)
            own, _ = clean(own_ref[:, at])
            q_s[r] = (dot(q_t, own) * scale).reshape(rows8, 8, LANES)
            for g in range(groups):
                block, gone = clean(all_ref[g, :, at])
                kv = dot(kv_t, block)
                k_s[g * run + r] = kv[:chans].reshape(rows8, 8, LANES)
                v_s[g * run + r] = kv[chans:].reshape(rows8, 8, LANES)
                m_s[g * run + r] = jnp.broadcast_to(jnp.where(gone, -1e9, 0.0), (8, LANES))

        def write(t, ctx, u=u):
            ctx_s[u * run + t] = ctx

        attend_tiles(q_s, k_s, v_s, s_s, run, lambda key: m_s[key], write)

    out_t = out_t_ref[...]
    for t in range(tiles):
        u, r = t // run, t % run
        at = slice(t * LANES, (t + 1) * LANES)
        second = first_ref[:, at].astype(F32) + dot(out_t, ctx_s[t])
        inner = norm_t(second, gain).astype(BF16)
        hidden = jax.nn.gelu(dot(up_t_ref[...], inner)).astype(BF16)
        third = second + dot(down_t_ref[...], hidden)
        third = jnp.where(slot_base(run, u, r)[0:1] < count, third, 0.0)
        bf_s[:, at] = third.astype(BF16)
        third = jnp.concatenate([third, jnp.zeros((2 * LANES - chans, LANES), F32)], 0)
        for half in range(2):
            rows = third[half * LANES : (half + 1) * LANES].T
            for i in range(4):
                for w in range(4):
                    x_s[half, pl.ds(w * WIN + (4 * u + i) * run + r, 8, stride=LANES), :] = rows[
                        (i * 4 + w) * 8 : (i * 4 + w + 1) * 8
                    ]
    feat_ref[:, :LANES] = x_s[0]
    feat_ref[:, LANES:] = x_s[1, :, : chans - LANES]
    codes = token_ref.shape[1]
    token = token_ref[...]
    picked = jnp.zeros((chans, codes), F32)
    step = 256
    for at in range(0, slots, step):
        hot = (token == iota((step, codes), 0) + at).astype(BF16)
        picked = picked + dot(bf_s[:, at : at + step], hot)
    picked = picked.astype(BF16)
    for o in range(codes // cap):
        votes_ref[o, :chans, :] = picked[:, o * cap : (o + 1) * cap]
        votes_ref[o, chans:, :] = label_ref[:, o * cap : (o + 1) * cap]


def sums_kernel(got_ref, out_ref):
    sources, rows, cap = got_ref.shape
    chans = out_ref.shape[1]
    total = jnp.zeros(out_ref.shape, F32)
    for s in range(sources):
        label = got_ref[s, chans:, :].astype(F32)[0:1]
        hot = (label == iota((out_ref.shape[0], cap), 0).astype(F32)).astype(BF16)
        total = total + dot_t(hot, got_ref[s, :chans, :])
    out_ref[...] = total


def call(kernel, outs, scratch, flops, in_smem=0, n_in=0):
    specs = [pl.BlockSpec(memory_space=pltpu.SMEM)] * in_smem
    specs += [pl.BlockSpec(memory_space=pltpu.VMEM)] * (n_in - in_smem)
    return pl.pallas_call(
        kernel,
        out_shape=outs,
        in_specs=specs,
        out_specs=[pl.BlockSpec(memory_space=pltpu.VMEM)] * len(outs),
        scratch_shapes=scratch,
        compiler_params=pltpu.CompilerParams(vmem_limit_bytes=VMEM),
        cost_estimate=pl.CostEstimate(flops=flops, bytes_accessed=2 << 20, transcendentals=0),
    )


def body(
    nodes,
    node_ids,
    node_count,
    pos_weight,
    gain_one,
    qkv_one,
    out_one,
    gain_two,
    qkv_two,
    out_two,
    gain_three,
    w_up,
    w_down,
    vote_slot,
    vote_owner,
    vote_voxel,
):
    slots, chans = nodes.shape
    groups, owners = lax.axis_size("grp"), lax.axis_size("tile")
    run = WIN // groups
    votes = vote_slot.shape[0]
    cap = 2 * votes // owners
    codes = owners * cap
    tiles = slots // LANES
    rows8 = chans // 8
    hidden = w_up.shape[1]
    sds = jax.ShapeDtypeStruct

    first, sent = call(
        functools.partial(first_kernel, run),
        [sds((chans, slots), BF16), sds((chans, slots), BF16)],
        [
            pltpu.VMEM((2, slots, LANES), F32),
            pltpu.VMEM((chans, slots), BF16),
            pltpu.VMEM((chans, slots), BF16),
            pltpu.VMEM((tiles, rows8, 8, LANES), F32),
            pltpu.VMEM((WIN, rows8, 8, LANES), F32),
            pltpu.VMEM((WIN, rows8, 8, LANES), F32),
            pltpu.VMEM((WIN, 2, 8, LANES), F32),
            pltpu.VMEM((tiles, chans, LANES), BF16),
        ],
        2_000_000_000,
        in_smem=1,
        n_in=8,
    )(
        node_count,
        nodes,
        node_ids.reshape(slots // LANES, LANES),
        pos_weight,
        gain_one.reshape(1, chans),
        gain_two.reshape(1, chans),
        qkv_one,
        out_one,
    )
    gathered = lax.all_gather(sent, "grp", axis=0, tiled=False)
    qkv_t, out_t, up_t, down_t, token, label = call(
        functools.partial(tables_kernel, run, cap),
        [
            sds((3 * chans, chans), BF16),
            sds((chans, chans), BF16),
            sds((hidden, chans), BF16),
            sds((chans, hidden), BF16),
            sds((1, codes), jnp.int32),
            sds((16, codes), BF16),
        ],
        [],
        2_000_000_000,
        n_in=7,
    )(
        qkv_two,
        out_two,
        w_up,
        w_down,
        vote_slot.reshape(1, votes),
        vote_owner.reshape(1, votes),
        vote_voxel.reshape(1, votes),
    )
    features_out, ballots = call(
        functools.partial(second_kernel, run, cap),
        [sds((slots, chans), F32), sds((owners, chans + 16, cap), BF16)],
        [
            pltpu.VMEM((run, rows8, 8, LANES), F32),
            pltpu.VMEM((WIN, rows8, 8, LANES), F32),
            pltpu.VMEM((WIN, rows8, 8, LANES), F32),
            pltpu.VMEM((WIN, 8, LANES), F32),
            pltpu.VMEM((WIN, 2, 8, LANES), F32),
            pltpu.VMEM((tiles, chans, LANES), BF16),
            pltpu.VMEM((chans, slots), BF16),
            pltpu.VMEM((2, slots, LANES), F32),
        ],
        3_000_000_000,
        in_smem=1,
        n_in=11,
    )(
        node_count,
        gathered,
        sent,
        first,
        gain_three.reshape(1, chans),
        qkv_t,
        out_t,
        up_t,
        down_t,
        token,
        label,
    )
    got = lax.all_to_all(ballots, "tile", split_axis=0, concat_axis=0, tiled=True)
    (voxel_sums,) = call(
        sums_kernel, [sds((VOX_DEV, chans), F32)], [], 200_000_000, n_in=1
    )(got)
    return (features_out, voxel_sums)


def solution(mesh):
    in_specs = (
        P(("grp", "tile"), None),
        P(("grp", "tile")),
        P(("grp", "tile")),
        P(),
        P(),
        P(),
        P(),
        P(),
        P(),
        P(),
        P(),
        P(),
        P(),
        P(("grp", "tile")),
        P(("grp", "tile"), None),
        P(("grp", "tile")),
    )
    out_specs = (P(("grp", "tile"), None), P(("grp", "tile"), None))
    return jax.shard_map(body, mesh=mesh, in_specs=in_specs, out_specs=out_specs, check_vma=False)
```

time: 106 us -> 91.2 us (0.86)
  Pallas kernels: 0 us -> 28.8 us
  matrix products: 21.9 us -> 0 us
  starting transfers between devices: 22.4 us -> 5.55 us
  other arithmetic: 16.6 us -> 0 us
  between operations: 1.72 us -> 14.8 us
  local copies, waits for them, and re-layouts: 20.9 us -> 9.37 us
  waiting for transfers between devices: 22 us -> 32.3 us
    pallas_call x0 -> x4, Pallas kernels: none -> 28.8 us  [the longest x1 15.4 us: body(): call(functools.partial(second_kernel, run, cap), [sds((slots, chans), F32...]
    dot_general x11 -> x0, matrix products: 21.9 us -> none  [the longest x2 8.76 us: attend(): jnp.einsum('nqhd,nkhd->nhqk', query, keys, preferred_element_type=jnp.flo...]
    all_gather x0 -> x1, waiting for transfers between devices: none -> 20.7 us  [body(): gathered = lax.all_gather(sent, 'grp', axis=0, tiled=False)]
    all_to_all x5 -> x1, starting transfers between devices: 22.4 us -> 5.52 us  [body(): lax.all_to_all(ballots, 'tile', split_axis=0, concat_axis=0, tiled=True)]
    sub x4 -> x0, other arithmetic: 13.3 us -> none  [the longest x2 12.6 us: attend(): probs = jax.nn.softmax(scores, -1).astype(jnp.bfloat16)]
    all_to_all x5 -> x1, waiting for transfers between devices: 22 us -> 11.6 us  [body(): lax.all_to_all(ballots, 'tile', split_axis=0, concat_axis=0, tiled=True)]
    convert_element_type x6 -> x0, local copies, waits for them, and re-layouts: 8.54 us -> none  [the longest x2 6.71 us: attend(): jnp.einsum('nwc,cd->nwd', inner, w_qkv, preferred_element_type=jnp.float32)]
    unnamed x23 -> x34, local copies, waits for them, and re-layouts: 1.87 us -> 9.37 us
  transfers between devices with their start and end apart: 5 -> 2, of which waited for: 4 -> 2; matrix products, arithmetic and copies ran while one was open for 35% -> 2% of each run, Pallas kernels for 0% -> 2%
where the time goes in v1:
time: 91.2 us; the launch traced here: 90.7 us
  waiting for transfers between devices  32.3 us (35%)
  Pallas kernels  28.8 us (32%)
  between operations  14.8 us (16%)
  local copies, waits for them, and re-layouts  9.37 us (10%)
  starting transfers between devices  5.55 us (6%)
    all_gather x1, waiting for transfers between devices, body(): gathered = lax.all_gather(sent, 'grp', axis=0, tiled=False)  20.7 us
    pallas_call x1, Pallas kernels, body(): call(functools.partial(second_kernel, run, cap), [sds((slots, chans), F32...  15.4 us
    all_to_all x1, waiting for transfers between devices, body(): lax.all_to_all(ballots, 'tile', split_axis=0, concat_axis=0, tiled=True)  11.6 us
    pallas_call x1, Pallas kernels, body(): call(functools.partial(first_kernel, run), [sds((chans, slots), BF16), sd...  11.3 us
    unnamed x34, local copies, waits for them, and re-layouts  9.37 us
    all_to_all x1, starting transfers between devices, body(): lax.all_to_all(ballots, 'tile', split_axis=0, concat_axis=0, tiled=True)  5.52 us
  transfers between devices with their start and end apart: 2, of which 2 were waited for; matrix products, arithmetic and copies ran while one was open for 2% of the time, Pallas kernels for 2%

profile of v1, /device:TPU:0, one launch (start us, length us, event | category | flops | bytes accessed | tf_op | source)
XLA Modules:
  0.0 90.7 jit_solution(7968178312512391536)
XLA Ops:
  7.2 0.0 all-gather.3.cloned.1.call-start
  7.9 1.2 %copy.18.nodes_ref = bf16[1024,192]{1,0:T(8,128)(2,1)S(1)} copy(bf16[1024,192]{0,1:T(8,128)(2,1)} %param.16) | data formatting | bytes 786432 | tf_op args[0]
  9.1 0.0 copy-start.2
  9.1 0.9 %copy-done.2 = bf16[192,576]{1,0:T(8,128)(2,1)S(1)} copy-done((bf16[192,576]{1,0:T(8,128)(2,1)S(1)}, bf16[192,576]{1,0:T(8,128)(2,1)}, u32[]{:S(2)}) %copy-start.2) | copy-done | bytes 221208
  10.0 0.9 copy-done.4
  10.9 0.7 copy-done.6
  11.6 0.7 copy-done.7
  12.3 0.7 copy-done.11
  13.0 0.7 copy-done.12
  13.6 0.0 copy-start.8
  13.7 0.0 copy-start.9
  13.7 0.0 copy-start.10
  13.7 11.3 %shard_map.167 = (bf16[192,1024]{1,0:T(8,128)(2,1)S(1)}, bf16[192,1024]{1,0:T(8,128)(2,1)}) custom-call(s32[1]{0:T(128)S(6)} %copy.22.count_ref, bf16[1024,192]{1,0:T(8,128)(2,1)S(1)} %copy.18.nodes_ref, s32[8,128]{1,0:T(8,128)S(1)} %bitcast.9, f32[3,192]{1,0:T(4,128)S(1)} %copy-done.7, f32[1,192]{1,0:T(1,128)S(1)} %bitcast.13, f32[1,192]{1,0:T(1,128)S(1)} %bitcast.14, ...), custom_call_target="tpu_custom_call" | custom-call | flops 2000000000 | bytes 2097152 | tf_op jit(solution)/shard_map/pallas_call | solution.py:379
  25.0 0.0 all-gather.3.cloned.1.call-update
  25.0 0.2 copy.19.down_ref
  25.2 0.0 copy-done.1
  25.2 0.0 copy-done.3
  25.2 0.0 copy-done.5
  25.3 0.0 copy-done.8
  25.3 0.0 copy-done.9
  25.3 0.0 copy-done.10
  25.3 0.0 copy-start.13
  25.3 1.6 %shard_map.168 = (bf16[576,192]{1,0:T(8,128)(2,1)S(1)}, bf16[192,192]{1,0:T(8,128)(2,1)S(1)}, bf16[768,192]{1,0:T(8,128)(2,1)S(1)}, bf16[192,768]{1,0:T(8,128)(2...) custom-call(bf16[192,576]{1,0:T(8,128)(2,1)S(1)} %copy-done.3, bf16[192,192]{1,0:T(8,128)(2,1)S(1)} %copy-done.5, ...), custom_call_target="tpu_custom_call" | custom-call | flops 2000000000 | bytes 2097152 | tf_op jit(solution)/shard_map/pallas_call | solution.py:406
  26.9 20.7 %all-gather.3.cloned.1.call-done = bf16[768,1024]{1,0:T(8,128)(2,1)} async-done(((bf16[192,1024]{1,0:T(8,128)(2,1)}), bf16[768,1024]{1,0:T(8,128)(2,1)}) %all-gather.3.cloned.1.call-update) | async-done | bytes 1572880 | tf_op jit(solution)/shard_map/all_gather | solution.py:405
  47.5 0.0 copy-done.13
  47.6 1.4 %copy-done = bf16[768,1024]{1,0:T(8,128)(2,1)S(1)} copy-done((bf16[768,1024]{1,0:T(8,128)(2,1)S(1)}, bf16[768,1024]{1,0:T(8,128)(2,1)}, u32[]{:S(2)}) %copy-start) | copy-done | bytes 1572888
  49.0 15.4 %shard_map.169 = (f32[1024,192]{1,0:T(8,128)S(1)}, bf16[8,208,128]{2,1,0:T(8,128)(2,1)}) custom-call(s32[1]{0:T(128)S(6)} %copy.22.count_ref, bf16[4,192,1024]{2,1,0:T(8,128)(2,1)S(1)} %bitcast.8, bf16[192,1024]{1,0:T(8,128)(2,1)} %get-tuple-element.12.own_ref, bf16[192,1024]{1,0:T(8,128)(2,1)S(1)} %get-tuple-element.13.first_ref, f32[1,192]{1,0:T(1,128)S(1)} %bitcast.15, ...), custom_call_target="tpu_custom_call" | custom-call | flops 3000000000 | bytes 2097152 | tf_op jit(solution)/shard_map/pallas_call | solution.py:428
  64.3 5.5 %all-to-all-start = ((bf16[8,208,128]{2,1,0:T(8,128)(2,1)}), bf16[8,208,128]{2,1,0:T(8,128)(2,1)S(1)}, u32[]{:S(2)}, u32[]{:S(2)}) async-start(bf16[8,208,128]{2,1,0:T(8,128)(2,1)} %get-tuple-element.21), calls=%async_computation | async-start | bytes 851968 | tf_op jit(solution)/shard_map/all_to_all | solution.py:457
  69.9 1.2 %copy.20 = f32[1024,192]{0,1:T(8,128)} copy(f32[1024,192]{1,0:T(8,128)S(1)} %get-tuple-element.22) | data formatting | bytes 1572864
  71.1 11.6 %all-to-all-done.got_ref = bf16[8,208,128]{2,1,0:T(8,128)(2,1)S(1)} async-done(((bf16[8,208,128]{2,1,0:T(8,128)(2,1)}), bf16[8,208,128]{2,1,0:T(8,128)(2,1)S(1)}, u32[]{:S(2)}, u32[]{:S(2)}) %all-to-all-start) | async-done | bytes 426016 | tf_op jit(solution)/shard_map/all_to_all | solution.py:457
  82.6 0.4 shard_map.170
  83.1 0.8 copy.21
  (11 shorter events, 0.0 us)
Async XLA Ops:
  7.2 40.4 %all-gather.3.cloned.1.call-start = ((), (), s32[]{:S(2)}) async-start(), calls=%async_computation.1 | async-start | bytes 1966080 | tf_op jit(solution)/shard_map/all_gather | solution.py:405
  9.1 0.9 %copy-start.2 = (bf16[192,576]{1,0:T(8,128)(2,1)S(1)}, bf16[192,576]{1,0:T(8,128)(2,1)}, u32[]{:S(2)}) copy-start(bf16[192,576]{1,0:T(8,128)(2,1)} %qkv_ref.2) | copy-start | bytes 663556
  10.0 0.9 copy-start.4
  10.9 0.7 copy-start.6
  11.6 0.7 copy-start.7
  12.3 0.7 copy-start.11
  13.0 0.7 copy-start.12
  13.6 11.4 %copy-start.14 = (bf16[768,192]{0,1:T(8,128)(2,1)S(1)}, bf16[768,192]{0,1:T(8,128)(2,1)}, u32[]{:S(2)}) copy-start(bf16[768,192]{0,1:T(8,128)(2,1)} %param.28) | copy-start | bytes 884740
  13.6 11.6 %copy-start.1 = (bf16[192,768]{1,0:T(8,128)(2,1)S(1)}, bf16[192,768]{1,0:T(8,128)(2,1)}, u32[]{:S(2)}) copy-start(bf16[192,768]{1,0:T(8,128)(2,1)} %up_ref.1) | copy-start | bytes 884740
  13.6 11.6 %copy-start.3 = (bf16[192,576]{1,0:T(8,128)(2,1)S(1)}, bf16[192,576]{1,0:T(8,128)(2,1)}, u32[]{:S(2)}) copy-start(bf16[192,576]{1,0:T(8,128)(2,1)} %qkv_ref.3) | copy-start | bytes 663556
  13.6 11.6 %copy-start.5 = (bf16[192,192]{1,0:T(8,128)(2,1)S(1)}, bf16[192,192]{1,0:T(8,128)(2,1)}, u32[]{:S(2)}) copy-start(bf16[192,192]{1,0:T(8,128)(2,1)} %out_ref.3) | copy-start | bytes 221188
  13.6 11.6 %copy-start.8 = (s32[512]{0:T(512)S(1)}, s32[512]{0:T(512)}, u32[]{:S(2)}) copy-start(s32[512]{0:T(512)} %param.29) | copy-start | bytes 6148
  13.7 11.6 %copy-start.9 = (s32[512,1]{0,1:T(1,128)S(1)}, s32[512,1]{0,1:T(1,128)}, u32[]{:S(2)}) copy-start(s32[512,1]{0,1:T(1,128)} %param.30) | copy-start | bytes 6148
  13.7 11.6 %copy-start.10 = (s32[512]{0:T(512)S(1)}, s32[512]{0:T(512)}, u32[]{:S(2)}) copy-start(s32[512]{0:T(512)} %param.31) | copy-start | bytes 6148
  25.3 22.3 %copy-start.13 = (f32[192]{0:T(256)S(1)}, f32[192]{0:T(256)}, u32[]{:S(2)}) copy-start(f32[192]{0:T(256)} %param.26) | copy-start | bytes 2308
  47.6 1.4 %copy-start = (bf16[768,1024]{1,0:T(8,128)(2,1)S(1)}, bf16[768,1024]{1,0:T(8,128)(2,1)}, u32[]{:S(2)}) copy-start(bf16[768,1024]{1,0:T(8,128)(2,1)} %all-gather.3.cloned.1.call-done) | copy-start | bytes 4718596
  64.3 18.3 %all-to-all-start = ((bf16[8,208,128]{2,1,0:T(8,128)(2,1)}), bf16[8,208,128]{2,1,0:T(8,128)(2,1)S(1)}, u32[]{:S(2)}, u32[]{:S(2)}) async-start(bf16[8,208,128]{2,1,0:T(8,128)(2,1)} %get-tuple-element.21), calls=%async_computation | async-start | bytes 851968 | tf_op jit(solution)/shard_map/all_to_all | solution.py:457
Sparse Core Ops, SparseCore 0:
  25.2 22.3 all-gather.2

commit v2 on v0

v2 whole, which is shorter than its diff:
```python
import functools
import math

import jax
import jax.numpy as jnp
from jax import lax
from jax.experimental import pallas as pl
from jax.experimental.pallas import tpu as pltpu
from jax.sharding import PartitionSpec as P

HEADS = 12
WIN = 32
VOX_DEV = 256
LANES = 128
FLAG = 16384.0
VMEM = 56 * 1024 * 1024
F32 = jnp.float32
BF16 = jnp.bfloat16
LOG2E = math.log2(math.e)


def iota(shape, dim):
    return lax.broadcasted_iota(jnp.int32, shape, dim)


def dot(a, b):
    return jnp.dot(a, b, preferred_element_type=F32)


def dot_t(a, b):
    return lax.dot_general(a, b, (((1,), (1,)), ((), ())), preferred_element_type=F32)


def eye(n):
    return (iota((n, n), 0) == iota((n, n), 1)).astype(BF16)


def transposed(a):
    return dot_t(eye(a.shape[1]), a).astype(BF16)


def tile(t):
    return slice(t * LANES, (t + 1) * LANES)


def head_order(chans):
    size = chans // HEADS
    cut = 8 * size
    j = iota((chans, 1), 0)
    high = j - cut
    low_src = (j % 8) * size + j // 8
    high_src = (8 + high % 4) * size + high // 8 + (size // 2) * ((high % 8) // 4)
    return jnp.where(j < cut, low_src, high_src)


def slot_of_lane(slots, run):
    t = iota((1, slots), 1)
    at, lane = t // LANES, t % LANES
    p = (4 * (at // run) + lane // WIN) * run + at % run
    return (lane % 8) * LANES + ((lane // 8) % 4) * WIN + p


def reorder(slots, run):
    return (iota((slots, slots), 0) == slot_of_lane(slots, run)).astype(BF16)


def norm_t(x, gain):
    inv = 1.0 / x.shape[0]
    mean = jnp.sum(x, 0, keepdims=True) * inv
    cent = x - mean
    var = jnp.sum(cent * cent, 0, keepdims=True) * inv
    return cent * lax.rsqrt(var + 1e-05) * gain


def load_all(pairs, sems):
    copies = [pltpu.make_async_copy(a, b, sems.at[n]) for n, (a, b) in enumerate(pairs)]
    for copy in copies:
        copy.start()
    for copy in copies:
        copy.wait()


def fold8(x, op):
    y = x[0]
    for n in range(1, x.shape[0]):
        y = op(y, x[n])
    for shift in (4, 2, 1):
        y = op(y, pltpu.roll(y, shift, 0))
    return y


def first_kernel(
    run, count_ref, nodes_hbm, ids_hbm, pos_hbm, gain_one_hbm, gain_two_hbm, qkv_hbm, out_hbm,
    first_ref, sent_ref, nodes_ref, ids_ref, pos_ref, gain_one_ref, gain_two_ref, qkv_ref, out_ref,
    sems, q_s, k_s, v_s, ctx_s, n_s
):
    load_all(
        [
            (nodes_hbm, nodes_ref),
            (ids_hbm, ids_ref),
            (pos_hbm, pos_ref),
            (gain_one_hbm, gain_one_ref),
            (gain_two_hbm, gain_two_ref),
            (qkv_hbm, qkv_ref),
            (out_hbm, out_ref),
        ],
        sems,
    )
    chans, slots = nodes_ref.shape
    tiles = slots // LANES
    size = chans // HEADS
    per = LANES // WIN
    count = count_ref[0]
    cols = jnp.concatenate(
        [pos_ref[...], gain_one_ref[...], gain_two_ref[...], jnp.zeros((3, chans), F32)], 0
    ).T
    qkv_t = transposed(qkv_ref[...])
    out_t = transposed(out_ref[...])
    ids = ids_ref[...]
    coords = []
    for axis in range(3):
        total = jnp.zeros(ids.shape, jnp.int32)
        for level in range(6):
            bit = jnp.bitwise_and(jnp.right_shift(ids, 3 * level + axis), 1)
            total = total + bit * 2**level
        coords.append(total.astype(F32) / 64.0 - 0.5)
    side = eye(LANES)
    spread = (
        iota((LANES, per * LANES), 0)
        == (iota((LANES, per * LANES), 1) // LANES) * WIN + iota((LANES, per * LANES), 1) % WIN
    ).astype(BF16)
    row_head = (iota((chans, LANES), 0) // size) % per
    own_head = row_head == iota((chans, LANES), 1) // WIN
    for t in range(tiles):
        at = tile(t)
        where = cols[:, 0:1] * coords[0][:, at]
        where = where + cols[:, 1:2] * coords[1][:, at]
        where = where + cols[:, 2:3] * coords[2][:, at]
        start = (nodes_ref[:, at].astype(F32) + where).astype(BF16)
        nodes_ref[:, at] = start
        normed = norm_t(start.astype(F32), cols[:, 3:4]).astype(BF16)
        n_s[:, at] = normed
        qv = dot(qkv_t, normed)
        q_s[t] = (qv[:chans] * (size**-0.5)).astype(BF16)
        wide = dot(qv[2 * chans :].astype(BF16), spread)
        for w in range(per):
            v_s[t, w] = jnp.where(own_head, wide[:, tile(w)], 0.0).astype(BF16)
        rows = dot_t(side, normed).astype(BF16)
        k_s[t] = dot_t(rows, qkv_t[chans : 2 * chans]).astype(BF16)

    lane_head = iota((WIN, chans), 1) // size
    window = iota((8, LANES), 1) // WIN
    rank = iota((WIN, LANES), 0) + WIN * (iota((WIN, LANES), 1) // WIN)

    def group(t, _):
        query = q_s[t]
        scores = None
        for w in range(per):
            keys = k_s[t, w * WIN : (w + 1) * WIN, :]
            by_head = jnp.concatenate(
                [jnp.where(lane_head == h, keys, jnp.zeros_like(keys)) for h in range(HEADS)], 0
            )
            got = dot(by_head, query).reshape(-1, 8, LANES)
            scores = got if w == 0 else jnp.where(window[None] == w, got, scores)
        mask = jnp.where(rank + t * LANES < count, 0.0, -1e9).astype(F32)
        mask = mask.reshape(WIN // 8, 8, LANES)
        probs, inverse = [], []
        for h in range(HEADS):
            mine = scores[h * (WIN // 8) : (h + 1) * (WIN // 8)] + mask
            top = fold8(mine, jnp.maximum)
            weight = jnp.exp(mine - top[None])
            inverse.append(1.0 / fold8(weight, jnp.add))
            probs.append(weight.reshape(WIN, LANES).astype(BF16))
        half = per * size
        parts = []
        for j in range(HEADS // per):
            weight = jnp.concatenate(probs[j * per : (j + 1) * per], 0)
            ctx = None
            for w in range(per):
                got = dot(v_s[t, w, j * half : (j + 1) * half, :], weight).reshape(-1, 8, LANES)
                ctx = got if w == 0 else jnp.where(window[None] == w, got, ctx)
            for h in range(per):
                block = ctx[h * (size // 8) : (h + 1) * (size // 8)] * inverse[j * per + h][None]
                parts.append(block.reshape(size, LANES))
        ctx_s[t] = jnp.concatenate(parts, 0).astype(BF16)
        return 0

    lax.fori_loop(0, tiles, group, 0, unroll=2)
    for t in range(tiles):
        at = tile(t)
        first = (nodes_ref[:, at].astype(F32) + dot(out_t, ctx_s[t])).astype(BF16)
        first_ref[:, at] = first
        normed = norm_t(first.astype(F32), cols[:, 4:5])
        kept = iota((1, LANES), 1) + t * LANES < count
        head = jnp.where((iota((16, LANES), 0) > 0) | kept, normed[:16], FLAG)
        n_s[:, at] = jnp.concatenate([head, normed[16:]], 0).astype(BF16)
    sent_ref[...] = dot(n_s[...], reorder(slots, run)).astype(BF16)


def tables_kernel(
    run, cap, qkv_hbm, out_hbm, up_hbm, slot_hbm, owner_hbm, voxel_hbm,
    qkv_t_ref, out_t_ref, up_t_ref, hot_ref, order_ref, label_ref,
    qkv_ref, out_ref, up_ref, slot_ref, owner_ref, voxel_ref, sems
):
    load_all(
        [
            (qkv_hbm, qkv_ref),
            (out_hbm, out_ref),
            (up_hbm, up_ref),
            (slot_hbm, slot_ref),
            (owner_hbm, owner_ref),
            (voxel_hbm, voxel_ref),
        ],
        sems,
    )
    votes = slot_ref.shape[1]
    slots, codes = hot_ref.shape
    owners = codes // cap
    chans = out_ref.shape[0]
    src = head_order(chans)
    src = jnp.concatenate([src, src + chans, src + 2 * chans], 0)
    shuffle = (src == iota((3 * chans, 3 * chans), 1)).astype(BF16)
    qkv_t_ref[...] = dot_t(shuffle, qkv_ref[...]).astype(BF16)
    out_t = transposed(out_ref[...])
    out_t_ref[...] = dot_t(out_t, shuffle[:chans, :chans]).astype(BF16)
    up_t_ref[...] = transposed(up_ref[...])
    order_ref[...] = reorder(slots, run)
    owner = jnp.bitwise_xor(owner_ref[...], lax.axis_index("tile"))
    hot = owner == iota((owners, votes), 0)
    upto = (iota((votes, votes), 0) <= iota((votes, votes), 1)).astype(BF16)
    rank = jnp.sum(jnp.where(hot, dot(hot.astype(BF16), upto), 0.0), 0, keepdims=True)
    code = owner * cap + rank.astype(jnp.int32) - 1
    member = (code == iota((codes, votes), 0)).astype(BF16)
    slot = slot_ref[...]
    row = iota((16, votes), 0)
    facts = jnp.where(
        row == 0,
        slot // 32,
        jnp.where(row == 1, slot % 32, jnp.where(row == 2, voxel_ref[...], 1)),
    )
    listed = dot_t(facts.astype(F32).astype(BF16), member)
    held = listed[3:4] > 0.5
    slot_of = jnp.where(held, listed[0:1] * 32.0 + listed[1:2], -1.0).astype(jnp.int32)
    hot_ref[...] = (slot_of == iota((slots, codes), 0)).astype(BF16)
    label = jnp.where(held, listed[2:3], -1.0)
    label_ref[...] = jnp.broadcast_to(label, label_ref.shape).astype(BF16)


def clean(block):
    head = block[:16].astype(F32)
    gone = head[0:1] > 0.5 * FLAG
    head = jnp.where((iota(head.shape, 0) == 0) & gone, 0.0, head)
    return jnp.concatenate([head.astype(BF16), block[16:]], 0), gone


def partial_attend(run, unit, blocks, kv_t, q_s, k_s, v_s, m_s, s_s, top_s, sum_s, acc_s, fresh):
    rows8 = q_s.shape[1]
    chans = 8 * rows8
    cut = 2 * rows8 // 3
    for n, block_ref in enumerate(blocks):
        for r in range(run):
            block, gone = clean(block_ref[:, tile(unit * run + r)])
            kv = dot(kv_t, block)
            k_s[n * run + r] = kv[:chans].reshape(rows8, 8, LANES)
            v_s[n * run + r] = kv[chans:].reshape(rows8, 8, LANES)
            m_s[n * run + r] = jnp.broadcast_to(jnp.where(gone, -1e9, 0.0), (8, LANES))
    keys = len(blocks) * run

    def one(r, _):
        t = unit * run + r
        query = q_s[t]

        def score(key, top):
            prod = query * k_s[key]
            a = jnp.sum(prod[:cut], 0)
            b = jnp.sum(prod[cut:], 0)
            b = b + pltpu.roll(b, 4, 0)
            mask = m_s[key]
            a = a + mask
            b = b + mask
            s_s[key, 0] = a
            s_s[key, 1] = b
            return jnp.maximum(top[0], a), jnp.maximum(top[1], b)

        if fresh:
            low = jnp.full((8, LANES), -3e38, F32)
            old = (low, low)
        else:
            old = (top_s[t, 0], top_s[t, 1])
        top_a, top_b = lax.fori_loop(0, keys, score, old, unroll=4)

        def gather(key, carry):
            sum_a, sum_b, acc_a, acc_b = carry
            pa = jnp.exp2(s_s[key, 0] - top_a)
            pb = jnp.exp2(s_s[key, 1] - top_b)
            value = v_s[key]
            return (
                sum_a + pa,
                sum_b + pb,
                acc_a + pa[None] * value[:cut],
                acc_b + pb[None] * value[cut:],
            )

        if fresh:
            zero = jnp.zeros((8, LANES), F32)
            held = (
                zero,
                zero,
                jnp.zeros((cut, 8, LANES), F32),
                jnp.zeros((rows8 - cut, 8, LANES), F32),
            )
        else:
            fade_a = jnp.exp2(old[0] - top_a)
            fade_b = jnp.exp2(old[1] - top_b)
            acc = acc_s[t]
            held = (
                sum_s[t, 0] * fade_a,
                sum_s[t, 1] * fade_b,
                acc[:cut] * fade_a[None],
                acc[cut:] * fade_b[None],
            )
        sum_a, sum_b, acc_a, acc_b = lax.fori_loop(0, keys, gather, held, unroll=4)
        return t, top_a, top_b, sum_a, sum_b, acc_a, acc_b

    return one


def near_kernel(
    run, own_ref, near_ref, qkv_t_ref, q_ref, top_ref, sum_ref, acc_ref, k_s, v_s, m_s, s_s
):
    chans, slots = own_ref.shape
    tiles = slots // LANES
    scale = (chans // HEADS) ** -0.5 * LOG2E
    q_t = qkv_t_ref[:chans, :]
    for t in range(tiles):
        own, _ = clean(own_ref[:, tile(t)])
        q_ref[t] = (dot(q_t, own) * scale).reshape(chans // 8, 8, LANES)
    for unit in range(tiles // run):
        one = partial_attend(
            run, unit, [own_ref, near_ref], qkv_t_ref[chans:, :], q_ref, k_s, v_s, m_s, s_s,
            None, None, None, True
        )

        def step(r, _, one=one):
            t, top_a, top_b, sum_a, sum_b, acc_a, acc_b = one(r, 0)
            top_ref[t, 0] = top_a
            top_ref[t, 1] = top_b
            sum_ref[t, 0] = sum_a
            sum_ref[t, 1] = sum_b
            acc_ref[t] = jnp.concatenate([acc_a, acc_b], 0)
            return 0

        lax.fori_loop(0, run, step, 0)


def second_kernel(
    run, cap, far, count_ref, *refs
):
    blocks, refs = refs[:far], refs[far:]
    (
        first_ref, q_ref, top_ref, sum_ref, acc_ref, gain_ref, qkv_t_ref, out_t_ref, up_t_ref,
        down_hbm, hot_ref, order_ref, label_ref
    ) = refs[:13]
    chans, slots = first_ref.shape
    codes = hot_ref.shape[1]
    owners = codes // cap
    feat_ref, votes_refs = refs[13], refs[14 : 14 + owners]
    k_s, v_s, m_s, s_s, ctx_s, bf_s, down_ref, sem = refs[14 + owners :]
    load_down = pltpu.make_async_copy(down_hbm, down_ref, sem)
    load_down.start()
    tiles = slots // LANES
    count = count_ref[0]
    for unit in range(tiles // run):
        one = partial_attend(
            run, unit, blocks, qkv_t_ref[chans:, :], q_ref, k_s, v_s, m_s, s_s,
            top_ref, sum_ref, acc_ref, False
        )

        def step(r, _, one=one):
            t, _, _, sum_a, sum_b, acc_a, acc_b = one(r, 0)
            ctx = jnp.concatenate([acc_a / sum_a[None], acc_b / sum_b[None]], 0)
            ctx_s[t] = ctx.reshape(chans, LANES).astype(BF16)
            return 0

        lax.fori_loop(0, run, step, 0)
    ctx = dot_t(
        jnp.concatenate([ctx_s[t] for t in range(tiles)], 1), order_ref[...]
    ).astype(BF16)
    gain = jnp.concatenate([gain_ref[...], jnp.zeros((7, chans), F32)], 0).T[:, 0:1]
    load_down.wait()
    for t in range(tiles):
        at = tile(t)
        second = first_ref[:, at].astype(F32) + dot(out_t_ref[...], ctx[:, at])
        inner = norm_t(second, gain).astype(BF16)
        hidden = jax.nn.gelu(dot(up_t_ref[...], inner)).astype(BF16)
        third = second + dot(down_ref[...], hidden)
        third = jnp.where(iota((1, LANES), 1) + t * LANES < count, third, 0.0)
        feat_ref[:, at] = third
        bf_s[:, at] = third.astype(BF16)
    picked = dot(bf_s[...], hot_ref[...]).astype(BF16)
    for o in range(owners):
        votes_refs[o][:chans, :] = picked[:, o * cap : (o + 1) * cap]
        votes_refs[o][chans:, :] = label_ref[:, o * cap : (o + 1) * cap]


def sums_kernel(*refs):
    got, out_ref = refs[:-1], refs[-1]
    chans, voxels = out_ref.shape
    cap = got[0].shape[1]
    total = jnp.zeros(out_ref.shape, F32)
    for ref in got:
        label = ref[chans:, :].astype(F32)[0:1]
        hot = (label == iota((voxels, cap), 0).astype(F32)).astype(BF16)
        total = total + dot_t(ref[:chans, :], hot)
    out_ref[...] = total


def call(kernel, outs, scratch, flops, spaces):
    return pl.pallas_call(
        kernel,
        out_shape=outs,
        in_specs=[
            pl.BlockSpec(memory_space={"s": pltpu.SMEM, "v": pltpu.VMEM, "a": pl.ANY}[c])
            for c in spaces
        ],
        out_specs=[pl.BlockSpec(memory_space=pltpu.VMEM)] * len(outs),
        scratch_shapes=scratch,
        compiler_params=pltpu.CompilerParams(vmem_limit_bytes=VMEM),
        cost_estimate=pl.CostEstimate(flops=flops, bytes_accessed=2 << 20, transcendentals=0),
    )


def turned(x, axis, bit):
    n = lax.axis_size(axis)
    return lax.ppermute(x, axis, [(i, i ^ bit) for i in range(n)])


def body(
    nodes,
    node_ids,
    node_count,
    pos_weight,
    gain_one,
    qkv_one,
    out_one,
    gain_two,
    qkv_two,
    out_two,
    gain_three,
    w_up,
    w_down,
    vote_slot,
    vote_owner,
    vote_voxel,
):
    slots, chans = nodes.shape
    groups, owners = lax.axis_size("grp"), lax.axis_size("tile")
    run = WIN // groups
    votes = vote_slot.shape[0]
    cap = 2 * votes // owners
    codes = owners * cap
    tiles = slots // LANES
    rows8 = chans // 8
    hidden = w_up.shape[1]
    per = LANES // WIN
    sds = jax.ShapeDtypeStruct
    vmem = pltpu.VMEM
    dma = pltpu.SemaphoreType.DMA

    first, sent = call(
        functools.partial(first_kernel, run),
        [sds((chans, slots), BF16), sds((chans, slots), BF16)],
        [
            vmem((chans, slots), BF16),
            vmem((1, slots), jnp.int32),
            vmem((3, chans), F32),
            vmem((1, chans), F32),
            vmem((1, chans), F32),
            vmem((chans, 3 * chans), BF16),
            vmem((chans, chans), BF16),
            dma((7,)),
            vmem((tiles, chans, LANES), BF16),
            vmem((tiles, LANES, chans), BF16),
            vmem((tiles, per, chans, LANES), BF16),
            vmem((tiles, chans, LANES), BF16),
            vmem((chans, slots), BF16),
        ],
        2_000_000_000,
        "saaaaaaa",
    )(
        node_count,
        nodes.T,
        node_ids.reshape(1, slots),
        pos_weight,
        gain_one.reshape(1, chans),
        gain_two.reshape(1, chans),
        qkv_one,
        out_one,
    )
    near = turned(sent, "grp", 1)
    bit = groups // 2
    far = []
    while bit > 1:
        far += [turned(block, "grp", bit) for block in [sent] + far]
        bit //= 2
    far += [turned(block, "grp", 1) for block in far]
    qkv_t, out_t, up_t, hot, order, label = call(
        functools.partial(tables_kernel, run, cap),
        [
            sds((3 * chans, chans), BF16),
            sds((chans, chans), BF16),
            sds((hidden, chans), BF16),
            sds((slots, codes), BF16),
            sds((slots, slots), BF16),
            sds((16, codes), BF16),
        ],
        [
            vmem((chans, 3 * chans), BF16),
            vmem((chans, chans), BF16),
            vmem((chans, hidden), BF16),
            vmem((1, votes), jnp.int32),
            vmem((1, votes), jnp.int32),
            vmem((1, votes), jnp.int32),
            dma((6,)),
        ],
        2_000_000_000,
        "aaaaaa",
    )(
        qkv_two,
        out_two,
        w_up,
        vote_slot.reshape(1, votes),
        vote_owner.reshape(1, votes),
        vote_voxel.reshape(1, votes),
    )
    state = [
        sds((tiles, rows8, 8, LANES), F32),
        sds((tiles, 2, 8, LANES), F32),
        sds((tiles, 2, 8, LANES), F32),
        sds((tiles, rows8, 8, LANES), F32),
    ]

    def key_scratch(keys):
        return [
            vmem((keys, rows8, 8, LANES), F32),
            vmem((keys, rows8, 8, LANES), F32),
            vmem((keys, 8, LANES), F32),
            vmem((keys, 2, 8, LANES), F32),
        ]

    query, top, total, acc = call(
        functools.partial(near_kernel, run),
        state,
        key_scratch(2 * run),
        3_000_000_000,
        "vvv",
    )(sent, near, qkv_t)
    features_t, *ballots = call(
        functools.partial(second_kernel, run, cap, len(far)),
        [sds((chans, slots), F32)] + [sds((chans + 16, cap), BF16)] * owners,
        key_scratch(len(far) * run)
        + [
            vmem((tiles, chans, LANES), BF16),
            vmem((chans, slots), BF16),
            vmem((chans, hidden), BF16),
            dma,
        ],
        3_000_000_000,
        "s" + "v" * len(far) + "vvvvvvvvvavvv",
    )(
        node_count,
        *far,
        first,
        query,
        top,
        total,
        acc,
        gain_three.reshape(1, chans),
        qkv_t,
        out_t,
        up_t,
        w_down.T,
        hot,
        order,
        label,
    )
    got = [ballots[0]] + [turned(ballots[k], "tile", k) for k in range(owners - 1, 0, -1)]
    (sums_t,) = call(
        sums_kernel, [sds((chans, VOX_DEV), F32)], [], 200_000_000, "v" * owners
    )(*got)
    return (features_t.T, sums_t.T)


def solution(mesh):
    in_specs = (
        P(("grp", "tile"), None),
        P(("grp", "tile")),
        P(("grp", "tile")),
        P(),
        P(),
        P(),
        P(),
        P(),
        P(),
        P(),
        P(),
        P(),
        P(),
        P(("grp", "tile")),
        P(("grp", "tile"), None),
        P(("grp", "tile")),
    )
    out_specs = (P(("grp", "tile"), None), P(("grp", "tile"), None))
    return jax.shard_map(body, mesh=mesh, in_specs=in_specs, out_specs=out_specs, check_vma=False)
```

time: 106 us -> 71.1 us (0.67)
  Pallas kernels: 0 us -> 39.1 us
  matrix products: 21.9 us -> 0 us
  local copies, waits for them, and re-layouts: 20.9 us -> 2.2 us
  other arithmetic: 16.6 us -> 0 us
  waiting for transfers between devices: 22 us -> 13.8 us
  starting transfers between devices: 22.4 us -> 14.4 us
    pallas_call x0 -> x5, Pallas kernels: none -> 39.1 us  [the longest x1 14.2 us: body(): call(functools.partial(second_kernel, run, cap, len(far)), [sds((chans, s...]
    all_to_all x5 -> x0, starting transfers between devices: 22.4 us -> none  [the longest x1 6.22 us: body(): lax.all_to_all(labels.reshape(tiles, capacity), 'tile', split_axis=0, con...]
    all_to_all x5 -> x0, waiting for transfers between devices: 22 us -> none  [the longest x1 9.72 us: body(): lax.all_to_all(buffer.reshape(tiles, capacity, width), 'tile', split_axis...]
    dot_general x11 -> x0, matrix products: 21.9 us -> none  [the longest x2 8.76 us: attend(): jnp.einsum('nqhd,nkhd->nhqk', query, keys, preferred_element_type=jnp.flo...]
    ppermute x0 -> x10, starting transfers between devices: none -> 14.4 us  [turned(): return lax.ppermute(x, axis, [(i, i ^ bit) for i in range(n)])]
    ppermute x0 -> x10, waiting for transfers between devices: none -> 13.8 us  [turned(): return lax.ppermute(x, axis, [(i, i ^ bit) for i in range(n)])]
    sub x4 -> x0, other arithmetic: 13.3 us -> none  [the longest x2 12.6 us: attend(): probs = jax.nn.softmax(scores, -1).astype(jnp.bfloat16)]
    convert_element_type x6 -> x0, local copies, waits for them, and re-layouts: 8.54 us -> none  [the longest x2 6.71 us: attend(): jnp.einsum('nwc,cd->nwd', inner, w_qkv, preferred_element_type=jnp.float32)]
  transfers between devices with their start and end apart: 5 -> 10, of which waited for: 4 -> 7; matrix products, arithmetic and copies ran while one was open for 35% -> 0% of each run, Pallas kernels for 0% -> 17%
where the time goes in v2:
time: 71.1 us; the launch traced here: 70.9 us
  Pallas kernels  39.1 us (55%)
  starting transfers between devices  14.4 us (20%)
  waiting for transfers between devices  13.8 us (19%)
  local copies, waits for them, and re-layouts  2.2 us (3%)
  between operations  1.36 us (2%)
    ppermute x10, starting transfers between devices, turned(): return lax.ppermute(x, axis, [(i, i ^ bit) for i in range(n)])  14.4 us
    pallas_call x1, Pallas kernels, body(): call(functools.partial(second_kernel, run, cap, len(far)), [sds((chans, s...  14.2 us
    ppermute x10, waiting for transfers between devices, turned(): return lax.ppermute(x, axis, [(i, i ^ bit) for i in range(n)])  13.8 us
    pallas_call x1, Pallas kernels, body(): call(functools.partial(first_kernel, run), [sds((chans, slots), BF16), sd...  10.9 us
    pallas_call x1, Pallas kernels, body(): call(functools.partial(near_kernel, run), state, key_scratch(2 * run), 30...  6.22 us
    pallas_call x1, Pallas kernels, body(): call(functools.partial(tables_kernel, run, cap), [sds((3 * chans, chans),...  5.73 us
    unnamed x20, local copies, waits for them, and re-layouts  2.2 us
    pallas_call x1, Pallas kernels, body(): call(sums_kernel, [sds((chans, VOX_DEV), F32)], [], 200000000, 'v' * owners)  2.04 us
  transfers between devices with their start and end apart: 10, of which 7 were waited for; matrix products, arithmetic and copies ran while one was open for 0% of the time, Pallas kernels for 17%

profile of v2, /device:TPU:0, one launch (start us, length us, event | category | flops | bytes accessed | tf_op | source)
XLA Modules:
  0.0 70.9 jit_solution(16087700461822361587)
XLA Ops:
  1.3 10.9 %shard_map.167 = (bf16[192,1024]{1,0:T(8,128)(2,1)}, bf16[192,1024]{1,0:T(8,128)(2,1)}) custom-call(s32[1]{0:T(128)S(6)} %copy.18.count_ref, bf16[192,1024]{1,0:T(8,128)(2,1)} %bitcast.11, s32[1,1024]{1,0:T(1,128)} %bitcast.13, f32[3,192]{1,0:T(4,128)} %pos_hbm.1, f32[1,192]{1,0:T(1,128)} %bitcast.17, f32[1,192]{1,0:T(1,128)} %bitcast.18, ...), custom_call_target="tpu_custom_call" | custom-call | flops 2000000000 | bytes 2097152 | tf_op jit(solution)/shard_map/pallas_call | solution.py:470
  12.2 3.0 %collective-permute-start = (bf16[192,1024]{1,0:T(8,128)(2,1)}, bf16[192,1024]{1,0:T(8,128)(2,1)S(1)}, u32[]{:S(2)}, u32[]{:S(2)}) collective-permute-start(bf16[192,1024]{1,0:T(8,128)(2,1)} %get-tuple-element.23.own_ref), channel_id=1, source_target_pairs={{0,16},{8,24},{16,0},{24,8},{1,17},{9,25},{17,1},{25,9},{2,18},{10... | collective-permute-start | bytes 1179656 | tf_op jit(solution)/shard_map/ppermute | solution.py:435
  15.2 0.0 collective-permute-start.2
  15.2 9.3 %collective-permute-done.refs_0_ = bf16[192,1024]{1,0:T(8,128)(2,1)S(1)} collective-permute-done((bf16[192,1024]{1,0:T(8,128)(2,1)}, bf16[192,1024]{1,0:T(8,128)(2,1)S(1)}, u32[]{:S(2)}, u32[]{:S(2)}) %collective-permute-start) | collective-permute-done | bytes 393248 | tf_op jit(solution)/shard_map/ppermute | solution.py:435
  24.5 0.0 collective-permute-start.1
  24.5 5.7 %shard_map.168 = (bf16[576,192]{1,0:T(8,128)(2,1)}, bf16[192,192]{1,0:T(8,128)(2,1)}, bf16[768,192]{1,0:T(8,128)(2,1)}, bf16[1024,1024]{1,0:T(8,128)(2,1)}, bf16...) custom-call(bf16[192,576]{1,0:T(8,128)(2,1)} %qkv_hbm.3, bf16[192,192]{1,0:T(8,128)(2,1)} %out_hbm.3, ...), custom_call_target="tpu_custom_call" | custom-call | flops 2000000000 | bytes 2097152 | tf_op jit(solution)/shard_map/pallas_call | solution.py:507
  30.3 0.0 copy-done
  30.3 0.0 collective-permute-done.2.near_ref
  30.3 0.0 copy-start.2
  30.3 0.8 %copy-done.2 = bf16[192,1024]{1,0:T(8,128)(2,1)} copy-done((bf16[192,1024]{1,0:T(8,128)(2,1)}, bf16[192,1024]{1,0:T(8,128)(2,1)S(1)}, u32[]{:S(2)}) %copy-start.2) | copy-done | bytes 393240
  31.1 6.2 %shard_map.169 = (f32[8,24,8,128]{3,2,1,0:T(8,128)}, f32[8,2,8,128]{3,2,1,0:T(8,128)}, f32[8,2,8,128]{3,2,1,0:T(8,128)}, f32[8,24,8,128]{3,2,1,0:T(8,128)}) custom-call(bf16[192,1024]{1,0:T(8,128)(2,1)} %get-tuple-element.23.own_ref, bf16[192,1024]{1,0:T(8,128)(2,1)} %copy-done.2, bf16[576,192]{1,0:T(8,128)(2,1)} %get-tuple-element.25.qkv_t_ref.refs_8_), custom_call_target="tpu_custom_call" | custom-call | flops 3000000000 | bytes 2097152 | tf_op jit(solution)/shard_map/pallas_call | solution.py:551
  37.3 0.0 collective-permute-done.1.refs_1_
  37.3 0.8 %copy-done.1 = bf16[192,1024]{1,0:T(8,128)(2,1)} copy-done((bf16[192,1024]{1,0:T(8,128)(2,1)}, bf16[192,1024]{1,0:T(8,128)(2,1)S(1)}, u32[]{:S(2)}) %copy-start.1) | copy-done | bytes 393240
  38.1 14.2 %shard_map.170 = (f32[192,1024]{1,0:T(8,128)}, bf16[208,128]{1,0:T(8,128)(2,1)}, bf16[208,128]{1,0:T(8,128)(2,1)}, bf16[208,128]{1,0:T(8,128)(2,1)}, bf16[208,12...) custom-call(s32[1]{0:T(128)S(6)} %copy.18.count_ref, ...), custom_call_target="tpu_custom_call" | custom-call | flops 3000000000 | bytes 2097152 | tf_op jit(solution)/shard_map/pallas_call | solution.py:558
  52.4 4.9 %collective-permute-start.3 = (bf16[208,128]{1,0:T(8,128)(2,1)}, bf16[208,128]{1,0:T(8,128)(2,1)S(1)}, u32[]{:S(2)}, u32[]{:S(2)}) collective-permute-start(bf16[208,128]{1,0:T(8,128)(2,1)} %get-tuple-element.37), channel_id=1, source_target_pairs={{0,7},{1,6},{2,5},{3,4},{4,3},{5,2},{6,1},{7,0},{8,15},{9,14},{10,... | collective-permute-start | bytes 159752 | tf_op jit(solution)/shard_map/ppermute | solution.py:435
  57.3 0.2 collective-permute-start.4
  57.5 0.7 %collective-permute-start.5 = (bf16[208,128]{1,0:T(8,128)(2,1)}, bf16[208,128]{1,0:T(8,128)(2,1)S(1)}, u32[]{:S(2)}, u32[]{:S(2)}) collective-permute-start(bf16[208,128]{1,0:T(8,128)(2,1)} %get-tuple-element.39), channel_id=1, source_target_pairs={{0,5},{1,4},{2,7},{3,6},{4,1},{5,0},{6,3},{7,2},{8,13},{9,12},{10,... | collective-permute-start | bytes 159752 | tf_op jit(solution)/shard_map/ppermute | solution.py:435
  58.2 2.0 %collective-permute-start.6 = (bf16[208,128]{1,0:T(8,128)(2,1)}, bf16[208,128]{1,0:T(8,128)(2,1)S(1)}, u32[]{:S(2)}, u32[]{:S(2)}) collective-permute-start(bf16[208,128]{1,0:T(8,128)(2,1)} %get-tuple-element.40), channel_id=1, source_target_pairs={{0,4},{1,5},{2,6},{3,7},{4,0},{5,1},{6,2},{7,3},{8,12},{9,13},{10,... | collective-permute-start | bytes 159752 | tf_op jit(solution)/shard_map/ppermute | solution.py:435
  60.3 2.3 %collective-permute-start.7 = (bf16[208,128]{1,0:T(8,128)(2,1)}, bf16[208,128]{1,0:T(8,128)(2,1)S(1)}, u32[]{:S(2)}, u32[]{:S(2)}) collective-permute-start(bf16[208,128]{1,0:T(8,128)(2,1)} %get-tuple-element.41), channel_id=1, source_target_pairs={{0,3},{1,2},{2,1},{3,0},{4,7},{5,6},{6,5},{7,4},{8,11},{9,10},{10,... | collective-permute-start | bytes 159752 | tf_op jit(solution)/shard_map/ppermute | solution.py:435
  62.6 0.0 collective-permute-done.3.refs_1_
  62.6 0.8 %collective-permute-start.8 = (bf16[208,128]{1,0:T(8,128)(2,1)}, bf16[208,128]{1,0:T(8,128)(2,1)S(1)}, u32[]{:S(2)}, u32[]{:S(2)}) collective-permute-start(bf16[208,128]{1,0:T(8,128)(2,1)} %get-tuple-element.42), channel_id=1, source_target_pairs={{0,2},{1,3},{2,0},{3,1},{4,6},{5,7},{6,4},{7,5},{8,10},{9,11},{10,... | collective-permute-start | bytes 159752 | tf_op jit(solution)/shard_map/ppermute | solution.py:435
  63.3 0.5 collective-permute-done.4.refs_2_
  63.9 0.4 collective-permute-start.9
  64.3 1.8 %collective-permute-done.5.refs_3_ = bf16[208,128]{1,0:T(8,128)(2,1)S(1)} collective-permute-done((bf16[208,128]{1,0:T(8,128)(2,1)}, bf16[208,128]{1,0:T(8,128)(2,1)S(1)}, u32[]{:S(2)}, u32[]{:S(2)}) %collective-permute-start.5) | collective-permute-done | bytes 53280 | tf_op jit(solution)/shard_map/ppermute | solution.py:435
  66.1 1.0 %collective-permute-done.6.refs_4_ = bf16[208,128]{1,0:T(8,128)(2,1)S(1)} collective-permute-done((bf16[208,128]{1,0:T(8,128)(2,1)}, bf16[208,128]{1,0:T(8,128)(2,1)S(1)}, u32[]{:S(2)}, u32[]{:S(2)}) %collective-permute-start.6) | collective-permute-done | bytes 53280 | tf_op jit(solution)/shard_map/ppermute | solution.py:435
  67.1 0.5 collective-permute-done.7.refs_5_
  67.6 0.3 collective-permute-done.8.refs_6_
  67.8 0.4 collective-permute-done.9.refs_7_
  68.2 0.0 copy-done.3
  68.2 0.2 copy-done.8
  68.5 0.4 copy-done.9
  68.8 2.0 %shard_map.171 = f32[192,256]{1,0:T(8,128)} custom-call(bf16[208,128]{1,0:T(8,128)(2,1)} %get-tuple-element.36.refs_0_, bf16[208,128]{1,0:T(8,128)(2,1)} %copy-done.3, bf16[208,128]{1,0:T(8,128)(2,1)} %copy-done.4, bf16[208,128]{1,0:T(8,128)(2,1)} %copy-done.5, bf16[208,128]{1,0:T(8,128)(2,1)} %copy-done.6, bf16[208,128]{1,0:T(8,128)(2,1)} %copy-done.7, ...), custom_call_target="tpu_custom_call" | custom-call | flops 200000000 | bytes 2097152 | tf_op jit(solution)/shard_map/pallas_call | solution.py:588
  (13 shorter events, 0.0 us)
Async XLA Ops:
  12.2 12.3 %collective-permute-start = (bf16[192,1024]{1,0:T(8,128)(2,1)}, bf16[192,1024]{1,0:T(8,128)(2,1)S(1)}, u32[]{:S(2)}, u32[]{:S(2)}) collective-permute-start(bf16[192,1024]{1,0:T(8,128)(2,1)} %get-tuple-element.23.own_ref), channel_id=1, source_target_pairs={{0,16},{8,24},{16,0},{24,8},{1,17},{9,25},{17,1},{25,9},{2,18},{10... | collective-permute-start | bytes 1179656 | tf_op jit(solution)/shard_map/ppermute | solution.py:435
  15.2 15.1 %collective-permute-start.2 = (bf16[192,1024]{1,0:T(8,128)(2,1)}, bf16[192,1024]{1,0:T(8,128)(2,1)S(1)}, u32[]{:S(2)}, u32[]{:S(2)}) collective-permute-start(bf16[192,1024]{1,0:T(8,128)(2,1)} %get-tuple-element.23.own_ref), channel_id=1, source_target_pairs={{0,8},{8,0},{16,24},{24,16},{1,9},{9,1},{17,25},{25,17},{2,10},{10... | collective-permute-start | bytes 1179656 | tf_op jit(solution)/shard_map/ppermute | solution.py:435
  24.5 5.7 %copy-start = (bf16[192,1024]{1,0:T(8,128)(2,1)}, bf16[192,1024]{1,0:T(8,128)(2,1)S(1)}, u32[]{:S(2)}) copy-start(bf16[192,1024]{1,0:T(8,128)(2,1)S(1)} %collective-permute-done.refs_0_) | copy-start | bytes 1179652
  24.5 12.8 %collective-permute-start.1 = (bf16[192,1024]{1,0:T(8,128)(2,1)S(1)}, bf16[192,1024]{1,0:T(8,128)(2,1)S(1)}, u32[]{:S(2)}, u32[]{:S(2)}) collective-permute-start(bf16[192,1024]{1,0:T(8,128)(2,1)S(1)} %collective-permute-done.refs_0_), channel_id=1, source_target_pairs={{0,8},{8,0},{16,24},{24,16},{1,9},{9,1},{17,25},{25,17},{2,10},{10... | collective-permute-start | bytes 1179656 | tf_op jit(solution)/shard_map/ppermute | solution.py:435
  30.3 0.8 %copy-start.2 = (bf16[192,1024]{1,0:T(8,128)(2,1)}, bf16[192,1024]{1,0:T(8,128)(2,1)S(1)}, u32[]{:S(2)}) copy-start(bf16[192,1024]{1,0:T(8,128)(2,1)S(1)} %collective-permute-done.2.near_ref) | copy-start | bytes 1179652
  37.3 0.8 %copy-start.1 = (bf16[192,1024]{1,0:T(8,128)(2,1)}, bf16[192,1024]{1,0:T(8,128)(2,1)S(1)}, u32[]{:S(2)}) copy-start(bf16[192,1024]{1,0:T(8,128)(2,1)S(1)} %collective-permute-done.1.refs_1_) | copy-start | bytes 1179652
  52.4 10.2 %collective-permute-start.3 = (bf16[208,128]{1,0:T(8,128)(2,1)}, bf16[208,128]{1,0:T(8,128)(2,1)S(1)}, u32[]{:S(2)}, u32[]{:S(2)}) collective-permute-start(bf16[208,128]{1,0:T(8,128)(2,1)} %get-tuple-element.37), channel_id=1, source_target_pairs={{0,7},{1,6},{2,5},{3,4},{4,3},{5,2},{6,1},{7,0},{8,15},{9,14},{10,... | collective-permute-start | bytes 159752 | tf_op jit(solution)/shard_map/ppermute | solution.py:435
  57.3 6.6 %collective-permute-start.4 = (bf16[208,128]{1,0:T(8,128)(2,1)}, bf16[208,128]{1,0:T(8,128)(2,1)S(1)}, u32[]{:S(2)}, u32[]{:S(2)}) collective-permute-start(bf16[208,128]{1,0:T(8,128)(2,1)} %get-tuple-element.38), channel_id=1, source_target_pairs={{0,6},{1,7},{2,4},{3,5},{4,2},{5,3},{6,0},{7,1},{8,14},{9,15},{10,... | collective-permute-start | bytes 159752 | tf_op jit(solution)/shard_map/ppermute | solution.py:435
  57.5 8.6 %collective-permute-start.5 = (bf16[208,128]{1,0:T(8,128)(2,1)}, bf16[208,128]{1,0:T(8,128)(2,1)S(1)}, u32[]{:S(2)}, u32[]{:S(2)}) collective-permute-start(bf16[208,128]{1,0:T(8,128)(2,1)} %get-tuple-element.39), channel_id=1, source_target_pairs={{0,5},{1,4},{2,7},{3,6},{4,1},{5,0},{6,3},{7,2},{8,13},{9,12},{10,... | collective-permute-start | bytes 159752 | tf_op jit(solution)/shard_map/ppermute | solution.py:435
  58.2 8.9 %collective-permute-start.6 = (bf16[208,128]{1,0:T(8,128)(2,1)}, bf16[208,128]{1,0:T(8,128)(2,1)S(1)}, u32[]{:S(2)}, u32[]{:S(2)}) collective-permute-start(bf16[208,128]{1,0:T(8,128)(2,1)} %get-tuple-element.40), channel_id=1, source_target_pairs={{0,4},{1,5},{2,6},{3,7},{4,0},{5,1},{6,2},{7,3},{8,12},{9,13},{10,... | collective-permute-start | bytes 159752 | tf_op jit(solution)/shard_map/ppermute | solution.py:435
  60.3 7.3 %collective-permute-start.7 = (bf16[208,128]{1,0:T(8,128)(2,1)}, bf16[208,128]{1,0:T(8,128)(2,1)S(1)}, u32[]{:S(2)}, u32[]{:S(2)}) collective-permute-start(bf16[208,128]{1,0:T(8,128)(2,1)} %get-tuple-element.41), channel_id=1, source_target_pairs={{0,3},{1,2},{2,1},{3,0},{4,7},{5,6},{6,5},{7,4},{8,11},{9,10},{10,... | collective-permute-start | bytes 159752 | tf_op jit(solution)/shard_map/ppermute | solution.py:435
  62.6 5.7 %copy-start.3 = (bf16[208,128]{1,0:T(8,128)(2,1)}, bf16[208,128]{1,0:T(8,128)(2,1)S(1)}, u32[]{:S(2)}) copy-start(bf16[208,128]{1,0:T(8,128)(2,1)S(1)} %collective-permute-done.3.refs_1_) | copy-start | bytes 159748
  62.6 5.3 %collective-permute-start.8 = (bf16[208,128]{1,0:T(8,128)(2,1)}, bf16[208,128]{1,0:T(8,128)(2,1)S(1)}, u32[]{:S(2)}, u32[]{:S(2)}) collective-permute-start(bf16[208,128]{1,0:T(8,128)(2,1)} %get-tuple-element.42), channel_id=1, source_target_pairs={{0,2},{1,3},{2,0},{3,1},{4,6},{5,7},{6,4},{7,5},{8,10},{9,11},{10,... | collective-permute-start | bytes 159752 | tf_op jit(solution)/shard_map/ppermute | solution.py:435
  63.9 4.4 %copy-start.4 = (bf16[208,128]{1,0:T(8,128)(2,1)}, bf16[208,128]{1,0:T(8,128)(2,1)S(1)}, u32[]{:S(2)}) copy-start(bf16[208,128]{1,0:T(8,128)(2,1)S(1)} %collective-permute-done.4.refs_2_) | copy-start | bytes 159748
  63.9 4.3 %collective-permute-start.9 = (bf16[208,128]{1,0:T(8,128)(2,1)}, bf16[208,128]{1,0:T(8,128)(2,1)S(1)}, u32[]{:S(2)}, u32[]{:S(2)}) collective-permute-start(bf16[208,128]{1,0:T(8,128)(2,1)} %get-tuple-element.43), channel_id=1, source_target_pairs={{0,1},{1,0},{2,3},{3,2},{4,5},{5,4},{6,7},{7,6},{8,9},{9,8},{10,11... | collective-permute-start | bytes 159752 | tf_op jit(solution)/shard_map/ppermute | solution.py:435
  66.1 2.2 %copy-start.5 = (bf16[208,128]{1,0:T(8,128)(2,1)}, bf16[208,128]{1,0:T(8,128)(2,1)S(1)}, u32[]{:S(2)}) copy-start(bf16[208,128]{1,0:T(8,128)(2,1)S(1)} %collective-permute-done.5.refs_3_) | copy-start | bytes 159748
  67.1 1.1 %copy-start.6 = (bf16[208,128]{1,0:T(8,128)(2,1)}, bf16[208,128]{1,0:T(8,128)(2,1)S(1)}, u32[]{:S(2)}) copy-start(bf16[208,128]{1,0:T(8,128)(2,1)S(1)} %collective-permute-done.6.refs_4_) | copy-start | bytes 159748
  67.6 0.7 copy-start.7
  67.8 0.6 copy-start.8
  68.2 0.6 copy-start.9

commit v3 on v2

--- a/solution.py
+++ b/solution.py
@@ -13,7 +13,7 @@
 VOX_DEV = 256
 LANES = 128
 FLAG = 16384.0
-VMEM = 56 * 1024 * 1024
+VMEM = 64 * 1024 * 1024 - 65536
 F32 = jnp.float32
 BF16 = jnp.bfloat16
 LOG2E = math.log2(math.e)
@@ -72,10 +72,14 @@
     return cent * lax.rsqrt(var + 1e-05) * gain
 
 
-def load_all(pairs, sems):
+def start_all(pairs, sems):
     copies = [pltpu.make_async_copy(a, b, sems.at[n]) for n, (a, b) in enumerate(pairs)]
     for copy in copies:
         copy.start()
+    return copies
+
+
+def wait_all(copies):
     for copy in copies:
         copy.wait()
 
@@ -92,9 +96,9 @@
 def first_kernel(
     run, count_ref, nodes_hbm, ids_hbm, pos_hbm, gain_one_hbm, gain_two_hbm, qkv_hbm, out_hbm,
     first_ref, sent_ref, nodes_ref, ids_ref, pos_ref, gain_one_ref, gain_two_ref, qkv_ref, out_ref,
-    sems, q_s, k_s, v_s, ctx_s, n_s
+    sems, qkv_s, q_s, k_s, v_s, ctx_s, n_s
 ):
-    load_all(
+    loads = start_all(
         [
             (nodes_hbm, nodes_ref),
             (ids_hbm, ids_ref),
@@ -111,19 +115,26 @@
     size = chans // HEADS
     per = LANES // WIN
     count = count_ref[0]
+    wait_all(loads[:5])
     cols = jnp.concatenate(
         [pos_ref[...], gain_one_ref[...], gain_two_ref[...], jnp.zeros((3, chans), F32)], 0
     ).T
-    qkv_t = transposed(qkv_ref[...])
-    out_t = transposed(out_ref[...])
     ids = ids_ref[...]
-    coords = []
+    start = None
     for axis in range(3):
         total = jnp.zeros(ids.shape, jnp.int32)
         for level in range(6):
             bit = jnp.bitwise_and(jnp.right_shift(ids, 3 * level + axis), 1)
             total = total + bit * 2**level
-        coords.append(total.astype(F32) / 64.0 - 0.5)
+        term = cols[:, axis : axis + 1] * (total.astype(F32) / 64.0 - 0.5)
+        start = term if start is None else start + term
+    start = (nodes_ref[...].astype(F32) + start).astype(BF16)
+    nodes_ref[...] = start
+    n_s[...] = norm_t(start.astype(F32), cols[:, 3:4]).astype(BF16)
+    wait_all(loads[5:])
+    qkv_t = transposed(qkv_ref[...])
+    out_t = transposed(out_ref[...])
+    qkv_s[...] = dot(qkv_t, n_s[...]).astype(BF16)
     side = eye(LANES)
     spread = (
         iota((LANES, per * LANES), 0)
@@ -132,21 +143,12 @@
     row_head = (iota((chans, LANES), 0) // size) % per
     own_head = row_head == iota((chans, LANES), 1) // WIN
     for t in range(tiles):
-        at = tile(t)
-        where = cols[:, 0:1] * coords[0][:, at]
-        where = where + cols[:, 1:2] * coords[1][:, at]
-        where = where + cols[:, 2:3] * coords[2][:, at]
-        start = (nodes_ref[:, at].astype(F32) + where).astype(BF16)
-        nodes_ref[:, at] = start
-        normed = norm_t(start.astype(F32), cols[:, 3:4]).astype(BF16)
-        n_s[:, at] = normed
-        qv = dot(qkv_t, normed)
-        q_s[t] = (qv[:chans] * (size**-0.5)).astype(BF16)
-        wide = dot(qv[2 * chans :].astype(BF16), spread)
+        q_s[t] = qkv_s[:chans, tile(t)] * jnp.asarray(size**-0.5, BF16)
+        k_s[t] = dot_t(side, qkv_s[chans : 2 * chans, tile(t)]).astype(BF16)
+    for t in range(tiles):
+        wide = dot(qkv_s[2 * chans :, tile(t)], spread)
         for w in range(per):
             v_s[t, w] = jnp.where(own_head, wide[:, tile(w)], 0.0).astype(BF16)
-        rows = dot_t(side, normed).astype(BF16)
-        k_s[t] = dot_t(rows, qkv_t[chans : 2 * chans]).astype(BF16)
 
     lane_head = iota((WIN, chans), 1) // size
     window = iota((8, LANES), 1) // WIN
@@ -186,15 +188,14 @@
         return 0
 
     lax.fori_loop(0, tiles, group, 0, unroll=2)
-    for t in range(tiles):
-        at = tile(t)
-        first = (nodes_ref[:, at].astype(F32) + dot(out_t, ctx_s[t])).astype(BF16)
-        first_ref[:, at] = first
-        normed = norm_t(first.astype(F32), cols[:, 4:5])
-        kept = iota((1, LANES), 1) + t * LANES < count
-        head = jnp.where((iota((16, LANES), 0) > 0) | kept, normed[:16], FLAG)
-        n_s[:, at] = jnp.concatenate([head, normed[16:]], 0).astype(BF16)
-    sent_ref[...] = dot(n_s[...], reorder(slots, run)).astype(BF16)
+    ctx = jnp.concatenate([ctx_s[t] for t in range(tiles)], 1)
+    first = (nodes_ref[...].astype(F32) + dot(out_t, ctx)).astype(BF16)
+    first_ref[...] = first
+    normed = norm_t(first.astype(F32), cols[:, 4:5])
+    kept = iota((1, slots), 1) < count
+    head = jnp.where((iota((16, slots), 0) > 0) | kept, normed[:16], FLAG)
+    normed = jnp.concatenate([head, normed[16:]], 0).astype(BF16)
+    sent_ref[...] = dot(normed, reorder(slots, run)).astype(BF16)
 
 
 def tables_kernel(
@@ -202,7 +203,7 @@
     qkv_t_ref, out_t_ref, up_t_ref, hot_ref, order_ref, label_ref,
     qkv_ref, out_ref, up_ref, slot_ref, owner_ref, voxel_ref, sems
 ):
-    load_all(
+    loads = start_all(
         [
             (qkv_hbm, qkv_ref),
             (out_hbm, out_ref),
@@ -213,6 +214,7 @@
         ],
         sems,
     )
+    wait_all(loads)
     votes = slot_ref.shape[1]
     slots, codes = hot_ref.shape
     owners = codes // cap
@@ -253,148 +255,198 @@
     return jnp.concatenate([head.astype(BF16), block[16:]], 0), gone
 
 
-def partial_attend(run, unit, blocks, kv_t, q_s, k_s, v_s, m_s, s_s, top_s, sum_s, acc_s, fresh):
-    rows8 = q_s.shape[1]
-    chans = 8 * rows8
-    cut = 2 * rows8 // 3
-    for n, block_ref in enumerate(blocks):
-        for r in range(run):
-            block, gone = clean(block_ref[:, tile(unit * run + r)])
-            kv = dot(kv_t, block)
-            k_s[n * run + r] = kv[:chans].reshape(rows8, 8, LANES)
-            v_s[n * run + r] = kv[chans:].reshape(rows8, 8, LANES)
-            m_s[n * run + r] = jnp.broadcast_to(jnp.where(gone, -1e9, 0.0), (8, LANES))
-    keys = len(blocks) * run
-
-    def one(r, _):
-        t = unit * run + r
-        query = q_s[t]
-
-        def score(key, top):
-            prod = query * k_s[key]
-            a = jnp.sum(prod[:cut], 0)
-            b = jnp.sum(prod[cut:], 0)
-            b = b + pltpu.roll(b, 4, 0)
-            mask = m_s[key]
-            a = a + mask
-            b = b + mask
-            s_s[key, 0] = a
-            s_s[key, 1] = b
-            return jnp.maximum(top[0], a), jnp.maximum(top[1], b)
-
-        if fresh:
-            low = jnp.full((8, LANES), -3e38, F32)
-            old = (low, low)
-        else:
-            old = (top_s[t, 0], top_s[t, 1])
-        top_a, top_b = lax.fori_loop(0, keys, score, old, unroll=4)
-
-        def gather(key, carry):
-            sum_a, sum_b, acc_a, acc_b = carry
+def fold16(x):
+    parts = [x[n] for n in range(x.shape[0])]
+    while len(parts) > 1:
+        parts = [a + b for a, b in zip(parts[::2], parts[1::2])]
+    wide = parts[0].astype(F32)
+    return wide[:8] + wide[8:]
+
+
+def twice(x):
+    return jnp.concatenate([x, x], 0).astype(BF16)
+
+
+def add_keys(blocks, kv_t, k_s, v_s, m_s):
+    chans = kv_t.shape[1]
+    rows16 = chans // 16
+    tiles = k_s.shape[1]
+    for n, block in enumerate(blocks):
+        block, gone = clean(block)
+        kv = dot(kv_t, block).astype(BF16)
+        mask = jnp.where(gone, -1e9, 0.0)
+        for t in range(tiles):
+            k_s[n, t] = kv[:chans, tile(t)].reshape(rows16, 16, LANES)
+            v_s[n, t] = kv[chans:, tile(t)].reshape(rows16, 16, LANES)
+            m_s[n, t] = jnp.broadcast_to(mask[:, tile(t)], (8, LANES))
+
+
+def attend_more(t, run, q_s, k_s, v_s, m_s, s_s, old):
+    rows16 = q_s.shape[1]
+    cut = 2 * rows16 // 3
+    blocks = k_s.shape[0]
+    keys = blocks * run
+    base = (t // run) * run
+    query = q_s[t]
+
+    def score(key, top):
+        n, at = key // run, base + key % run
+        prod = query * k_s[n, at]
+        a = fold16(prod[:cut])
+        b = fold16(prod[cut:])
+        b = b + pltpu.roll(b, 4, 0)
+        mask = m_s[n, at]
+        a = a * LOG2E + mask
+        b = b * LOG2E + mask
+        s_s[key, 0] = a
+        s_s[key, 1] = b
+        return jnp.maximum(top[0], a), jnp.maximum(top[1], b)
+
+    if old is None:
+        low = jnp.full((8, LANES), -3e38, F32)
+        zero = jnp.zeros((8, LANES), F32)
+        top_a, top_b = lax.fori_loop(0, keys, score, (low, low), unroll=4)
+        held = (zero, zero, jnp.zeros((cut, 16, LANES), F32),
+                jnp.zeros((rows16 - cut, 16, LANES), F32))
+    else:
+        top, total, acc = old
+        top_a, top_b = lax.fori_loop(0, keys, score, (top[0], top[1]), unroll=4)
+        fade_a = jnp.exp2(top[0] - top_a)
+        fade_b = jnp.exp2(top[1] - top_b)
+        both_a = jnp.concatenate([fade_a, fade_a], 0)
+        both_b = jnp.concatenate([fade_b, fade_b], 0)
+        held = (total[0] * fade_a, total[1] * fade_b, acc[:cut] * both_a[None],
+                acc[cut:] * both_b[None])
+
+    def gather(step, carry):
+        sum_a, sum_b, acc_a, acc_b = carry
+        got_a, got_b = [], []
+        for key in range(4):
+            key = 4 * step + key
             pa = jnp.exp2(s_s[key, 0] - top_a)
             pb = jnp.exp2(s_s[key, 1] - top_b)
-            value = v_s[key]
-            return (
-                sum_a + pa,
-                sum_b + pb,
-                acc_a + pa[None] * value[:cut],
-                acc_b + pb[None] * value[cut:],
-            )
-
-        if fresh:
-            zero = jnp.zeros((8, LANES), F32)
-            held = (
-                zero,
-                zero,
-                jnp.zeros((cut, 8, LANES), F32),
-                jnp.zeros((rows8 - cut, 8, LANES), F32),
-            )
-        else:
-            fade_a = jnp.exp2(old[0] - top_a)
-            fade_b = jnp.exp2(old[1] - top_b)
-            acc = acc_s[t]
-            held = (
-                sum_s[t, 0] * fade_a,
-                sum_s[t, 1] * fade_b,
-                acc[:cut] * fade_a[None],
-                acc[cut:] * fade_b[None],
-            )
-        sum_a, sum_b, acc_a, acc_b = lax.fori_loop(0, keys, gather, held, unroll=4)
-        return t, top_a, top_b, sum_a, sum_b, acc_a, acc_b
-
-    return one
+            sum_a = sum_a + pa
+            sum_b = sum_b + pb
+            value = v_s[key // run, base + key % run]
+            got_a.append(twice(pa)[None] * value[:cut])
+            got_b.append(twice(pb)[None] * value[cut:])
+        acc_a = acc_a + ((got_a[0] + got_a[1]) + (got_a[2] + got_a[3])).astype(F32)
+        acc_b = acc_b + ((got_b[0] + got_b[1]) + (got_b[2] + got_b[3])).astype(F32)
+        return sum_a, sum_b, acc_a, acc_b
+
+    sum_a, sum_b, acc_a, acc_b = lax.fori_loop(0, keys // 4, gather, held)
+    return (top_a, top_b), (sum_a, sum_b), (acc_a, acc_b)
+
+
+def keep_state(t, state, top_ref, sum_ref, acc_ref):
+    top, total, acc = state
+    for n in range(2):
+        top_ref[t, n] = top[n]
+        sum_ref[t, n] = total[n]
+    acc_ref[t] = jnp.concatenate(acc, 0)
 
 
 def near_kernel(
-    run, own_ref, near_ref, qkv_t_ref, q_ref, top_ref, sum_ref, acc_ref, k_s, v_s, m_s, s_s
+    run, own_ref, near_hbm, qkv_t_ref, q_ref, top_ref, sum_ref, acc_ref,
+    near_ref, sem, k_s, v_s, m_s, s_s
 ):
+    load = pltpu.make_async_copy(near_hbm, near_ref, sem)
+    load.start()
     chans, slots = own_ref.shape
     tiles = slots // LANES
-    scale = (chans // HEADS) ** -0.5 * LOG2E
-    q_t = qkv_t_ref[:chans, :]
+    scale = (chans // HEADS) ** -0.5
+    own, _ = clean(own_ref[...])
+    query = (dot(qkv_t_ref[:chans, :], own) * scale).astype(BF16)
     for t in range(tiles):
-        own, _ = clean(own_ref[:, tile(t)])
-        q_ref[t] = (dot(q_t, own) * scale).reshape(chans // 8, 8, LANES)
-    for unit in range(tiles // run):
-        one = partial_attend(
-            run, unit, [own_ref, near_ref], qkv_t_ref[chans:, :], q_ref, k_s, v_s, m_s, s_s,
-            None, None, None, True
-        )
-
-        def step(r, _, one=one):
-            t, top_a, top_b, sum_a, sum_b, acc_a, acc_b = one(r, 0)
-            top_ref[t, 0] = top_a
-            top_ref[t, 1] = top_b
-            sum_ref[t, 0] = sum_a
-            sum_ref[t, 1] = sum_b
-            acc_ref[t] = jnp.concatenate([acc_a, acc_b], 0)
-            return 0
-
-        lax.fori_loop(0, run, step, 0)
-
-
-def second_kernel(
-    run, cap, far, count_ref, *refs
-):
+        q_ref[t] = query[:, tile(t)].reshape(chans // 16, 16, LANES)
+    kv_t = qkv_t_ref[chans:, :]
+    load.wait()
+    add_keys([own_ref[...], near_ref[...]], kv_t, k_s, v_s, m_s)
+
+    def step(t, _):
+        state = attend_more(t, run, q_ref, k_s, v_s, m_s, s_s, None)
+        keep_state(t, state, top_ref, sum_ref, acc_ref)
+        return 0
+
+    lax.fori_loop(0, tiles, step, 0)
+
+
+def middle_kernel(run, count, *refs):
+    blocks, refs = refs[:count], refs[count:]
+    q_ref, top_in, sum_in, acc_in, qkv_t_ref, top_ref, sum_ref, acc_ref = refs[:8]
+    block_s, sems, k_s, v_s, m_s, s_s = refs[8:]
+    wait_all(start_all([(blocks[n], block_s.at[n]) for n in range(count)], sems))
+    chans = qkv_t_ref.shape[1]
+    add_keys([block_s[n] for n in range(count)], qkv_t_ref[chans:, :], k_s, v_s, m_s)
+
+    def step(t, _):
+        old = (top_in[t], sum_in[t], acc_in[t])
+        state = attend_more(t, run, q_ref, k_s, v_s, m_s, s_s, old)
+        keep_state(t, state, top_ref, sum_ref, acc_ref)
+        return 0
+
+    lax.fori_loop(0, q_ref.shape[0], step, 0)
+
+
+def second_kernel(run, cap, far, count_ref, *refs):
     blocks, refs = refs[:far], refs[far:]
     (
-        first_ref, q_ref, top_ref, sum_ref, acc_ref, gain_ref, qkv_t_ref, out_t_ref, up_t_ref,
-        down_hbm, hot_ref, order_ref, label_ref
+        first_hbm, q_ref, top_in, sum_in, acc_in, gain_ref, qkv_t_ref, out_t_ref, up_t_hbm,
+        down_hbm, hot_hbm, order_hbm, label_ref
     ) = refs[:13]
-    chans, slots = first_ref.shape
-    codes = hot_ref.shape[1]
+    chans, slots = first_hbm.shape
+    codes = hot_hbm.shape[1]
     owners = codes // cap
     feat_ref, votes_refs = refs[13], refs[14 : 14 + owners]
-    k_s, v_s, m_s, s_s, ctx_s, bf_s, down_ref, sem = refs[14 + owners :]
-    load_down = pltpu.make_async_copy(down_hbm, down_ref, sem)
-    load_down.start()
+    (
+        block_s, sems, k_s, v_s, m_s, s_s, ctx_s, bf_s, first_ref, up_t_ref, down_ref, hot_ref,
+        order_ref, late_sems
+    ) = refs[14 + owners :]
+    loads = start_all([(blocks[n], block_s.at[n]) for n in range(far)], sems)
+    late = start_all(
+        [
+            (order_hbm, order_ref),
+            (first_hbm, first_ref),
+            (up_t_hbm, up_t_ref),
+            (down_hbm, down_ref),
+            (hot_hbm, hot_ref),
+        ],
+        late_sems,
+    )
+    wait_all(loads)
     tiles = slots // LANES
     count = count_ref[0]
-    for unit in range(tiles // run):
-        one = partial_attend(
-            run, unit, blocks, qkv_t_ref[chans:, :], q_ref, k_s, v_s, m_s, s_s,
-            top_ref, sum_ref, acc_ref, False
+    add_keys([block_s[n] for n in range(far)], qkv_t_ref[chans:, :], k_s, v_s, m_s)
+
+    def step(t, _):
+        old = (top_in[t], sum_in[t], acc_in[t])
+        _, total, acc = attend_more(t, run, q_ref, k_s, v_s, m_s, s_s, old)
+        share = [1.0 / total[n] for n in range(2)]
+        ctx = jnp.concatenate(
+            [acc[n] * jnp.concatenate([share[n], share[n]], 0)[None] for n in range(2)], 0
         )
-
-        def step(r, _, one=one):
-            t, _, _, sum_a, sum_b, acc_a, acc_b = one(r, 0)
-            ctx = jnp.concatenate([acc_a / sum_a[None], acc_b / sum_b[None]], 0)
-            ctx_s[t] = ctx.reshape(chans, LANES).astype(BF16)
-            return 0
-
-        lax.fori_loop(0, run, step, 0)
-    ctx = dot_t(
-        jnp.concatenate([ctx_s[t] for t in range(tiles)], 1), order_ref[...]
-    ).astype(BF16)
+        ctx_s[t] = ctx.reshape(chans, LANES).astype(BF16)
+        return 0
+
+    lax.fori_loop(0, tiles, step, 0)
+    ctx = jnp.concatenate([ctx_s[t] for t in range(tiles)], 1)
+    wait_all(late)
+    ctx = dot_t(ctx, order_ref[...]).astype(BF16)
     gain = jnp.concatenate([gain_ref[...], jnp.zeros((7, chans), F32)], 0).T[:, 0:1]
-    load_down.wait()
-    for t in range(tiles):
-        at = tile(t)
-        second = first_ref[:, at].astype(F32) + dot(out_t_ref[...], ctx[:, at])
-        inner = norm_t(second, gain).astype(BF16)
-        hidden = jax.nn.gelu(dot(up_t_ref[...], inner)).astype(BF16)
-        third = second + dot(down_ref[...], hidden)
-        third = jnp.where(iota((1, LANES), 1) + t * LANES < count, third, 0.0)
+    second = first_ref[...].astype(F32) + dot(out_t_ref[...], ctx)
+    inner = norm_t(second, gain).astype(BF16)
+    kept = iota((1, slots), 1) < count
+    wide = 2 * LANES
+    cuts = [slice(at, at + wide) for at in range(0, slots, wide)]
+    up_t = up_t_ref[...]
+    raised = dot(up_t, inner[:, cuts[0]])
+    for n, at in enumerate(cuts):
+        now = raised
+        if n + 1 < len(cuts):
+            raised = dot(up_t, inner[:, cuts[n + 1]])
+        hidden = jax.nn.gelu(now).astype(BF16)
+        third = second[:, at] + dot(down_ref[...], hidden)
+        third = jnp.where(kept[:, at], third, 0.0)
         feat_ref[:, at] = third
         bf_s[:, at] = third.astype(BF16)
     picked = dot(bf_s[...], hot_ref[...]).astype(BF16)
@@ -403,15 +455,16 @@
         votes_refs[o][chans:, :] = label_ref[:, o * cap : (o + 1) * cap]
 
 
-def sums_kernel(*refs):
-    got, out_ref = refs[:-1], refs[-1]
+def sums_kernel(owners, *refs):
+    got, out_ref, got_s, sems = refs[:owners], refs[owners], refs[owners + 1], refs[owners + 2]
+    wait_all(start_all([(got[n], got_s.at[n]) for n in range(owners)], sems))
     chans, voxels = out_ref.shape
-    cap = got[0].shape[1]
+    cap = got_s.shape[2]
     total = jnp.zeros(out_ref.shape, F32)
-    for ref in got:
-        label = ref[chans:, :].astype(F32)[0:1]
+    for n in range(owners):
+        label = got_s[n, chans:, :].astype(F32)[0:1]
         hot = (label == iota((voxels, cap), 0).astype(F32)).astype(BF16)
-        total = total + dot_t(ref[:chans, :], hot)
+        total = total + dot_t(got_s[n, :chans, :], hot)
     out_ref[...] = total
 
 
@@ -460,7 +513,7 @@
     cap = 2 * votes // owners
     codes = owners * cap
     tiles = slots // LANES
-    rows8 = chans // 8
+    rows16 = chans // 16
     hidden = w_up.shape[1]
     per = LANES // WIN
     sds = jax.ShapeDtypeStruct
@@ -479,6 +532,7 @@
             vmem((chans, 3 * chans), BF16),
             vmem((chans, chans), BF16),
             dma((7,)),
+            vmem((3 * chans, slots), BF16),
             vmem((tiles, chans, LANES), BF16),
             vmem((tiles, LANES, chans), BF16),
             vmem((tiles, per, chans, LANES), BF16),
@@ -499,11 +553,10 @@
     )
     near = turned(sent, "grp", 1)
     bit = groups // 2
-    far = []
+    mid = []
     while bit > 1:
-        far += [turned(block, "grp", bit) for block in [sent] + far]
+        mid += [turned(block, "grp", bit) for block in [sent] + mid]
         bit //= 2
-    far += [turned(block, "grp", 1) for block in far]
     qkv_t, out_t, up_t, hot, order, label = call(
         functools.partial(tables_kernel, run, cap),
         [
@@ -534,47 +587,58 @@
         vote_voxel.reshape(1, votes),
     )
     state = [
-        sds((tiles, rows8, 8, LANES), F32),
         sds((tiles, 2, 8, LANES), F32),
         sds((tiles, 2, 8, LANES), F32),
-        sds((tiles, rows8, 8, LANES), F32),
+        sds((tiles, rows16, 16, LANES), F32),
     ]
 
-    def key_scratch(keys):
+    def key_scratch(blocks):
         return [
-            vmem((keys, rows8, 8, LANES), F32),
-            vmem((keys, rows8, 8, LANES), F32),
-            vmem((keys, 8, LANES), F32),
-            vmem((keys, 2, 8, LANES), F32),
+            vmem((blocks, tiles, rows16, 16, LANES), BF16),
+            vmem((blocks, tiles, rows16, 16, LANES), BF16),
+            vmem((blocks, tiles, 8, LANES), F32),
+            vmem((blocks * run, 2, 8, LANES), F32),
         ]
 
-    query, top, total, acc = call(
+    query, *held = call(
         functools.partial(near_kernel, run),
+        [sds((tiles, rows16, 16, LANES), BF16)] + state,
+        [vmem((chans, slots), BF16), dma] + key_scratch(2),
+        3_000_000_000,
+        "vav",
+    )(sent, near, qkv_t)
+    mid, query = lax.optimization_barrier((mid, query))
+    far = [turned(block, "grp", 1) for block in mid]
+    held = call(
+        functools.partial(middle_kernel, run, len(mid)),
         state,
-        key_scratch(2 * run),
-        3_000_000_000,
-        "vvv",
-    )(sent, near, qkv_t)
+        [vmem((len(mid), chans, slots), BF16), dma((len(mid),))] + key_scratch(len(mid)),
+        2_000_000_000,
+        "a" * len(mid) + "vvvvv",
+    )(*mid, query, *held, qkv_t)
     features_t, *ballots = call(
         functools.partial(second_kernel, run, cap, len(far)),
         [sds((chans, slots), F32)] + [sds((chans + 16, cap), BF16)] * owners,
-        key_scratch(len(far) * run)
+        [vmem((len(far), chans, slots), BF16), dma((len(far),))]
+        + key_scratch(len(far))
         + [
             vmem((tiles, chans, LANES), BF16),
             vmem((chans, slots), BF16),
+            vmem((chans, slots), BF16),
+            vmem((hidden, chans), BF16),
             vmem((chans, hidden), BF16),
-            dma,
+            vmem((slots, codes), BF16),
+            vmem((slots, slots), BF16),
+            dma((5,)),
         ],
         3_000_000_000,
-        "s" + "v" * len(far) + "vvvvvvvvvavvv",
+        "s" + "a" * len(far) + "avvvvvvvaaaav",
     )(
         node_count,
         *far,
         first,
         query,
-        top,
-        total,
-        acc,
+        *held,
         gain_three.reshape(1, chans),
         qkv_t,
         out_t,
@@ -586,7 +650,11 @@
     )
     got = [ballots[0]] + [turned(ballots[k], "tile", k) for k in range(owners - 1, 0, -1)]
     (sums_t,) = call(
-        sums_kernel, [sds((chans, VOX_DEV), F32)], [], 200_000_000, "v" * owners
+        functools.partial(sums_kernel, owners),
+        [sds((chans, VOX_DEV), F32)],
+        [vmem((owners, chans + 16, cap), BF16), dma((owners,))],
+        200_000_000,
+        "a" * owners,
     )(*got)
     return (features_t.T, sums_t.T)
 

time: 71.1 us -> 60.9 us (0.86)
  waiting for transfers between devices: 13.8 us -> 4.66 us
  local copies, waits for them, and re-layouts: 2.2 us -> 0 us
  Pallas kernels: 39.1 us -> 40.1 us
    ppermute x10, waiting for transfers between devices: 13.8 us -> 4.66 us  [turned(): return lax.ppermute(x, axis, [(i, i ^ bit) for i in range(n)])]
    pallas_call x2 -> x3, Pallas kernels: 8.25 us -> 15 us  [the longest x1 7.32 us: body(): call(functools.partial(near_kernel, run), [sds((tiles, rows16, 16, LANES)...]
    pallas_call x1, Pallas kernels: 14.2 us -> 10.1 us  [body(): call(functools.partial(second_kernel, run, cap, len(far)), [sds((chans, s...]
    unnamed x20 -> x0, local copies, waits for them, and re-layouts: 2.2 us -> none
    pallas_call x1, Pallas kernels: 10.9 us -> 9.37 us  [body(): call(functools.partial(first_kernel, run), [sds((chans, slots), BF16), sd...]
  transfers between devices with their start and end apart: 10 -> 10, of which waited for: 7 -> 6; matrix products, arithmetic and copies ran while one was open for 0% -> 0% of each run, Pallas kernels for 17% -> 31%
where the time goes in v3:
time: 60.9 us; the launch traced here: 60.5 us
  Pallas kernels  40.1 us (66%)
  starting transfers between devices  14.4 us (24%)
  waiting for transfers between devices  4.66 us (8%)
  between operations  1.35 us (2%)
    ppermute x10, starting transfers between devices, turned(): return lax.ppermute(x, axis, [(i, i ^ bit) for i in range(n)])  14.4 us
    pallas_call x1, Pallas kernels, body(): call(functools.partial(second_kernel, run, cap, len(far)), [sds((chans, s...  10.1 us
    pallas_call x1, Pallas kernels, body(): call(functools.partial(first_kernel, run), [sds((chans, slots), BF16), sd...  9.37 us
    pallas_call x1, Pallas kernels, body(): call(functools.partial(near_kernel, run), [sds((tiles, rows16, 16, LANES)...  7.32 us
    pallas_call x1, Pallas kernels, body(): call(functools.partial(middle_kernel, run, len(mid)), state, [vmem((len(m...  5.62 us
    pallas_call x1, Pallas kernels, body(): call(functools.partial(tables_kernel, run, cap), [sds((3 * chans, chans),...  5.57 us
    ppermute x10, waiting for transfers between devices, turned(): return lax.ppermute(x, axis, [(i, i ^ bit) for i in range(n)])  4.66 us
    pallas_call x1, Pallas kernels, body(): call(functools.partial(sums_kernel, owners), [sds((chans, VOX_DEV), F32)]...  2.1 us
  transfers between devices with their start and end apart: 10, of which 6 were waited for; matrix products, arithmetic and copies ran while one was open for 0% of the time, Pallas kernels for 31%

profile of v3, /device:TPU:0, one launch (start us, length us, event | category | flops | bytes accessed | tf_op | source)
XLA Modules:
  0.0 60.5 jit_solution(8316908402485191489)
XLA Ops:
  1.3 9.4 %shard_map.167 = (bf16[192,1024]{1,0:T(8,128)(2,1)}, bf16[192,1024]{1,0:T(8,128)(2,1)}) custom-call(s32[1]{0:T(128)S(6)} %copy.18.count_ref, bf16[192,1024]{1,0:T(8,128)(2,1)} %bitcast.11, s32[1,1024]{1,0:T(1,128)} %bitcast.13, f32[3,192]{1,0:T(4,128)} %pos_hbm.1, f32[1,192]{1,0:T(1,128)} %bitcast.17, f32[1,192]{1,0:T(1,128)} %bitcast.18, ...), custom_call_target="tpu_custom_call" | custom-call | flops 2000000000 | bytes 2097152 | tf_op jit(solution)/shard_map/pallas_call | solution.py:523
  10.7 0.5 collective-permute-start.1
  11.2 2.6 %collective-permute-start = (bf16[192,1024]{1,0:T(8,128)(2,1)}, bf16[192,1024]{1,0:T(8,128)(2,1)}, u32[]{:S(2)}, u32[]{:S(2)}) collective-permute-start(bf16[192,1024]{1,0:T(8,128)(2,1)} %get-tuple-element.28.own_ref), channel_id=1, source_target_pairs={{0,16},{8,24},{16,0},{24,8},{1,17},{9,25},{17,1},{25,9},{2,18},{10... | collective-permute-start | bytes 1179656 | tf_op jit(solution)/shard_map/ppermute | solution.py:488
  13.7 5.6 %shard_map.168 = (bf16[576,192]{1,0:T(8,128)(2,1)}, bf16[192,192]{1,0:T(8,128)(2,1)}, bf16[768,192]{1,0:T(8,128)(2,1)}, bf16[1024,1024]{1,0:T(8,128)(2,1)}, bf16...) custom-call(bf16[192,576]{1,0:T(8,128)(2,1)} %qkv_hbm.3, bf16[192,192]{1,0:T(8,128)(2,1)} %out_hbm.3, ...), custom_call_target="tpu_custom_call" | custom-call | flops 2000000000 | bytes 2097152 | tf_op jit(solution)/shard_map/pallas_call | solution.py:560
  19.3 0.0 collective-permute-done.1.near_hbm
  19.3 7.3 %shard_map.169 = (bf16[8,12,16,128]{3,2,1,0:T(8,128)(2,1)}, f32[8,2,8,128]{3,2,1,0:T(8,128)}, f32[8,2,8,128]{3,2,1,0:T(8,128)}, f32[8,12,16,128]{3,2,1,0:T(8,128)}) custom-call(bf16[192,1024]{1,0:T(8,128)(2,1)} %get-tuple-element.28.own_ref, bf16[192,1024]{1,0:T(8,128)(2,1)} %collective-permute-done.1.near_hbm, ...), custom_call_target="tpu_custom_call" | custom-call | flops 3000000000 | bytes 2097152 | tf_op jit(solution)/shard_map/pallas_call | solution.py:603
  26.7 0.0 collective-permute-done.refs_0_
  26.7 0.2 collective-permute-start.2
  26.9 5.6 %shard_map.170 = (f32[8,2,8,128]{3,2,1,0:T(8,128)}, f32[8,2,8,128]{3,2,1,0:T(8,128)}, f32[8,12,16,128]{3,2,1,0:T(8,128)}) custom-call(bf16[192,1024]{1,0:T(8,128)(2,1)} %collective-permute-done.refs_0_, bf16[8,12,16,128]{3,2,1,0:T(8,128)(2,1)} %get-tuple-element.33.refs_1_.refs_2_, f32[8,2,8,128]{3,2,1,0:T(8,128)} %get-tuple-element.34.refs_2_, ...), custom_call_target="tpu_custom_call" | custom-call | flops 2000000000 | bytes 2097152 | tf_op jit(solution)/shard_map/pallas_call | solution.py:612
  32.5 0.0 collective-permute-done.2.refs_0_
  32.5 10.1 %shard_map.171 = (f32[192,1024]{1,0:T(8,128)}, bf16[208,128]{1,0:T(8,128)(2,1)}, bf16[208,128]{1,0:T(8,128)(2,1)}, bf16[208,128]{1,0:T(8,128)(2,1)}, bf16[208,12...) custom-call(s32[1]{0:T(128)S(6)} %copy.18.count_ref, ...), custom_call_target="tpu_custom_call" | custom-call | flops 3000000000 | bytes 2097152 | tf_op jit(solution)/shard_map/pallas_call | solution.py:619
  42.6 4.6 %collective-permute-start.3 = (bf16[208,128]{1,0:T(8,128)(2,1)}, bf16[208,128]{1,0:T(8,128)(2,1)}, u32[]{:S(2)}, u32[]{:S(2)}) collective-permute-start(bf16[208,128]{1,0:T(8,128)(2,1)} %get-tuple-element.47), channel_id=1, source_target_pairs={{0,7},{1,6},{2,5},{3,4},{4,3},{5,2},{6,1},{7,0},{8,15},{9,14},{10,... | collective-permute-start | bytes 159752 | tf_op jit(solution)/shard_map/ppermute | solution.py:488
  47.2 0.2 collective-permute-start.4
  47.5 0.7 %collective-permute-start.5 = (bf16[208,128]{1,0:T(8,128)(2,1)}, bf16[208,128]{1,0:T(8,128)(2,1)}, u32[]{:S(2)}, u32[]{:S(2)}) collective-permute-start(bf16[208,128]{1,0:T(8,128)(2,1)} %get-tuple-element.49), channel_id=1, source_target_pairs={{0,5},{1,4},{2,7},{3,6},{4,1},{5,0},{6,3},{7,2},{8,13},{9,12},{10,... | collective-permute-start | bytes 159752 | tf_op jit(solution)/shard_map/ppermute | solution.py:488
  48.2 2.1 %collective-permute-start.6 = (bf16[208,128]{1,0:T(8,128)(2,1)}, bf16[208,128]{1,0:T(8,128)(2,1)}, u32[]{:S(2)}, u32[]{:S(2)}) collective-permute-start(bf16[208,128]{1,0:T(8,128)(2,1)} %get-tuple-element.50), channel_id=1, source_target_pairs={{0,4},{1,5},{2,6},{3,7},{4,0},{5,1},{6,2},{7,3},{8,12},{9,13},{10,... | collective-permute-start | bytes 159752 | tf_op jit(solution)/shard_map/ppermute | solution.py:488
  50.3 2.2 %collective-permute-start.7 = (bf16[208,128]{1,0:T(8,128)(2,1)}, bf16[208,128]{1,0:T(8,128)(2,1)}, u32[]{:S(2)}, u32[]{:S(2)}) collective-permute-start(bf16[208,128]{1,0:T(8,128)(2,1)} %get-tuple-element.51), channel_id=1, source_target_pairs={{0,3},{1,2},{2,1},{3,0},{4,7},{5,6},{6,5},{7,4},{8,11},{9,10},{10,... | collective-permute-start | bytes 159752 | tf_op jit(solution)/shard_map/ppermute | solution.py:488
  52.5 0.0 collective-permute-done.3.refs_1_
  52.5 0.8 %collective-permute-start.8 = (bf16[208,128]{1,0:T(8,128)(2,1)}, bf16[208,128]{1,0:T(8,128)(2,1)}, u32[]{:S(2)}, u32[]{:S(2)}) collective-permute-start(bf16[208,128]{1,0:T(8,128)(2,1)} %get-tuple-element.52), channel_id=1, source_target_pairs={{0,2},{1,3},{2,0},{3,1},{4,6},{5,7},{6,4},{7,5},{8,10},{9,11},{10,... | collective-permute-start | bytes 159752 | tf_op jit(solution)/shard_map/ppermute | solution.py:488
  53.3 0.6 %collective-permute-done.4.refs_2_ = bf16[208,128]{1,0:T(8,128)(2,1)} collective-permute-done((bf16[208,128]{1,0:T(8,128)(2,1)}, bf16[208,128]{1,0:T(8,128)(2,1)}, u32[]{:S(2)}, u32[]{:S(2)}) %collective-permute-start.4) | collective-permute-done | bytes 53280 | tf_op jit(solution)/shard_map/ppermute | solution.py:488
  53.9 0.4 collective-permute-start.9
  54.4 1.8 %collective-permute-done.5.refs_3_ = bf16[208,128]{1,0:T(8,128)(2,1)} collective-permute-done((bf16[208,128]{1,0:T(8,128)(2,1)}, bf16[208,128]{1,0:T(8,128)(2,1)}, u32[]{:S(2)}, u32[]{:S(2)}) %collective-permute-start.5) | collective-permute-done | bytes 53280 | tf_op jit(solution)/shard_map/ppermute | solution.py:488
  56.2 1.0 %collective-permute-done.6.refs_4_ = bf16[208,128]{1,0:T(8,128)(2,1)} collective-permute-done((bf16[208,128]{1,0:T(8,128)(2,1)}, bf16[208,128]{1,0:T(8,128)(2,1)}, u32[]{:S(2)}, u32[]{:S(2)}) %collective-permute-start.6) | collective-permute-done | bytes 53280 | tf_op jit(solution)/shard_map/ppermute | solution.py:488
  57.2 0.5 collective-permute-done.7.refs_5_
  57.7 0.3 collective-permute-done.8.refs_6_
  57.9 0.5 collective-permute-done.9.refs_7_
  58.4 2.1 %shard_map.172 = f32[192,256]{1,0:T(8,128)} custom-call(bf16[208,128]{1,0:T(8,128)(2,1)} %get-tuple-element.46.refs_0_, bf16[208,128]{1,0:T(8,128)(2,1)} %collective-permute-done.3.refs_1_, bf16[208,128]{1,0:T(8,128)(2,1)} %collective-permute-done.4.refs_2_, bf16[208,128]{1,0:T(8,128)(2,1)} %collective-permute-done.5.refs_3_, ...), custom_call_target="tpu_custom_call" | custom-call | flops 200000000 | bytes 2097152 | tf_op jit(solution)/shard_map/pallas_call | solution.py:652
Async XLA Ops:
  10.7 8.7 %collective-permute-start.1 = (bf16[192,1024]{1,0:T(8,128)(2,1)}, bf16[192,1024]{1,0:T(8,128)(2,1)}, u32[]{:S(2)}, u32[]{:S(2)}) collective-permute-start(bf16[192,1024]{1,0:T(8,128)(2,1)} %get-tuple-element.28.own_ref), channel_id=1, source_target_pairs={{0,8},{8,0},{16,24},{24,16},{1,9},{9,1},{17,25},{25,17},{2,10},{10... | collective-permute-start | bytes 1179656 | tf_op jit(solution)/shard_map/ppermute | solution.py:488
  11.2 15.5 %collective-permute-start = (bf16[192,1024]{1,0:T(8,128)(2,1)}, bf16[192,1024]{1,0:T(8,128)(2,1)}, u32[]{:S(2)}, u32[]{:S(2)}) collective-permute-start(bf16[192,1024]{1,0:T(8,128)(2,1)} %get-tuple-element.28.own_ref), channel_id=1, source_target_pairs={{0,16},{8,24},{16,0},{24,8},{1,17},{9,25},{17,1},{25,9},{2,18},{10... | collective-permute-start | bytes 1179656 | tf_op jit(solution)/shard_map/ppermute | solution.py:488
  26.7 5.9 %collective-permute-start.2 = (bf16[192,1024]{1,0:T(8,128)(2,1)}, bf16[192,1024]{1,0:T(8,128)(2,1)}, u32[]{:S(2)}, u32[]{:S(2)}) collective-permute-start(bf16[192,1024]{1,0:T(8,128)(2,1)} %collective-permute-done.refs_0_), channel_id=1, source_target_pairs={{0,8},{8,0},{16,24},{24,16},{1,9},{9,1},{17,25},{25,17},{2,10},{10... | collective-permute-start | bytes 1179656 | tf_op jit(solution)/shard_map/ppermute | solution.py:488
  42.6 9.9 %collective-permute-start.3 = (bf16[208,128]{1,0:T(8,128)(2,1)}, bf16[208,128]{1,0:T(8,128)(2,1)}, u32[]{:S(2)}, u32[]{:S(2)}) collective-permute-start(bf16[208,128]{1,0:T(8,128)(2,1)} %get-tuple-element.47), channel_id=1, source_target_pairs={{0,7},{1,6},{2,5},{3,4},{4,3},{5,2},{6,1},{7,0},{8,15},{9,14},{10,... | collective-permute-start | bytes 159752 | tf_op jit(solution)/shard_map/ppermute | solution.py:488
  47.2 6.7 %collective-permute-start.4 = (bf16[208,128]{1,0:T(8,128)(2,1)}, bf16[208,128]{1,0:T(8,128)(2,1)}, u32[]{:S(2)}, u32[]{:S(2)}) collective-permute-start(bf16[208,128]{1,0:T(8,128)(2,1)} %get-tuple-element.48), channel_id=1, source_target_pairs={{0,6},{1,7},{2,4},{3,5},{4,2},{5,3},{6,0},{7,1},{8,14},{9,15},{10,... | collective-permute-start | bytes 159752 | tf_op jit(solution)/shard_map/ppermute | solution.py:488
  47.5 8.7 %collective-permute-start.5 = (bf16[208,128]{1,0:T(8,128)(2,1)}, bf16[208,128]{1,0:T(8,128)(2,1)}, u32[]{:S(2)}, u32[]{:S(2)}) collective-permute-start(bf16[208,128]{1,0:T(8,128)(2,1)} %get-tuple-element.49), channel_id=1, source_target_pairs={{0,5},{1,4},{2,7},{3,6},{4,1},{5,0},{6,3},{7,2},{8,13},{9,12},{10,... | collective-permute-start | bytes 159752 | tf_op jit(solution)/shard_map/ppermute | solution.py:488
  48.2 9.0 %collective-permute-start.6 = (bf16[208,128]{1,0:T(8,128)(2,1)}, bf16[208,128]{1,0:T(8,128)(2,1)}, u32[]{:S(2)}, u32[]{:S(2)}) collective-permute-start(bf16[208,128]{1,0:T(8,128)(2,1)} %get-tuple-element.50), channel_id=1, source_target_pairs={{0,4},{1,5},{2,6},{3,7},{4,0},{5,1},{6,2},{7,3},{8,12},{9,13},{10,... | collective-permute-start | bytes 159752 | tf_op jit(solution)/shard_map/ppermute | solution.py:488
  50.3 7.3 %collective-permute-start.7 = (bf16[208,128]{1,0:T(8,128)(2,1)}, bf16[208,128]{1,0:T(8,128)(2,1)}, u32[]{:S(2)}, u32[]{:S(2)}) collective-permute-start(bf16[208,128]{1,0:T(8,128)(2,1)} %get-tuple-element.51), channel_id=1, source_target_pairs={{0,3},{1,2},{2,1},{3,0},{4,7},{5,6},{6,5},{7,4},{8,11},{9,10},{10,... | collective-permute-start | bytes 159752 | tf_op jit(solution)/shard_map/ppermute | solution.py:488
  52.5 5.4 %collective-permute-start.8 = (bf16[208,128]{1,0:T(8,128)(2,1)}, bf16[208,128]{1,0:T(8,128)(2,1)}, u32[]{:S(2)}, u32[]{:S(2)}) collective-permute-start(bf16[208,128]{1,0:T(8,128)(2,1)} %get-tuple-element.52), channel_id=1, source_target_pairs={{0,2},{1,3},{2,0},{3,1},{4,6},{5,7},{6,4},{7,5},{8,10},{9,11},{10,... | collective-permute-start | bytes 159752 | tf_op jit(solution)/shard_map/ppermute | solution.py:488
  53.9 4.5 %collective-permute-start.9 = (bf16[208,128]{1,0:T(8,128)(2,1)}, bf16[208,128]{1,0:T(8,128)(2,1)}, u32[]{:S(2)}, u32[]{:S(2)}) collective-permute-start(bf16[208,128]{1,0:T(8,128)(2,1)} %get-tuple-element.53), channel_id=1, source_target_pairs={{0,1},{1,0},{2,3},{3,2},{4,5},{5,4},{6,7},{7,6},{8,9},{9,8},{10,11... | collective-permute-start | bytes 159752 | tf_op jit(solution)/shard_map/ppermute | solution.py:488

commit v4 on v3

--- a/solution.py
+++ b/solution.py
@@ -36,7 +36,7 @@
 
 
 def transposed(a):
-    return dot_t(eye(a.shape[1]), a).astype(BF16)
+    return a.astype(F32).T.astype(BF16)
 
 
 def tile(t):
@@ -60,8 +60,17 @@
     return (lane % 8) * LANES + ((lane // 8) % 4) * WIN + p
 
 
+def place(low, high, blocks):
+    base = jnp.where(low == iota((LANES, low.shape[1]), 0), 1.0, 0.0).astype(BF16)
+    high = jnp.broadcast_to(high, base.shape).astype(F32).astype(BF16)
+    nil = jnp.zeros_like(base)
+    parts = [jnp.where(high == jnp.asarray(n, BF16), base, nil) for n in range(blocks)]
+    return jnp.concatenate(parts, 0)
+
+
 def reorder(slots, run):
-    return (iota((slots, slots), 0) == slot_of_lane(slots, run)).astype(BF16)
+    slot = slot_of_lane(slots, run)
+    return place(slot % LANES, slot // LANES, slots // LANES)
 
 
 def norm_t(x, gain):
@@ -95,8 +104,8 @@
 
 def first_kernel(
     run, count_ref, nodes_hbm, ids_hbm, pos_hbm, gain_one_hbm, gain_two_hbm, qkv_hbm, out_hbm,
-    first_ref, sent_ref, nodes_ref, ids_ref, pos_ref, gain_one_ref, gain_two_ref, qkv_ref, out_ref,
-    sems, qkv_s, q_s, k_s, v_s, ctx_s, n_s
+    first_hbm, sent_hbm, nodes_ref, ids_ref, pos_ref, gain_one_ref, gain_two_ref, qkv_ref, out_ref,
+    sems, qkv_s, q_s, k_s, v_s, ctx_s, n_s, first_s, stores
 ):
     loads = start_all(
         [
@@ -190,18 +199,22 @@
     lax.fori_loop(0, tiles, group, 0, unroll=2)
     ctx = jnp.concatenate([ctx_s[t] for t in range(tiles)], 1)
     first = (nodes_ref[...].astype(F32) + dot(out_t, ctx)).astype(BF16)
-    first_ref[...] = first
+    first_s[...] = first
+    keep_first = pltpu.make_async_copy(first_s, first_hbm, stores.at[0])
+    keep_first.start()
     normed = norm_t(first.astype(F32), cols[:, 4:5])
     kept = iota((1, slots), 1) < count
     head = jnp.where((iota((16, slots), 0) > 0) | kept, normed[:16], FLAG)
     normed = jnp.concatenate([head, normed[16:]], 0).astype(BF16)
-    sent_ref[...] = dot(normed, reorder(slots, run)).astype(BF16)
+    n_s[...] = dot(normed, reorder(slots, run)).astype(BF16)
+    send = pltpu.make_async_copy(n_s, sent_hbm, stores.at[1])
+    send.start()
+    wait_all([keep_first, send])
 
 
 def tables_kernel(
-    run, cap, qkv_hbm, out_hbm, up_hbm, slot_hbm, owner_hbm, voxel_hbm,
-    qkv_t_ref, out_t_ref, up_t_ref, hot_ref, order_ref, label_ref,
-    qkv_ref, out_ref, up_ref, slot_ref, owner_ref, voxel_ref, sems
+    cap, qkv_hbm, out_hbm, up_hbm, slot_hbm, owner_hbm, voxel_hbm, weights_hbm, facts_hbm,
+    qkv_ref, out_ref, up_ref, slot_ref, owner_ref, voxel_ref, sems, weights_s, facts_s, stores
 ):
     loads = start_all(
         [
@@ -216,36 +229,36 @@
     )
     wait_all(loads)
     votes = slot_ref.shape[1]
-    slots, codes = hot_ref.shape
+    codes = facts_s.shape[1]
     owners = codes // cap
     chans = out_ref.shape[0]
     src = head_order(chans)
     src = jnp.concatenate([src, src + chans, src + 2 * chans], 0)
     shuffle = (src == iota((3 * chans, 3 * chans), 1)).astype(BF16)
-    qkv_t_ref[...] = dot_t(shuffle, qkv_ref[...]).astype(BF16)
-    out_t = transposed(out_ref[...])
-    out_t_ref[...] = dot_t(out_t, shuffle[:chans, :chans]).astype(BF16)
-    up_t_ref[...] = transposed(up_ref[...])
-    order_ref[...] = reorder(slots, run)
-    owner = jnp.bitwise_xor(owner_ref[...], lax.axis_index("tile"))
+    weights_s[: 3 * chans] = dot_t(shuffle, qkv_ref[...]).astype(BF16)
+    out_t = dot(shuffle[:chans, :chans], out_ref[...])
+    weights_s[3 * chans : 4 * chans] = transposed(out_t)
+    weights_s[4 * chans :] = transposed(up_ref[...])
+    keep_weights = pltpu.make_async_copy(weights_s, weights_hbm, stores.at[0])
+    keep_weights.start()
+    owner = owner_ref[...]
     hot = owner == iota((owners, votes), 0)
     upto = (iota((votes, votes), 0) <= iota((votes, votes), 1)).astype(BF16)
     rank = jnp.sum(jnp.where(hot, dot(hot.astype(BF16), upto), 0.0), 0, keepdims=True)
     code = owner * cap + rank.astype(jnp.int32) - 1
-    member = (code == iota((codes, votes), 0)).astype(BF16)
+    member = place(code % LANES, code // LANES, codes // LANES)
     slot = slot_ref[...]
     row = iota((16, votes), 0)
     facts = jnp.where(
         row == 0,
-        slot // 32,
-        jnp.where(row == 1, slot % 32, jnp.where(row == 2, voxel_ref[...], 1)),
+        voxel_ref[...],
+        jnp.where(row == 1, slot // LANES, jnp.where(row == 2, slot % LANES, 1)),
     )
     listed = dot_t(facts.astype(F32).astype(BF16), member)
-    held = listed[3:4] > 0.5
-    slot_of = jnp.where(held, listed[0:1] * 32.0 + listed[1:2], -1.0).astype(jnp.int32)
-    hot_ref[...] = (slot_of == iota((slots, codes), 0)).astype(BF16)
-    label = jnp.where(held, listed[2:3], -1.0)
-    label_ref[...] = jnp.broadcast_to(label, label_ref.shape).astype(BF16)
+    facts_s[...] = jnp.where(listed[3:4] > 0.5, listed, -1.0).astype(BF16)
+    keep_facts = pltpu.make_async_copy(facts_s, facts_hbm, stores.at[1])
+    keep_facts.start()
+    wait_all([keep_weights, keep_facts])
 
 
 def clean(block):
@@ -338,89 +351,118 @@
     return (top_a, top_b), (sum_a, sum_b), (acc_a, acc_b)
 
 
-def keep_state(t, state, top_ref, sum_ref, acc_ref):
+def hold(t, state, ends_s, acc_s):
     top, total, acc = state
     for n in range(2):
-        top_ref[t, n] = top[n]
-        sum_ref[t, n] = total[n]
-    acc_ref[t] = jnp.concatenate(acc, 0)
+        ends_s[t, n] = top[n]
+        ends_s[t, 2 + n] = total[n]
+    acc_s[t] = jnp.concatenate(acc, 0)
+
+
+def held(t, ends_s, acc_s):
+    return (ends_s[t, 0], ends_s[t, 1]), (ends_s[t, 2], ends_s[t, 3]), acc_s[t]
 
 
 def near_kernel(
-    run, own_ref, near_hbm, qkv_t_ref, q_ref, top_ref, sum_ref, acc_ref,
-    near_ref, sem, k_s, v_s, m_s, s_s
+    run, own_hbm, near_hbm, weights_hbm, q_hbm, ends_hbm, acc_hbm,
+    own_ref, near_ref, qkv_t_ref, sems, q_s, ends_s, acc_s, stores, k_s, v_s, m_s, s_s
 ):
-    load = pltpu.make_async_copy(near_hbm, near_ref, sem)
-    load.start()
     chans, slots = own_ref.shape
+    loads = start_all(
+        [
+            (own_hbm, own_ref),
+            (weights_hbm.at[pl.ds(0, 3 * chans)], qkv_t_ref),
+            (near_hbm, near_ref),
+        ],
+        sems,
+    )
     tiles = slots // LANES
     scale = (chans // HEADS) ** -0.5
+    wait_all(loads[:2])
     own, _ = clean(own_ref[...])
     query = (dot(qkv_t_ref[:chans, :], own) * scale).astype(BF16)
     for t in range(tiles):
-        q_ref[t] = query[:, tile(t)].reshape(chans // 16, 16, LANES)
-    kv_t = qkv_t_ref[chans:, :]
-    load.wait()
-    add_keys([own_ref[...], near_ref[...]], kv_t, k_s, v_s, m_s)
+        q_s[t] = query[:, tile(t)].reshape(chans // 16, 16, LANES)
+    keep_q = pltpu.make_async_copy(q_s, q_hbm, stores.at[0])
+    keep_q.start()
+    wait_all(loads[2:])
+    add_keys([own_ref[...], near_ref[...]], qkv_t_ref[chans:, :], k_s, v_s, m_s)
 
     def step(t, _):
-        state = attend_more(t, run, q_ref, k_s, v_s, m_s, s_s, None)
-        keep_state(t, state, top_ref, sum_ref, acc_ref)
+        hold(t, attend_more(t, run, q_s, k_s, v_s, m_s, s_s, None), ends_s, acc_s)
         return 0
 
     lax.fori_loop(0, tiles, step, 0)
+    keep_ends = pltpu.make_async_copy(ends_s, ends_hbm, stores.at[1])
+    keep_acc = pltpu.make_async_copy(acc_s, acc_hbm, stores.at[2])
+    keep_ends.start()
+    keep_acc.start()
+    wait_all([keep_q, keep_ends, keep_acc])
 
 
 def middle_kernel(run, count, *refs):
     blocks, refs = refs[:count], refs[count:]
-    q_ref, top_in, sum_in, acc_in, qkv_t_ref, top_ref, sum_ref, acc_ref = refs[:8]
-    block_s, sems, k_s, v_s, m_s, s_s = refs[8:]
-    wait_all(start_all([(blocks[n], block_s.at[n]) for n in range(count)], sems))
-    chans = qkv_t_ref.shape[1]
-    add_keys([block_s[n] for n in range(count)], qkv_t_ref[chans:, :], k_s, v_s, m_s)
+    q_hbm, ends_hbm, acc_hbm, weights_hbm, ends_out, acc_out = refs[:6]
+    block_s, sems, q_s, ends_s, acc_s, kv_t_ref, rest, stores, k_s, v_s, m_s, s_s = refs[6:]
+    chans = kv_t_ref.shape[1]
+    loads = start_all([(blocks[n], block_s.at[n]) for n in range(count)], sems)
+    later = start_all(
+        [
+            (weights_hbm.at[pl.ds(chans, 2 * chans)], kv_t_ref),
+            (q_hbm, q_s),
+            (ends_hbm, ends_s),
+            (acc_hbm, acc_s),
+        ],
+        rest,
+    )
+    wait_all(loads + later[:1])
+    add_keys([block_s[n] for n in range(count)], kv_t_ref[...], k_s, v_s, m_s)
+    wait_all(later[1:])
 
     def step(t, _):
-        old = (top_in[t], sum_in[t], acc_in[t])
-        state = attend_more(t, run, q_ref, k_s, v_s, m_s, s_s, old)
-        keep_state(t, state, top_ref, sum_ref, acc_ref)
+        old = held(t, ends_s, acc_s)
+        hold(t, attend_more(t, run, q_s, k_s, v_s, m_s, s_s, old), ends_s, acc_s)
         return 0
 
-    lax.fori_loop(0, q_ref.shape[0], step, 0)
+    lax.fori_loop(0, q_s.shape[0], step, 0)
+    wait_all(start_all([(ends_s, ends_out), (acc_s, acc_out)], stores))
 
 
 def second_kernel(run, cap, far, count_ref, *refs):
     blocks, refs = refs[:far], refs[far:]
     (
-        first_hbm, q_ref, top_in, sum_in, acc_in, gain_ref, qkv_t_ref, out_t_ref, up_t_hbm,
-        down_hbm, hot_hbm, order_hbm, label_ref
-    ) = refs[:13]
-    chans, slots = first_hbm.shape
-    codes = hot_hbm.shape[1]
-    owners = codes // cap
-    feat_ref, votes_refs = refs[13], refs[14 : 14 + owners]
+        q_hbm, ends_hbm, acc_hbm, weights_hbm, first_hbm, gain_hbm, down_hbm, facts_hbm,
+        feat_hbm, votes_hbm
+    ) = refs[:10]
     (
-        block_s, sems, k_s, v_s, m_s, s_s, ctx_s, bf_s, first_ref, up_t_ref, down_ref, hot_ref,
-        order_ref, late_sems
-    ) = refs[14 + owners :]
+        block_s, sems, weights_s, q_s, ends_s, acc_s, first_s, gain_s, down_s, facts_s, rest,
+        feat_s, votes_s, stores, k_s, v_s, m_s, s_s, ctx_s, bf_s
+    ) = refs[10:]
     loads = start_all([(blocks[n], block_s.at[n]) for n in range(far)], sems)
-    late = start_all(
-        [
-            (order_hbm, order_ref),
-            (first_hbm, first_ref),
-            (up_t_hbm, up_t_ref),
-            (down_hbm, down_ref),
-            (hot_hbm, hot_ref),
+    later = start_all(
+        [
+            (weights_hbm, weights_s),
+            (q_hbm, q_s),
+            (ends_hbm, ends_s),
+            (acc_hbm, acc_s),
+            (first_hbm, first_s),
+            (gain_hbm, gain_s),
+            (down_hbm, down_s),
+            (facts_hbm, facts_s),
         ],
-        late_sems,
-    )
-    wait_all(loads)
+        rest,
+    )
+    chans, slots = first_s.shape
+    owners = votes_s.shape[0]
     tiles = slots // LANES
     count = count_ref[0]
-    add_keys([block_s[n] for n in range(far)], qkv_t_ref[chans:, :], k_s, v_s, m_s)
+    wait_all(loads + later[:1])
+    add_keys([block_s[n] for n in range(far)], weights_s[chans : 3 * chans], k_s, v_s, m_s)
+    wait_all(later[1:])
 
     def step(t, _):
-        old = (top_in[t], sum_in[t], acc_in[t])
-        _, total, acc = attend_more(t, run, q_ref, k_s, v_s, m_s, s_s, old)
+        old = held(t, ends_s, acc_s)
+        _, total, acc = attend_more(t, run, q_s, k_s, v_s, m_s, s_s, old)
         share = [1.0 / total[n] for n in range(2)]
         ctx = jnp.concatenate(
             [acc[n] * jnp.concatenate([share[n], share[n]], 0)[None] for n in range(2)], 0
@@ -430,45 +472,49 @@
 
     lax.fori_loop(0, tiles, step, 0)
     ctx = jnp.concatenate([ctx_s[t] for t in range(tiles)], 1)
-    wait_all(late)
-    ctx = dot_t(ctx, order_ref[...]).astype(BF16)
-    gain = jnp.concatenate([gain_ref[...], jnp.zeros((7, chans), F32)], 0).T[:, 0:1]
-    second = first_ref[...].astype(F32) + dot(out_t_ref[...], ctx)
+    ctx = dot_t(ctx, reorder(slots, run)).astype(BF16)
+    gain = jnp.concatenate([gain_s[...], jnp.zeros((7, chans), F32)], 0).T[:, 0:1]
+    second = first_s[...].astype(F32) + dot(weights_s[3 * chans : 4 * chans], ctx)
     inner = norm_t(second, gain).astype(BF16)
     kept = iota((1, slots), 1) < count
     wide = 2 * LANES
     cuts = [slice(at, at + wide) for at in range(0, slots, wide)]
-    up_t = up_t_ref[...]
+    up_t = weights_s[4 * chans :]
     raised = dot(up_t, inner[:, cuts[0]])
     for n, at in enumerate(cuts):
         now = raised
         if n + 1 < len(cuts):
             raised = dot(up_t, inner[:, cuts[n + 1]])
         hidden = jax.nn.gelu(now).astype(BF16)
-        third = second[:, at] + dot(down_ref[...], hidden)
+        third = second[:, at] + dot(down_s[...], hidden)
         third = jnp.where(kept[:, at], third, 0.0)
-        feat_ref[:, at] = third
+        feat_s[:, at] = third
         bf_s[:, at] = third.astype(BF16)
-    picked = dot(bf_s[...], hot_ref[...]).astype(BF16)
+    keep_feat = pltpu.make_async_copy(feat_s, feat_hbm, stores.at[0])
+    keep_feat.start()
+    facts = facts_s[...].astype(F32)
+    low, high = facts[2:3].astype(jnp.int32), facts[1:2].astype(jnp.int32)
+    picked = dot(bf_s[...], place(low, high, tiles)).astype(BF16)
     for o in range(owners):
-        votes_refs[o][:chans, :] = picked[:, o * cap : (o + 1) * cap]
-        votes_refs[o][chans:, :] = label_ref[:, o * cap : (o + 1) * cap]
-
-
-def sums_kernel(owners, *refs):
-    got, out_ref, got_s, sems = refs[:owners], refs[owners], refs[owners + 1], refs[owners + 2]
-    wait_all(start_all([(got[n], got_s.at[n]) for n in range(owners)], sems))
+        votes_s[o, :chans, :] = picked[:, o * cap : (o + 1) * cap]
+        votes_s[o, chans:, :] = facts_s[:, o * cap : (o + 1) * cap]
+    keep_votes = pltpu.make_async_copy(votes_s, votes_hbm, stores.at[1])
+    keep_votes.start()
+    wait_all([keep_feat, keep_votes])
+
+
+def sums_kernel(got_ref, out_ref):
+    sources, _, cap = got_ref.shape
     chans, voxels = out_ref.shape
-    cap = got_s.shape[2]
     total = jnp.zeros(out_ref.shape, F32)
-    for n in range(owners):
-        label = got_s[n, chans:, :].astype(F32)[0:1]
+    for n in range(sources):
+        label = got_ref[n, chans:, :].astype(F32)[0:1]
         hot = (label == iota((voxels, cap), 0).astype(F32)).astype(BF16)
-        total = total + dot_t(got_s[n, :chans, :], hot)
+        total = total + dot_t(got_ref[n, :chans, :], hot)
     out_ref[...] = total
 
 
-def call(kernel, outs, scratch, flops, spaces):
+def call(kernel, outs, scratch, flops, spaces, out_space=pl.ANY, limit=VMEM):
     return pl.pallas_call(
         kernel,
         out_shape=outs,
@@ -476,9 +522,9 @@
             pl.BlockSpec(memory_space={"s": pltpu.SMEM, "v": pltpu.VMEM, "a": pl.ANY}[c])
             for c in spaces
         ],
-        out_specs=[pl.BlockSpec(memory_space=pltpu.VMEM)] * len(outs),
+        out_specs=[pl.BlockSpec(memory_space=out_space)] * len(outs),
         scratch_shapes=scratch,
-        compiler_params=pltpu.CompilerParams(vmem_limit_bytes=VMEM),
+        compiler_params=pltpu.CompilerParams(vmem_limit_bytes=limit),
         cost_estimate=pl.CostEstimate(flops=flops, bytes_accessed=2 << 20, transcendentals=0),
     )
 
@@ -538,6 +584,8 @@
             vmem((tiles, per, chans, LANES), BF16),
             vmem((tiles, chans, LANES), BF16),
             vmem((chans, slots), BF16),
+            vmem((chans, slots), BF16),
+            dma((2,)),
         ],
         2_000_000_000,
         "saaaaaaa",
@@ -557,16 +605,9 @@
     while bit > 1:
         mid += [turned(block, "grp", bit) for block in [sent] + mid]
         bit //= 2
-    qkv_t, out_t, up_t, hot, order, label = call(
-        functools.partial(tables_kernel, run, cap),
-        [
-            sds((3 * chans, chans), BF16),
-            sds((chans, chans), BF16),
-            sds((hidden, chans), BF16),
-            sds((slots, codes), BF16),
-            sds((slots, slots), BF16),
-            sds((16, codes), BF16),
-        ],
+    weights, facts = call(
+        functools.partial(tables_kernel, cap),
+        [sds((4 * chans + hidden, chans), BF16), sds((16, codes), BF16)],
         [
             vmem((chans, 3 * chans), BF16),
             vmem((chans, chans), BF16),
@@ -575,6 +616,9 @@
             vmem((1, votes), jnp.int32),
             vmem((1, votes), jnp.int32),
             dma((6,)),
+            vmem((4 * chans + hidden, chans), BF16),
+            vmem((16, codes), BF16),
+            dma((2,)),
         ],
         2_000_000_000,
         "aaaaaa",
@@ -586,11 +630,9 @@
         vote_owner.reshape(1, votes),
         vote_voxel.reshape(1, votes),
     )
-    state = [
-        sds((tiles, 2, 8, LANES), F32),
-        sds((tiles, 2, 8, LANES), F32),
-        sds((tiles, rows16, 16, LANES), F32),
-    ]
+    q_like = ((tiles, rows16, 16, LANES), BF16)
+    ends_like = ((tiles, 4, 8, LANES), F32)
+    acc_like = ((tiles, rows16, 16, LANES), F32)
 
     def key_scratch(blocks):
         return [
@@ -600,62 +642,81 @@
             vmem((blocks * run, 2, 8, LANES), F32),
         ]
 
-    query, *held = call(
+    query, ends, acc = call(
         functools.partial(near_kernel, run),
-        [sds((tiles, rows16, 16, LANES), BF16)] + state,
-        [vmem((chans, slots), BF16), dma] + key_scratch(2),
+        [sds(*q_like), sds(*ends_like), sds(*acc_like)],
+        [
+            vmem((chans, slots), BF16),
+            vmem((chans, slots), BF16),
+            vmem((3 * chans, chans), BF16),
+            dma((3,)),
+            vmem(*q_like),
+            vmem(*ends_like),
+            vmem(*acc_like),
+            dma((3,)),
+        ]
+        + key_scratch(2),
         3_000_000_000,
-        "vav",
-    )(sent, near, qkv_t)
+        "aaa",
+    )(sent, near, weights)
     mid, query = lax.optimization_barrier((mid, query))
     far = [turned(block, "grp", 1) for block in mid]
-    held = call(
+    ends, acc = call(
         functools.partial(middle_kernel, run, len(mid)),
-        state,
-        [vmem((len(mid), chans, slots), BF16), dma((len(mid),))] + key_scratch(len(mid)),
+        [sds(*ends_like), sds(*acc_like)],
+        [
+            vmem((len(mid), chans, slots), BF16),
+            dma((len(mid),)),
+            vmem(*q_like),
+            vmem(*ends_like),
+            vmem(*acc_like),
+            vmem((2 * chans, chans), BF16),
+            dma((4,)),
+            dma((2,)),
+        ]
+        + key_scratch(len(mid)),
         2_000_000_000,
-        "a" * len(mid) + "vvvvv",
-    )(*mid, query, *held, qkv_t)
-    features_t, *ballots = call(
+        "a" * len(mid) + "aaaa",
+    )(*mid, query, ends, acc, weights)
+    features_t, ballots = call(
         functools.partial(second_kernel, run, cap, len(far)),
-        [sds((chans, slots), F32)] + [sds((chans + 16, cap), BF16)] * owners,
-        [vmem((len(far), chans, slots), BF16), dma((len(far),))]
+        [sds((chans, slots), F32), sds((owners, chans + 16, cap), BF16)],
+        [
+            vmem((len(far), chans, slots), BF16),
+            dma((len(far),)),
+            vmem((4 * chans + hidden, chans), BF16),
+            vmem(*q_like),
+            vmem(*ends_like),
+            vmem(*acc_like),
+            vmem((chans, slots), BF16),
+            vmem((1, chans), F32),
+            vmem((chans, hidden), BF16),
+            vmem((16, codes), BF16),
+            dma((8,)),
+            vmem((chans, slots), F32),
+            vmem((owners, chans + 16, cap), BF16),
+            dma((2,)),
+        ]
         + key_scratch(len(far))
-        + [
-            vmem((tiles, chans, LANES), BF16),
-            vmem((chans, slots), BF16),
-            vmem((chans, slots), BF16),
-            vmem((hidden, chans), BF16),
-            vmem((chans, hidden), BF16),
-            vmem((slots, codes), BF16),
-            vmem((slots, slots), BF16),
-            dma((5,)),
-        ],
+        + [vmem((tiles, chans, LANES), BF16), vmem((chans, slots), BF16)],
         3_000_000_000,
-        "s" + "a" * len(far) + "avvvvvvvaaaav",
+        "s" + "a" * (len(far) + 8),
     )(
         node_count,
         *far,
+        query,
+        ends,
+        acc,
+        weights,
         first,
-        query,
-        *held,
         gain_three.reshape(1, chans),
-        qkv_t,
-        out_t,
-        up_t,
         w_down.T,
-        hot,
-        order,
-        label,
-    )
-    got = [ballots[0]] + [turned(ballots[k], "tile", k) for k in range(owners - 1, 0, -1)]
+        facts,
+    )
+    got = lax.all_to_all(ballots, "tile", split_axis=0, concat_axis=0, tiled=True)
     (sums_t,) = call(
-        functools.partial(sums_kernel, owners),
-        [sds((chans, VOX_DEV), F32)],
-        [vmem((owners, chans + 16, cap), BF16), dma((owners,))],
-        200_000_000,
-        "a" * owners,
-    )(*got)
+        sums_kernel, [sds((chans, VOX_DEV), F32)], [], 200_000_000, "v", pltpu.VMEM, 16 << 20
+    )(got)
     return (features_t.T, sums_t.T)
 
 

time: 60.9 us -> 56.5 us (0.928)
  blocking collectives: 0 us -> 19.4 us
  starting transfers between devices: 14.4 us -> 3.08 us
  Pallas kernels: 40.1 us -> 31.8 us
  waiting for transfers between devices: 4.66 us -> 0.56 us
    all_to_all x0 -> x1, blocking collectives: none -> 19.4 us  [body(): lax.all_to_all(ballots, 'tile', split_axis=0, concat_axis=0, tiled=True)]
    ppermute x10 -> x3, starting transfers between devices: 14.4 us -> 3.08 us  [turned(): return lax.ppermute(x, axis, [(i, i ^ bit) for i in range(n)])]
    pallas_call x4, Pallas kernels: 20.6 us -> 15 us  [the longest x1 6.51 us: body(): call(functools.partial(near_kernel, run), [sds(*q_like), sds(*ends_like),...]
    ppermute x10 -> x3, waiting for transfers between devices: 4.66 us -> 0.56 us  [turned(): return lax.ppermute(x, axis, [(i, i ^ bit) for i in range(n)])]
    pallas_call x1, Pallas kernels: 10.1 us -> 8.05 us  [body(): call(functools.partial(second_kernel, run, cap, len(far)), [sds((chans, s...]
    pallas_call x1, Pallas kernels: 9.37 us -> 8.72 us  [body(): call(functools.partial(first_kernel, run), [sds((chans, slots), BF16), sd...]
  transfers between devices with their start and end apart: 10 -> 3, of which waited for: 6 -> 1; matrix products, arithmetic and copies ran while one was open for 0% -> 0% of each run, Pallas kernels for 31% -> 25%
where the time goes in v4:
time: 56.5 us; the launch traced here: 56.2 us
  Pallas kernels  31.8 us (56%)
  blocking collectives  19.4 us (34%)
  starting transfers between devices  3.08 us (5%)
  between operations  1.34 us (2%)
    all_to_all x1, blocking collectives, body(): lax.all_to_all(ballots, 'tile', split_axis=0, concat_axis=0, tiled=True)  19.4 us
    pallas_call x1, Pallas kernels, body(): call(functools.partial(first_kernel, run), [sds((chans, slots), BF16), sd...  8.72 us
    pallas_call x1, Pallas kernels, body(): call(functools.partial(second_kernel, run, cap, len(far)), [sds((chans, s...  8.05 us
    pallas_call x1, Pallas kernels, body(): call(functools.partial(near_kernel, run), [sds(*q_like), sds(*ends_like),...  6.51 us
    pallas_call x1, Pallas kernels, body(): call(functools.partial(middle_kernel, run, len(mid)), [sds(*ends_like), s...  4.55 us
    ppermute x3, starting transfers between devices, turned(): return lax.ppermute(x, axis, [(i, i ^ bit) for i in range(n)])  3.08 us
    pallas_call x1, Pallas kernels, body(): call(functools.partial(tables_kernel, cap), [sds((4 * chans + hidden, cha...  2.93 us
  transfers between devices with their start and end apart: 3, of which 1 were waited for; matrix products, arithmetic and copies ran while one was open for 0% of the time, Pallas kernels for 25%

profile of v4, /device:TPU:0, one launch (start us, length us, event | category | flops | bytes accessed | tf_op | source)
XLA Modules:
  0.0 56.2 jit_solution(12465378349160639144)
XLA Ops:
  1.3 8.7 %shard_map.167 = (bf16[192,1024]{1,0:T(8,128)(2,1)}, bf16[192,1024]{1,0:T(8,128)(2,1)}) custom-call(s32[1]{0:T(128)S(6)} %copy.18.count_ref, bf16[192,1024]{1,0:T(8,128)(2,1)} %bitcast.11, s32[1,1024]{1,0:T(1,128)} %bitcast.13, f32[3,192]{1,0:T(4,128)} %pos_hbm.1, f32[1,192]{1,0:T(1,128)} %bitcast.17, f32[1,192]{1,0:T(1,128)} %bitcast.18, ...), custom_call_target="tpu_custom_call" | custom-call | flops 2000000000 | bytes 2097152 | tf_op jit(solution)/shard_map/pallas_call | solution.py:569
  10.0 0.5 collective-permute-start.1
  10.5 2.6 %collective-permute-start = (bf16[192,1024]{1,0:T(8,128)(2,1)}, bf16[192,1024]{1,0:T(8,128)(2,1)}, u32[]{:S(2)}, u32[]{:S(2)}) collective-permute-start(bf16[192,1024]{1,0:T(8,128)(2,1)} %get-tuple-element.15.own_hbm), channel_id=1, source_target_pairs={{0,16},{8,24},{16,0},{24,8},{1,17},{9,25},{17,1},{25,9},{2,18},{10... | collective-permute-start | bytes 1179656 | tf_op jit(solution)/shard_map/ppermute | solution.py:534
  13.1 2.9 %shard_map.168 = (bf16[1536,192]{1,0:T(8,128)(2,1)}, bf16[16,1024]{1,0:T(8,128)(2,1)}) custom-call(bf16[192,576]{1,0:T(8,128)(2,1)} %qkv_hbm.3, bf16[192,192]{1,0:T(8,128)(2,1)} %out_hbm.3, bf16[192,768]{1,0:T(8,128)(2,1)} %up_hbm.1, s32[1,512]{1,0:T(1,128)} %bitcast.14, s32[1,512]{1,0:T(1,128)} %bitcast.15, s32[1,512]{1,0:T(1,128)} %bitcast.16), custom_call_target="tpu_custom_call" | custom-call | flops 2000000000 | bytes 2097152 | tf_op jit(solution)/shard_map/pallas_call | solution.py:608
  16.0 0.0 collective-permute-done.1.near_hbm
  16.0 6.5 %shard_map.169 = (bf16[8,12,16,128]{3,2,1,0:T(8,128)(2,1)}, f32[8,4,8,128]{3,2,1,0:T(8,128)}, f32[8,12,16,128]{3,2,1,0:T(8,128)}) custom-call(bf16[192,1024]{1,0:T(8,128)(2,1)} %get-tuple-element.15.own_hbm, bf16[192,1024]{1,0:T(8,128)(2,1)} %collective-permute-done.1.near_hbm, bf16[1536,192]{1,0:T(8,128)(2,1)} %get-tuple-element.16.weights_hbm.refs_4_), custom_call_target="tpu_custom_call" | custom-call | flops 3000000000 | bytes 2097152 | tf_op jit(solution)/shard_map/pallas_call | solution.py:645
  22.6 0.6 collective-permute-done.refs_0_
  23.1 0.0 collective-permute-start.2
  23.1 4.5 %shard_map.170 = (f32[8,4,8,128]{3,2,1,0:T(8,128)}, f32[8,12,16,128]{3,2,1,0:T(8,128)}) custom-call(bf16[192,1024]{1,0:T(8,128)(2,1)} %collective-permute-done.refs_0_, bf16[8,12,16,128]{3,2,1,0:T(8,128)(2,1)} %get-tuple-element.19.refs_1_, f32[8,4,8,128]{3,2,1,0:T(8,128)} %get-tuple-element.20.refs_2_, f32[8,12,16,128]{3,2,1,0:T(8,128)} %get-tuple-element.21.refs_3_, ...), custom_call_target="tpu_custom_call" | custom-call | flops 2000000000 | bytes 2097152 | tf_op jit(solution)/shard_map/pallas_call | solution.py:664
  27.7 0.0 collective-permute-done.2.refs_0_
  27.7 8.1 %shard_map.171 = (f32[192,1024]{1,0:T(8,128)}, bf16[8,208,128]{2,1,0:T(8,128)(2,1)}) custom-call(s32[1]{0:T(128)S(6)} %copy.18.count_ref, bf16[192,1024]{1,0:T(8,128)(2,1)} %collective-permute-done.2.refs_0_, bf16[8,12,16,128]{3,2,1,0:T(8,128)(2,1)} %get-tuple-element.19.refs_1_, f32[8,4,8,128]{3,2,1,0:T(8,128)} %get-tuple-element.22.refs_2_, ...), custom_call_target="tpu_custom_call" | custom-call | flops 3000000000 | bytes 2097152 | tf_op jit(solution)/shard_map/pallas_call | solution.py:681
  35.7 19.4 %all_to_all.5.got_ref = bf16[8,208,128]{2,1,0:T(8,128)(2,1)S(1)} all-to-all(bf16[8,208,128]{2,1,0:T(8,128)(2,1)} %get-tuple-element.27), channel_id=1, replica_groups=mesh['grp'=4,'tile'=8] {'tile'}, dimensions={0} | all-to-all | bytes 851968 | tf_op jit(solution)/shard_map/all_to_all | solution.py:716
  55.1 1.0 %shard_map.172 = f32[192,256]{1,0:T(8,128)} custom-call(bf16[8,208,128]{2,1,0:T(8,128)(2,1)S(1)} %all_to_all.5.got_ref), custom_call_target="tpu_custom_call" | custom-call | flops 200000000 | bytes 2097152 | tf_op jit(solution)/shard_map/pallas_call | solution.py:717
Async XLA Ops:
  10.0 6.0 %collective-permute-start.1 = (bf16[192,1024]{1,0:T(8,128)(2,1)}, bf16[192,1024]{1,0:T(8,128)(2,1)}, u32[]{:S(2)}, u32[]{:S(2)}) collective-permute-start(bf16[192,1024]{1,0:T(8,128)(2,1)} %get-tuple-element.15.own_hbm), channel_id=1, source_target_pairs={{0,8},{8,0},{16,24},{24,16},{1,9},{9,1},{17,25},{25,17},{2,10},{10... | collective-permute-start | bytes 1179656 | tf_op jit(solution)/shard_map/ppermute | solution.py:534
  10.5 12.6 %collective-permute-start = (bf16[192,1024]{1,0:T(8,128)(2,1)}, bf16[192,1024]{1,0:T(8,128)(2,1)}, u32[]{:S(2)}, u32[]{:S(2)}) collective-permute-start(bf16[192,1024]{1,0:T(8,128)(2,1)} %get-tuple-element.15.own_hbm), channel_id=1, source_target_pairs={{0,16},{8,24},{16,0},{24,8},{1,17},{9,25},{17,1},{25,9},{2,18},{10... | collective-permute-start | bytes 1179656 | tf_op jit(solution)/shard_map/ppermute | solution.py:534
  23.1 4.6 %collective-permute-start.2 = (bf16[192,1024]{1,0:T(8,128)(2,1)}, bf16[192,1024]{1,0:T(8,128)(2,1)}, u32[]{:S(2)}, u32[]{:S(2)}) collective-permute-start(bf16[192,1024]{1,0:T(8,128)(2,1)} %collective-permute-done.refs_0_), channel_id=1, source_target_pairs={{0,8},{8,0},{16,24},{24,16},{1,9},{9,1},{17,25},{25,17},{2,10},{10... | collective-permute-start | bytes 1179656 | tf_op jit(solution)/shard_map/ppermute | solution.py:534

commit v5 on v4

--- a/solution.py
+++ b/solution.py
@@ -105,7 +105,7 @@
 def first_kernel(
     run, count_ref, nodes_hbm, ids_hbm, pos_hbm, gain_one_hbm, gain_two_hbm, qkv_hbm, out_hbm,
     first_hbm, sent_hbm, nodes_ref, ids_ref, pos_ref, gain_one_ref, gain_two_ref, qkv_ref, out_ref,
-    sems, qkv_s, q_s, k_s, v_s, ctx_s, n_s, first_s, stores
+    sems, qkv_s, q_s, k_s, v_s, ctx_s, n_s, first_s, sent_s, stores
 ):
     loads = start_all(
         [
@@ -129,17 +129,21 @@
         [pos_ref[...], gain_one_ref[...], gain_two_ref[...], jnp.zeros((3, chans), F32)], 0
     ).T
     ids = ids_ref[...]
-    start = None
+    coords = []
     for axis in range(3):
         total = jnp.zeros(ids.shape, jnp.int32)
         for level in range(6):
             bit = jnp.bitwise_and(jnp.right_shift(ids, 3 * level + axis), 1)
             total = total + bit * 2**level
-        term = cols[:, axis : axis + 1] * (total.astype(F32) / 64.0 - 0.5)
-        start = term if start is None else start + term
-    start = (nodes_ref[...].astype(F32) + start).astype(BF16)
-    nodes_ref[...] = start
-    n_s[...] = norm_t(start.astype(F32), cols[:, 3:4]).astype(BF16)
+        coords.append(total.astype(F32) / 64.0 - 0.5)
+    for t in range(tiles):
+        at = tile(t)
+        start = cols[:, 0:1] * coords[0][:, at]
+        for axis in range(1, 3):
+            start = start + cols[:, axis : axis + 1] * coords[axis][:, at]
+        start = (nodes_ref[:, at].astype(F32) + start).astype(BF16)
+        nodes_ref[:, at] = start
+        n_s[:, at] = norm_t(start.astype(F32), cols[:, 3:4]).astype(BF16)
     wait_all(loads[5:])
     qkv_t = transposed(qkv_ref[...])
     out_t = transposed(out_ref[...])
@@ -160,54 +164,70 @@
             v_s[t, w] = jnp.where(own_head, wide[:, tile(w)], 0.0).astype(BF16)
 
     lane_head = iota((WIN, chans), 1) // size
+    head_mask = [jnp.where(lane_head == h, 1.0, 0.0).astype(BF16) for h in range(HEADS)]
     window = iota((8, LANES), 1) // WIN
     rank = iota((WIN, LANES), 0) + WIN * (iota((WIN, LANES), 1) // WIN)
+    half = per * size
+
+    def by_window(made):
+        out = made(0)
+        for w in range(1, per):
+            out = jnp.where(window[None] == w, made(w), out)
+        return out
 
     def group(t, _):
         query = q_s[t]
-        scores = None
-        for w in range(per):
-            keys = k_s[t, w * WIN : (w + 1) * WIN, :]
-            by_head = jnp.concatenate(
-                [jnp.where(lane_head == h, keys, jnp.zeros_like(keys)) for h in range(HEADS)], 0
-            )
-            got = dot(by_head, query).reshape(-1, 8, LANES)
-            scores = got if w == 0 else jnp.where(window[None] == w, got, scores)
         mask = jnp.where(rank + t * LANES < count, 0.0, -1e9).astype(F32)
         mask = mask.reshape(WIN // 8, 8, LANES)
-        probs, inverse = [], []
-        for h in range(HEADS):
-            mine = scores[h * (WIN // 8) : (h + 1) * (WIN // 8)] + mask
-            top = fold8(mine, jnp.maximum)
-            weight = jnp.exp(mine - top[None])
-            inverse.append(1.0 / fold8(weight, jnp.add))
-            probs.append(weight.reshape(WIN, LANES).astype(BF16))
-        half = per * size
+
+        def scores_of(j):
+            def made(w):
+                keys = k_s[t, w * WIN : (w + 1) * WIN, :]
+                heads = [keys * head_mask[j * per + h] for h in range(per)]
+                return dot(jnp.concatenate(heads, 0), query).reshape(-1, 8, LANES)
+
+            return by_window(made)
+
         parts = []
+        coming = scores_of(0)
         for j in range(HEADS // per):
-            weight = jnp.concatenate(probs[j * per : (j + 1) * per], 0)
-            ctx = None
-            for w in range(per):
-                got = dot(v_s[t, w, j * half : (j + 1) * half, :], weight).reshape(-1, 8, LANES)
-                ctx = got if w == 0 else jnp.where(window[None] == w, got, ctx)
+            scores = coming
+            if j + 1 < HEADS // per:
+                coming = scores_of(j + 1)
+            probs, inverse = [], []
             for h in range(per):
-                block = ctx[h * (size // 8) : (h + 1) * (size // 8)] * inverse[j * per + h][None]
+                mine = scores[h * (WIN // 8) : (h + 1) * (WIN // 8)] + mask
+                top = fold8(mine, jnp.maximum)
+                weight = jnp.exp(mine - top[None])
+                inverse.append(1.0 / fold8(weight, jnp.add))
+                probs.append(weight.reshape(WIN, LANES).astype(BF16))
+            weight = jnp.concatenate(probs, 0)
+            ctx = by_window(
+                lambda w: dot(v_s[t, w, j * half : (j + 1) * half, :], weight).reshape(
+                    -1, 8, LANES
+                )
+            )
+            for h in range(per):
+                block = ctx[h * (size // 8) : (h + 1) * (size // 8)] * inverse[h][None]
                 parts.append(block.reshape(size, LANES))
         ctx_s[t] = jnp.concatenate(parts, 0).astype(BF16)
         return 0
 
     lax.fori_loop(0, tiles, group, 0, unroll=2)
     ctx = jnp.concatenate([ctx_s[t] for t in range(tiles)], 1)
-    first = (nodes_ref[...].astype(F32) + dot(out_t, ctx)).astype(BF16)
-    first_s[...] = first
+    moved = dot(out_t, ctx)
+    for t in range(tiles):
+        at = tile(t)
+        first = (nodes_ref[:, at].astype(F32) + moved[:, at]).astype(BF16)
+        first_s[:, at] = first
+        normed = norm_t(first.astype(F32), cols[:, 4:5])
+        kept = iota((1, LANES), 1) + t * LANES < count
+        head = jnp.where((iota((16, LANES), 0) > 0) | kept, normed[:16], FLAG)
+        n_s[:, at] = jnp.concatenate([head, normed[16:]], 0).astype(BF16)
     keep_first = pltpu.make_async_copy(first_s, first_hbm, stores.at[0])
     keep_first.start()
-    normed = norm_t(first.astype(F32), cols[:, 4:5])
-    kept = iota((1, slots), 1) < count
-    head = jnp.where((iota((16, slots), 0) > 0) | kept, normed[:16], FLAG)
-    normed = jnp.concatenate([head, normed[16:]], 0).astype(BF16)
-    n_s[...] = dot(normed, reorder(slots, run)).astype(BF16)
-    send = pltpu.make_async_copy(n_s, sent_hbm, stores.at[1])
+    sent_s[...] = dot(n_s[...], reorder(slots, run)).astype(BF16)
+    send = pltpu.make_async_copy(sent_s, sent_hbm, stores.at[1])
     send.start()
     wait_all([keep_first, send])
 
@@ -241,7 +261,7 @@
     weights_s[4 * chans :] = transposed(up_ref[...])
     keep_weights = pltpu.make_async_copy(weights_s, weights_hbm, stores.at[0])
     keep_weights.start()
-    owner = owner_ref[...]
+    owner = jnp.bitwise_xor(owner_ref[...], lax.axis_index("tile"))
     hot = owner == iota((owners, votes), 0)
     upto = (iota((votes, votes), 0) <= iota((votes, votes), 1)).astype(BF16)
     rank = jnp.sum(jnp.where(hot, dot(hot.astype(BF16), upto), 0.0), 0, keepdims=True)
@@ -428,16 +448,16 @@
     wait_all(start_all([(ends_s, ends_out), (acc_s, acc_out)], stores))
 
 
-def second_kernel(run, cap, far, count_ref, *refs):
+def second_kernel(run, cap, far, owners, count_ref, *refs):
     blocks, refs = refs[:far], refs[far:]
     (
-        q_hbm, ends_hbm, acc_hbm, weights_hbm, first_hbm, gain_hbm, down_hbm, facts_hbm,
-        feat_hbm, votes_hbm
-    ) = refs[:10]
+        q_hbm, ends_hbm, acc_hbm, weights_hbm, first_hbm, gain_hbm, down_hbm, facts_hbm, feat_hbm
+    ) = refs[:9]
+    votes_hbm, refs = refs[9 : 9 + owners], refs[9 + owners :]
     (
         block_s, sems, weights_s, q_s, ends_s, acc_s, first_s, gain_s, down_s, facts_s, rest,
-        feat_s, votes_s, stores, k_s, v_s, m_s, s_s, ctx_s, bf_s
-    ) = refs[10:]
+        feat_s, votes_s, stores, k_s, v_s, m_s, s_s, ctx_s, bf_s, inner_s, hidden_s
+    ) = refs
     loads = start_all([(blocks[n], block_s.at[n]) for n in range(far)], sems)
     later = start_all(
         [
@@ -453,7 +473,6 @@
         rest,
     )
     chans, slots = first_s.shape
-    owners = votes_s.shape[0]
     tiles = slots // LANES
     count = count_ref[0]
     wait_all(loads + later[:1])
@@ -474,47 +493,56 @@
     ctx = jnp.concatenate([ctx_s[t] for t in range(tiles)], 1)
     ctx = dot_t(ctx, reorder(slots, run)).astype(BF16)
     gain = jnp.concatenate([gain_s[...], jnp.zeros((7, chans), F32)], 0).T[:, 0:1]
-    second = first_s[...].astype(F32) + dot(weights_s[3 * chans : 4 * chans], ctx)
-    inner = norm_t(second, gain).astype(BF16)
+    moved = dot(weights_s[3 * chans : 4 * chans], ctx)
+    for t in range(tiles):
+        at = tile(t)
+        second = first_s[:, at].astype(F32) + moved[:, at]
+        feat_s[:, at] = second
+        inner_s[:, at] = norm_t(second, gain).astype(BF16)
     kept = iota((1, slots), 1) < count
     wide = 2 * LANES
-    cuts = [slice(at, at + wide) for at in range(0, slots, wide)]
-    up_t = weights_s[4 * chans :]
-    raised = dot(up_t, inner[:, cuts[0]])
-    for n, at in enumerate(cuts):
-        now = raised
-        if n + 1 < len(cuts):
-            raised = dot(up_t, inner[:, cuts[n + 1]])
-        hidden = jax.nn.gelu(now).astype(BF16)
-        third = second[:, at] + dot(down_s[...], hidden)
-        third = jnp.where(kept[:, at], third, 0.0)
-        feat_s[:, at] = third
-        bf_s[:, at] = third.astype(BF16)
-    keep_feat = pltpu.make_async_copy(feat_s, feat_hbm, stores.at[0])
-    keep_feat.start()
+    part = chans // 2
+    for n in range(slots // wide):
+        at = slice(n * wide, (n + 1) * wide)
+        inner = inner_s[:, at]
+        for m in range(down_s.shape[1] // part):
+            row = 4 * chans + m * part
+            raised = dot(weights_s[row : row + part], inner)
+            hidden_s[n % 2, m * part : (m + 1) * part] = jax.nn.gelu(raised).astype(BF16)
+        for m in range(chans // part):
+            rows = slice(m * part, (m + 1) * part)
+            third = feat_s[rows, at] + dot(down_s[rows, :], hidden_s[n % 2])
+            third = jnp.where(kept[:, at], third, 0.0)
+            feat_s[rows, at] = third
+            bf_s[rows, at] = third.astype(BF16)
+    keep = [pltpu.make_async_copy(feat_s, feat_hbm, stores.at[owners])]
+    keep[0].start()
     facts = facts_s[...].astype(F32)
     low, high = facts[2:3].astype(jnp.int32), facts[1:2].astype(jnp.int32)
     picked = dot(bf_s[...], place(low, high, tiles)).astype(BF16)
     for o in range(owners):
         votes_s[o, :chans, :] = picked[:, o * cap : (o + 1) * cap]
         votes_s[o, chans:, :] = facts_s[:, o * cap : (o + 1) * cap]
-    keep_votes = pltpu.make_async_copy(votes_s, votes_hbm, stores.at[1])
-    keep_votes.start()
-    wait_all([keep_feat, keep_votes])
-
-
-def sums_kernel(got_ref, out_ref):
-    sources, _, cap = got_ref.shape
+        keep.append(pltpu.make_async_copy(votes_s.at[o], votes_hbm[o], stores.at[o]))
+        keep[-1].start()
+    wait_all(keep)
+
+
+def sums_kernel(owners, *refs):
+    got, out_ref, got_s, sems = refs[:owners], refs[owners], refs[owners + 1], refs[owners + 2]
+    loads = start_all([(got[n], got_s.at[n]) for n in range(owners)], sems)
     chans, voxels = out_ref.shape
+    cap = got_s.shape[2]
     total = jnp.zeros(out_ref.shape, F32)
-    for n in range(sources):
-        label = got_ref[n, chans:, :].astype(F32)[0:1]
+    wait_all(loads)
+    for n in range(owners):
+        label = got_s[n, chans:, :].astype(F32)[0:1]
         hot = (label == iota((voxels, cap), 0).astype(F32)).astype(BF16)
-        total = total + dot_t(got_ref[n, :chans, :], hot)
+        total = total + dot_t(got_s[n, :chans, :], hot)
     out_ref[...] = total
 
 
-def call(kernel, outs, scratch, flops, spaces, out_space=pl.ANY, limit=VMEM):
+def call(kernel, outs, scratch, flops, spaces, out_space=pl.ANY):
     return pl.pallas_call(
         kernel,
         out_shape=outs,
@@ -524,7 +552,7 @@
         ],
         out_specs=[pl.BlockSpec(memory_space=out_space)] * len(outs),
         scratch_shapes=scratch,
-        compiler_params=pltpu.CompilerParams(vmem_limit_bytes=limit),
+        compiler_params=pltpu.CompilerParams(vmem_limit_bytes=VMEM),
         cost_estimate=pl.CostEstimate(flops=flops, bytes_accessed=2 << 20, transcendentals=0),
     )
 
@@ -585,6 +613,7 @@
             vmem((tiles, chans, LANES), BF16),
             vmem((chans, slots), BF16),
             vmem((chans, slots), BF16),
+            vmem((chans, slots), BF16),
             dma((2,)),
         ],
         2_000_000_000,
@@ -678,9 +707,9 @@
         2_000_000_000,
         "a" * len(mid) + "aaaa",
     )(*mid, query, ends, acc, weights)
-    features_t, ballots = call(
-        functools.partial(second_kernel, run, cap, len(far)),
-        [sds((chans, slots), F32), sds((owners, chans + 16, cap), BF16)],
+    features_t, *ballots = call(
+        functools.partial(second_kernel, run, cap, len(far), owners),
+        [sds((chans, slots), F32)] + [sds((chans + 16, cap), BF16)] * owners,
         [
             vmem((len(far), chans, slots), BF16),
             dma((len(far),)),
@@ -695,10 +724,15 @@
             dma((8,)),
             vmem((chans, slots), F32),
             vmem((owners, chans + 16, cap), BF16),
-            dma((2,)),
+            dma((owners + 1,)),
         ]
         + key_scratch(len(far))
-        + [vmem((tiles, chans, LANES), BF16), vmem((chans, slots), BF16)],
+        + [
+            vmem((tiles, chans, LANES), BF16),
+            vmem((chans, slots), BF16),
+            vmem((chans, slots), BF16),
+            vmem((2, hidden, 2 * LANES), BF16),
+        ],
         3_000_000_000,
         "s" + "a" * (len(far) + 8),
     )(
@@ -713,10 +747,15 @@
         w_down.T,
         facts,
     )
-    got = lax.all_to_all(ballots, "tile", split_axis=0, concat_axis=0, tiled=True)
+    got = [ballots[0]] + [turned(ballots[k], "tile", k) for k in range(owners - 1, 0, -1)]
     (sums_t,) = call(
-        sums_kernel, [sds((chans, VOX_DEV), F32)], [], 200_000_000, "v", pltpu.VMEM, 16 << 20
-    )(got)
+        functools.partial(sums_kernel, owners),
+        [sds((chans, VOX_DEV), F32)],
+        [vmem((owners, chans + 16, cap), BF16), dma((owners,))],
+        200_000_000,
+        "a" * owners,
+        pltpu.VMEM,
+    )(*got)
     return (features_t.T, sums_t.T)
 
 

time: 56.5 us -> 56.1 us (level)
  blocking collectives: 19.4 us -> 0 us
  starting transfers between devices: 3.08 us -> 14.5 us
  waiting for transfers between devices: 0.56 us -> 5.29 us
  Pallas kernels: 31.8 us -> 34.6 us
    all_to_all x1 -> x0, blocking collectives: 19.4 us -> none  [body(): lax.all_to_all(ballots, 'tile', split_axis=0, concat_axis=0, tiled=True)]
    ppermute x3 -> x10, starting transfers between devices: 3.08 us -> 14.5 us  [turned(): return lax.ppermute(x, axis, [(i, i ^ bit) for i in range(n)])]
    ppermute x3 -> x10, waiting for transfers between devices: 0.56 us -> 5.29 us  [turned(): return lax.ppermute(x, axis, [(i, i ^ bit) for i in range(n)])]
    pallas_call x2, Pallas kernels: 9.1 us -> 10.7 us  [the longest x1 8.58 us: body(): call(functools.partial(second_kernel, run, cap, len(far), owners), [sds((...]
    pallas_call x1, Pallas kernels: 8.72 us -> 9.93 us  [body(): call(functools.partial(first_kernel, run), [sds((chans, slots), BF16), sd...]
  transfers between devices with their start and end apart: 3 -> 10, of which waited for: 1 -> 7; matrix products, arithmetic and copies ran while one was open for 0% -> 0% of each run, Pallas kernels for 25% -> 25%
where the time goes in v5:
time: 56.1 us; the launch traced here: 55.8 us
  Pallas kernels  34.6 us (62%)
  starting transfers between devices  14.5 us (26%)
  waiting for transfers between devices  5.29 us (9%)
  between operations  1.34 us (2%)
    ppermute x10, starting transfers between devices, turned(): return lax.ppermute(x, axis, [(i, i ^ bit) for i in range(n)])  14.5 us
    pallas_call x1, Pallas kernels, body(): call(functools.partial(first_kernel, run), [sds((chans, slots), BF16), sd...  9.93 us
    pallas_call x1, Pallas kernels, body(): call(functools.partial(second_kernel, run, cap, len(far), owners), [sds((...  8.58 us
    pallas_call x1, Pallas kernels, body(): call(functools.partial(near_kernel, run), [sds(*q_like), sds(*ends_like),...  6.51 us
    ppermute x10, waiting for transfers between devices, turned(): return lax.ppermute(x, axis, [(i, i ^ bit) for i in range(n)])  5.29 us
    pallas_call x1, Pallas kernels, body(): call(functools.partial(middle_kernel, run, len(mid)), [sds(*ends_like), s...  4.58 us
    pallas_call x1, Pallas kernels, body(): call(functools.partial(tables_kernel, cap), [sds((4 * chans + hidden, cha...  2.95 us
    pallas_call x1, Pallas kernels, body(): call(functools.partial(sums_kernel, owners), [sds((chans, VOX_DEV), F32)]...  2.1 us
  transfers between devices with their start and end apart: 10, of which 7 were waited for; matrix products, arithmetic and copies ran while one was open for 0% of the time, Pallas kernels for 25%

profile of v5, /device:TPU:0, one launch (start us, length us, event | category | flops | bytes accessed | tf_op | source)
XLA Modules:
  0.0 55.8 jit_solution(884916931276615023)
XLA Ops:
  1.3 9.9 %shard_map.167 = (bf16[192,1024]{1,0:T(8,128)(2,1)}, bf16[192,1024]{1,0:T(8,128)(2,1)}) custom-call(s32[1]{0:T(128)S(6)} %copy.18.count_ref, bf16[192,1024]{1,0:T(8,128)(2,1)} %bitcast.11, s32[1,1024]{1,0:T(1,128)} %bitcast.13, f32[3,192]{1,0:T(4,128)} %pos_hbm.1, f32[1,192]{1,0:T(1,128)} %bitcast.17, f32[1,192]{1,0:T(1,128)} %bitcast.18, ...), custom_call_target="tpu_custom_call" | custom-call | flops 2000000000 | bytes 2097152 | tf_op jit(solution)/shard_map/pallas_call | solution.py:597
  11.2 0.5 collective-permute-start.1
  11.7 2.6 %collective-permute-start = (bf16[192,1024]{1,0:T(8,128)(2,1)}, bf16[192,1024]{1,0:T(8,128)(2,1)}, u32[]{:S(2)}, u32[]{:S(2)}) collective-permute-start(bf16[192,1024]{1,0:T(8,128)(2,1)} %get-tuple-element.22.own_hbm), channel_id=1, source_target_pairs={{0,16},{8,24},{16,0},{24,8},{1,17},{9,25},{17,1},{25,9},{2,18},{10... | collective-permute-start | bytes 1179656 | tf_op jit(solution)/shard_map/ppermute | solution.py:562
  14.3 2.9 %shard_map.168 = (bf16[1536,192]{1,0:T(8,128)(2,1)}, bf16[16,1024]{1,0:T(8,128)(2,1)}) custom-call(bf16[192,576]{1,0:T(8,128)(2,1)} %qkv_hbm.3, bf16[192,192]{1,0:T(8,128)(2,1)} %out_hbm.3, bf16[192,768]{1,0:T(8,128)(2,1)} %up_hbm.1, s32[1,512]{1,0:T(1,128)} %bitcast.14, s32[1,512]{1,0:T(1,128)} %bitcast.15, s32[1,512]{1,0:T(1,128)} %bitcast.16), custom_call_target="tpu_custom_call" | custom-call | flops 2000000000 | bytes 2097152 | tf_op jit(solution)/shard_map/pallas_call | solution.py:637
  17.3 0.0 collective-permute-done.1.near_hbm
  17.3 6.5 %shard_map.169 = (bf16[8,12,16,128]{3,2,1,0:T(8,128)(2,1)}, f32[8,4,8,128]{3,2,1,0:T(8,128)}, f32[8,12,16,128]{3,2,1,0:T(8,128)}) custom-call(bf16[192,1024]{1,0:T(8,128)(2,1)} %get-tuple-element.22.own_hbm, bf16[192,1024]{1,0:T(8,128)(2,1)} %collective-permute-done.1.near_hbm, bf16[1536,192]{1,0:T(8,128)(2,1)} %get-tuple-element.23.weights_hbm.refs_4_), custom_call_target="tpu_custom_call" | custom-call | flops 3000000000 | bytes 2097152 | tf_op jit(solution)/shard_map/pallas_call | solution.py:674
  23.8 0.5 collective-permute-done.refs_0_
  24.3 0.0 collective-permute-start.2
  24.3 4.6 %shard_map.170 = (f32[8,4,8,128]{3,2,1,0:T(8,128)}, f32[8,12,16,128]{3,2,1,0:T(8,128)}) custom-call(bf16[192,1024]{1,0:T(8,128)(2,1)} %collective-permute-done.refs_0_, bf16[8,12,16,128]{3,2,1,0:T(8,128)(2,1)} %get-tuple-element.26.refs_1_, f32[8,4,8,128]{3,2,1,0:T(8,128)} %get-tuple-element.27.refs_2_, f32[8,12,16,128]{3,2,1,0:T(8,128)} %get-tuple-element.28.refs_3_, ...), custom_call_target="tpu_custom_call" | custom-call | flops 2000000000 | bytes 2097152 | tf_op jit(solution)/shard_map/pallas_call | solution.py:693
  28.9 0.0 collective-permute-done.2.refs_0_
  28.9 8.6 %shard_map.171 = (f32[192,1024]{1,0:T(8,128)}, bf16[208,128]{1,0:T(8,128)(2,1)}, bf16[208,128]{1,0:T(8,128)(2,1)}, bf16[208,128]{1,0:T(8,128)(2,1)}, bf16[208,12...) custom-call(s32[1]{0:T(128)S(6)} %copy.18.count_ref, ...), custom_call_target="tpu_custom_call" | custom-call | flops 3000000000 | bytes 2097152 | tf_op jit(solution)/shard_map/pallas_call | solution.py:710
  37.5 4.9 %collective-permute-start.3 = (bf16[208,128]{1,0:T(8,128)(2,1)}, bf16[208,128]{1,0:T(8,128)(2,1)}, u32[]{:S(2)}, u32[]{:S(2)}) collective-permute-start(bf16[208,128]{1,0:T(8,128)(2,1)} %get-tuple-element.35), channel_id=1, source_target_pairs={{0,7},{1,6},{2,5},{3,4},{4,3},{5,2},{6,1},{7,0},{8,15},{9,14},{10,... | collective-permute-start | bytes 159752 | tf_op jit(solution)/shard_map/ppermute | solution.py:562
  42.4 0.2 collective-permute-start.4
  42.6 0.7 %collective-permute-start.5 = (bf16[208,128]{1,0:T(8,128)(2,1)}, bf16[208,128]{1,0:T(8,128)(2,1)}, u32[]{:S(2)}, u32[]{:S(2)}) collective-permute-start(bf16[208,128]{1,0:T(8,128)(2,1)} %get-tuple-element.37), channel_id=1, source_target_pairs={{0,5},{1,4},{2,7},{3,6},{4,1},{5,0},{6,3},{7,2},{8,13},{9,12},{10,... | collective-permute-start | bytes 159752 | tf_op jit(solution)/shard_map/ppermute | solution.py:562
  43.4 2.0 %collective-permute-start.6 = (bf16[208,128]{1,0:T(8,128)(2,1)}, bf16[208,128]{1,0:T(8,128)(2,1)}, u32[]{:S(2)}, u32[]{:S(2)}) collective-permute-start(bf16[208,128]{1,0:T(8,128)(2,1)} %get-tuple-element.38), channel_id=1, source_target_pairs={{0,4},{1,5},{2,6},{3,7},{4,0},{5,1},{6,2},{7,3},{8,12},{9,13},{10,... | collective-permute-start | bytes 159752 | tf_op jit(solution)/shard_map/ppermute | solution.py:562
  45.4 2.3 %collective-permute-start.7 = (bf16[208,128]{1,0:T(8,128)(2,1)}, bf16[208,128]{1,0:T(8,128)(2,1)}, u32[]{:S(2)}, u32[]{:S(2)}) collective-permute-start(bf16[208,128]{1,0:T(8,128)(2,1)} %get-tuple-element.39), channel_id=1, source_target_pairs={{0,3},{1,2},{2,1},{3,0},{4,7},{5,6},{6,5},{7,4},{8,11},{9,10},{10,... | collective-permute-start | bytes 159752 | tf_op jit(solution)/shard_map/ppermute | solution.py:562
  47.7 0.0 collective-permute-done.3.refs_1_
  47.7 0.8 %collective-permute-start.8 = (bf16[208,128]{1,0:T(8,128)(2,1)}, bf16[208,128]{1,0:T(8,128)(2,1)}, u32[]{:S(2)}, u32[]{:S(2)}) collective-permute-start(bf16[208,128]{1,0:T(8,128)(2,1)} %get-tuple-element.40), channel_id=1, source_target_pairs={{0,2},{1,3},{2,0},{3,1},{4,6},{5,7},{6,4},{7,5},{8,10},{9,11},{10,... | collective-permute-start | bytes 159752 | tf_op jit(solution)/shard_map/ppermute | solution.py:562
  48.5 0.8 %collective-permute-done.4.refs_2_ = bf16[208,128]{1,0:T(8,128)(2,1)} collective-permute-done((bf16[208,128]{1,0:T(8,128)(2,1)}, bf16[208,128]{1,0:T(8,128)(2,1)}, u32[]{:S(2)}, u32[]{:S(2)}) %collective-permute-start.4) | collective-permute-done | bytes 53280 | tf_op jit(solution)/shard_map/ppermute | solution.py:562
  49.2 0.5 collective-permute-start.9
  49.7 1.7 %collective-permute-done.5.refs_3_ = bf16[208,128]{1,0:T(8,128)(2,1)} collective-permute-done((bf16[208,128]{1,0:T(8,128)(2,1)}, bf16[208,128]{1,0:T(8,128)(2,1)}, u32[]{:S(2)}, u32[]{:S(2)}) %collective-permute-start.5) | collective-permute-done | bytes 53280 | tf_op jit(solution)/shard_map/ppermute | solution.py:562
  51.4 1.0 %collective-permute-done.6.refs_4_ = bf16[208,128]{1,0:T(8,128)(2,1)} collective-permute-done((bf16[208,128]{1,0:T(8,128)(2,1)}, bf16[208,128]{1,0:T(8,128)(2,1)}, u32[]{:S(2)}, u32[]{:S(2)}) %collective-permute-start.6) | collective-permute-done | bytes 53280 | tf_op jit(solution)/shard_map/ppermute | solution.py:562
  52.4 0.5 collective-permute-done.7.refs_5_
  52.9 0.2 collective-permute-done.8.refs_6_
  53.2 0.5 collective-permute-done.9.refs_7_
  53.7 2.1 %shard_map.172 = f32[192,256]{1,0:T(8,128)} custom-call(bf16[208,128]{1,0:T(8,128)(2,1)} %get-tuple-element.34.refs_0_, bf16[208,128]{1,0:T(8,128)(2,1)} %collective-permute-done.3.refs_1_, bf16[208,128]{1,0:T(8,128)(2,1)} %collective-permute-done.4.refs_2_, bf16[208,128]{1,0:T(8,128)(2,1)} %collective-permute-done.5.refs_3_, ...), custom_call_target="tpu_custom_call" | custom-call | flops 200000000 | bytes 2097152 | tf_op jit(solution)/shard_map/pallas_call | solution.py:751
Async XLA Ops:
  11.2 6.0 %collective-permute-start.1 = (bf16[192,1024]{1,0:T(8,128)(2,1)}, bf16[192,1024]{1,0:T(8,128)(2,1)}, u32[]{:S(2)}, u32[]{:S(2)}) collective-permute-start(bf16[192,1024]{1,0:T(8,128)(2,1)} %get-tuple-element.22.own_hbm), channel_id=1, source_target_pairs={{0,8},{8,0},{16,24},{24,16},{1,9},{9,1},{17,25},{25,17},{2,10},{10... | collective-permute-start | bytes 1179656 | tf_op jit(solution)/shard_map/ppermute | solution.py:562
  11.7 12.6 %collective-permute-start = (bf16[192,1024]{1,0:T(8,128)(2,1)}, bf16[192,1024]{1,0:T(8,128)(2,1)}, u32[]{:S(2)}, u32[]{:S(2)}) collective-permute-start(bf16[192,1024]{1,0:T(8,128)(2,1)} %get-tuple-element.22.own_hbm), channel_id=1, source_target_pairs={{0,16},{8,24},{16,0},{24,8},{1,17},{9,25},{17,1},{25,9},{2,18},{10... | collective-permute-start | bytes 1179656 | tf_op jit(solution)/shard_map/ppermute | solution.py:562
  24.3 4.6 %collective-permute-start.2 = (bf16[192,1024]{1,0:T(8,128)(2,1)}, bf16[192,1024]{1,0:T(8,128)(2,1)}, u32[]{:S(2)}, u32[]{:S(2)}) collective-permute-start(bf16[192,1024]{1,0:T(8,128)(2,1)} %collective-permute-done.refs_0_), channel_id=1, source_target_pairs={{0,8},{8,0},{16,24},{24,16},{1,9},{9,1},{17,25},{25,17},{2,10},{10... | collective-permute-start | bytes 1179656 | tf_op jit(solution)/shard_map/ppermute | solution.py:562
  37.5 10.2 %collective-permute-start.3 = (bf16[208,128]{1,0:T(8,128)(2,1)}, bf16[208,128]{1,0:T(8,128)(2,1)}, u32[]{:S(2)}, u32[]{:S(2)}) collective-permute-start(bf16[208,128]{1,0:T(8,128)(2,1)} %get-tuple-element.35), channel_id=1, source_target_pairs={{0,7},{1,6},{2,5},{3,4},{4,3},{5,2},{6,1},{7,0},{8,15},{9,14},{10,... | collective-permute-start | bytes 159752 | tf_op jit(solution)/shard_map/ppermute | solution.py:562
  42.4 6.9 %collective-permute-start.4 = (bf16[208,128]{1,0:T(8,128)(2,1)}, bf16[208,128]{1,0:T(8,128)(2,1)}, u32[]{:S(2)}, u32[]{:S(2)}) collective-permute-start(bf16[208,128]{1,0:T(8,128)(2,1)} %get-tuple-element.36), channel_id=1, source_target_pairs={{0,6},{1,7},{2,4},{3,5},{4,2},{5,3},{6,0},{7,1},{8,14},{9,15},{10,... | collective-permute-start | bytes 159752 | tf_op jit(solution)/shard_map/ppermute | solution.py:562
  42.6 8.8 %collective-permute-start.5 = (bf16[208,128]{1,0:T(8,128)(2,1)}, bf16[208,128]{1,0:T(8,128)(2,1)}, u32[]{:S(2)}, u32[]{:S(2)}) collective-permute-start(bf16[208,128]{1,0:T(8,128)(2,1)} %get-tuple-element.37), channel_id=1, source_target_pairs={{0,5},{1,4},{2,7},{3,6},{4,1},{5,0},{6,3},{7,2},{8,13},{9,12},{10,... | collective-permute-start | bytes 159752 | tf_op jit(solution)/shard_map/ppermute | solution.py:562
  43.4 9.1 %collective-permute-start.6 = (bf16[208,128]{1,0:T(8,128)(2,1)}, bf16[208,128]{1,0:T(8,128)(2,1)}, u32[]{:S(2)}, u32[]{:S(2)}) collective-permute-start(bf16[208,128]{1,0:T(8,128)(2,1)} %get-tuple-element.38), channel_id=1, source_target_pairs={{0,4},{1,5},{2,6},{3,7},{4,0},{5,1},{6,2},{7,3},{8,12},{9,13},{10,... | collective-permute-start | bytes 159752 | tf_op jit(solution)/shard_map/ppermute | solution.py:562
  45.4 7.5 %collective-permute-start.7 = (bf16[208,128]{1,0:T(8,128)(2,1)}, bf16[208,128]{1,0:T(8,128)(2,1)}, u32[]{:S(2)}, u32[]{:S(2)}) collective-permute-start(bf16[208,128]{1,0:T(8,128)(2,1)} %get-tuple-element.39), channel_id=1, source_target_pairs={{0,3},{1,2},{2,1},{3,0},{4,7},{5,6},{6,5},{7,4},{8,11},{9,10},{10,... | collective-permute-start | bytes 159752 | tf_op jit(solution)/shard_map/ppermute | solution.py:562
  47.7 5.5 %collective-permute-start.8 = (bf16[208,128]{1,0:T(8,128)(2,1)}, bf16[208,128]{1,0:T(8,128)(2,1)}, u32[]{:S(2)}, u32[]{:S(2)}) collective-permute-start(bf16[208,128]{1,0:T(8,128)(2,1)} %get-tuple-element.40), channel_id=1, source_target_pairs={{0,2},{1,3},{2,0},{3,1},{4,6},{5,7},{6,4},{7,5},{8,10},{9,11},{10,... | collective-permute-start | bytes 159752 | tf_op jit(solution)/shard_map/ppermute | solution.py:562
  49.2 4.5 %collective-permute-start.9 = (bf16[208,128]{1,0:T(8,128)(2,1)}, bf16[208,128]{1,0:T(8,128)(2,1)}, u32[]{:S(2)}, u32[]{:S(2)}) collective-permute-start(bf16[208,128]{1,0:T(8,128)(2,1)} %get-tuple-element.41), channel_id=1, source_target_pairs={{0,1},{1,0},{2,3},{3,2},{4,5},{5,4},{6,7},{7,6},{8,9},{9,8},{10,11... | collective-permute-start | bytes 159752 | tf_op jit(solution)/shard_map/ppermute | solution.py:562

commit v6 on v5

--- a/solution.py
+++ b/solution.py
@@ -53,11 +53,27 @@
     return jnp.where(j < cut, low_src, high_src)
 
 
-def slot_of_lane(slots, run):
-    t = iota((1, slots), 1)
-    at, lane = t // LANES, t % LANES
-    p = (4 * (at // run) + lane // WIN) * run + at % run
-    return (lane % 8) * LANES + ((lane // 8) % 4) * WIN + p
+def within(run):
+    lane = iota((1, LANES), 1)
+    q, e = lane // 16, lane % 16
+    p = (4 * (q // run) + e // 4) * run + q % run
+    return ((e % 4) * WIN + p == iota((LANES, LANES), 0)).astype(BF16)
+
+
+def swap_blocks(tiles):
+    tiles = list(tiles)
+    block = iota(tiles[0].shape, 1) // 16
+    step = len(tiles) // 2
+    while step:
+        for n in range(len(tiles)):
+            if n & step:
+                continue
+            a, b = tiles[n], tiles[n + step]
+            low = block // step % 2 == 0
+            tiles[n] = jnp.where(low, a, pltpu.roll(b, 16 * step, 1))
+            tiles[n + step] = jnp.where(low, pltpu.roll(a, LANES - 16 * step, 1), b)
+        step //= 2
+    return tiles
 
 
 def place(low, high, blocks):
@@ -66,11 +82,6 @@
     nil = jnp.zeros_like(base)
     parts = [jnp.where(high == jnp.asarray(n, BF16), base, nil) for n in range(blocks)]
     return jnp.concatenate(parts, 0)
-
-
-def reorder(slots, run):
-    slot = slot_of_lane(slots, run)
-    return place(slot % LANES, slot // LANES, slots // LANES)
 
 
 def norm_t(x, gain):
@@ -155,60 +166,55 @@
     ).astype(BF16)
     row_head = (iota((chans, LANES), 0) // size) % per
     own_head = row_head == iota((chans, LANES), 1) // WIN
+    even_row = row_head % 2 == 0
     for t in range(tiles):
-        q_s[t] = qkv_s[:chans, tile(t)] * jnp.asarray(size**-0.5, BF16)
+        query = qkv_s[:chans, tile(t)].astype(F32) * size**-0.5
+        q_s[t, :, :LANES] = jnp.where(even_row, query, 0.0).astype(BF16)
+        q_s[t, :, LANES:] = jnp.where(even_row, 0.0, query).astype(BF16)
         k_s[t] = dot_t(side, qkv_s[chans : 2 * chans, tile(t)]).astype(BF16)
     for t in range(tiles):
         wide = dot(qkv_s[2 * chans :, tile(t)], spread)
         for w in range(per):
             v_s[t, w] = jnp.where(own_head, wide[:, tile(w)], 0.0).astype(BF16)
 
-    lane_head = iota((WIN, chans), 1) // size
-    head_mask = [jnp.where(lane_head == h, 1.0, 0.0).astype(BF16) for h in range(HEADS)]
+    lane_pair = iota((WIN, chans), 1) // (2 * size)
     window = iota((8, LANES), 1) // WIN
     rank = iota((WIN, LANES), 0) + WIN * (iota((WIN, LANES), 1) // WIN)
-    half = per * size
-
-    def by_window(made):
-        out = made(0)
-        for w in range(1, per):
-            out = jnp.where(window[None] == w, made(w), out)
-        return out
 
     def group(t, _):
         query = q_s[t]
+        even, odd = None, None
+        for w in range(per):
+            keys = k_s[t, w * WIN : (w + 1) * WIN, :]
+            by_pair = jnp.concatenate(
+                [jnp.where(lane_pair == m, keys, jnp.zeros_like(keys)) for m in range(HEADS // 2)],
+                0,
+            )
+            got = dot(by_pair, query)
+            left = got[:, :LANES].reshape(-1, 8, LANES)
+            right = got[:, LANES:].reshape(-1, 8, LANES)
+            even = left if w == 0 else jnp.where(window[None] == w, left, even)
+            odd = right if w == 0 else jnp.where(window[None] == w, right, odd)
         mask = jnp.where(rank + t * LANES < count, 0.0, -1e9).astype(F32)
         mask = mask.reshape(WIN // 8, 8, LANES)
-
-        def scores_of(j):
-            def made(w):
-                keys = k_s[t, w * WIN : (w + 1) * WIN, :]
-                heads = [keys * head_mask[j * per + h] for h in range(per)]
-                return dot(jnp.concatenate(heads, 0), query).reshape(-1, 8, LANES)
-
-            return by_window(made)
-
+        probs, inverse = [], []
+        for h in range(HEADS):
+            scores = (even, odd)[h % 2]
+            mine = scores[h // 2 * (WIN // 8) : (h // 2 + 1) * (WIN // 8)] + mask
+            top = fold8(mine, jnp.maximum)
+            weight = jnp.exp(mine - top[None])
+            inverse.append(1.0 / fold8(weight, jnp.add))
+            probs.append(weight.reshape(WIN, LANES).astype(BF16))
+        half = per * size
         parts = []
-        coming = scores_of(0)
         for j in range(HEADS // per):
-            scores = coming
-            if j + 1 < HEADS // per:
-                coming = scores_of(j + 1)
-            probs, inverse = [], []
+            weight = jnp.concatenate(probs[j * per : (j + 1) * per], 0)
+            ctx = None
+            for w in range(per):
+                got = dot(v_s[t, w, j * half : (j + 1) * half, :], weight).reshape(-1, 8, LANES)
+                ctx = got if w == 0 else jnp.where(window[None] == w, got, ctx)
             for h in range(per):
-                mine = scores[h * (WIN // 8) : (h + 1) * (WIN // 8)] + mask
-                top = fold8(mine, jnp.maximum)
-                weight = jnp.exp(mine - top[None])
-                inverse.append(1.0 / fold8(weight, jnp.add))
-                probs.append(weight.reshape(WIN, LANES).astype(BF16))
-            weight = jnp.concatenate(probs, 0)
-            ctx = by_window(
-                lambda w: dot(v_s[t, w, j * half : (j + 1) * half, :], weight).reshape(
-                    -1, 8, LANES
-                )
-            )
-            for h in range(per):
-                block = ctx[h * (size // 8) : (h + 1) * (size // 8)] * inverse[h][None]
+                block = ctx[h * (size // 8) : (h + 1) * (size // 8)] * inverse[j * per + h][None]
                 parts.append(block.reshape(size, LANES))
         ctx_s[t] = jnp.concatenate(parts, 0).astype(BF16)
         return 0
@@ -226,7 +232,9 @@
         n_s[:, at] = jnp.concatenate([head, normed[16:]], 0).astype(BF16)
     keep_first = pltpu.make_async_copy(first_s, first_hbm, stores.at[0])
     keep_first.start()
-    sent_s[...] = dot(n_s[...], reorder(slots, run)).astype(BF16)
+    inside = within(run)
+    for t, block in enumerate(swap_blocks([dot(n_s[:, tile(t)], inside) for t in range(tiles)])):
+        sent_s[:, tile(t)] = block.astype(BF16)
     send = pltpu.make_async_copy(sent_s, sent_hbm, stores.at[1])
     send.start()
     wait_all([keep_first, send])
@@ -288,99 +296,90 @@
     return jnp.concatenate([head.astype(BF16), block[16:]], 0), gone
 
 
-def fold16(x):
-    parts = [x[n] for n in range(x.shape[0])]
-    while len(parts) > 1:
-        parts = [a + b for a, b in zip(parts[::2], parts[1::2])]
-    wide = parts[0].astype(F32)
-    return wide[:8] + wide[8:]
-
-
-def twice(x):
-    return jnp.concatenate([x, x], 0).astype(BF16)
-
-
 def add_keys(blocks, kv_t, k_s, v_s, m_s):
     chans = kv_t.shape[1]
-    rows16 = chans // 16
     tiles = k_s.shape[1]
     for n, block in enumerate(blocks):
         block, gone = clean(block)
-        kv = dot(kv_t, block).astype(BF16)
+        kv = dot(kv_t, block)
         mask = jnp.where(gone, -1e9, 0.0)
         for t in range(tiles):
-            k_s[n, t] = kv[:chans, tile(t)].reshape(rows16, 16, LANES)
-            v_s[n, t] = kv[chans:, tile(t)].reshape(rows16, 16, LANES)
+            k_s[n, t] = kv[:chans, tile(t)].reshape(chans // 8, 8, LANES)
+            v_s[n, t] = kv[chans:, tile(t)].reshape(chans // 8, 8, LANES)
             m_s[n, t] = jnp.broadcast_to(mask[:, tile(t)], (8, LANES))
 
 
-def attend_more(t, run, q_s, k_s, v_s, m_s, s_s, old):
-    rows16 = q_s.shape[1]
-    cut = 2 * rows16 // 3
-    blocks = k_s.shape[0]
-    keys = blocks * run
+def attend_two(t, run, q_s, k_s, v_s, m_s, s_s, ends_s, acc_s, fresh):
+    rows8 = q_s.shape[1]
+    cut = 2 * rows8 // 3
+    keys = k_s.shape[0] * run
     base = (t // run) * run
-    query = q_s[t]
+    both = range(2)
+    query = [[q_s[t + n, i] for i in range(rows8)] for n in both]
 
     def score(key, top):
-        n, at = key // run, base + key % run
-        prod = query * k_s[n, at]
-        a = fold16(prod[:cut])
-        b = fold16(prod[cut:])
-        b = b + pltpu.roll(b, 4, 0)
-        mask = m_s[n, at]
-        a = a * LOG2E + mask
-        b = b * LOG2E + mask
-        s_s[key, 0] = a
-        s_s[key, 1] = b
-        return jnp.maximum(top[0], a), jnp.maximum(top[1], b)
-
-    if old is None:
-        low = jnp.full((8, LANES), -3e38, F32)
+        block, at = key // run, base + key % run
+        mask = m_s[block, at]
+        sums = [[None, None], [None, None]]
+        for i in range(rows8):
+            part = int(i >= cut)
+            row = k_s[block, at, i]
+            for n in both:
+                term = query[n][i] * row
+                held = sums[n][part]
+                sums[n][part] = term if held is None else held + term
+        tops = []
+        for n in both:
+            a, b = sums[n]
+            b = b + pltpu.roll(b, 4, 0)
+            a = a + mask
+            b = b + mask
+            s_s[key, 2 * n] = a
+            s_s[key, 2 * n + 1] = b
+            tops += [jnp.maximum(top[2 * n], a), jnp.maximum(top[2 * n + 1], b)]
+        return tuple(tops)
+
+    if fresh:
+        old = tuple(jnp.full((8, LANES), -3e38, F32) for _ in range(4))
+    else:
+        old = tuple(ends_s[t + n, part] for n in both for part in both)
+    tops = lax.fori_loop(0, keys, score, old, unroll=2)
+    if fresh:
         zero = jnp.zeros((8, LANES), F32)
-        top_a, top_b = lax.fori_loop(0, keys, score, (low, low), unroll=4)
-        held = (zero, zero, jnp.zeros((cut, 16, LANES), F32),
-                jnp.zeros((rows16 - cut, 16, LANES), F32))
+        sums = tuple(zero for _ in range(4))
+        accs = tuple(zero for _ in range(2 * rows8))
     else:
-        top, total, acc = old
-        top_a, top_b = lax.fori_loop(0, keys, score, (top[0], top[1]), unroll=4)
-        fade_a = jnp.exp2(top[0] - top_a)
-        fade_b = jnp.exp2(top[1] - top_b)
-        both_a = jnp.concatenate([fade_a, fade_a], 0)
-        both_b = jnp.concatenate([fade_b, fade_b], 0)
-        held = (total[0] * fade_a, total[1] * fade_b, acc[:cut] * both_a[None],
-                acc[cut:] * both_b[None])
-
-    def gather(step, carry):
-        sum_a, sum_b, acc_a, acc_b = carry
-        got_a, got_b = [], []
-        for key in range(4):
-            key = 4 * step + key
-            pa = jnp.exp2(s_s[key, 0] - top_a)
-            pb = jnp.exp2(s_s[key, 1] - top_b)
-            sum_a = sum_a + pa
-            sum_b = sum_b + pb
-            value = v_s[key // run, base + key % run]
-            got_a.append(twice(pa)[None] * value[:cut])
-            got_b.append(twice(pb)[None] * value[cut:])
-        acc_a = acc_a + ((got_a[0] + got_a[1]) + (got_a[2] + got_a[3])).astype(F32)
-        acc_b = acc_b + ((got_b[0] + got_b[1]) + (got_b[2] + got_b[3])).astype(F32)
-        return sum_a, sum_b, acc_a, acc_b
-
-    sum_a, sum_b, acc_a, acc_b = lax.fori_loop(0, keys // 4, gather, held)
-    return (top_a, top_b), (sum_a, sum_b), (acc_a, acc_b)
-
-
-def hold(t, state, ends_s, acc_s):
-    top, total, acc = state
+        fade = [jnp.exp2(old[n] - tops[n]) for n in range(4)]
+        sums = tuple(ends_s[t + n, 2 + part] * fade[2 * n + part] for n in both for part in both)
+        accs = tuple(
+            acc_s[t + n, i] * fade[2 * n + int(i >= cut)] for n in both for i in range(rows8)
+        )
+
+    def gather(key, carry):
+        sums, accs = carry
+        block, at = key // run, base + key % run
+        weight = [jnp.exp2(s_s[key, n] - tops[n]) for n in range(4)]
+        accs = list(accs)
+        for i in range(rows8):
+            row = v_s[block, at, i]
+            for n in both:
+                at_acc = n * rows8 + i
+                accs[at_acc] = accs[at_acc] + weight[2 * n + int(i >= cut)] * row
+        return tuple(sums[n] + weight[n] for n in range(4)), tuple(accs)
+
+    sums, accs = lax.fori_loop(0, keys, gather, (sums, accs), unroll=2)
+    return tops, sums, accs
+
+
+def hold_two(t, state, ends_s, acc_s):
+    tops, sums, accs = state
+    rows8 = acc_s.shape[1]
     for n in range(2):
-        ends_s[t, n] = top[n]
-        ends_s[t, 2 + n] = total[n]
-    acc_s[t] = jnp.concatenate(acc, 0)
-
-
-def held(t, ends_s, acc_s):
-    return (ends_s[t, 0], ends_s[t, 1]), (ends_s[t, 2], ends_s[t, 3]), acc_s[t]
+        for part in range(2):
+            ends_s[t + n, part] = tops[2 * n + part]
+            ends_s[t + n, 2 + part] = sums[2 * n + part]
+        for i in range(rows8):
+            acc_s[t + n, i] = accs[n * rows8 + i]
 
 
 def near_kernel(
@@ -397,22 +396,24 @@
         sems,
     )
     tiles = slots // LANES
-    scale = (chans // HEADS) ** -0.5
+    scale = (chans // HEADS) ** -0.5 * LOG2E
     wait_all(loads[:2])
     own, _ = clean(own_ref[...])
-    query = (dot(qkv_t_ref[:chans, :], own) * scale).astype(BF16)
+    query = dot(qkv_t_ref[:chans, :], own) * scale
     for t in range(tiles):
-        q_s[t] = query[:, tile(t)].reshape(chans // 16, 16, LANES)
+        q_s[t] = query[:, tile(t)].reshape(chans // 8, 8, LANES)
     keep_q = pltpu.make_async_copy(q_s, q_hbm, stores.at[0])
     keep_q.start()
     wait_all(loads[2:])
     add_keys([own_ref[...], near_ref[...]], qkv_t_ref[chans:, :], k_s, v_s, m_s)
 
-    def step(t, _):
-        hold(t, attend_more(t, run, q_s, k_s, v_s, m_s, s_s, None), ends_s, acc_s)
+    def step(n, _):
+        t = 2 * n
+        state = attend_two(t, run, q_s, k_s, v_s, m_s, s_s, ends_s, acc_s, True)
+        hold_two(t, state, ends_s, acc_s)
         return 0
 
-    lax.fori_loop(0, tiles, step, 0)
+    lax.fori_loop(0, tiles // 2, step, 0)
     keep_ends = pltpu.make_async_copy(ends_s, ends_hbm, stores.at[1])
     keep_acc = pltpu.make_async_copy(acc_s, acc_hbm, stores.at[2])
     keep_ends.start()
@@ -439,12 +440,13 @@
     add_keys([block_s[n] for n in range(count)], kv_t_ref[...], k_s, v_s, m_s)
     wait_all(later[1:])
 
-    def step(t, _):
-        old = held(t, ends_s, acc_s)
-        hold(t, attend_more(t, run, q_s, k_s, v_s, m_s, s_s, old), ends_s, acc_s)
+    def step(n, _):
+        t = 2 * n
+        state = attend_two(t, run, q_s, k_s, v_s, m_s, s_s, ends_s, acc_s, False)
+        hold_two(t, state, ends_s, acc_s)
         return 0
 
-    lax.fori_loop(0, q_s.shape[0], step, 0)
+    lax.fori_loop(0, q_s.shape[0] // 2, step, 0)
     wait_all(start_all([(ends_s, ends_out), (acc_s, acc_out)], stores))
 
 
@@ -456,7 +458,7 @@
     votes_hbm, refs = refs[9 : 9 + owners], refs[9 + owners :]
     (
         block_s, sems, weights_s, q_s, ends_s, acc_s, first_s, gain_s, down_s, facts_s, rest,
-        feat_s, votes_s, stores, k_s, v_s, m_s, s_s, ctx_s, bf_s, inner_s, hidden_s
+        feat_s, votes_s, stores, k_s, v_s, m_s, s_s, bf_s, inner_s, hidden_s
     ) = refs
     loads = start_all([(blocks[n], block_s.at[n]) for n in range(far)], sems)
     later = start_all(
@@ -479,19 +481,22 @@
     add_keys([block_s[n] for n in range(far)], weights_s[chans : 3 * chans], k_s, v_s, m_s)
     wait_all(later[1:])
 
-    def step(t, _):
-        old = held(t, ends_s, acc_s)
-        _, total, acc = attend_more(t, run, q_s, k_s, v_s, m_s, s_s, old)
-        share = [1.0 / total[n] for n in range(2)]
-        ctx = jnp.concatenate(
-            [acc[n] * jnp.concatenate([share[n], share[n]], 0)[None] for n in range(2)], 0
-        )
-        ctx_s[t] = ctx.reshape(chans, LANES).astype(BF16)
+    rows8 = chans // 8
+
+    def step(n, _):
+        t = 2 * n
+        _, sums, accs = attend_two(t, run, q_s, k_s, v_s, m_s, s_s, ends_s, acc_s, False)
+        share = [1.0 / total for total in sums]
+        cut = 2 * rows8 // 3
+        for n in range(2):
+            for i in range(rows8):
+                acc_s[t + n, i] = accs[n * rows8 + i] * share[2 * n + int(i >= cut)]
         return 0
 
-    lax.fori_loop(0, tiles, step, 0)
-    ctx = jnp.concatenate([ctx_s[t] for t in range(tiles)], 1)
-    ctx = dot_t(ctx, reorder(slots, run)).astype(BF16)
+    lax.fori_loop(0, tiles // 2, step, 0)
+    inside = within(run)
+    ctx = swap_blocks([acc_s[t].reshape(chans, LANES) for t in range(tiles)])
+    ctx = jnp.concatenate([dot_t(c.astype(BF16), inside).astype(BF16) for c in ctx], 1)
     gain = jnp.concatenate([gain_s[...], jnp.zeros((7, chans), F32)], 0).T[:, 0:1]
     moved = dot(weights_s[3 * chans : 4 * chans], ctx)
     for t in range(tiles):
@@ -587,7 +592,7 @@
     cap = 2 * votes // owners
     codes = owners * cap
     tiles = slots // LANES
-    rows16 = chans // 16
+    rows8 = chans // 8
     hidden = w_up.shape[1]
     per = LANES // WIN
     sds = jax.ShapeDtypeStruct
@@ -607,7 +612,7 @@
             vmem((chans, chans), BF16),
             dma((7,)),
             vmem((3 * chans, slots), BF16),
-            vmem((tiles, chans, LANES), BF16),
+            vmem((tiles, chans, 2 * LANES), BF16),
             vmem((tiles, LANES, chans), BF16),
             vmem((tiles, per, chans, LANES), BF16),
             vmem((tiles, chans, LANES), BF16),
@@ -659,16 +664,16 @@
         vote_owner.reshape(1, votes),
         vote_voxel.reshape(1, votes),
     )
-    q_like = ((tiles, rows16, 16, LANES), BF16)
+    q_like = ((tiles, rows8, 8, LANES), F32)
     ends_like = ((tiles, 4, 8, LANES), F32)
-    acc_like = ((tiles, rows16, 16, LANES), F32)
+    acc_like = ((tiles, rows8, 8, LANES), F32)
 
     def key_scratch(blocks):
         return [
-            vmem((blocks, tiles, rows16, 16, LANES), BF16),
-            vmem((blocks, tiles, rows16, 16, LANES), BF16),
+            vmem((blocks, tiles, rows8, 8, LANES), F32),
+            vmem((blocks, tiles, rows8, 8, LANES), F32),
             vmem((blocks, tiles, 8, LANES), F32),
-            vmem((blocks * run, 2, 8, LANES), F32),
+            vmem((blocks * run, 4, 8, LANES), F32),
         ]
 
     query, ends, acc = call(
@@ -728,7 +733,6 @@
         ]
         + key_scratch(len(far))
         + [
-            vmem((tiles, chans, LANES), BF16),
             vmem((chans, slots), BF16),
             vmem((chans, slots), BF16),
             vmem((2, hidden, 2 * LANES), BF16),

time: 56.1 us -> 53.8 us (0.959)
  Pallas kernels: 34.6 us -> 31.9 us
    pallas_call x1, Pallas kernels: 9.93 us -> 8.24 us  [body(): call(functools.partial(first_kernel, run), [sds((chans, slots), BF16), sd...]
where the time goes in v6:
time: 53.8 us; the launch traced here: 53.5 us
  Pallas kernels  31.9 us (59%)
  starting transfers between devices  14.5 us (27%)
  waiting for transfers between devices  5.72 us (11%)
  between operations  1.34 us (2%)
    ppermute x10, starting transfers between devices, turned(): return lax.ppermute(x, axis, [(i, i ^ bit) for i in range(n)])  14.5 us
    pallas_call x1, Pallas kernels, body(): call(functools.partial(first_kernel, run), [sds((chans, slots), BF16), sd...  8.24 us
    pallas_call x1, Pallas kernels, body(): call(functools.partial(second_kernel, run, cap, len(far), owners), [sds((...  8.16 us
    pallas_call x1, Pallas kernels, body(): call(functools.partial(near_kernel, run), [sds(*q_like), sds(*ends_like),...  6.05 us
    ppermute x10, waiting for transfers between devices, turned(): return lax.ppermute(x, axis, [(i, i ^ bit) for i in range(n)])  5.72 us
    pallas_call x1, Pallas kernels, body(): call(functools.partial(middle_kernel, run, len(mid)), [sds(*ends_like), s...  4.34 us
    pallas_call x1, Pallas kernels, body(): call(functools.partial(tables_kernel, cap), [sds((4 * chans + hidden, cha...  2.96 us
    pallas_call x1, Pallas kernels, body(): call(functools.partial(sums_kernel, owners), [sds((chans, VOX_DEV), F32)]...  2.11 us
  transfers between devices with their start and end apart: 10, of which 7 were waited for; matrix products, arithmetic and copies ran while one was open for 0% of the time, Pallas kernels for 25%

profile of v6, /device:TPU:0, one launch (start us, length us, event | category | flops | bytes accessed | tf_op | source)
XLA Modules:
  0.0 53.5 jit_solution(8840960785554782851)
XLA Ops:
  1.3 8.2 %shard_map.167 = (bf16[192,1024]{1,0:T(8,128)(2,1)}, bf16[192,1024]{1,0:T(8,128)(2,1)}) custom-call(s32[1]{0:T(128)S(6)} %copy.18.count_ref, bf16[192,1024]{1,0:T(8,128)(2,1)} %bitcast.11, s32[1,1024]{1,0:T(1,128)} %bitcast.13, f32[3,192]{1,0:T(4,128)} %pos_hbm.1, f32[1,192]{1,0:T(1,128)} %bitcast.17, f32[1,192]{1,0:T(1,128)} %bitcast.18, ...), custom_call_target="tpu_custom_call" | custom-call | flops 2000000000 | bytes 2097152 | tf_op jit(solution)/shard_map/pallas_call | solution.py:602
  9.5 0.5 collective-permute-start.1
  10.1 2.6 %collective-permute-start = (bf16[192,1024]{1,0:T(8,128)(2,1)}, bf16[192,1024]{1,0:T(8,128)(2,1)}, u32[]{:S(2)}, u32[]{:S(2)}) collective-permute-start(bf16[192,1024]{1,0:T(8,128)(2,1)} %get-tuple-element.22.own_hbm), channel_id=1, source_target_pairs={{0,16},{8,24},{16,0},{24,8},{1,17},{9,25},{17,1},{25,9},{2,18},{10... | collective-permute-start | bytes 1179656 | tf_op jit(solution)/shard_map/ppermute | solution.py:567
  12.6 3.0 %shard_map.168 = (bf16[1536,192]{1,0:T(8,128)(2,1)}, bf16[16,1024]{1,0:T(8,128)(2,1)}) custom-call(bf16[192,576]{1,0:T(8,128)(2,1)} %qkv_hbm.3, bf16[192,192]{1,0:T(8,128)(2,1)} %out_hbm.3, bf16[192,768]{1,0:T(8,128)(2,1)} %up_hbm.1, s32[1,512]{1,0:T(1,128)} %bitcast.14, s32[1,512]{1,0:T(1,128)} %bitcast.15, s32[1,512]{1,0:T(1,128)} %bitcast.16), custom_call_target="tpu_custom_call" | custom-call | flops 2000000000 | bytes 2097152 | tf_op jit(solution)/shard_map/pallas_call | solution.py:642
  15.6 0.0 collective-permute-done.1.near_hbm
  15.6 6.0 %shard_map.169 = (f32[8,24,8,128]{3,2,1,0:T(8,128)}, f32[8,4,8,128]{3,2,1,0:T(8,128)}, f32[8,24,8,128]{3,2,1,0:T(8,128)}) custom-call(bf16[192,1024]{1,0:T(8,128)(2,1)} %get-tuple-element.22.own_hbm, bf16[192,1024]{1,0:T(8,128)(2,1)} %collective-permute-done.1.near_hbm, bf16[1536,192]{1,0:T(8,128)(2,1)} %get-tuple-element.23.weights_hbm.refs_4_), custom_call_target="tpu_custom_call" | custom-call | flops 3000000000 | bytes 2097152 | tf_op jit(solution)/shard_map/pallas_call | solution.py:679
  21.7 1.0 %collective-permute-done.refs_0_ = bf16[192,1024]{1,0:T(8,128)(2,1)} collective-permute-done((bf16[192,1024]{1,0:T(8,128)(2,1)}, bf16[192,1024]{1,0:T(8,128)(2,1)}, u32[]{:S(2)}, u32[]{:S(2)}) %collective-permute-start) | collective-permute-done | bytes 393248 | tf_op jit(solution)/shard_map/ppermute | solution.py:567
  22.7 0.0 collective-permute-start.2
  22.7 4.3 %shard_map.170 = (f32[8,4,8,128]{3,2,1,0:T(8,128)}, f32[8,24,8,128]{3,2,1,0:T(8,128)}) custom-call(bf16[192,1024]{1,0:T(8,128)(2,1)} %collective-permute-done.refs_0_, f32[8,24,8,128]{3,2,1,0:T(8,128)} %get-tuple-element.26.refs_1_, f32[8,4,8,128]{3,2,1,0:T(8,128)} %get-tuple-element.27.refs_2_, f32[8,24,8,128]{3,2,1,0:T(8,128)} %get-tuple-element.28.refs_3_, ...), custom_call_target="tpu_custom_call" | custom-call | flops 2000000000 | bytes 2097152 | tf_op jit(solution)/shard_map/pallas_call | solution.py:698
  27.0 0.0 collective-permute-done.2.refs_0_
  27.0 8.2 %shard_map.171 = (f32[192,1024]{1,0:T(8,128)}, bf16[208,128]{1,0:T(8,128)(2,1)}, bf16[208,128]{1,0:T(8,128)(2,1)}, bf16[208,128]{1,0:T(8,128)(2,1)}, bf16[208,12...) custom-call(s32[1]{0:T(128)S(6)} %copy.18.count_ref, ...), custom_call_target="tpu_custom_call" | custom-call | flops 3000000000 | bytes 2097152 | tf_op jit(solution)/shard_map/pallas_call | solution.py:715
  35.2 4.9 %collective-permute-start.3 = (bf16[208,128]{1,0:T(8,128)(2,1)}, bf16[208,128]{1,0:T(8,128)(2,1)}, u32[]{:S(2)}, u32[]{:S(2)}) collective-permute-start(bf16[208,128]{1,0:T(8,128)(2,1)} %get-tuple-element.35), channel_id=1, source_target_pairs={{0,7},{1,6},{2,5},{3,4},{4,3},{5,2},{6,1},{7,0},{8,15},{9,14},{10,... | collective-permute-start | bytes 159752 | tf_op jit(solution)/shard_map/ppermute | solution.py:567
  40.1 0.2 collective-permute-start.4
  40.3 0.7 %collective-permute-start.5 = (bf16[208,128]{1,0:T(8,128)(2,1)}, bf16[208,128]{1,0:T(8,128)(2,1)}, u32[]{:S(2)}, u32[]{:S(2)}) collective-permute-start(bf16[208,128]{1,0:T(8,128)(2,1)} %get-tuple-element.37), channel_id=1, source_target_pairs={{0,5},{1,4},{2,7},{3,6},{4,1},{5,0},{6,3},{7,2},{8,13},{9,12},{10,... | collective-permute-start | bytes 159752 | tf_op jit(solution)/shard_map/ppermute | solution.py:567
  41.0 2.0 %collective-permute-start.6 = (bf16[208,128]{1,0:T(8,128)(2,1)}, bf16[208,128]{1,0:T(8,128)(2,1)}, u32[]{:S(2)}, u32[]{:S(2)}) collective-permute-start(bf16[208,128]{1,0:T(8,128)(2,1)} %get-tuple-element.38), channel_id=1, source_target_pairs={{0,4},{1,5},{2,6},{3,7},{4,0},{5,1},{6,2},{7,3},{8,12},{9,13},{10,... | collective-permute-start | bytes 159752 | tf_op jit(solution)/shard_map/ppermute | solution.py:567
  43.1 2.3 %collective-permute-start.7 = (bf16[208,128]{1,0:T(8,128)(2,1)}, bf16[208,128]{1,0:T(8,128)(2,1)}, u32[]{:S(2)}, u32[]{:S(2)}) collective-permute-start(bf16[208,128]{1,0:T(8,128)(2,1)} %get-tuple-element.39), channel_id=1, source_target_pairs={{0,3},{1,2},{2,1},{3,0},{4,7},{5,6},{6,5},{7,4},{8,11},{9,10},{10,... | collective-permute-start | bytes 159752 | tf_op jit(solution)/shard_map/ppermute | solution.py:567
  45.4 0.0 collective-permute-done.3.refs_1_
  45.4 0.8 %collective-permute-start.8 = (bf16[208,128]{1,0:T(8,128)(2,1)}, bf16[208,128]{1,0:T(8,128)(2,1)}, u32[]{:S(2)}, u32[]{:S(2)}) collective-permute-start(bf16[208,128]{1,0:T(8,128)(2,1)} %get-tuple-element.40), channel_id=1, source_target_pairs={{0,2},{1,3},{2,0},{3,1},{4,6},{5,7},{6,4},{7,5},{8,10},{9,11},{10,... | collective-permute-start | bytes 159752 | tf_op jit(solution)/shard_map/ppermute | solution.py:567
  46.1 0.8 %collective-permute-done.4.refs_2_ = bf16[208,128]{1,0:T(8,128)(2,1)} collective-permute-done((bf16[208,128]{1,0:T(8,128)(2,1)}, bf16[208,128]{1,0:T(8,128)(2,1)}, u32[]{:S(2)}, u32[]{:S(2)}) %collective-permute-start.4) | collective-permute-done | bytes 53280 | tf_op jit(solution)/shard_map/ppermute | solution.py:567
  46.9 0.5 collective-permute-start.9
  47.4 1.7 %collective-permute-done.5.refs_3_ = bf16[208,128]{1,0:T(8,128)(2,1)} collective-permute-done((bf16[208,128]{1,0:T(8,128)(2,1)}, bf16[208,128]{1,0:T(8,128)(2,1)}, u32[]{:S(2)}, u32[]{:S(2)}) %collective-permute-start.5) | collective-permute-done | bytes 53280 | tf_op jit(solution)/shard_map/ppermute | solution.py:567
  49.1 1.0 %collective-permute-done.6.refs_4_ = bf16[208,128]{1,0:T(8,128)(2,1)} collective-permute-done((bf16[208,128]{1,0:T(8,128)(2,1)}, bf16[208,128]{1,0:T(8,128)(2,1)}, u32[]{:S(2)}, u32[]{:S(2)}) %collective-permute-start.6) | collective-permute-done | bytes 53280 | tf_op jit(solution)/shard_map/ppermute | solution.py:567
  50.1 0.5 collective-permute-done.7.refs_5_
  50.6 0.2 collective-permute-done.8.refs_6_
  50.8 0.5 collective-permute-done.9.refs_7_
  51.4 2.1 %shard_map.172 = f32[192,256]{1,0:T(8,128)} custom-call(bf16[208,128]{1,0:T(8,128)(2,1)} %get-tuple-element.34.refs_0_, bf16[208,128]{1,0:T(8,128)(2,1)} %collective-permute-done.3.refs_1_, bf16[208,128]{1,0:T(8,128)(2,1)} %collective-permute-done.4.refs_2_, bf16[208,128]{1,0:T(8,128)(2,1)} %collective-permute-done.5.refs_3_, ...), custom_call_target="tpu_custom_call" | custom-call | flops 200000000 | bytes 2097152 | tf_op jit(solution)/shard_map/pallas_call | solution.py:755
Async XLA Ops:
  9.5 6.1 %collective-permute-start.1 = (bf16[192,1024]{1,0:T(8,128)(2,1)}, bf16[192,1024]{1,0:T(8,128)(2,1)}, u32[]{:S(2)}, u32[]{:S(2)}) collective-permute-start(bf16[192,1024]{1,0:T(8,128)(2,1)} %get-tuple-element.22.own_hbm), channel_id=1, source_target_pairs={{0,8},{8,0},{16,24},{24,16},{1,9},{9,1},{17,25},{25,17},{2,10},{10... | collective-permute-start | bytes 1179656 | tf_op jit(solution)/shard_map/ppermute | solution.py:567
  10.1 12.6 %collective-permute-start = (bf16[192,1024]{1,0:T(8,128)(2,1)}, bf16[192,1024]{1,0:T(8,128)(2,1)}, u32[]{:S(2)}, u32[]{:S(2)}) collective-permute-start(bf16[192,1024]{1,0:T(8,128)(2,1)} %get-tuple-element.22.own_hbm), channel_id=1, source_target_pairs={{0,16},{8,24},{16,0},{24,8},{1,17},{9,25},{17,1},{25,9},{2,18},{10... | collective-permute-start | bytes 1179656 | tf_op jit(solution)/shard_map/ppermute | solution.py:567
  22.7 4.3 %collective-permute-start.2 = (bf16[192,1024]{1,0:T(8,128)(2,1)}, bf16[192,1024]{1,0:T(8,128)(2,1)}, u32[]{:S(2)}, u32[]{:S(2)}) collective-permute-start(bf16[192,1024]{1,0:T(8,128)(2,1)} %collective-permute-done.refs_0_), channel_id=1, source_target_pairs={{0,8},{8,0},{16,24},{24,16},{1,9},{9,1},{17,25},{25,17},{2,10},{10... | collective-permute-start | bytes 1179656 | tf_op jit(solution)/shard_map/ppermute | solution.py:567
  35.2 10.2 %collective-permute-start.3 = (bf16[208,128]{1,0:T(8,128)(2,1)}, bf16[208,128]{1,0:T(8,128)(2,1)}, u32[]{:S(2)}, u32[]{:S(2)}) collective-permute-start(bf16[208,128]{1,0:T(8,128)(2,1)} %get-tuple-element.35), channel_id=1, source_target_pairs={{0,7},{1,6},{2,5},{3,4},{4,3},{5,2},{6,1},{7,0},{8,15},{9,14},{10,... | collective-permute-start | bytes 159752 | tf_op jit(solution)/shard_map/ppermute | solution.py:567
  40.1 6.8 %collective-permute-start.4 = (bf16[208,128]{1,0:T(8,128)(2,1)}, bf16[208,128]{1,0:T(8,128)(2,1)}, u32[]{:S(2)}, u32[]{:S(2)}) collective-permute-start(bf16[208,128]{1,0:T(8,128)(2,1)} %get-tuple-element.36), channel_id=1, source_target_pairs={{0,6},{1,7},{2,4},{3,5},{4,2},{5,3},{6,0},{7,1},{8,14},{9,15},{10,... | collective-permute-start | bytes 159752 | tf_op jit(solution)/shard_map/ppermute | solution.py:567
  40.3 8.8 %collective-permute-start.5 = (bf16[208,128]{1,0:T(8,128)(2,1)}, bf16[208,128]{1,0:T(8,128)(2,1)}, u32[]{:S(2)}, u32[]{:S(2)}) collective-permute-start(bf16[208,128]{1,0:T(8,128)(2,1)} %get-tuple-element.37), channel_id=1, source_target_pairs={{0,5},{1,4},{2,7},{3,6},{4,1},{5,0},{6,3},{7,2},{8,13},{9,12},{10,... | collective-permute-start | bytes 159752 | tf_op jit(solution)/shard_map/ppermute | solution.py:567
  41.0 9.1 %collective-permute-start.6 = (bf16[208,128]{1,0:T(8,128)(2,1)}, bf16[208,128]{1,0:T(8,128)(2,1)}, u32[]{:S(2)}, u32[]{:S(2)}) collective-permute-start(bf16[208,128]{1,0:T(8,128)(2,1)} %get-tuple-element.38), channel_id=1, source_target_pairs={{0,4},{1,5},{2,6},{3,7},{4,0},{5,1},{6,2},{7,3},{8,12},{9,13},{10,... | collective-permute-start | bytes 159752 | tf_op jit(solution)/shard_map/ppermute | solution.py:567
  43.1 7.5 %collective-permute-start.7 = (bf16[208,128]{1,0:T(8,128)(2,1)}, bf16[208,128]{1,0:T(8,128)(2,1)}, u32[]{:S(2)}, u32[]{:S(2)}) collective-permute-start(bf16[208,128]{1,0:T(8,128)(2,1)} %get-tuple-element.39), channel_id=1, source_target_pairs={{0,3},{1,2},{2,1},{3,0},{4,7},{5,6},{6,5},{7,4},{8,11},{9,10},{10,... | collective-permute-start | bytes 159752 | tf_op jit(solution)/shard_map/ppermute | solution.py:567
  45.4 5.5 %collective-permute-start.8 = (bf16[208,128]{1,0:T(8,128)(2,1)}, bf16[208,128]{1,0:T(8,128)(2,1)}, u32[]{:S(2)}, u32[]{:S(2)}) collective-permute-start(bf16[208,128]{1,0:T(8,128)(2,1)} %get-tuple-element.40), channel_id=1, source_target_pairs={{0,2},{1,3},{2,0},{3,1},{4,6},{5,7},{6,4},{7,5},{8,10},{9,11},{10,... | collective-permute-start | bytes 159752 | tf_op jit(solution)/shard_map/ppermute | solution.py:567
  46.9 4.5 %collective-permute-start.9 = (bf16[208,128]{1,0:T(8,128)(2,1)}, bf16[208,128]{1,0:T(8,128)(2,1)}, u32[]{:S(2)}, u32[]{:S(2)}) collective-permute-start(bf16[208,128]{1,0:T(8,128)(2,1)} %get-tuple-element.41), channel_id=1, source_target_pairs={{0,1},{1,0},{2,3},{3,2},{4,5},{5,4},{6,7},{7,6},{8,9},{9,8},{10,11... | collective-permute-start | bytes 159752 | tf_op jit(solution)/shard_map/ppermute | solution.py:567

commit v7 on v6

--- a/solution.py
+++ b/solution.py
@@ -116,7 +116,7 @@
 def first_kernel(
     run, count_ref, nodes_hbm, ids_hbm, pos_hbm, gain_one_hbm, gain_two_hbm, qkv_hbm, out_hbm,
     first_hbm, sent_hbm, nodes_ref, ids_ref, pos_ref, gain_one_ref, gain_two_ref, qkv_ref, out_ref,
-    sems, qkv_s, q_s, k_s, v_s, ctx_s, n_s, first_s, sent_s, stores
+    sems, qkv_s, q_s, k_s, v_s, ctx_s, inner_s, n_s, first_s, sent_s, stores
 ):
     loads = start_all(
         [
@@ -154,11 +154,11 @@
             start = start + cols[:, axis : axis + 1] * coords[axis][:, at]
         start = (nodes_ref[:, at].astype(F32) + start).astype(BF16)
         nodes_ref[:, at] = start
-        n_s[:, at] = norm_t(start.astype(F32), cols[:, 3:4]).astype(BF16)
+        inner_s[:, at] = norm_t(start.astype(F32), cols[:, 3:4]).astype(BF16)
     wait_all(loads[5:])
     qkv_t = transposed(qkv_ref[...])
     out_t = transposed(out_ref[...])
-    qkv_s[...] = dot(qkv_t, n_s[...]).astype(BF16)
+    qkv_s[...] = dot(qkv_t, inner_s[...]).astype(BF16)
     side = eye(LANES)
     spread = (
         iota((LANES, per * LANES), 0)
@@ -172,29 +172,36 @@
         q_s[t, :, :LANES] = jnp.where(even_row, query, 0.0).astype(BF16)
         q_s[t, :, LANES:] = jnp.where(even_row, 0.0, query).astype(BF16)
         k_s[t] = dot_t(side, qkv_s[chans : 2 * chans, tile(t)]).astype(BF16)
+    half = per * size
+    values = jnp.concatenate([qkv_s[2 * chans :, tile(t)] for t in range(tiles)], 0)
+    values = dot(values, spread)
     for t in range(tiles):
-        wide = dot(qkv_s[2 * chans :, tile(t)], spread)
         for w in range(per):
-            v_s[t, w] = jnp.where(own_head, wide[:, tile(w)], 0.0).astype(BF16)
+            wide = values[t * chans : (t + 1) * chans, tile(w)]
+            wide = jnp.where(own_head, wide, 0.0).astype(BF16)
+            for j in range(HEADS // per):
+                v_s[t, j, w * half : (w + 1) * half] = wide[j * half : (j + 1) * half]
 
     lane_pair = iota((WIN, chans), 1) // (2 * size)
     window = iota((8, LANES), 1) // WIN
     rank = iota((WIN, LANES), 0) + WIN * (iota((WIN, LANES), 1) // WIN)
 
+    def by_window(blocks):
+        out = blocks[0]
+        for w in range(1, per):
+            out = jnp.where(window[None] == w, blocks[w], out)
+        return out
+
     def group(t, _):
         query = q_s[t]
-        even, odd = None, None
+        by_pair = []
         for w in range(per):
             keys = k_s[t, w * WIN : (w + 1) * WIN, :]
-            by_pair = jnp.concatenate(
-                [jnp.where(lane_pair == m, keys, jnp.zeros_like(keys)) for m in range(HEADS // 2)],
-                0,
-            )
-            got = dot(by_pair, query)
-            left = got[:, :LANES].reshape(-1, 8, LANES)
-            right = got[:, LANES:].reshape(-1, 8, LANES)
-            even = left if w == 0 else jnp.where(window[None] == w, left, even)
-            odd = right if w == 0 else jnp.where(window[None] == w, right, odd)
+            nil = jnp.zeros_like(keys)
+            by_pair += [jnp.where(lane_pair == m, keys, nil) for m in range(HEADS // 2)]
+        got = dot(jnp.concatenate(by_pair, 0), query)
+        even = by_window(got[:, :LANES].reshape(per, -1, 8, LANES))
+        odd = by_window(got[:, LANES:].reshape(per, -1, 8, LANES))
         mask = jnp.where(rank + t * LANES < count, 0.0, -1e9).astype(F32)
         mask = mask.reshape(WIN // 8, 8, LANES)
         probs, inverse = [], []
@@ -205,14 +212,10 @@
             weight = jnp.exp(mine - top[None])
             inverse.append(1.0 / fold8(weight, jnp.add))
             probs.append(weight.reshape(WIN, LANES).astype(BF16))
-        half = per * size
         parts = []
         for j in range(HEADS // per):
             weight = jnp.concatenate(probs[j * per : (j + 1) * per], 0)
-            ctx = None
-            for w in range(per):
-                got = dot(v_s[t, w, j * half : (j + 1) * half, :], weight).reshape(-1, 8, LANES)
-                ctx = got if w == 0 else jnp.where(window[None] == w, got, ctx)
+            ctx = by_window(dot(v_s[t, j], weight).reshape(per, -1, 8, LANES))
             for h in range(per):
                 block = ctx[h * (size // 8) : (h + 1) * (size // 8)] * inverse[j * per + h][None]
                 parts.append(block.reshape(size, LANES))
@@ -229,12 +232,13 @@
         normed = norm_t(first.astype(F32), cols[:, 4:5])
         kept = iota((1, LANES), 1) + t * LANES < count
         head = jnp.where((iota((16, LANES), 0) > 0) | kept, normed[:16], FLAG)
-        n_s[:, at] = jnp.concatenate([head, normed[16:]], 0).astype(BF16)
+        n_s[t * chans : (t + 1) * chans] = jnp.concatenate([head, normed[16:]], 0).astype(BF16)
     keep_first = pltpu.make_async_copy(first_s, first_hbm, stores.at[0])
     keep_first.start()
-    inside = within(run)
-    for t, block in enumerate(swap_blocks([dot(n_s[:, tile(t)], inside) for t in range(tiles)])):
-        sent_s[:, tile(t)] = block.astype(BF16)
+    moved = dot(n_s[...], within(run))
+    moved = swap_blocks([moved[t * chans : (t + 1) * chans] for t in range(tiles)])
+    for t in range(tiles):
+        sent_s[:, tile(t)] = moved[t].astype(BF16)
     send = pltpu.make_async_copy(sent_s, sent_hbm, stores.at[1])
     send.start()
     wait_all([keep_first, send])
@@ -458,7 +462,7 @@
     votes_hbm, refs = refs[9 : 9 + owners], refs[9 + owners :]
     (
         block_s, sems, weights_s, q_s, ends_s, acc_s, first_s, gain_s, down_s, facts_s, rest,
-        feat_s, votes_s, stores, k_s, v_s, m_s, s_s, bf_s, inner_s, hidden_s
+        feat_s, votes_s, stores, k_s, v_s, m_s, s_s, bf_s, inner_s
     ) = refs
     loads = start_all([(blocks[n], block_s.at[n]) for n in range(far)], sems)
     later = start_all(
@@ -494,9 +498,9 @@
         return 0
 
     lax.fori_loop(0, tiles // 2, step, 0)
-    inside = within(run)
     ctx = swap_blocks([acc_s[t].reshape(chans, LANES) for t in range(tiles)])
-    ctx = jnp.concatenate([dot_t(c.astype(BF16), inside).astype(BF16) for c in ctx], 1)
+    ctx = dot_t(jnp.concatenate(ctx, 0).astype(BF16), within(run)).astype(BF16)
+    ctx = jnp.concatenate([ctx[t * chans : (t + 1) * chans] for t in range(tiles)], 1)
     gain = jnp.concatenate([gain_s[...], jnp.zeros((7, chans), F32)], 0).T[:, 0:1]
     moved = dot(weights_s[3 * chans : 4 * chans], ctx)
     for t in range(tiles):
@@ -506,20 +510,18 @@
         inner_s[:, at] = norm_t(second, gain).astype(BF16)
     kept = iota((1, slots), 1) < count
     wide = 2 * LANES
-    part = chans // 2
-    for n in range(slots // wide):
-        at = slice(n * wide, (n + 1) * wide)
-        inner = inner_s[:, at]
-        for m in range(down_s.shape[1] // part):
-            row = 4 * chans + m * part
-            raised = dot(weights_s[row : row + part], inner)
-            hidden_s[n % 2, m * part : (m + 1) * part] = jax.nn.gelu(raised).astype(BF16)
-        for m in range(chans // part):
-            rows = slice(m * part, (m + 1) * part)
-            third = feat_s[rows, at] + dot(down_s[rows, :], hidden_s[n % 2])
-            third = jnp.where(kept[:, at], third, 0.0)
-            feat_s[rows, at] = third
-            bf_s[rows, at] = third.astype(BF16)
+    cuts = [slice(at, at + wide) for at in range(0, slots, wide)]
+    up_t = weights_s[4 * chans :]
+    raised = dot(up_t, inner_s[:, cuts[0]])
+    for n, at in enumerate(cuts):
+        now = raised
+        if n + 1 < len(cuts):
+            raised = dot(up_t, inner_s[:, cuts[n + 1]])
+        hidden = jax.nn.gelu(now).astype(BF16)
+        third = feat_s[:, at] + dot(down_s[...], hidden)
+        third = jnp.where(kept[:, at], third, 0.0)
+        feat_s[:, at] = third
+        bf_s[:, at] = third.astype(BF16)
     keep = [pltpu.make_async_copy(feat_s, feat_hbm, stores.at[owners])]
     keep[0].start()
     facts = facts_s[...].astype(F32)
@@ -614,9 +616,10 @@
             vmem((3 * chans, slots), BF16),
             vmem((tiles, chans, 2 * LANES), BF16),
             vmem((tiles, LANES, chans), BF16),
-            vmem((tiles, per, chans, LANES), BF16),
+            vmem((tiles, HEADS // per, per * per * (chans // HEADS), LANES), BF16),
             vmem((tiles, chans, LANES), BF16),
             vmem((chans, slots), BF16),
+            vmem((tiles * chans, LANES), BF16),
             vmem((chans, slots), BF16),
             vmem((chans, slots), BF16),
             dma((2,)),
@@ -735,7 +738,6 @@
         + [
             vmem((chans, slots), BF16),
             vmem((chans, slots), BF16),
-            vmem((2, hidden, 2 * LANES), BF16),
         ],
         3_000_000_000,
         "s" + "a" * (len(far) + 8),

time: 53.8 us -> 53.9 us (level)
  no operation moved by 1% of the time
where the time goes in v7:
time: 53.9 us; the launch traced here: 53.6 us
  Pallas kernels  32 us (59%)
  starting transfers between devices  14.6 us (27%)
  waiting for transfers between devices  5.7 us (11%)
  between operations  1.34 us (2%)
    ppermute x10, starting transfers between devices, turned(): return lax.ppermute(x, axis, [(i, i ^ bit) for i in range(n)])  14.6 us
    pallas_call x1, Pallas kernels, body(): call(functools.partial(first_kernel, run), [sds((chans, slots), BF16), sd...  8.74 us
    pallas_call x1, Pallas kernels, body(): call(functools.partial(second_kernel, run, cap, len(far), owners), [sds((...  7.76 us
    pallas_call x1, Pallas kernels, body(): call(functools.partial(near_kernel, run), [sds(*q_like), sds(*ends_like),...  6.05 us
    ppermute x10, waiting for transfers between devices, turned(): return lax.ppermute(x, axis, [(i, i ^ bit) for i in range(n)])  5.7 us
    pallas_call x1, Pallas kernels, body(): call(functools.partial(middle_kernel, run, len(mid)), [sds(*ends_like), s...  4.34 us
    pallas_call x1, Pallas kernels, body(): call(functools.partial(tables_kernel, cap), [sds((4 * chans + hidden, cha...  2.96 us
    pallas_call x1, Pallas kernels, body(): call(functools.partial(sums_kernel, owners), [sds((chans, VOX_DEV), F32)]...  2.11 us
  transfers between devices with their start and end apart: 10, of which 7 were waited for; matrix products, arithmetic and copies ran while one was open for 0% of the time, Pallas kernels for 25%

profile of v7, /device:TPU:0, one launch (start us, length us, event | category | flops | bytes accessed | tf_op | source)
XLA Modules:
  0.0 53.6 jit_solution(6732469751005293008)
XLA Ops:
  1.3 8.7 %shard_map.167 = (bf16[192,1024]{1,0:T(8,128)(2,1)}, bf16[192,1024]{1,0:T(8,128)(2,1)}) custom-call(s32[1]{0:T(128)S(6)} %copy.18.count_ref, bf16[192,1024]{1,0:T(8,128)(2,1)} %bitcast.11, s32[1,1024]{1,0:T(1,128)} %bitcast.13, f32[3,192]{1,0:T(4,128)} %pos_hbm.1, f32[1,192]{1,0:T(1,128)} %bitcast.17, f32[1,192]{1,0:T(1,128)} %bitcast.18, ...), custom_call_target="tpu_custom_call" | custom-call | flops 2000000000 | bytes 2097152 | tf_op jit(solution)/shard_map/pallas_call | solution.py:604
  10.0 0.5 collective-permute-start.1
  10.5 2.6 %collective-permute-start = (bf16[192,1024]{1,0:T(8,128)(2,1)}, bf16[192,1024]{1,0:T(8,128)(2,1)}, u32[]{:S(2)}, u32[]{:S(2)}) collective-permute-start(bf16[192,1024]{1,0:T(8,128)(2,1)} %get-tuple-element.22.own_hbm), channel_id=1, source_target_pairs={{0,16},{8,24},{16,0},{24,8},{1,17},{9,25},{17,1},{25,9},{2,18},{10... | collective-permute-start | bytes 1179656 | tf_op jit(solution)/shard_map/ppermute | solution.py:569
  13.1 3.0 %shard_map.168 = (bf16[1536,192]{1,0:T(8,128)(2,1)}, bf16[16,1024]{1,0:T(8,128)(2,1)}) custom-call(bf16[192,576]{1,0:T(8,128)(2,1)} %qkv_hbm.3, bf16[192,192]{1,0:T(8,128)(2,1)} %out_hbm.3, bf16[192,768]{1,0:T(8,128)(2,1)} %up_hbm.1, s32[1,512]{1,0:T(1,128)} %bitcast.14, s32[1,512]{1,0:T(1,128)} %bitcast.15, s32[1,512]{1,0:T(1,128)} %bitcast.16), custom_call_target="tpu_custom_call" | custom-call | flops 2000000000 | bytes 2097152 | tf_op jit(solution)/shard_map/pallas_call | solution.py:645
  16.1 0.0 collective-permute-done.1.near_hbm
  16.1 6.0 %shard_map.169 = (f32[8,24,8,128]{3,2,1,0:T(8,128)}, f32[8,4,8,128]{3,2,1,0:T(8,128)}, f32[8,24,8,128]{3,2,1,0:T(8,128)}) custom-call(bf16[192,1024]{1,0:T(8,128)(2,1)} %get-tuple-element.22.own_hbm, bf16[192,1024]{1,0:T(8,128)(2,1)} %collective-permute-done.1.near_hbm, bf16[1536,192]{1,0:T(8,128)(2,1)} %get-tuple-element.23.weights_hbm.refs_4_), custom_call_target="tpu_custom_call" | custom-call | flops 3000000000 | bytes 2097152 | tf_op jit(solution)/shard_map/pallas_call | solution.py:682
  22.2 1.0 %collective-permute-done.refs_0_ = bf16[192,1024]{1,0:T(8,128)(2,1)} collective-permute-done((bf16[192,1024]{1,0:T(8,128)(2,1)}, bf16[192,1024]{1,0:T(8,128)(2,1)}, u32[]{:S(2)}, u32[]{:S(2)}) %collective-permute-start) | collective-permute-done | bytes 393248 | tf_op jit(solution)/shard_map/ppermute | solution.py:569
  23.1 0.0 collective-permute-start.2
  23.1 4.3 %shard_map.170 = (f32[8,4,8,128]{3,2,1,0:T(8,128)}, f32[8,24,8,128]{3,2,1,0:T(8,128)}) custom-call(bf16[192,1024]{1,0:T(8,128)(2,1)} %collective-permute-done.refs_0_, f32[8,24,8,128]{3,2,1,0:T(8,128)} %get-tuple-element.26.refs_1_, f32[8,4,8,128]{3,2,1,0:T(8,128)} %get-tuple-element.27.refs_2_, f32[8,24,8,128]{3,2,1,0:T(8,128)} %get-tuple-element.28.refs_3_, ...), custom_call_target="tpu_custom_call" | custom-call | flops 2000000000 | bytes 2097152 | tf_op jit(solution)/shard_map/pallas_call | solution.py:701
  27.5 0.0 collective-permute-done.2.refs_0_
  27.5 7.8 %shard_map.171 = (f32[192,1024]{1,0:T(8,128)}, bf16[208,128]{1,0:T(8,128)(2,1)}, bf16[208,128]{1,0:T(8,128)(2,1)}, bf16[208,128]{1,0:T(8,128)(2,1)}, bf16[208,12...) custom-call(s32[1]{0:T(128)S(6)} %copy.18.count_ref, ...), custom_call_target="tpu_custom_call" | custom-call | flops 3000000000 | bytes 2097152 | tf_op jit(solution)/shard_map/pallas_call | solution.py:718
  35.3 4.9 %collective-permute-start.3 = (bf16[208,128]{1,0:T(8,128)(2,1)}, bf16[208,128]{1,0:T(8,128)(2,1)}, u32[]{:S(2)}, u32[]{:S(2)}) collective-permute-start(bf16[208,128]{1,0:T(8,128)(2,1)} %get-tuple-element.35), channel_id=1, source_target_pairs={{0,7},{1,6},{2,5},{3,4},{4,3},{5,2},{6,1},{7,0},{8,15},{9,14},{10,... | collective-permute-start | bytes 159752 | tf_op jit(solution)/shard_map/ppermute | solution.py:569
  40.2 0.2 collective-permute-start.4
  40.4 0.7 %collective-permute-start.5 = (bf16[208,128]{1,0:T(8,128)(2,1)}, bf16[208,128]{1,0:T(8,128)(2,1)}, u32[]{:S(2)}, u32[]{:S(2)}) collective-permute-start(bf16[208,128]{1,0:T(8,128)(2,1)} %get-tuple-element.37), channel_id=1, source_target_pairs={{0,5},{1,4},{2,7},{3,6},{4,1},{5,0},{6,3},{7,2},{8,13},{9,12},{10,... | collective-permute-start | bytes 159752 | tf_op jit(solution)/shard_map/ppermute | solution.py:569
  41.1 2.0 %collective-permute-start.6 = (bf16[208,128]{1,0:T(8,128)(2,1)}, bf16[208,128]{1,0:T(8,128)(2,1)}, u32[]{:S(2)}, u32[]{:S(2)}) collective-permute-start(bf16[208,128]{1,0:T(8,128)(2,1)} %get-tuple-element.38), channel_id=1, source_target_pairs={{0,4},{1,5},{2,6},{3,7},{4,0},{5,1},{6,2},{7,3},{8,12},{9,13},{10,... | collective-permute-start | bytes 159752 | tf_op jit(solution)/shard_map/ppermute | solution.py:569
  43.2 2.3 %collective-permute-start.7 = (bf16[208,128]{1,0:T(8,128)(2,1)}, bf16[208,128]{1,0:T(8,128)(2,1)}, u32[]{:S(2)}, u32[]{:S(2)}) collective-permute-start(bf16[208,128]{1,0:T(8,128)(2,1)} %get-tuple-element.39), channel_id=1, source_target_pairs={{0,3},{1,2},{2,1},{3,0},{4,7},{5,6},{6,5},{7,4},{8,11},{9,10},{10,... | collective-permute-start | bytes 159752 | tf_op jit(solution)/shard_map/ppermute | solution.py:569
  45.4 0.0 collective-permute-done.3.refs_1_
  45.4 0.8 %collective-permute-start.8 = (bf16[208,128]{1,0:T(8,128)(2,1)}, bf16[208,128]{1,0:T(8,128)(2,1)}, u32[]{:S(2)}, u32[]{:S(2)}) collective-permute-start(bf16[208,128]{1,0:T(8,128)(2,1)} %get-tuple-element.40), channel_id=1, source_target_pairs={{0,2},{1,3},{2,0},{3,1},{4,6},{5,7},{6,4},{7,5},{8,10},{9,11},{10,... | collective-permute-start | bytes 159752 | tf_op jit(solution)/shard_map/ppermute | solution.py:569
  46.2 0.8 %collective-permute-done.4.refs_2_ = bf16[208,128]{1,0:T(8,128)(2,1)} collective-permute-done((bf16[208,128]{1,0:T(8,128)(2,1)}, bf16[208,128]{1,0:T(8,128)(2,1)}, u32[]{:S(2)}, u32[]{:S(2)}) %collective-permute-start.4) | collective-permute-done | bytes 53280 | tf_op jit(solution)/shard_map/ppermute | solution.py:569
  47.0 0.5 collective-permute-start.9
  47.5 1.7 %collective-permute-done.5.refs_3_ = bf16[208,128]{1,0:T(8,128)(2,1)} collective-permute-done((bf16[208,128]{1,0:T(8,128)(2,1)}, bf16[208,128]{1,0:T(8,128)(2,1)}, u32[]{:S(2)}, u32[]{:S(2)}) %collective-permute-start.5) | collective-permute-done | bytes 53280 | tf_op jit(solution)/shard_map/ppermute | solution.py:569
  49.2 1.0 %collective-permute-done.6.refs_4_ = bf16[208,128]{1,0:T(8,128)(2,1)} collective-permute-done((bf16[208,128]{1,0:T(8,128)(2,1)}, bf16[208,128]{1,0:T(8,128)(2,1)}, u32[]{:S(2)}, u32[]{:S(2)}) %collective-permute-start.6) | collective-permute-done | bytes 53280 | tf_op jit(solution)/shard_map/ppermute | solution.py:569
  50.2 0.5 collective-permute-done.7.refs_5_
  50.7 0.3 collective-permute-done.8.refs_6_
  51.0 0.5 collective-permute-done.9.refs_7_
  51.4 2.1 %shard_map.172 = f32[192,256]{1,0:T(8,128)} custom-call(bf16[208,128]{1,0:T(8,128)(2,1)} %get-tuple-element.34.refs_0_, bf16[208,128]{1,0:T(8,128)(2,1)} %collective-permute-done.3.refs_1_, bf16[208,128]{1,0:T(8,128)(2,1)} %collective-permute-done.4.refs_2_, bf16[208,128]{1,0:T(8,128)(2,1)} %collective-permute-done.5.refs_3_, ...), custom_call_target="tpu_custom_call" | custom-call | flops 200000000 | bytes 2097152 | tf_op jit(solution)/shard_map/pallas_call | solution.py:757
Async XLA Ops:
  10.0 6.1 %collective-permute-start.1 = (bf16[192,1024]{1,0:T(8,128)(2,1)}, bf16[192,1024]{1,0:T(8,128)(2,1)}, u32[]{:S(2)}, u32[]{:S(2)}) collective-permute-start(bf16[192,1024]{1,0:T(8,128)(2,1)} %get-tuple-element.22.own_hbm), channel_id=1, source_target_pairs={{0,8},{8,0},{16,24},{24,16},{1,9},{9,1},{17,25},{25,17},{2,10},{10... | collective-permute-start | bytes 1179656 | tf_op jit(solution)/shard_map/ppermute | solution.py:569
  10.5 12.6 %collective-permute-start = (bf16[192,1024]{1,0:T(8,128)(2,1)}, bf16[192,1024]{1,0:T(8,128)(2,1)}, u32[]{:S(2)}, u32[]{:S(2)}) collective-permute-start(bf16[192,1024]{1,0:T(8,128)(2,1)} %get-tuple-element.22.own_hbm), channel_id=1, source_target_pairs={{0,16},{8,24},{16,0},{24,8},{1,17},{9,25},{17,1},{25,9},{2,18},{10... | collective-permute-start | bytes 1179656 | tf_op jit(solution)/shard_map/ppermute | solution.py:569
  23.1 4.3 %collective-permute-start.2 = (bf16[192,1024]{1,0:T(8,128)(2,1)}, bf16[192,1024]{1,0:T(8,128)(2,1)}, u32[]{:S(2)}, u32[]{:S(2)}) collective-permute-start(bf16[192,1024]{1,0:T(8,128)(2,1)} %collective-permute-done.refs_0_), channel_id=1, source_target_pairs={{0,8},{8,0},{16,24},{24,16},{1,9},{9,1},{17,25},{25,17},{2,10},{10... | collective-permute-start | bytes 1179656 | tf_op jit(solution)/shard_map/ppermute | solution.py:569
  35.3 10.2 %collective-permute-start.3 = (bf16[208,128]{1,0:T(8,128)(2,1)}, bf16[208,128]{1,0:T(8,128)(2,1)}, u32[]{:S(2)}, u32[]{:S(2)}) collective-permute-start(bf16[208,128]{1,0:T(8,128)(2,1)} %get-tuple-element.35), channel_id=1, source_target_pairs={{0,7},{1,6},{2,5},{3,4},{4,3},{5,2},{6,1},{7,0},{8,15},{9,14},{10,... | collective-permute-start | bytes 159752 | tf_op jit(solution)/shard_map/ppermute | solution.py:569
  40.2 6.8 %collective-permute-start.4 = (bf16[208,128]{1,0:T(8,128)(2,1)}, bf16[208,128]{1,0:T(8,128)(2,1)}, u32[]{:S(2)}, u32[]{:S(2)}) collective-permute-start(bf16[208,128]{1,0:T(8,128)(2,1)} %get-tuple-element.36), channel_id=1, source_target_pairs={{0,6},{1,7},{2,4},{3,5},{4,2},{5,3},{6,0},{7,1},{8,14},{9,15},{10,... | collective-permute-start | bytes 159752 | tf_op jit(solution)/shard_map/ppermute | solution.py:569
  40.4 8.8 %collective-permute-start.5 = (bf16[208,128]{1,0:T(8,128)(2,1)}, bf16[208,128]{1,0:T(8,128)(2,1)}, u32[]{:S(2)}, u32[]{:S(2)}) collective-permute-start(bf16[208,128]{1,0:T(8,128)(2,1)} %get-tuple-element.37), channel_id=1, source_target_pairs={{0,5},{1,4},{2,7},{3,6},{4,1},{5,0},{6,3},{7,2},{8,13},{9,12},{10,... | collective-permute-start | bytes 159752 | tf_op jit(solution)/shard_map/ppermute | solution.py:569
  41.1 9.1 %collective-permute-start.6 = (bf16[208,128]{1,0:T(8,128)(2,1)}, bf16[208,128]{1,0:T(8,128)(2,1)}, u32[]{:S(2)}, u32[]{:S(2)}) collective-permute-start(bf16[208,128]{1,0:T(8,128)(2,1)} %get-tuple-element.38), channel_id=1, source_target_pairs={{0,4},{1,5},{2,6},{3,7},{4,0},{5,1},{6,2},{7,3},{8,12},{9,13},{10,... | collective-permute-start | bytes 159752 | tf_op jit(solution)/shard_map/ppermute | solution.py:569
  43.2 7.5 %collective-permute-start.7 = (bf16[208,128]{1,0:T(8,128)(2,1)}, bf16[208,128]{1,0:T(8,128)(2,1)}, u32[]{:S(2)}, u32[]{:S(2)}) collective-permute-start(bf16[208,128]{1,0:T(8,128)(2,1)} %get-tuple-element.39), channel_id=1, source_target_pairs={{0,3},{1,2},{2,1},{3,0},{4,7},{5,6},{6,5},{7,4},{8,11},{9,10},{10,... | collective-permute-start | bytes 159752 | tf_op jit(solution)/shard_map/ppermute | solution.py:569
  45.4 5.5 %collective-permute-start.8 = (bf16[208,128]{1,0:T(8,128)(2,1)}, bf16[208,128]{1,0:T(8,128)(2,1)}, u32[]{:S(2)}, u32[]{:S(2)}) collective-permute-start(bf16[208,128]{1,0:T(8,128)(2,1)} %get-tuple-element.40), channel_id=1, source_target_pairs={{0,2},{1,3},{2,0},{3,1},{4,6},{5,7},{6,4},{7,5},{8,10},{9,11},{10,... | collective-permute-start | bytes 159752 | tf_op jit(solution)/shard_map/ppermute | solution.py:569
  47.0 4.5 %collective-permute-start.9 = (bf16[208,128]{1,0:T(8,128)(2,1)}, bf16[208,128]{1,0:T(8,128)(2,1)}, u32[]{:S(2)}, u32[]{:S(2)}) collective-permute-start(bf16[208,128]{1,0:T(8,128)(2,1)} %get-tuple-element.41), channel_id=1, source_target_pairs={{0,1},{1,0},{2,3},{3,2},{4,5},{5,4},{6,7},{7,6},{8,9},{9,8},{10,11... | collective-permute-start | bytes 159752 | tf_op jit(solution)/shard_map/ppermute | solution.py:569

commit v8 on v6

--- a/solution.py
+++ b/solution.py
@@ -14,6 +14,7 @@
 LANES = 128
 FLAG = 16384.0
 VMEM = 64 * 1024 * 1024 - 65536
+ROOMY = 24 * 1024 * 1024
 F32 = jnp.float32
 BF16 = jnp.bfloat16
 LOG2E = math.log2(math.e)
@@ -90,6 +91,12 @@
     cent = x - mean
     var = jnp.sum(cent * cent, 0, keepdims=True) * inv
     return cent * lax.rsqrt(var + 1e-05) * gain
+
+
+def gelu(x):
+    half = 0.5 * x
+    scale = math.sqrt(2 / math.pi)
+    return half + half * jnp.tanh(x * (scale + (0.044715 * scale) * (x * x)))
 
 
 def start_all(pairs, sems):
@@ -219,7 +226,7 @@
         ctx_s[t] = jnp.concatenate(parts, 0).astype(BF16)
         return 0
 
-    lax.fori_loop(0, tiles, group, 0, unroll=2)
+    lax.fori_loop(0, tiles, group, 0, unroll=4)
     ctx = jnp.concatenate([ctx_s[t] for t in range(tiles)], 1)
     moved = dot(out_t, ctx)
     for t in range(tiles):
@@ -309,7 +316,7 @@
             m_s[n, t] = jnp.broadcast_to(mask[:, tile(t)], (8, LANES))
 
 
-def attend_two(t, run, q_s, k_s, v_s, m_s, s_s, ends_s, acc_s, fresh):
+def attend_two(t, run, q_s, k_s, v_s, m_s, s_s, state_s, fresh):
     rows8 = q_s.shape[1]
     cut = 2 * rows8 // 3
     keys = k_s.shape[0] * run
@@ -342,7 +349,7 @@
     if fresh:
         old = tuple(jnp.full((8, LANES), -3e38, F32) for _ in range(4))
     else:
-        old = tuple(ends_s[t + n, part] for n in both for part in both)
+        old = tuple(state_s[t + n, rows8 + part] for n in both for part in both)
     tops = lax.fori_loop(0, keys, score, old, unroll=2)
     if fresh:
         zero = jnp.zeros((8, LANES), F32)
@@ -350,9 +357,11 @@
         accs = tuple(zero for _ in range(2 * rows8))
     else:
         fade = [jnp.exp2(old[n] - tops[n]) for n in range(4)]
-        sums = tuple(ends_s[t + n, 2 + part] * fade[2 * n + part] for n in both for part in both)
+        sums = tuple(
+            state_s[t + n, rows8 + 2 + part] * fade[2 * n + part] for n in both for part in both
+        )
         accs = tuple(
-            acc_s[t + n, i] * fade[2 * n + int(i >= cut)] for n in both for i in range(rows8)
+            state_s[t + n, i] * fade[2 * n + int(i >= cut)] for n in both for i in range(rows8)
         )
 
     def gather(key, carry):
@@ -371,102 +380,92 @@
     return tops, sums, accs
 
 
-def hold_two(t, state, ends_s, acc_s):
+def store_pair(n, state_s, state_hbm, stores):
+    pair = pl.ds(2 * n, 2)
+    return pltpu.make_async_copy(state_s.at[pair], state_hbm.at[pair], stores.at[n])
+
+
+def hold_two(n, state, state_s, state_hbm, stores):
     tops, sums, accs = state
-    rows8 = acc_s.shape[1]
-    for n in range(2):
+    rows8 = len(accs) // 2
+    for m in range(2):
+        for i in range(rows8):
+            state_s[2 * n + m, i] = accs[m * rows8 + i]
         for part in range(2):
-            ends_s[t + n, part] = tops[2 * n + part]
-            ends_s[t + n, 2 + part] = sums[2 * n + part]
-        for i in range(rows8):
-            acc_s[t + n, i] = accs[n * rows8 + i]
+            state_s[2 * n + m, rows8 + part] = tops[2 * m + part]
+            state_s[2 * n + m, rows8 + 2 + part] = sums[2 * m + part]
+    store_pair(n, state_s, state_hbm, stores).start()
 
 
 def near_kernel(
-    run, own_hbm, near_hbm, weights_hbm, q_hbm, ends_hbm, acc_hbm,
-    own_ref, near_ref, qkv_t_ref, sems, q_s, ends_s, acc_s, stores, k_s, v_s, m_s, s_s
+    run, own_ref, near_ref, weights_hbm, q_hbm, state_hbm,
+    qkv_t_ref, sems, q_s, state_s, stores, k_s, v_s, m_s, s_s
 ):
     chans, slots = own_ref.shape
-    loads = start_all(
-        [
-            (own_hbm, own_ref),
-            (weights_hbm.at[pl.ds(0, 3 * chans)], qkv_t_ref),
-            (near_hbm, near_ref),
-        ],
-        sems,
-    )
+    loads = start_all([(weights_hbm.at[pl.ds(0, 3 * chans)], qkv_t_ref)], sems)
     tiles = slots // LANES
     scale = (chans // HEADS) ** -0.5 * LOG2E
-    wait_all(loads[:2])
+    wait_all(loads)
     own, _ = clean(own_ref[...])
     query = dot(qkv_t_ref[:chans, :], own) * scale
     for t in range(tiles):
         q_s[t] = query[:, tile(t)].reshape(chans // 8, 8, LANES)
-    keep_q = pltpu.make_async_copy(q_s, q_hbm, stores.at[0])
+    pairs = tiles // 2
+    keep_q = pltpu.make_async_copy(q_s, q_hbm, stores.at[pairs])
     keep_q.start()
-    wait_all(loads[2:])
     add_keys([own_ref[...], near_ref[...]], qkv_t_ref[chans:, :], k_s, v_s, m_s)
 
     def step(n, _):
-        t = 2 * n
-        state = attend_two(t, run, q_s, k_s, v_s, m_s, s_s, ends_s, acc_s, True)
-        hold_two(t, state, ends_s, acc_s)
+        state = attend_two(2 * n, run, q_s, k_s, v_s, m_s, s_s, state_s, True)
+        hold_two(n, state, state_s, state_hbm, stores)
         return 0
 
-    lax.fori_loop(0, tiles // 2, step, 0)
-    keep_ends = pltpu.make_async_copy(ends_s, ends_hbm, stores.at[1])
-    keep_acc = pltpu.make_async_copy(acc_s, acc_hbm, stores.at[2])
-    keep_ends.start()
-    keep_acc.start()
-    wait_all([keep_q, keep_ends, keep_acc])
+    lax.fori_loop(0, pairs, step, 0)
+    wait_all([keep_q] + [store_pair(n, state_s, state_hbm, stores) for n in range(pairs)])
 
 
 def middle_kernel(run, count, *refs):
     blocks, refs = refs[:count], refs[count:]
-    q_hbm, ends_hbm, acc_hbm, weights_hbm, ends_out, acc_out = refs[:6]
-    block_s, sems, q_s, ends_s, acc_s, kv_t_ref, rest, stores, k_s, v_s, m_s, s_s = refs[6:]
+    q_hbm, state_in, weights_hbm, state_hbm = refs[:4]
+    q_s, state_s, kv_t_ref, rest, stores, k_s, v_s, m_s, s_s = refs[4:]
     chans = kv_t_ref.shape[1]
-    loads = start_all([(blocks[n], block_s.at[n]) for n in range(count)], sems)
+    pairs = q_s.shape[0] // 2
     later = start_all(
         [
             (weights_hbm.at[pl.ds(chans, 2 * chans)], kv_t_ref),
             (q_hbm, q_s),
-            (ends_hbm, ends_s),
-            (acc_hbm, acc_s),
+            (state_in, state_s),
         ],
         rest,
     )
-    wait_all(loads + later[:1])
-    add_keys([block_s[n] for n in range(count)], kv_t_ref[...], k_s, v_s, m_s)
+    wait_all(later[:1])
+    add_keys([block[...] for block in blocks], kv_t_ref[...], k_s, v_s, m_s)
     wait_all(later[1:])
 
     def step(n, _):
-        t = 2 * n
-        state = attend_two(t, run, q_s, k_s, v_s, m_s, s_s, ends_s, acc_s, False)
-        hold_two(t, state, ends_s, acc_s)
+        state = attend_two(2 * n, run, q_s, k_s, v_s, m_s, s_s, state_s, False)
+        hold_two(n, state, state_s, state_hbm, stores)
         return 0
 
-    lax.fori_loop(0, q_s.shape[0] // 2, step, 0)
-    wait_all(start_all([(ends_s, ends_out), (acc_s, acc_out)], stores))
+    lax.fori_loop(0, pairs, step, 0)
+    wait_all([store_pair(n, state_s, state_hbm, stores) for n in range(pairs)])
 
 
 def second_kernel(run, cap, far, owners, count_ref, *refs):
     blocks, refs = refs[:far], refs[far:]
     (
-        q_hbm, ends_hbm, acc_hbm, weights_hbm, first_hbm, gain_hbm, down_hbm, facts_hbm, feat_hbm
-    ) = refs[:9]
-    votes_hbm, refs = refs[9 : 9 + owners], refs[9 + owners :]
+        q_hbm, state_hbm, weights_hbm, first_hbm, gain_hbm, down_hbm, facts_hbm, feat_hbm
+    ) = refs[:8]
+    votes_hbm, refs = refs[8 : 8 + owners], refs[8 + owners :]
     (
-        block_s, sems, weights_s, q_s, ends_s, acc_s, first_s, gain_s, down_s, facts_s, rest,
-        feat_s, votes_s, stores, k_s, v_s, m_s, s_s, bf_s, inner_s, hidden_s
+        weights_s, q_s, state_s, first_s, gain_s, down_s, facts_s, rest,
+        feat_s, votes_s, stores, k_s, v_s, m_s, s_s, bf_s, inner_s
     ) = refs
-    loads = start_all([(blocks[n], block_s.at[n]) for n in range(far)], sems)
     later = start_all(
         [
             (weights_hbm, weights_s),
             (q_hbm, q_s),
-            (ends_hbm, ends_s),
-            (acc_hbm, acc_s),
+            (state_hbm, state_s),
             (first_hbm, first_s),
             (gain_hbm, gain_s),
             (down_hbm, down_s),
@@ -477,26 +476,26 @@
     chans, slots = first_s.shape
     tiles = slots // LANES
     count = count_ref[0]
-    wait_all(loads + later[:1])
-    add_keys([block_s[n] for n in range(far)], weights_s[chans : 3 * chans], k_s, v_s, m_s)
+    wait_all(later[:1])
+    add_keys([block[...] for block in blocks], weights_s[chans : 3 * chans], k_s, v_s, m_s)
     wait_all(later[1:])
 
     rows8 = chans // 8
 
     def step(n, _):
         t = 2 * n
-        _, sums, accs = attend_two(t, run, q_s, k_s, v_s, m_s, s_s, ends_s, acc_s, False)
+        _, sums, accs = attend_two(t, run, q_s, k_s, v_s, m_s, s_s, state_s, False)
         share = [1.0 / total for total in sums]
         cut = 2 * rows8 // 3
         for n in range(2):
             for i in range(rows8):
-                acc_s[t + n, i] = accs[n * rows8 + i] * share[2 * n + int(i >= cut)]
+                state_s[t + n, i] = accs[n * rows8 + i] * share[2 * n + int(i >= cut)]
         return 0
 
     lax.fori_loop(0, tiles // 2, step, 0)
-    inside = within(run)
-    ctx = swap_blocks([acc_s[t].reshape(chans, LANES) for t in range(tiles)])
-    ctx = jnp.concatenate([dot_t(c.astype(BF16), inside).astype(BF16) for c in ctx], 1)
+    ctx = swap_blocks([state_s[t, :rows8].reshape(chans, LANES) for t in range(tiles)])
+    ctx = dot_t(jnp.concatenate(ctx, 0).astype(BF16), within(run)).astype(BF16)
+    ctx = jnp.concatenate([ctx[t * chans : (t + 1) * chans] for t in range(tiles)], 1)
     gain = jnp.concatenate([gain_s[...], jnp.zeros((7, chans), F32)], 0).T[:, 0:1]
     moved = dot(weights_s[3 * chans : 4 * chans], ctx)
     for t in range(tiles):
@@ -506,20 +505,18 @@
         inner_s[:, at] = norm_t(second, gain).astype(BF16)
     kept = iota((1, slots), 1) < count
     wide = 2 * LANES
-    part = chans // 2
-    for n in range(slots // wide):
-        at = slice(n * wide, (n + 1) * wide)
-        inner = inner_s[:, at]
-        for m in range(down_s.shape[1] // part):
-            row = 4 * chans + m * part
-            raised = dot(weights_s[row : row + part], inner)
-            hidden_s[n % 2, m * part : (m + 1) * part] = jax.nn.gelu(raised).astype(BF16)
-        for m in range(chans // part):
-            rows = slice(m * part, (m + 1) * part)
-            third = feat_s[rows, at] + dot(down_s[rows, :], hidden_s[n % 2])
-            third = jnp.where(kept[:, at], third, 0.0)
-            feat_s[rows, at] = third
-            bf_s[rows, at] = third.astype(BF16)
+    cuts = [slice(at, at + wide) for at in range(0, slots, wide)]
+    up_t = weights_s[4 * chans :]
+    raised = dot(up_t, inner_s[:, cuts[0]])
+    for n, at in enumerate(cuts):
+        now = raised
+        if n + 1 < len(cuts):
+            raised = dot(up_t, inner_s[:, cuts[n + 1]])
+        hidden = gelu(now).astype(BF16)
+        third = feat_s[:, at] + dot(down_s[...], hidden)
+        third = jnp.where(kept[:, at], third, 0.0)
+        feat_s[:, at] = third
+        bf_s[:, at] = third.astype(BF16)
     keep = [pltpu.make_async_copy(feat_s, feat_hbm, stores.at[owners])]
     keep[0].start()
     facts = facts_s[...].astype(F32)
@@ -533,21 +530,23 @@
     wait_all(keep)
 
 
-def sums_kernel(owners, *refs):
-    got, out_ref, got_s, sems = refs[:owners], refs[owners], refs[owners + 1], refs[owners + 2]
-    loads = start_all([(got[n], got_s.at[n]) for n in range(owners)], sems)
+def sums_kernel(own_hbm, *refs):
+    got, out_ref, own_ref, sem = refs[:-3], refs[-3], refs[-2], refs[-1]
+    load = pltpu.make_async_copy(own_hbm, own_ref, sem)
+    load.start()
     chans, voxels = out_ref.shape
-    cap = got_s.shape[2]
+    cap = own_ref.shape[1]
     total = jnp.zeros(out_ref.shape, F32)
-    wait_all(loads)
-    for n in range(owners):
-        label = got_s[n, chans:, :].astype(F32)[0:1]
+    for ref in got + (own_ref,):
+        if ref is own_ref:
+            load.wait()
+        label = ref[chans:, :].astype(F32)[0:1]
         hot = (label == iota((voxels, cap), 0).astype(F32)).astype(BF16)
-        total = total + dot_t(got_s[n, :chans, :], hot)
+        total = total + dot_t(ref[:chans, :], hot)
     out_ref[...] = total
 
 
-def call(kernel, outs, scratch, flops, spaces, out_space=pl.ANY):
+def call(kernel, outs, scratch, flops, spaces, out_space=pl.ANY, limit=VMEM):
     return pl.pallas_call(
         kernel,
         out_shape=outs,
@@ -557,7 +556,7 @@
         ],
         out_specs=[pl.BlockSpec(memory_space=out_space)] * len(outs),
         scratch_shapes=scratch,
-        compiler_params=pltpu.CompilerParams(vmem_limit_bytes=VMEM),
+        compiler_params=pltpu.CompilerParams(vmem_limit_bytes=limit),
         cost_estimate=pl.CostEstimate(flops=flops, bytes_accessed=2 << 20, transcendentals=0),
     )
 
@@ -633,12 +632,12 @@
         qkv_one,
         out_one,
     )
-    near = turned(sent, "grp", 1)
     bit = groups // 2
     mid = []
     while bit > 1:
         mid += [turned(block, "grp", bit) for block in [sent] + mid]
         bit //= 2
+    near = turned(sent, "grp", 1)
     weights, facts = call(
         functools.partial(tables_kernel, cap),
         [sds((4 * chans + hidden, chans), BF16), sds((16, codes), BF16)],
@@ -656,6 +655,7 @@
         ],
         2_000_000_000,
         "aaaaaa",
+        limit=ROOMY,
     )(
         qkv_two,
         out_two,
@@ -665,8 +665,7 @@
         vote_voxel.reshape(1, votes),
     )
     q_like = ((tiles, rows8, 8, LANES), F32)
-    ends_like = ((tiles, 4, 8, LANES), F32)
-    acc_like = ((tiles, rows8, 8, LANES), F32)
+    state_like = ((tiles, rows8 + 4, 8, LANES), F32)
 
     def key_scratch(blocks):
         return [
@@ -676,57 +675,50 @@
             vmem((blocks * run, 4, 8, LANES), F32),
         ]
 
-    query, ends, acc = call(
+    query, state = call(
         functools.partial(near_kernel, run),
-        [sds(*q_like), sds(*ends_like), sds(*acc_like)],
-        [
-            vmem((chans, slots), BF16),
-            vmem((chans, slots), BF16),
+        [sds(*q_like), sds(*state_like)],
+        [
             vmem((3 * chans, chans), BF16),
-            dma((3,)),
+            dma((1,)),
             vmem(*q_like),
-            vmem(*ends_like),
-            vmem(*acc_like),
-            dma((3,)),
+            vmem(*state_like),
+            dma((tiles // 2 + 1,)),
         ]
         + key_scratch(2),
         3_000_000_000,
-        "aaa",
+        "vva",
+        limit=ROOMY,
     )(sent, near, weights)
     mid, query = lax.optimization_barrier((mid, query))
     far = [turned(block, "grp", 1) for block in mid]
-    ends, acc = call(
+    (state,) = call(
         functools.partial(middle_kernel, run, len(mid)),
-        [sds(*ends_like), sds(*acc_like)],
-        [
-            vmem((len(mid), chans, slots), BF16),
-            dma((len(mid),)),
+        [sds(*state_like)],
+        [
             vmem(*q_like),
-            vmem(*ends_like),
-            vmem(*acc_like),
+            vmem(*state_like),
             vmem((2 * chans, chans), BF16),
-            dma((4,)),
-            dma((2,)),
+            dma((3,)),
+            dma((tiles // 2,)),
         ]
         + key_scratch(len(mid)),
         2_000_000_000,
-        "a" * len(mid) + "aaaa",
-    )(*mid, query, ends, acc, weights)
+        "v" * len(mid) + "aaa",
+        limit=ROOMY,
+    )(*mid, query, state, weights)
     features_t, *ballots = call(
         functools.partial(second_kernel, run, cap, len(far), owners),
         [sds((chans, slots), F32)] + [sds((chans + 16, cap), BF16)] * owners,
         [
-            vmem((len(far), chans, slots), BF16),
-            dma((len(far),)),
             vmem((4 * chans + hidden, chans), BF16),
             vmem(*q_like),
-            vmem(*ends_like),
-            vmem(*acc_like),
+            vmem(*state_like),
             vmem((chans, slots), BF16),
             vmem((1, chans), F32),
             vmem((chans, hidden), BF16),
             vmem((16, codes), BF16),
-            dma((8,)),
+            dma((7,)),
             vmem((chans, slots), F32),
             vmem((owners, chans + 16, cap), BF16),
             dma((owners + 1,)),
@@ -735,30 +727,30 @@
         + [
             vmem((chans, slots), BF16),
             vmem((chans, slots), BF16),
-            vmem((2, hidden, 2 * LANES), BF16),
         ],
         3_000_000_000,
-        "s" + "a" * (len(far) + 8),
+        "s" + "v" * len(far) + "a" * 7,
+        limit=ROOMY,
     )(
         node_count,
         *far,
         query,
-        ends,
-        acc,
+        state,
         weights,
         first,
         gain_three.reshape(1, chans),
         w_down.T,
         facts,
     )
-    got = [ballots[0]] + [turned(ballots[k], "tile", k) for k in range(owners - 1, 0, -1)]
+    got = [ballots[0]] + [turned(ballots[k], "tile", k) for k in [1] + list(range(owners - 1, 1, -1))]
     (sums_t,) = call(
-        functools.partial(sums_kernel, owners),
+        sums_kernel,
         [sds((chans, VOX_DEV), F32)],
-        [vmem((owners, chans + 16, cap), BF16), dma((owners,))],
+        [vmem((chans + 16, cap), BF16), dma],
         200_000_000,
-        "a" * owners,
+        "a" + "v" * (owners - 1),
         pltpu.VMEM,
+        ROOMY,
     )(*got)
     return (features_t.T, sums_t.T)
 

time: 53.8 us -> 51.7 us (0.961)
  Pallas kernels: 31.9 us -> 26.8 us
  local copies, waits for them, and re-layouts: 0 us -> 4.16 us
  waiting for transfers between devices: 5.72 us -> 4.57 us
    unnamed x0 -> x20, local copies, waits for them, and re-layouts: none -> 4.16 us
    pallas_call x3, Pallas kernels: 12.5 us -> 10.4 us  [the longest x1 5.36 us: body(): call(functools.partial(near_kernel, run), [sds(*q_like), sds(*state_like)...]
    pallas_call x1, Pallas kernels: 8.16 us -> 6.29 us  [body(): call(functools.partial(second_kernel, run, cap, len(far), owners), [sds((...]
    ppermute x10, waiting for transfers between devices: 5.72 us -> 4.57 us  [turned(): return lax.ppermute(x, axis, [(i, i ^ bit) for i in range(n)])]
    pallas_call x1, Pallas kernels: 2.96 us -> 2.12 us  [body(): call(functools.partial(tables_kernel, cap), [sds((4 * chans + hidden, cha...]
  transfers between devices with their start and end apart: 10 -> 10, of which waited for: 7 -> 3; matrix products, arithmetic and copies ran while one was open for 0% -> 0% of each run, Pallas kernels for 25% -> 22%
where the time goes in v8:
time: 51.7 us; the launch traced here: 51.5 us
  Pallas kernels  26.8 us (52%)
  starting transfers between devices  14.5 us (28%)
  waiting for transfers between devices  4.57 us (9%)
  local copies, waits for them, and re-layouts  4.16 us (8%)
  between operations  1.4 us (3%)
    ppermute x10, starting transfers between devices, turned(): return lax.ppermute(x, axis, [(i, i ^ bit) for i in range(n)])  14.5 us
    pallas_call x1, Pallas kernels, body(): call(functools.partial(first_kernel, run), [sds((chans, slots), BF16), sd...  8 us
    pallas_call x1, Pallas kernels, body(): call(functools.partial(second_kernel, run, cap, len(far), owners), [sds((...  6.29 us
    pallas_call x1, Pallas kernels, body(): call(functools.partial(near_kernel, run), [sds(*q_like), sds(*state_like)...  5.36 us
    ppermute x10, waiting for transfers between devices, turned(): return lax.ppermute(x, axis, [(i, i ^ bit) for i in range(n)])  4.57 us
    unnamed x20, local copies, waits for them, and re-layouts  4.16 us
    pallas_call x1, Pallas kernels, body(): call(functools.partial(middle_kernel, run, len(mid)), [sds(*state_like)],...  3.75 us
    pallas_call x1, Pallas kernels, body(): call(functools.partial(tables_kernel, cap), [sds((4 * chans + hidden, cha...  2.12 us
  transfers between devices with their start and end apart: 10, of which 3 were waited for; matrix products, arithmetic and copies ran while one was open for 0% of the time, Pallas kernels for 22%

profile of v8, /device:TPU:0, one launch (start us, length us, event | category | flops | bytes accessed | tf_op | source)
XLA Modules:
  0.0 51.5 jit_solution(6957298303390851659)
XLA Ops:
  1.3 8.0 %shard_map.167 = (bf16[192,1024]{1,0:T(8,128)(2,1)}, bf16[192,1024]{1,0:T(8,128)(2,1)}) custom-call(s32[1]{0:T(128)S(6)} %copy.18.count_ref, bf16[192,1024]{1,0:T(8,128)(2,1)} %bitcast.16, s32[1,1024]{1,0:T(1,128)} %bitcast.17, f32[3,192]{1,0:T(4,128)} %pos_hbm.1, f32[1,192]{1,0:T(1,128)} %bitcast.18, f32[1,192]{1,0:T(1,128)} %bitcast.19, ...), custom_call_target="tpu_custom_call" | custom-call | flops 2000000000 | bytes 2097152 | tf_op jit(solution)/shard_map/pallas_call | solution.py:601
  9.3 0.0 copy-start.7
  9.3 0.5 %collective-permute-start.1 = (bf16[192,1024]{1,0:T(8,128)(2,1)}, bf16[192,1024]{1,0:T(8,128)(2,1)S(1)}, u32[]{:S(2)}, u32[]{:S(2)}) collective-permute-start(bf16[192,1024]{1,0:T(8,128)(2,1)} %get-tuple-element.19.own_ref), channel_id=1, source_target_pairs={{0,8},{8,0},{16,24},{24,16},{1,9},{9,1},{17,25},{25,17},{2,10},{10... | collective-permute-start | bytes 1179656 | tf_op jit(solution)/shard_map/ppermute | solution.py:566
  9.8 2.6 %collective-permute-start = (bf16[192,1024]{1,0:T(8,128)(2,1)}, bf16[192,1024]{1,0:T(8,128)(2,1)S(1)}, u32[]{:S(2)}, u32[]{:S(2)}) collective-permute-start(bf16[192,1024]{1,0:T(8,128)(2,1)} %get-tuple-element.19.own_ref), channel_id=1, source_target_pairs={{0,16},{8,24},{16,0},{24,8},{1,17},{9,25},{17,1},{25,9},{2,18},{10... | collective-permute-start | bytes 1179656 | tf_op jit(solution)/shard_map/ppermute | solution.py:566
  12.4 0.7 %copy-done.6 = s32[512,1]{0,1:T(1,128)S(1)} copy-done((s32[512,1]{0,1:T(1,128)S(1)}, s32[512,1]{0,1:T(1,128)}, u32[]{:S(2)}) %copy-start.6) | copy-done | bytes 2072
  13.1 0.0 copy-done.5
  13.1 1.0 %copy-done.1 = bf16[192,768]{1,0:T(8,128)(2,1)S(1)} copy-done((bf16[192,768]{1,0:T(8,128)(2,1)S(1)}, bf16[192,768]{1,0:T(8,128)(2,1)}, u32[]{:S(2)}) %copy-start.1) | copy-done | bytes 294936
  14.1 0.9 %copy-done.3 = bf16[192,576]{1,0:T(8,128)(2,1)S(1)} copy-done((bf16[192,576]{1,0:T(8,128)(2,1)S(1)}, bf16[192,576]{1,0:T(8,128)(2,1)}, u32[]{:S(2)}) %copy-start.3) | copy-done | bytes 221208
  15.0 0.9 %copy-done.4 = bf16[192,192]{1,0:T(8,128)(2,1)S(1)} copy-done((bf16[192,192]{1,0:T(8,128)(2,1)S(1)}, bf16[192,192]{1,0:T(8,128)(2,1)}, u32[]{:S(2)}) %copy-start.4) | copy-done | bytes 73752
  15.9 2.1 %shard_map.168 = (bf16[1536,192]{1,0:T(8,128)(2,1)S(1)}, bf16[16,1024]{1,0:T(8,128)(2,1)S(1)}) custom-call(bf16[192,576]{1,0:T(8,128)(2,1)S(1)} %copy-done.3, bf16[192,192]{1,0:T(8,128)(2,1)S(1)} %copy-done.4, bf16[192,768]{1,0:T(8,128)(2,1)S(1)} %copy-done.1, s32[1,512]{1,0:T(1,128)S(1)} %bitcast.12, s32[1,512]{1,0:T(1,128)S(1)} %bitcast.13, ...), custom_call_target="tpu_custom_call" | custom-call | flops 2000000000 | bytes 2097152 | tf_op jit(solution)/shard_map/pallas_call | solution.py:641
  18.0 0.0 collective-permute-done.1.near_ref
  18.0 5.4 %shard_map.169 = (f32[8,24,8,128]{3,2,1,0:T(8,128)S(1)}, f32[8,28,8,128]{3,2,1,0:T(8,128)S(1)}) custom-call(bf16[192,1024]{1,0:T(8,128)(2,1)S(1)} %copy-done, bf16[192,1024]{1,0:T(8,128)(2,1)S(1)} %collective-permute-done.1.near_ref, bf16[1536,192]{1,0:T(8,128)(2,1)S(1)} %get-tuple-element.20.weights_hbm.refs_3_), custom_call_target="tpu_custom_call" | custom-call | flops 3000000000 | bytes 2097152 | tf_op jit(solution)/shard_map/pallas_call | solution.py:678
  23.4 0.0 collective-permute-done.refs_0_
  23.4 0.2 collective-permute-start.2
  23.7 3.7 %shard_map.170.refs_2_ = f32[8,28,8,128]{3,2,1,0:T(8,128)S(1)} custom-call(bf16[192,1024]{1,0:T(8,128)(2,1)S(1)} %collective-permute-done.refs_0_, f32[8,24,8,128]{3,2,1,0:T(8,128)S(1)} %get-tuple-element.23.refs_1_, f32[8,28,8,128]{3,2,1,0:T(8,128)S(1)} %get-tuple-element.24.refs_2_, bf16[1536,192]{1,0:T(8,128)(2,1)S(1)} %get-tuple-element.20.weights_hbm.refs_3_), custom_call_target="tpu_custom_call" | custom-call | flops 2000000000 | bytes 2097152 | tf_op jit(solution)/shard_map/pallas_call | solution.py:695
  27.4 0.0 copy-start.8
  27.5 0.7 %copy-done.8 = f32[192]{0:T(256)S(1)} copy-done((f32[192]{0:T(256)S(1)}, f32[192]{0:T(256)}, u32[]{:S(2)}) %copy-start.8) | copy-done | bytes 792
  28.1 6.3 %shard_map.171 = (f32[192,1024]{1,0:T(8,128)}, bf16[208,128]{1,0:T(8,128)(2,1)S(1)}, bf16[208,128]{1,0:T(8,128)(2,1)S(1)}, bf16[208,128]{1,0:T(8,128)(2,1)S(1)},...) custom-call(s32[1]{0:T(128)S(6)} %copy.18.count_ref, ...), custom_call_target="tpu_custom_call" | custom-call | flops 3000000000 | bytes 2097152 | tf_op jit(solution)/shard_map/pallas_call | solution.py:710
  34.4 1.6 %collective-permute-start.3 = (bf16[208,128]{1,0:T(8,128)(2,1)S(1)}, bf16[208,128]{1,0:T(8,128)(2,1)S(1)}, u32[]{:S(2)}, u32[]{:S(2)}) collective-permute-start(bf16[208,128]{1,0:T(8,128)(2,1)S(1)} %get-tuple-element.29), channel_id=1, source_target_pairs={{0,1},{1,0},{2,3},{3,2},{4,5},{5,4},{6,7},{7,6},{8,9},{9,8},{10,11... | collective-permute-start | bytes 159752 | tf_op jit(solution)/shard_map/ppermute | solution.py:566
  36.0 3.5 %collective-permute-start.4 = (bf16[208,128]{1,0:T(8,128)(2,1)S(1)}, bf16[208,128]{1,0:T(8,128)(2,1)S(1)}, u32[]{:S(2)}, u32[]{:S(2)}) collective-permute-start(bf16[208,128]{1,0:T(8,128)(2,1)S(1)} %get-tuple-element.30), channel_id=1, source_target_pairs={{0,7},{1,6},{2,5},{3,4},{4,3},{5,2},{6,1},{7,0},{8,15},{9,14},{10,... | collective-permute-start | bytes 159752 | tf_op jit(solution)/shard_map/ppermute | solution.py:566
  39.5 0.2 collective-permute-start.5
  39.8 1.7 %collective-permute-start.6 = (bf16[208,128]{1,0:T(8,128)(2,1)S(1)}, bf16[208,128]{1,0:T(8,128)(2,1)S(1)}, u32[]{:S(2)}, u32[]{:S(2)}) collective-permute-start(bf16[208,128]{1,0:T(8,128)(2,1)S(1)} %get-tuple-element.32), channel_id=1, source_target_pairs={{0,5},{1,4},{2,7},{3,6},{4,1},{5,0},{6,3},{7,2},{8,13},{9,12},{10,... | collective-permute-start | bytes 159752 | tf_op jit(solution)/shard_map/ppermute | solution.py:566
  41.5 2.1 %collective-permute-start.7 = (bf16[208,128]{1,0:T(8,128)(2,1)S(1)}, bf16[208,128]{1,0:T(8,128)(2,1)S(1)}, u32[]{:S(2)}, u32[]{:S(2)}) collective-permute-start(bf16[208,128]{1,0:T(8,128)(2,1)S(1)} %get-tuple-element.33), channel_id=1, source_target_pairs={{0,4},{1,5},{2,6},{3,7},{4,0},{5,1},{6,2},{7,3},{8,12},{9,13},{10,... | collective-permute-start | bytes 159752 | tf_op jit(solution)/shard_map/ppermute | solution.py:566
  43.6 0.0 collective-permute-done.3.refs_0_
  43.6 1.2 %collective-permute-start.8 = (bf16[208,128]{1,0:T(8,128)(2,1)S(1)}, bf16[208,128]{1,0:T(8,128)(2,1)S(1)}, u32[]{:S(2)}, u32[]{:S(2)}) collective-permute-start(bf16[208,128]{1,0:T(8,128)(2,1)S(1)} %get-tuple-element.34), channel_id=1, source_target_pairs={{0,3},{1,2},{2,1},{3,0},{4,7},{5,6},{6,5},{7,4},{8,11},{9,10},{10,... | collective-permute-start | bytes 159752 | tf_op jit(solution)/shard_map/ppermute | solution.py:566
  44.9 0.0 collective-permute-done.4.refs_1_
  44.9 0.7 %collective-permute-start.9 = (bf16[208,128]{1,0:T(8,128)(2,1)S(1)}, bf16[208,128]{1,0:T(8,128)(2,1)S(1)}, u32[]{:S(2)}, u32[]{:S(2)}) collective-permute-start(bf16[208,128]{1,0:T(8,128)(2,1)S(1)} %get-tuple-element.35), channel_id=1, source_target_pairs={{0,2},{1,3},{2,0},{3,1},{4,6},{5,7},{6,4},{7,5},{8,10},{9,11},{10,... | collective-permute-start | bytes 159752 | tf_op jit(solution)/shard_map/ppermute | solution.py:566
  45.6 0.0 collective-permute-done.5.refs_2_
  45.6 3.2 %collective-permute-done.6.refs_3_ = bf16[208,128]{1,0:T(8,128)(2,1)S(1)} collective-permute-done((bf16[208,128]{1,0:T(8,128)(2,1)S(1)}, bf16[208,128]{1,0:T(8,128)(2,1)S(1)}, u32[]{:S(2)}, u32[]{:S(2)}) %collective-permute-start.6) | collective-permute-done | bytes 53280 | tf_op jit(solution)/shard_map/ppermute | solution.py:566
  48.9 0.1 collective-permute-done.7.refs_4_
  49.0 1.2 %collective-permute-done.8.refs_5_ = bf16[208,128]{1,0:T(8,128)(2,1)S(1)} collective-permute-done((bf16[208,128]{1,0:T(8,128)(2,1)S(1)}, bf16[208,128]{1,0:T(8,128)(2,1)S(1)}, u32[]{:S(2)}, u32[]{:S(2)}) %collective-permute-start.8) | collective-permute-done | bytes 53280 | tf_op jit(solution)/shard_map/ppermute | solution.py:566
  50.2 1.3 %shard_map.172 = f32[192,256]{1,0:T(8,128)} custom-call(bf16[208,128]{1,0:T(8,128)(2,1)S(1)} %get-tuple-element.28.own_hbm, bf16[208,128]{1,0:T(8,128)(2,1)S(1)} %collective-permute-done.3.refs_0_, bf16[208,128]{1,0:T(8,128)(2,1)S(1)} %collective-permute-done.4.refs_1_, bf16[208,128]{1,0:T(8,128)(2,1)S(1)} %collective-permute-done.5.refs_2_, ...), custom_call_target="tpu_custom_call" | custom-call | flops 200000000 | bytes 2097152 | tf_op jit(solution)/shard_map/pallas_call | solution.py:746
  (14 shorter events, 0.0 us)
Async XLA Ops:
  9.3 3.1 %copy-start.7 = (s32[512]{0:T(512)S(1)}, s32[512]{0:T(512)}, u32[]{:S(2)}) copy-start(s32[512]{0:T(512)} %param.31) | copy-start | bytes 6148
  9.3 8.7 %collective-permute-start.1 = (bf16[192,1024]{1,0:T(8,128)(2,1)}, bf16[192,1024]{1,0:T(8,128)(2,1)S(1)}, u32[]{:S(2)}, u32[]{:S(2)}) collective-permute-start(bf16[192,1024]{1,0:T(8,128)(2,1)} %get-tuple-element.19.own_ref), channel_id=1, source_target_pairs={{0,8},{8,0},{16,24},{24,16},{1,9},{9,1},{17,25},{25,17},{2,10},{10... | collective-permute-start | bytes 1179656 | tf_op jit(solution)/shard_map/ppermute | solution.py:566
  9.8 13.6 %collective-permute-start = (bf16[192,1024]{1,0:T(8,128)(2,1)}, bf16[192,1024]{1,0:T(8,128)(2,1)S(1)}, u32[]{:S(2)}, u32[]{:S(2)}) collective-permute-start(bf16[192,1024]{1,0:T(8,128)(2,1)} %get-tuple-element.19.own_ref), channel_id=1, source_target_pairs={{0,16},{8,24},{16,0},{24,8},{1,17},{9,25},{17,1},{25,9},{2,18},{10... | collective-permute-start | bytes 1179656 | tf_op jit(solution)/shard_map/ppermute | solution.py:566
  12.4 0.7 %copy-start.6 = (s32[512,1]{0,1:T(1,128)S(1)}, s32[512,1]{0,1:T(1,128)}, u32[]{:S(2)}) copy-start(s32[512,1]{0,1:T(1,128)} %param.30) | copy-start | bytes 6148
  12.4 0.7 %copy-start.5 = (s32[512]{0:T(512)S(1)}, s32[512]{0:T(512)}, u32[]{:S(2)}) copy-start(s32[512]{0:T(512)} %param.29) | copy-start | bytes 6148
  13.1 1.0 %copy-start.1 = (bf16[192,768]{1,0:T(8,128)(2,1)S(1)}, bf16[192,768]{1,0:T(8,128)(2,1)}, u32[]{:S(2)}) copy-start(bf16[192,768]{1,0:T(8,128)(2,1)} %up_hbm.1) | copy-start | bytes 884740
  14.1 0.9 %copy-start.3 = (bf16[192,576]{1,0:T(8,128)(2,1)S(1)}, bf16[192,576]{1,0:T(8,128)(2,1)}, u32[]{:S(2)}) copy-start(bf16[192,576]{1,0:T(8,128)(2,1)} %qkv_hbm.3) | copy-start | bytes 663556
  15.0 0.9 %copy-start.4 = (bf16[192,192]{1,0:T(8,128)(2,1)S(1)}, bf16[192,192]{1,0:T(8,128)(2,1)}, u32[]{:S(2)}) copy-start(bf16[192,192]{1,0:T(8,128)(2,1)} %out_hbm.3) | copy-start | bytes 221188
  15.9 2.1 %copy-start = (bf16[192,1024]{1,0:T(8,128)(2,1)S(1)}, bf16[192,1024]{1,0:T(8,128)(2,1)}, u32[]{:S(2)}) copy-start(bf16[192,1024]{1,0:T(8,128)(2,1)} %get-tuple-element.19.own_ref) | copy-start | bytes 1179652
  23.4 4.0 %collective-permute-start.2 = (bf16[192,1024]{1,0:T(8,128)(2,1)S(1)}, bf16[192,1024]{1,0:T(8,128)(2,1)S(1)}, u32[]{:S(2)}, u32[]{:S(2)}) collective-permute-start(bf16[192,1024]{1,0:T(8,128)(2,1)S(1)} %collective-permute-done.refs_0_), channel_id=1, source_target_pairs={{0,8},{8,0},{16,24},{24,16},{1,9},{9,1},{17,25},{25,17},{2,10},{10... | collective-permute-start | bytes 1179656 | tf_op jit(solution)/shard_map/ppermute | solution.py:566
  23.7 3.8 %copy-start.2 = (bf16[768,192]{0,1:T(8,128)(2,1)S(1)}, bf16[768,192]{0,1:T(8,128)(2,1)}, u32[]{:S(2)}) copy-start(bf16[768,192]{0,1:T(8,128)(2,1)} %param.28) | copy-start | bytes 884740
  23.7 3.8 %copy-start.9 = (bf16[192,1024]{1,0:T(8,128)(2,1)S(1)}, bf16[192,1024]{1,0:T(8,128)(2,1)}, u32[]{:S(2)}) copy-start(bf16[192,1024]{1,0:T(8,128)(2,1)} %get-tuple-element.25.refs_4_) | copy-start | bytes 1179652
  27.4 0.7 %copy-start.8 = (f32[192]{0:T(256)S(1)}, f32[192]{0:T(256)}, u32[]{:S(2)}) copy-start(f32[192]{0:T(256)} %param.26) | copy-start | bytes 2308
  34.4 9.2 %collective-permute-start.3 = (bf16[208,128]{1,0:T(8,128)(2,1)S(1)}, bf16[208,128]{1,0:T(8,128)(2,1)S(1)}, u32[]{:S(2)}, u32[]{:S(2)}) collective-permute-start(bf16[208,128]{1,0:T(8,128)(2,1)S(1)} %get-tuple-element.29), channel_id=1, source_target_pairs={{0,1},{1,0},{2,3},{3,2},{4,5},{5,4},{6,7},{7,6},{8,9},{9,8},{10,11... | collective-permute-start | bytes 159752 | tf_op jit(solution)/shard_map/ppermute | solution.py:566
  36.0 8.9 %collective-permute-start.4 = (bf16[208,128]{1,0:T(8,128)(2,1)S(1)}, bf16[208,128]{1,0:T(8,128)(2,1)S(1)}, u32[]{:S(2)}, u32[]{:S(2)}) collective-permute-start(bf16[208,128]{1,0:T(8,128)(2,1)S(1)} %get-tuple-element.30), channel_id=1, source_target_pairs={{0,7},{1,6},{2,5},{3,4},{4,3},{5,2},{6,1},{7,0},{8,15},{9,14},{10,... | collective-permute-start | bytes 159752 | tf_op jit(solution)/shard_map/ppermute | solution.py:566
  39.5 6.1 %collective-permute-start.5 = (bf16[208,128]{1,0:T(8,128)(2,1)S(1)}, bf16[208,128]{1,0:T(8,128)(2,1)S(1)}, u32[]{:S(2)}, u32[]{:S(2)}) collective-permute-start(bf16[208,128]{1,0:T(8,128)(2,1)S(1)} %get-tuple-element.31), channel_id=1, source_target_pairs={{0,6},{1,7},{2,4},{3,5},{4,2},{5,3},{6,0},{7,1},{8,14},{9,15},{10,... | collective-permute-start | bytes 159752 | tf_op jit(solution)/shard_map/ppermute | solution.py:566
  39.8 9.1 %collective-permute-start.6 = (bf16[208,128]{1,0:T(8,128)(2,1)S(1)}, bf16[208,128]{1,0:T(8,128)(2,1)S(1)}, u32[]{:S(2)}, u32[]{:S(2)}) collective-permute-start(bf16[208,128]{1,0:T(8,128)(2,1)S(1)} %get-tuple-element.32), channel_id=1, source_target_pairs={{0,5},{1,4},{2,7},{3,6},{4,1},{5,0},{6,3},{7,2},{8,13},{9,12},{10,... | collective-permute-start | bytes 159752 | tf_op jit(solution)/shard_map/ppermute | solution.py:566
  41.5 7.5 %collective-permute-start.7 = (bf16[208,128]{1,0:T(8,128)(2,1)S(1)}, bf16[208,128]{1,0:T(8,128)(2,1)S(1)}, u32[]{:S(2)}, u32[]{:S(2)}) collective-permute-start(bf16[208,128]{1,0:T(8,128)(2,1)S(1)} %get-tuple-element.33), channel_id=1, source_target_pairs={{0,4},{1,5},{2,6},{3,7},{4,0},{5,1},{6,2},{7,3},{8,12},{9,13},{10,... | collective-permute-start | bytes 159752 | tf_op jit(solution)/shard_map/ppermute | solution.py:566
  43.6 6.5 %collective-permute-start.8 = (bf16[208,128]{1,0:T(8,128)(2,1)S(1)}, bf16[208,128]{1,0:T(8,128)(2,1)S(1)}, u32[]{:S(2)}, u32[]{:S(2)}) collective-permute-start(bf16[208,128]{1,0:T(8,128)(2,1)S(1)} %get-tuple-element.34), channel_id=1, source_target_pairs={{0,3},{1,2},{2,1},{3,0},{4,7},{5,6},{6,5},{7,4},{8,11},{9,10},{10,... | collective-permute-start | bytes 159752 | tf_op jit(solution)/shard_map/ppermute | solution.py:566
  44.9 5.3 %collective-permute-start.9 = (bf16[208,128]{1,0:T(8,128)(2,1)S(1)}, bf16[208,128]{1,0:T(8,128)(2,1)S(1)}, u32[]{:S(2)}, u32[]{:S(2)}) collective-permute-start(bf16[208,128]{1,0:T(8,128)(2,1)S(1)} %get-tuple-element.35), channel_id=1, source_target_pairs={{0,2},{1,3},{2,0},{3,1},{4,6},{5,7},{6,4},{7,5},{8,10},{9,11},{10,... | collective-permute-start | bytes 159752 | tf_op jit(solution)/shard_map/ppermute | solution.py:566

commit v9 on v8

--- a/solution.py
+++ b/solution.py
@@ -167,25 +167,18 @@
     out_t = transposed(out_ref[...])
     qkv_s[...] = dot(qkv_t, n_s[...]).astype(BF16)
     side = eye(LANES)
-    spread = (
-        iota((LANES, per * LANES), 0)
-        == (iota((LANES, per * LANES), 1) // LANES) * WIN + iota((LANES, per * LANES), 1) % WIN
-    ).astype(BF16)
-    row_head = (iota((chans, LANES), 0) // size) % per
-    own_head = row_head == iota((chans, LANES), 1) // WIN
+    row_head = iota((chans, LANES), 0) // size
     even_row = row_head % 2 == 0
     for t in range(tiles):
         query = qkv_s[:chans, tile(t)].astype(F32) * size**-0.5
         q_s[t, :, :LANES] = jnp.where(even_row, query, 0.0).astype(BF16)
         q_s[t, :, LANES:] = jnp.where(even_row, 0.0, query).astype(BF16)
         k_s[t] = dot_t(side, qkv_s[chans : 2 * chans, tile(t)]).astype(BF16)
-    for t in range(tiles):
-        wide = dot(qkv_s[2 * chans :, tile(t)], spread)
-        for w in range(per):
-            v_s[t, w] = jnp.where(own_head, wide[:, tile(w)], 0.0).astype(BF16)
+        v_s[t] = qkv_s[2 * chans :, tile(t)]
 
     lane_pair = iota((WIN, chans), 1) // (2 * size)
     window = iota((8, LANES), 1) // WIN
+    wide_window = iota((WIN, LANES), 1) // WIN
     rank = iota((WIN, LANES), 0) + WIN * (iota((WIN, LANES), 1) // WIN)
 
     def group(t, _):
@@ -212,16 +205,21 @@
             weight = jnp.exp(mine - top[None])
             inverse.append(1.0 / fold8(weight, jnp.add))
             probs.append(weight.reshape(WIN, LANES).astype(BF16))
-        half = per * size
         parts = []
-        for j in range(HEADS // per):
-            weight = jnp.concatenate(probs[j * per : (j + 1) * per], 0)
-            ctx = None
-            for w in range(per):
-                got = dot(v_s[t, w, j * half : (j + 1) * half, :], weight).reshape(-1, 8, LANES)
-                ctx = got if w == 0 else jnp.where(window[None] == w, got, ctx)
-            for h in range(per):
-                block = ctx[h * (size // 8) : (h + 1) * (size // 8)] * inverse[j * per + h][None]
+        for m in range(HEADS // 2):
+            both = []
+            for h in (2 * m, 2 * m + 1):
+                nil = jnp.zeros_like(probs[h])
+                both.append(
+                    jnp.concatenate(
+                        [jnp.where(wide_window == w, probs[h], nil) for w in range(per)], 0
+                    )
+                )
+            rows = slice(2 * m * size, 2 * (m + 1) * size)
+            got = dot(v_s[t, rows, :], jnp.concatenate(both, 1))
+            for n in range(2):
+                block = got[n * size : (n + 1) * size, tile(n)].reshape(-1, 8, LANES)
+                block = block * inverse[2 * m + n][None]
                 parts.append(block.reshape(size, LANES))
         ctx_s[t] = jnp.concatenate(parts, 0).astype(BF16)
         return 0
@@ -248,8 +246,8 @@
 
 
 def tables_kernel(
-    cap, qkv_hbm, out_hbm, up_hbm, slot_hbm, owner_hbm, voxel_hbm, weights_hbm, facts_hbm,
-    qkv_ref, out_ref, up_ref, slot_ref, owner_ref, voxel_ref, sems, weights_s, facts_s, stores
+    cap, qkv_hbm, out_hbm, up_hbm, slot_hbm, owner_hbm, voxel_hbm, gain_hbm, weights_s, facts_s,
+    gain_s, qkv_ref, out_ref, up_ref, slot_ref, owner_ref, voxel_ref, gain_ref, sems
 ):
     loads = start_all(
         [
@@ -259,10 +257,13 @@
             (slot_hbm, slot_ref),
             (owner_hbm, owner_ref),
             (voxel_hbm, voxel_ref),
+            (gain_hbm, gain_ref),
         ],
         sems,
     )
     wait_all(loads)
+    gain = jnp.concatenate([gain_ref[...], jnp.zeros((7, gain_ref.shape[1]), F32)], 0)
+    gain_s[...] = jnp.broadcast_to(gain.T[:, 0:1], gain_s.shape)
     votes = slot_ref.shape[1]
     codes = facts_s.shape[1]
     owners = codes // cap
@@ -274,8 +275,6 @@
     out_t = dot(shuffle[:chans, :chans], out_ref[...])
     weights_s[3 * chans : 4 * chans] = transposed(out_t)
     weights_s[4 * chans :] = transposed(up_ref[...])
-    keep_weights = pltpu.make_async_copy(weights_s, weights_hbm, stores.at[0])
-    keep_weights.start()
     owner = jnp.bitwise_xor(owner_ref[...], lax.axis_index("tile"))
     hot = owner == iota((owners, votes), 0)
     upto = (iota((votes, votes), 0) <= iota((votes, votes), 1)).astype(BF16)
@@ -291,9 +290,6 @@
     )
     listed = dot_t(facts.astype(F32).astype(BF16), member)
     facts_s[...] = jnp.where(listed[3:4] > 0.5, listed, -1.0).astype(BF16)
-    keep_facts = pltpu.make_async_copy(facts_s, facts_hbm, stores.at[1])
-    keep_facts.start()
-    wait_all([keep_weights, keep_facts])
 
 
 def clean(block):
@@ -380,12 +376,7 @@
     return tops, sums, accs
 
 
-def store_pair(n, state_s, state_hbm, stores):
-    pair = pl.ds(2 * n, 2)
-    return pltpu.make_async_copy(state_s.at[pair], state_hbm.at[pair], stores.at[n])
-
-
-def hold_two(n, state, state_s, state_hbm, stores):
+def hold_two(n, state, state_s):
     tops, sums, accs = state
     rows8 = len(accs) // 2
     for m in range(2):
@@ -394,92 +385,48 @@
         for part in range(2):
             state_s[2 * n + m, rows8 + part] = tops[2 * m + part]
             state_s[2 * n + m, rows8 + 2 + part] = sums[2 * m + part]
-    store_pair(n, state_s, state_hbm, stores).start()
-
-
-def near_kernel(
-    run, own_ref, near_ref, weights_hbm, q_hbm, state_hbm,
-    qkv_t_ref, sems, q_s, state_s, stores, k_s, v_s, m_s, s_s
-):
+
+
+def near_kernel(run, own_ref, near_ref, weights_ref, q_s, state_s, k_s, v_s, m_s, s_s):
     chans, slots = own_ref.shape
-    loads = start_all([(weights_hbm.at[pl.ds(0, 3 * chans)], qkv_t_ref)], sems)
     tiles = slots // LANES
     scale = (chans // HEADS) ** -0.5 * LOG2E
-    wait_all(loads)
     own, _ = clean(own_ref[...])
-    query = dot(qkv_t_ref[:chans, :], own) * scale
+    query = dot(weights_ref[:chans, :], own) * scale
     for t in range(tiles):
         q_s[t] = query[:, tile(t)].reshape(chans // 8, 8, LANES)
-    pairs = tiles // 2
-    keep_q = pltpu.make_async_copy(q_s, q_hbm, stores.at[pairs])
-    keep_q.start()
-    add_keys([own_ref[...], near_ref[...]], qkv_t_ref[chans:, :], k_s, v_s, m_s)
+    add_keys([own_ref[...], near_ref[...]], weights_ref[chans : 3 * chans, :], k_s, v_s, m_s)
 
     def step(n, _):
-        state = attend_two(2 * n, run, q_s, k_s, v_s, m_s, s_s, state_s, True)
-        hold_two(n, state, state_s, state_hbm, stores)
+        hold_two(n, attend_two(2 * n, run, q_s, k_s, v_s, m_s, s_s, state_s, True), state_s)
         return 0
 
-    lax.fori_loop(0, pairs, step, 0)
-    wait_all([keep_q] + [store_pair(n, state_s, state_hbm, stores) for n in range(pairs)])
+    lax.fori_loop(0, tiles // 2, step, 0)
 
 
 def middle_kernel(run, count, *refs):
     blocks, refs = refs[:count], refs[count:]
-    q_hbm, state_in, weights_hbm, state_hbm = refs[:4]
-    q_s, state_s, kv_t_ref, rest, stores, k_s, v_s, m_s, s_s = refs[4:]
-    chans = kv_t_ref.shape[1]
-    pairs = q_s.shape[0] // 2
-    later = start_all(
-        [
-            (weights_hbm.at[pl.ds(chans, 2 * chans)], kv_t_ref),
-            (q_hbm, q_s),
-            (state_in, state_s),
-        ],
-        rest,
-    )
-    wait_all(later[:1])
-    add_keys([block[...] for block in blocks], kv_t_ref[...], k_s, v_s, m_s)
-    wait_all(later[1:])
+    q_s, old_s, weights_ref, state_s, k_s, v_s, m_s, s_s = refs
+    chans = weights_ref.shape[1]
+    kv_t = weights_ref[chans : 3 * chans, :]
+    add_keys([block[...] for block in blocks], kv_t, k_s, v_s, m_s)
 
     def step(n, _):
-        state = attend_two(2 * n, run, q_s, k_s, v_s, m_s, s_s, state_s, False)
-        hold_two(n, state, state_s, state_hbm, stores)
+        hold_two(n, attend_two(2 * n, run, q_s, k_s, v_s, m_s, s_s, old_s, False), state_s)
         return 0
 
-    lax.fori_loop(0, pairs, step, 0)
-    wait_all([store_pair(n, state_s, state_hbm, stores) for n in range(pairs)])
+    lax.fori_loop(0, q_s.shape[0] // 2, step, 0)
 
 
 def second_kernel(run, cap, far, owners, count_ref, *refs):
     blocks, refs = refs[:far], refs[far:]
-    (
-        q_hbm, state_hbm, weights_hbm, first_hbm, gain_hbm, down_hbm, facts_hbm, feat_hbm
-    ) = refs[:8]
-    votes_hbm, refs = refs[8 : 8 + owners], refs[8 + owners :]
-    (
-        weights_s, q_s, state_s, first_s, gain_s, down_s, facts_s, rest,
-        feat_s, votes_s, stores, k_s, v_s, m_s, s_s, bf_s, inner_s
-    ) = refs
-    later = start_all(
-        [
-            (weights_hbm, weights_s),
-            (q_hbm, q_s),
-            (state_hbm, state_s),
-            (first_hbm, first_s),
-            (gain_hbm, gain_s),
-            (down_hbm, down_s),
-            (facts_hbm, facts_s),
-        ],
-        rest,
-    )
+    q_s, state_s, weights_s, first_s, gain_s, down_s, facts_s, feat_hbm = refs[:8]
+    votes_s, refs = refs[8 : 8 + owners], refs[8 + owners :]
+    feat_s, store, k_s, v_s, m_s, s_s, ctx_s, bf_s, inner_s = refs
     chans, slots = first_s.shape
     tiles = slots // LANES
     count = count_ref[0]
-    wait_all(later[:1])
     add_keys([block[...] for block in blocks], weights_s[chans : 3 * chans], k_s, v_s, m_s)
-    wait_all(later[1:])
-
     rows8 = chans // 8
 
     def step(n, _):
@@ -489,14 +436,14 @@
         cut = 2 * rows8 // 3
         for n in range(2):
             for i in range(rows8):
-                state_s[t + n, i] = accs[n * rows8 + i] * share[2 * n + int(i >= cut)]
+                ctx_s[t + n, i] = accs[n * rows8 + i] * share[2 * n + int(i >= cut)]
         return 0
 
     lax.fori_loop(0, tiles // 2, step, 0)
-    ctx = swap_blocks([state_s[t, :rows8].reshape(chans, LANES) for t in range(tiles)])
+    ctx = swap_blocks([ctx_s[t].reshape(chans, LANES) for t in range(tiles)])
     ctx = dot_t(jnp.concatenate(ctx, 0).astype(BF16), within(run)).astype(BF16)
     ctx = jnp.concatenate([ctx[t * chans : (t + 1) * chans] for t in range(tiles)], 1)
-    gain = jnp.concatenate([gain_s[...], jnp.zeros((7, chans), F32)], 0).T[:, 0:1]
+    gain = gain_s[...]
     moved = dot(weights_s[3 * chans : 4 * chans], ctx)
     for t in range(tiles):
         at = tile(t)
@@ -517,44 +464,36 @@
         third = jnp.where(kept[:, at], third, 0.0)
         feat_s[:, at] = third
         bf_s[:, at] = third.astype(BF16)
-    keep = [pltpu.make_async_copy(feat_s, feat_hbm, stores.at[owners])]
-    keep[0].start()
+    keep = pltpu.make_async_copy(feat_s, feat_hbm, store)
+    keep.start()
     facts = facts_s[...].astype(F32)
     low, high = facts[2:3].astype(jnp.int32), facts[1:2].astype(jnp.int32)
     picked = dot(bf_s[...], place(low, high, tiles)).astype(BF16)
     for o in range(owners):
-        votes_s[o, :chans, :] = picked[:, o * cap : (o + 1) * cap]
-        votes_s[o, chans:, :] = facts_s[:, o * cap : (o + 1) * cap]
-        keep.append(pltpu.make_async_copy(votes_s.at[o], votes_hbm[o], stores.at[o]))
-        keep[-1].start()
-    wait_all(keep)
-
-
-def sums_kernel(own_hbm, *refs):
-    got, out_ref, own_ref, sem = refs[:-3], refs[-3], refs[-2], refs[-1]
-    load = pltpu.make_async_copy(own_hbm, own_ref, sem)
-    load.start()
+        votes_s[o][:chans, :] = picked[:, o * cap : (o + 1) * cap]
+        votes_s[o][chans:, :] = facts_s[:, o * cap : (o + 1) * cap]
+    keep.wait()
+
+
+def sums_kernel(*refs):
+    got, out_ref = refs[:-1], refs[-1]
     chans, voxels = out_ref.shape
-    cap = own_ref.shape[1]
+    cap = got[0].shape[1]
     total = jnp.zeros(out_ref.shape, F32)
-    for ref in got + (own_ref,):
-        if ref is own_ref:
-            load.wait()
+    for ref in got:
         label = ref[chans:, :].astype(F32)[0:1]
         hot = (label == iota((voxels, cap), 0).astype(F32)).astype(BF16)
         total = total + dot_t(ref[:chans, :], hot)
     out_ref[...] = total
 
 
-def call(kernel, outs, scratch, flops, spaces, out_space=pl.ANY, limit=VMEM):
+def call(kernel, outs, scratch, flops, spaces, out_spaces, limit=VMEM):
+    place_of = {"s": pltpu.SMEM, "v": pltpu.VMEM, "a": pl.ANY}
     return pl.pallas_call(
         kernel,
         out_shape=outs,
-        in_specs=[
-            pl.BlockSpec(memory_space={"s": pltpu.SMEM, "v": pltpu.VMEM, "a": pl.ANY}[c])
-            for c in spaces
-        ],
-        out_specs=[pl.BlockSpec(memory_space=out_space)] * len(outs),
+        in_specs=[pl.BlockSpec(memory_space=place_of[c]) for c in spaces],
+        out_specs=[pl.BlockSpec(memory_space=place_of[c]) for c in out_spaces],
         scratch_shapes=scratch,
         compiler_params=pltpu.CompilerParams(vmem_limit_bytes=limit),
         cost_estimate=pl.CostEstimate(flops=flops, bytes_accessed=2 << 20, transcendentals=0),
@@ -613,7 +552,7 @@
             vmem((3 * chans, slots), BF16),
             vmem((tiles, chans, 2 * LANES), BF16),
             vmem((tiles, LANES, chans), BF16),
-            vmem((tiles, per, chans, LANES), BF16),
+            vmem((tiles, chans, LANES), BF16),
             vmem((tiles, chans, LANES), BF16),
             vmem((chans, slots), BF16),
             vmem((chans, slots), BF16),
@@ -622,6 +561,7 @@
         ],
         2_000_000_000,
         "saaaaaaa",
+        "aa",
     )(
         node_count,
         nodes.T,
@@ -638,9 +578,13 @@
         mid += [turned(block, "grp", bit) for block in [sent] + mid]
         bit //= 2
     near = turned(sent, "grp", 1)
-    weights, facts = call(
+    weights, facts, gain = call(
         functools.partial(tables_kernel, cap),
-        [sds((4 * chans + hidden, chans), BF16), sds((16, codes), BF16)],
+        [
+            sds((4 * chans + hidden, chans), BF16),
+            sds((16, codes), BF16),
+            sds((chans, LANES), F32),
+        ],
         [
             vmem((chans, 3 * chans), BF16),
             vmem((chans, chans), BF16),
@@ -648,13 +592,12 @@
             vmem((1, votes), jnp.int32),
             vmem((1, votes), jnp.int32),
             vmem((1, votes), jnp.int32),
-            dma((6,)),
-            vmem((4 * chans + hidden, chans), BF16),
-            vmem((16, codes), BF16),
-            dma((2,)),
+            vmem((1, chans), F32),
+            dma((7,)),
         ],
         2_000_000_000,
-        "aaaaaa",
+        "aaaaaaa",
+        "vvv",
         limit=ROOMY,
     )(
         qkv_two,
@@ -663,6 +606,7 @@
         vote_slot.reshape(1, votes),
         vote_owner.reshape(1, votes),
         vote_voxel.reshape(1, votes),
+        gain_three.reshape(1, chans),
     )
     q_like = ((tiles, rows8, 8, LANES), F32)
     state_like = ((tiles, rows8 + 4, 8, LANES), F32)
@@ -678,16 +622,10 @@
     query, state = call(
         functools.partial(near_kernel, run),
         [sds(*q_like), sds(*state_like)],
-        [
-            vmem((3 * chans, chans), BF16),
-            dma((1,)),
-            vmem(*q_like),
-            vmem(*state_like),
-            dma((tiles // 2 + 1,)),
-        ]
-        + key_scratch(2),
+        key_scratch(2),
         3_000_000_000,
-        "vva",
+        "vvv",
+        "vv",
         limit=ROOMY,
     )(sent, near, weights)
     mid, query = lax.optimization_barrier((mid, query))
@@ -695,41 +633,21 @@
     (state,) = call(
         functools.partial(middle_kernel, run, len(mid)),
         [sds(*state_like)],
-        [
-            vmem(*q_like),
-            vmem(*state_like),
-            vmem((2 * chans, chans), BF16),
-            dma((3,)),
-            dma((tiles // 2,)),
-        ]
-        + key_scratch(len(mid)),
+        key_scratch(len(mid)),
         2_000_000_000,
-        "v" * len(mid) + "aaa",
+        "v" * len(mid) + "vvv",
+        "v",
         limit=ROOMY,
     )(*mid, query, state, weights)
     features_t, *ballots = call(
         functools.partial(second_kernel, run, cap, len(far), owners),
         [sds((chans, slots), F32)] + [sds((chans + 16, cap), BF16)] * owners,
-        [
-            vmem((4 * chans + hidden, chans), BF16),
-            vmem(*q_like),
-            vmem(*state_like),
-            vmem((chans, slots), BF16),
-            vmem((1, chans), F32),
-            vmem((chans, hidden), BF16),
-            vmem((16, codes), BF16),
-            dma((7,)),
-            vmem((chans, slots), F32),
-            vmem((owners, chans + 16, cap), BF16),
-            dma((owners + 1,)),
-        ]
+        [vmem((chans, slots), F32), dma]
         + key_scratch(len(far))
-        + [
-            vmem((chans, slots), BF16),
-            vmem((chans, slots), BF16),
-        ],
+        + [vmem(*q_like), vmem((chans, slots), BF16), vmem((chans, slots), BF16)],
         3_000_000_000,
-        "s" + "v" * len(far) + "a" * 7,
+        "s" + "v" * (len(far) + 7),
+        "a" + "v" * owners,
         limit=ROOMY,
     )(
         node_count,
@@ -738,7 +656,7 @@
         state,
         weights,
         first,
-        gain_three.reshape(1, chans),
+        gain,
         w_down.T,
         facts,
     )
@@ -746,11 +664,11 @@
     (sums_t,) = call(
         sums_kernel,
         [sds((chans, VOX_DEV), F32)],
-        [vmem((chans + 16, cap), BF16), dma],
+        [],
         200_000_000,
-        "a" + "v" * (owners - 1),
-        pltpu.VMEM,
-        ROOMY,
+        "v" * owners,
+        "v",
+        limit=ROOMY,
     )(*got)
     return (features_t.T, sums_t.T)
 

time: 51.7 us -> 46.2 us (0.89)
  Pallas kernels: 26.8 us -> 20.8 us
  waiting for transfers between devices: 4.57 us -> 5.89 us
  local copies, waits for them, and re-layouts: 4.16 us -> 3.53 us
    pallas_call x1, Pallas kernels: 3.75 us -> 2.01 us  [body(): call(functools.partial(middle_kernel, run, len(mid)), [sds(*state_like)],...]
    pallas_call x1, Pallas kernels: 5.36 us -> 3.83 us  [body(): call(functools.partial(near_kernel, run), [sds(*q_like), sds(*state_like)...]
    ppermute x10, waiting for transfers between devices: 4.57 us -> 5.89 us  [turned(): return lax.ppermute(x, axis, [(i, i ^ bit) for i in range(n)])]
    pallas_call x1, Pallas kernels: 6.29 us -> 5.25 us  [body(): call(functools.partial(second_kernel, run, cap, len(far), owners), [sds((...]
    pallas_call x1, Pallas kernels: 8 us -> 7.16 us  [body(): call(functools.partial(first_kernel, run), [sds((chans, slots), BF16), sd...]
    pallas_call x1, Pallas kernels: 2.12 us -> 1.48 us  [body(): call(functools.partial(tables_kernel, cap), [sds((4 * chans + hidden, cha...]
    unnamed x20, local copies, waits for them, and re-layouts: 4.16 us -> 3.53 us
  transfers between devices with their start and end apart: 10 -> 10, of which waited for: 3 -> 4; matrix products, arithmetic and copies ran while one was open for 0% -> 0% of each run, Pallas kernels for 22% -> 16%
where the time goes in v9:
time: 46.2 us; the launch traced here: 46 us
  Pallas kernels  20.8 us (45%)
  starting transfers between devices  14.4 us (31%)
  waiting for transfers between devices  5.89 us (13%)
  local copies, waits for them, and re-layouts  3.53 us (8%)
  between operations  1.37 us (3%)
    ppermute x10, starting transfers between devices, turned(): return lax.ppermute(x, axis, [(i, i ^ bit) for i in range(n)])  14.4 us
    pallas_call x1, Pallas kernels, body(): call(functools.partial(first_kernel, run), [sds((chans, slots), BF16), sd...  7.16 us
    ppermute x10, waiting for transfers between devices, turned(): return lax.ppermute(x, axis, [(i, i ^ bit) for i in range(n)])  5.89 us
    pallas_call x1, Pallas kernels, body(): call(functools.partial(second_kernel, run, cap, len(far), owners), [sds((...  5.25 us
    pallas_call x1, Pallas kernels, body(): call(functools.partial(near_kernel, run), [sds(*q_like), sds(*state_like)...  3.83 us
    unnamed x20, local copies, waits for them, and re-layouts  3.53 us
    pallas_call x1, Pallas kernels, body(): call(functools.partial(middle_kernel, run, len(mid)), [sds(*state_like)],...  2.01 us
    pallas_call x1, Pallas kernels, body(): call(functools.partial(tables_kernel, cap), [sds((4 * chans + hidden, cha...  1.48 us
  transfers between devices with their start and end apart: 10, of which 4 were waited for; matrix products, arithmetic and copies ran while one was open for 0% of the time, Pallas kernels for 16%

profile of v9, /device:TPU:0, one launch (start us, length us, event | category | flops | bytes accessed | tf_op | source)
XLA Modules:
  0.0 46.0 jit_solution(17945987594950157456)
XLA Ops:
  1.3 7.2 %shard_map.167 = (bf16[192,1024]{1,0:T(8,128)(2,1)}, bf16[192,1024]{1,0:T(8,128)(2,1)}) custom-call(s32[1]{0:T(128)S(6)} %copy.18.count_ref, bf16[192,1024]{1,0:T(8,128)(2,1)} %bitcast.16, s32[1,1024]{1,0:T(1,128)} %bitcast.17, f32[3,192]{1,0:T(4,128)} %pos_hbm.1, f32[1,192]{1,0:T(1,128)} %bitcast.18, f32[1,192]{1,0:T(1,128)} %bitcast.19, ...), custom_call_target="tpu_custom_call" | custom-call | flops 2000000000 | bytes 2097152 | tf_op jit(solution)/shard_map/pallas_call | solution.py:540
  8.4 0.5 %collective-permute-start.1 = (bf16[192,1024]{1,0:T(8,128)(2,1)}, bf16[192,1024]{1,0:T(8,128)(2,1)S(1)}, u32[]{:S(2)}, u32[]{:S(2)}) collective-permute-start(bf16[192,1024]{1,0:T(8,128)(2,1)} %get-tuple-element.20.own_ref), channel_id=1, source_target_pairs={{0,8},{8,0},{16,24},{24,16},{1,9},{9,1},{17,25},{25,17},{2,10},{10... | collective-permute-start | bytes 1179656 | tf_op jit(solution)/shard_map/ppermute | solution.py:505
  8.9 2.6 %collective-permute-start = (bf16[192,1024]{1,0:T(8,128)(2,1)}, bf16[192,1024]{1,0:T(8,128)(2,1)S(1)}, u32[]{:S(2)}, u32[]{:S(2)}) collective-permute-start(bf16[192,1024]{1,0:T(8,128)(2,1)} %get-tuple-element.20.own_ref), channel_id=1, source_target_pairs={{0,16},{8,24},{16,0},{24,8},{1,17},{9,25},{17,1},{25,9},{2,18},{10... | collective-permute-start | bytes 1179656 | tf_op jit(solution)/shard_map/ppermute | solution.py:505
  11.5 0.7 %copy-done.7 = s32[512]{0:T(512)S(1)} copy-done((s32[512]{0:T(512)S(1)}, s32[512]{0:T(512)}, u32[]{:S(2)}) %copy-start.7) | copy-done | bytes 2072
  12.2 0.0 copy-done.6
  12.2 0.0 copy-done.5
  12.2 0.0 copy-done.8
  12.3 1.0 %copy-done.1 = bf16[192,768]{1,0:T(8,128)(2,1)S(1)} copy-done((bf16[192,768]{1,0:T(8,128)(2,1)S(1)}, bf16[192,768]{1,0:T(8,128)(2,1)}, u32[]{:S(2)}) %copy-start.1) | copy-done | bytes 294936
  13.2 0.9 %copy-done.3 = bf16[192,576]{1,0:T(8,128)(2,1)S(1)} copy-done((bf16[192,576]{1,0:T(8,128)(2,1)S(1)}, bf16[192,576]{1,0:T(8,128)(2,1)}, u32[]{:S(2)}) %copy-start.3) | copy-done | bytes 221208
  14.2 0.9 %copy-done.4 = bf16[192,192]{1,0:T(8,128)(2,1)S(1)} copy-done((bf16[192,192]{1,0:T(8,128)(2,1)S(1)}, bf16[192,192]{1,0:T(8,128)(2,1)}, u32[]{:S(2)}) %copy-start.4) | copy-done | bytes 73752
  15.1 1.5 %shard_map.168 = (bf16[1536,192]{1,0:T(8,128)(2,1)S(1)}, bf16[16,1024]{1,0:T(8,128)(2,1)S(1)}, f32[192,128]{1,0:T(8,128)S(1)}) custom-call(bf16[192,576]{1,0:T(8,128)(2,1)S(1)} %copy-done.3, bf16[192,192]{1,0:T(8,128)(2,1)S(1)} %copy-done.4, bf16[192,768]{1,0:T(8,128)(2,1)S(1)} %copy-done.1, s32[1,512]{1,0:T(1,128)S(1)} %bitcast.12, s32[1,512]{1,0:T(1,128)S(1)} %bitcast.13, ...), custom_call_target="tpu_custom_call" | custom-call | flops 2000000000 | bytes 2097152 | tf_op jit(solution)/shard_map/pallas_call | solution.py:581
  16.6 0.0 collective-permute-done.1.near_ref
  16.6 3.8 %shard_map.169 = (f32[8,24,8,128]{3,2,1,0:T(8,128)S(1)}, f32[8,28,8,128]{3,2,1,0:T(8,128)S(1)}) custom-call(bf16[192,1024]{1,0:T(8,128)(2,1)S(1)} %copy-done, bf16[192,1024]{1,0:T(8,128)(2,1)S(1)} %collective-permute-done.1.near_ref, bf16[1536,192]{1,0:T(8,128)(2,1)S(1)} %get-tuple-element.21.weights_ref.refs_3_), custom_call_target="tpu_custom_call" | custom-call | flops 3000000000 | bytes 2097152 | tf_op jit(solution)/shard_map/pallas_call | solution.py:622
  20.4 1.0 %collective-permute-done.refs_0_ = bf16[192,1024]{1,0:T(8,128)(2,1)S(1)} collective-permute-done((bf16[192,1024]{1,0:T(8,128)(2,1)}, bf16[192,1024]{1,0:T(8,128)(2,1)S(1)}, u32[]{:S(2)}, u32[]{:S(2)}) %collective-permute-start) | collective-permute-done | bytes 393248 | tf_op jit(solution)/shard_map/ppermute | solution.py:505
  21.4 0.0 collective-permute-start.2
  21.5 2.0 %shard_map.170.refs_2_ = f32[8,28,8,128]{3,2,1,0:T(8,128)S(1)} custom-call(bf16[192,1024]{1,0:T(8,128)(2,1)S(1)} %collective-permute-done.refs_0_, f32[8,24,8,128]{3,2,1,0:T(8,128)S(1)} %get-tuple-element.24.refs_1_, f32[8,28,8,128]{3,2,1,0:T(8,128)S(1)} %get-tuple-element.25.refs_2_, bf16[1536,192]{1,0:T(8,128)(2,1)S(1)} %get-tuple-element.21.weights_ref.refs_3_), custom_call_target="tpu_custom_call" | custom-call | flops 2000000000 | bytes 2097152 | tf_op jit(solution)/shard_map/pallas_call | solution.py:633
  23.5 0.0 collective-permute-done.2.refs_0_
  23.5 5.3 %shard_map.171 = (f32[192,1024]{1,0:T(8,128)}, bf16[208,128]{1,0:T(8,128)(2,1)S(1)}, bf16[208,128]{1,0:T(8,128)(2,1)S(1)}, bf16[208,128]{1,0:T(8,128)(2,1)S(1)},...) custom-call(s32[1]{0:T(128)S(6)} %copy.18.count_ref, ...), custom_call_target="tpu_custom_call" | custom-call | flops 3000000000 | bytes 2097152 | tf_op jit(solution)/shard_map/pallas_call | solution.py:642
  28.8 1.9 %collective-permute-start.3 = (bf16[208,128]{1,0:T(8,128)(2,1)S(1)}, bf16[208,128]{1,0:T(8,128)(2,1)S(1)}, u32[]{:S(2)}, u32[]{:S(2)}) collective-permute-start(bf16[208,128]{1,0:T(8,128)(2,1)S(1)} %get-tuple-element.31), channel_id=1, source_target_pairs={{0,1},{1,0},{2,3},{3,2},{4,5},{5,4},{6,7},{7,6},{8,9},{9,8},{10,11... | collective-permute-start | bytes 159752 | tf_op jit(solution)/shard_map/ppermute | solution.py:505
  30.6 3.5 %collective-permute-start.4 = (bf16[208,128]{1,0:T(8,128)(2,1)S(1)}, bf16[208,128]{1,0:T(8,128)(2,1)S(1)}, u32[]{:S(2)}, u32[]{:S(2)}) collective-permute-start(bf16[208,128]{1,0:T(8,128)(2,1)S(1)} %get-tuple-element.32), channel_id=1, source_target_pairs={{0,7},{1,6},{2,5},{3,4},{4,3},{5,2},{6,1},{7,0},{8,15},{9,14},{10,... | collective-permute-start | bytes 159752 | tf_op jit(solution)/shard_map/ppermute | solution.py:505
  34.1 0.1 collective-permute-start.5
  34.2 1.9 %collective-permute-start.6 = (bf16[208,128]{1,0:T(8,128)(2,1)S(1)}, bf16[208,128]{1,0:T(8,128)(2,1)S(1)}, u32[]{:S(2)}, u32[]{:S(2)}) collective-permute-start(bf16[208,128]{1,0:T(8,128)(2,1)S(1)} %get-tuple-element.34), channel_id=1, source_target_pairs={{0,5},{1,4},{2,7},{3,6},{4,1},{5,0},{6,3},{7,2},{8,13},{9,12},{10,... | collective-permute-start | bytes 159752 | tf_op jit(solution)/shard_map/ppermute | solution.py:505
  36.1 2.2 %collective-permute-start.7 = (bf16[208,128]{1,0:T(8,128)(2,1)S(1)}, bf16[208,128]{1,0:T(8,128)(2,1)S(1)}, u32[]{:S(2)}, u32[]{:S(2)}) collective-permute-start(bf16[208,128]{1,0:T(8,128)(2,1)S(1)} %get-tuple-element.35), channel_id=1, source_target_pairs={{0,4},{1,5},{2,6},{3,7},{4,0},{5,1},{6,2},{7,3},{8,12},{9,13},{10,... | collective-permute-start | bytes 159752 | tf_op jit(solution)/shard_map/ppermute | solution.py:505
  38.3 0.0 collective-permute-done.3.refs_1_
  38.3 1.2 %collective-permute-start.8 = (bf16[208,128]{1,0:T(8,128)(2,1)S(1)}, bf16[208,128]{1,0:T(8,128)(2,1)S(1)}, u32[]{:S(2)}, u32[]{:S(2)}) collective-permute-start(bf16[208,128]{1,0:T(8,128)(2,1)S(1)} %get-tuple-element.36), channel_id=1, source_target_pairs={{0,3},{1,2},{2,1},{3,0},{4,7},{5,6},{6,5},{7,4},{8,11},{9,10},{10,... | collective-permute-start | bytes 159752 | tf_op jit(solution)/shard_map/ppermute | solution.py:505
  39.5 0.0 collective-permute-done.4.refs_2_
  39.5 0.6 %collective-permute-start.9 = (bf16[208,128]{1,0:T(8,128)(2,1)S(1)}, bf16[208,128]{1,0:T(8,128)(2,1)S(1)}, u32[]{:S(2)}, u32[]{:S(2)}) collective-permute-start(bf16[208,128]{1,0:T(8,128)(2,1)S(1)} %get-tuple-element.37), channel_id=1, source_target_pairs={{0,2},{1,3},{2,0},{3,1},{4,6},{5,7},{6,4},{7,5},{8,10},{9,11},{10,... | collective-permute-start | bytes 159752 | tf_op jit(solution)/shard_map/ppermute | solution.py:505
  40.1 0.2 collective-permute-done.5.refs_3_
  40.3 3.9 %collective-permute-done.6.refs_4_ = bf16[208,128]{1,0:T(8,128)(2,1)S(1)} collective-permute-done((bf16[208,128]{1,0:T(8,128)(2,1)S(1)}, bf16[208,128]{1,0:T(8,128)(2,1)S(1)}, u32[]{:S(2)}, u32[]{:S(2)}) %collective-permute-start.6) | collective-permute-done | bytes 53280 | tf_op jit(solution)/shard_map/ppermute | solution.py:505
  44.2 0.7 %collective-permute-done.8.refs_6_ = bf16[208,128]{1,0:T(8,128)(2,1)S(1)} collective-permute-done((bf16[208,128]{1,0:T(8,128)(2,1)S(1)}, bf16[208,128]{1,0:T(8,128)(2,1)S(1)}, u32[]{:S(2)}, u32[]{:S(2)}) %collective-permute-start.8) | collective-permute-done | bytes 53280 | tf_op jit(solution)/shard_map/ppermute | solution.py:505
  44.9 0.0 collective-permute-done.9.refs_7_
  44.9 1.0 %shard_map.172 = f32[192,256]{1,0:T(8,128)} custom-call(bf16[208,128]{1,0:T(8,128)(2,1)S(1)} %get-tuple-element.30.refs_0_, bf16[208,128]{1,0:T(8,128)(2,1)S(1)} %collective-permute-done.3.refs_1_, bf16[208,128]{1,0:T(8,128)(2,1)S(1)} %collective-permute-done.4.refs_2_, bf16[208,128]{1,0:T(8,128)(2,1)S(1)} %collective-permute-done.5.refs_3_, ...), custom_call_target="tpu_custom_call" | custom-call | flops 200000000 | bytes 2097152 | tf_op jit(solution)/shard_map/pallas_call | solution.py:664
  (14 shorter events, 0.0 us)
Async XLA Ops:
  8.4 8.1 %collective-permute-start.1 = (bf16[192,1024]{1,0:T(8,128)(2,1)}, bf16[192,1024]{1,0:T(8,128)(2,1)S(1)}, u32[]{:S(2)}, u32[]{:S(2)}) collective-permute-start(bf16[192,1024]{1,0:T(8,128)(2,1)} %get-tuple-element.20.own_ref), channel_id=1, source_target_pairs={{0,8},{8,0},{16,24},{24,16},{1,9},{9,1},{17,25},{25,17},{2,10},{10... | collective-permute-start | bytes 1179656 | tf_op jit(solution)/shard_map/ppermute | solution.py:505
  8.9 12.5 %collective-permute-start = (bf16[192,1024]{1,0:T(8,128)(2,1)}, bf16[192,1024]{1,0:T(8,128)(2,1)S(1)}, u32[]{:S(2)}, u32[]{:S(2)}) collective-permute-start(bf16[192,1024]{1,0:T(8,128)(2,1)} %get-tuple-element.20.own_ref), channel_id=1, source_target_pairs={{0,16},{8,24},{16,0},{24,8},{1,17},{9,25},{17,1},{25,9},{2,18},{10... | collective-permute-start | bytes 1179656 | tf_op jit(solution)/shard_map/ppermute | solution.py:505
  11.5 0.7 %copy-start.7 = (s32[512]{0:T(512)S(1)}, s32[512]{0:T(512)}, u32[]{:S(2)}) copy-start(s32[512]{0:T(512)} %param.31) | copy-start | bytes 6148
  11.5 0.7 %copy-start.6 = (s32[512,1]{0,1:T(1,128)S(1)}, s32[512,1]{0,1:T(1,128)}, u32[]{:S(2)}) copy-start(s32[512,1]{0,1:T(1,128)} %param.30) | copy-start | bytes 6148
  11.5 0.7 %copy-start.5 = (s32[512]{0:T(512)S(1)}, s32[512]{0:T(512)}, u32[]{:S(2)}) copy-start(s32[512]{0:T(512)} %param.29) | copy-start | bytes 6148
  11.5 0.7 %copy-start.8 = (f32[192]{0:T(256)S(1)}, f32[192]{0:T(256)}, u32[]{:S(2)}) copy-start(f32[192]{0:T(256)} %param.26) | copy-start | bytes 2308
  12.3 1.0 %copy-start.1 = (bf16[192,768]{1,0:T(8,128)(2,1)S(1)}, bf16[192,768]{1,0:T(8,128)(2,1)}, u32[]{:S(2)}) copy-start(bf16[192,768]{1,0:T(8,128)(2,1)} %up_hbm.1) | copy-start | bytes 884740
  13.2 0.9 %copy-start.3 = (bf16[192,576]{1,0:T(8,128)(2,1)S(1)}, bf16[192,576]{1,0:T(8,128)(2,1)}, u32[]{:S(2)}) copy-start(bf16[192,576]{1,0:T(8,128)(2,1)} %qkv_hbm.3) | copy-start | bytes 663556
  14.2 0.9 %copy-start.4 = (bf16[192,192]{1,0:T(8,128)(2,1)S(1)}, bf16[192,192]{1,0:T(8,128)(2,1)}, u32[]{:S(2)}) copy-start(bf16[192,192]{1,0:T(8,128)(2,1)} %out_hbm.3) | copy-start | bytes 221188
  15.1 1.5 %copy-start = (bf16[192,1024]{1,0:T(8,128)(2,1)S(1)}, bf16[192,1024]{1,0:T(8,128)(2,1)}, u32[]{:S(2)}) copy-start(bf16[192,1024]{1,0:T(8,128)(2,1)} %get-tuple-element.20.own_ref) | copy-start | bytes 1179652
  21.4 2.0 %collective-permute-start.2 = (bf16[192,1024]{1,0:T(8,128)(2,1)S(1)}, bf16[192,1024]{1,0:T(8,128)(2,1)S(1)}, u32[]{:S(2)}, u32[]{:S(2)}) collective-permute-start(bf16[192,1024]{1,0:T(8,128)(2,1)S(1)} %collective-permute-done.refs_0_), channel_id=1, source_target_pairs={{0,8},{8,0},{16,24},{24,16},{1,9},{9,1},{17,25},{25,17},{2,10},{10... | collective-permute-start | bytes 1179656 | tf_op jit(solution)/shard_map/ppermute | solution.py:505
  21.5 2.0 %copy-start.2 = (bf16[768,192]{0,1:T(8,128)(2,1)S(1)}, bf16[768,192]{0,1:T(8,128)(2,1)}, u32[]{:S(2)}) copy-start(bf16[768,192]{0,1:T(8,128)(2,1)} %param.28) | copy-start | bytes 884740
  21.5 2.0 %copy-start.9 = (bf16[192,1024]{1,0:T(8,128)(2,1)S(1)}, bf16[192,1024]{1,0:T(8,128)(2,1)}, u32[]{:S(2)}) copy-start(bf16[192,1024]{1,0:T(8,128)(2,1)} %get-tuple-element.26.refs_4_) | copy-start | bytes 1179652
  28.8 9.5 %collective-permute-start.3 = (bf16[208,128]{1,0:T(8,128)(2,1)S(1)}, bf16[208,128]{1,0:T(8,128)(2,1)S(1)}, u32[]{:S(2)}, u32[]{:S(2)}) collective-permute-start(bf16[208,128]{1,0:T(8,128)(2,1)S(1)} %get-tuple-element.31), channel_id=1, source_target_pairs={{0,1},{1,0},{2,3},{3,2},{4,5},{5,4},{6,7},{7,6},{8,9},{9,8},{10,11... | collective-permute-start | bytes 159752 | tf_op jit(solution)/shard_map/ppermute | solution.py:505
  30.6 8.9 %collective-permute-start.4 = (bf16[208,128]{1,0:T(8,128)(2,1)S(1)}, bf16[208,128]{1,0:T(8,128)(2,1)S(1)}, u32[]{:S(2)}, u32[]{:S(2)}) collective-permute-start(bf16[208,128]{1,0:T(8,128)(2,1)S(1)} %get-tuple-element.32), channel_id=1, source_target_pairs={{0,7},{1,6},{2,5},{3,4},{4,3},{5,2},{6,1},{7,0},{8,15},{9,14},{10,... | collective-permute-start | bytes 159752 | tf_op jit(solution)/shard_map/ppermute | solution.py:505
  34.1 6.2 %collective-permute-start.5 = (bf16[208,128]{1,0:T(8,128)(2,1)S(1)}, bf16[208,128]{1,0:T(8,128)(2,1)S(1)}, u32[]{:S(2)}, u32[]{:S(2)}) collective-permute-start(bf16[208,128]{1,0:T(8,128)(2,1)S(1)} %get-tuple-element.33), channel_id=1, source_target_pairs={{0,6},{1,7},{2,4},{3,5},{4,2},{5,3},{6,0},{7,1},{8,14},{9,15},{10,... | collective-permute-start | bytes 159752 | tf_op jit(solution)/shard_map/ppermute | solution.py:505
  34.2 9.9 %collective-permute-start.6 = (bf16[208,128]{1,0:T(8,128)(2,1)S(1)}, bf16[208,128]{1,0:T(8,128)(2,1)S(1)}, u32[]{:S(2)}, u32[]{:S(2)}) collective-permute-start(bf16[208,128]{1,0:T(8,128)(2,1)S(1)} %get-tuple-element.34), channel_id=1, source_target_pairs={{0,5},{1,4},{2,7},{3,6},{4,1},{5,0},{6,3},{7,2},{8,13},{9,12},{10,... | collective-permute-start | bytes 159752 | tf_op jit(solution)/shard_map/ppermute | solution.py:505
  36.1 8.1 %collective-permute-start.7 = (bf16[208,128]{1,0:T(8,128)(2,1)S(1)}, bf16[208,128]{1,0:T(8,128)(2,1)S(1)}, u32[]{:S(2)}, u32[]{:S(2)}) collective-permute-start(bf16[208,128]{1,0:T(8,128)(2,1)S(1)} %get-tuple-element.35), channel_id=1, source_target_pairs={{0,4},{1,5},{2,6},{3,7},{4,0},{5,1},{6,2},{7,3},{8,12},{9,13},{10,... | collective-permute-start | bytes 159752 | tf_op jit(solution)/shard_map/ppermute | solution.py:505
  38.3 6.6 %collective-permute-start.8 = (bf16[208,128]{1,0:T(8,128)(2,1)S(1)}, bf16[208,128]{1,0:T(8,128)(2,1)S(1)}, u32[]{:S(2)}, u32[]{:S(2)}) collective-permute-start(bf16[208,128]{1,0:T(8,128)(2,1)S(1)} %get-tuple-element.36), channel_id=1, source_target_pairs={{0,3},{1,2},{2,1},{3,0},{4,7},{5,6},{6,5},{7,4},{8,11},{9,10},{10,... | collective-permute-start | bytes 159752 | tf_op jit(solution)/shard_map/ppermute | solution.py:505
  39.5 5.4 %collective-permute-start.9 = (bf16[208,128]{1,0:T(8,128)(2,1)S(1)}, bf16[208,128]{1,0:T(8,128)(2,1)S(1)}, u32[]{:S(2)}, u32[]{:S(2)}) collective-permute-start(bf16[208,128]{1,0:T(8,128)(2,1)S(1)} %get-tuple-element.37), channel_id=1, source_target_pairs={{0,2},{1,3},{2,0},{3,1},{4,6},{5,7},{6,4},{7,5},{8,10},{9,11},{10,... | collective-permute-start | bytes 159752 | tf_op jit(solution)/shard_map/ppermute | solution.py:505

commit v10 on v9

--- a/solution.py
+++ b/solution.py
@@ -14,6 +14,7 @@
 LANES = 128
 FLAG = 16384.0
 VMEM = 64 * 1024 * 1024 - 65536
+TIGHT = VMEM - 2 * 1024 * 1024
 ROOMY = 24 * 1024 * 1024
 F32 = jnp.float32
 BF16 = jnp.bfloat16
@@ -142,7 +143,7 @@
     size = chans // HEADS
     per = LANES // WIN
     count = count_ref[0]
-    wait_all(loads[:5])
+    wait_all(loads)
     cols = jnp.concatenate(
         [pos_ref[...], gain_one_ref[...], gain_two_ref[...], jnp.zeros((3, chans), F32)], 0
     ).T
@@ -162,7 +163,6 @@
         start = (nodes_ref[:, at].astype(F32) + start).astype(BF16)
         nodes_ref[:, at] = start
         n_s[:, at] = norm_t(start.astype(F32), cols[:, 3:4]).astype(BF16)
-    wait_all(loads[5:])
     qkv_t = transposed(qkv_ref[...])
     out_t = transposed(out_ref[...])
     qkv_s[...] = dot(qkv_t, n_s[...]).astype(BF16)
@@ -475,16 +475,23 @@
     keep.wait()
 
 
-def sums_kernel(*refs):
-    got, out_ref = refs[:-1], refs[-1]
-    chans, voxels = out_ref.shape
-    cap = got[0].shape[1]
-    total = jnp.zeros(out_ref.shape, F32)
-    for ref in got:
+def summed(blocks, chans, voxels):
+    cap = blocks[0].shape[1]
+    total = jnp.zeros((chans, voxels), F32)
+    for ref in blocks:
         label = ref[chans:, :].astype(F32)[0:1]
         hot = (label == iota((voxels, cap), 0).astype(F32)).astype(BF16)
         total = total + dot_t(ref[:chans, :], hot)
-    out_ref[...] = total
+    return total
+
+
+def proxy_kernel(*refs):
+    refs[-1][...] = summed(refs[:-1], *refs[-1].shape).astype(BF16)
+
+
+def sums_kernel(*refs):
+    got, other_ref, out_ref = refs[:-2], refs[-2], refs[-1]
+    out_ref[...] = summed(got, *out_ref.shape) + other_ref[...].astype(F32)
 
 
 def call(kernel, outs, scratch, flops, spaces, out_spaces, limit=VMEM):
@@ -598,7 +605,7 @@
         2_000_000_000,
         "aaaaaaa",
         "vvv",
-        limit=ROOMY,
+        limit=TIGHT,
     )(
         qkv_two,
         out_two,
@@ -660,16 +667,27 @@
         w_down.T,
         facts,
     )
-    got = [ballots[0]] + [turned(ballots[k], "tile", k) for k in [1] + list(range(owners - 1, 1, -1))]
+    half = owners // 2
+    passed = [ballots[half]] + [turned(ballots[half + k], "tile", k) for k in range(1, half)]
+    direct = [ballots[0]] + [turned(ballots[k], "tile", k) for k in range(1, half)]
+    (partial,) = call(
+        proxy_kernel,
+        [sds((chans, VOX_DEV), BF16)],
+        [],
+        200_000_000,
+        "v" * half,
+        "v",
+        limit=ROOMY,
+    )(*passed)
     (sums_t,) = call(
         sums_kernel,
         [sds((chans, VOX_DEV), F32)],
         [],
         200_000_000,
-        "v" * owners,
+        "v" * (half + 1),
         "v",
         limit=ROOMY,
-    )(*got)
+    )(*direct, turned(partial, "tile", half))
     return (features_t.T, sums_t.T)
 
 

time: 46.2 us -> 48 us (1.039)
  waiting for transfers between devices: 5.89 us -> 9.91 us
  local copies, waits for them, and re-layouts: 3.53 us -> 1.15 us
  Pallas kernels: 20.8 us -> 22.5 us
  starting transfers between devices: 14.4 us -> 12.8 us
    ppermute x10, waiting for transfers between devices: 5.89 us -> 9.91 us  [turned(): return lax.ppermute(x, axis, [(i, i ^ bit) for i in range(n)])]
    unnamed x20 -> x14, local copies, waits for them, and re-layouts: 3.53 us -> 1.15 us
    ppermute x10, starting transfers between devices: 14.4 us -> 12.8 us  [turned(): return lax.ppermute(x, axis, [(i, i ^ bit) for i in range(n)])]
    pallas_call x1, Pallas kernels: 1.48 us -> 2.98 us  [body(): call(functools.partial(tables_kernel, cap), [sds((4 * chans + hidden, cha...]
    pallas_call x1 -> x2, Pallas kernels: 1.05 us -> 1.24 us  [the longest x1 0.96 us: body(): call(sums_kernel, [sds((chans, VOX_DEV), F32)], [], 200000000, 'v' * (hal...]
  transfers between devices with their start and end apart: 10 -> 10, of which waited for: 4 -> 7; matrix products, arithmetic and copies ran while one was open for 0% -> 0% of each run, Pallas kernels for 16% -> 18%
where the time goes in v10:
time: 48 us; the launch traced here: 47.7 us
  Pallas kernels  22.5 us (47%)
  starting transfers between devices  12.8 us (27%)
  waiting for transfers between devices  9.91 us (21%)
  between operations  1.42 us (3%)
  local copies, waits for them, and re-layouts  1.15 us (2%)
    ppermute x10, starting transfers between devices, turned(): return lax.ppermute(x, axis, [(i, i ^ bit) for i in range(n)])  12.8 us
    ppermute x10, waiting for transfers between devices, turned(): return lax.ppermute(x, axis, [(i, i ^ bit) for i in range(n)])  9.91 us
    pallas_call x1, Pallas kernels, body(): call(functools.partial(first_kernel, run), [sds((chans, slots), BF16), sd...  7.18 us
    pallas_call x1, Pallas kernels, body(): call(functools.partial(second_kernel, run, cap, len(far), owners), [sds((...  5.25 us
    pallas_call x1, Pallas kernels, body(): call(functools.partial(near_kernel, run), [sds(*q_like), sds(*state_like)...  3.82 us
    pallas_call x1, Pallas kernels, body(): call(functools.partial(tables_kernel, cap), [sds((4 * chans + hidden, cha...  2.98 us
    pallas_call x1, Pallas kernels, body(): call(functools.partial(middle_kernel, run, len(mid)), [sds(*state_like)],...  2.01 us
    unnamed x14, local copies, waits for them, and re-layouts  1.15 us
  transfers between devices with their start and end apart: 10, of which 7 were waited for; matrix products, arithmetic and copies ran while one was open for 0% of the time, Pallas kernels for 18%

profile of v10, /device:TPU:0, one launch (start us, length us, event | category | flops | bytes accessed | tf_op | source)
XLA Modules:
  0.0 47.7 jit_solution(15210170953479544846)
XLA Ops:
  1.3 7.2 %shard_map.167 = (bf16[192,1024]{1,0:T(8,128)(2,1)}, bf16[192,1024]{1,0:T(8,128)(2,1)}) custom-call(s32[1]{0:T(128)S(6)} %copy.18.count_ref, bf16[192,1024]{1,0:T(8,128)(2,1)} %bitcast.12, s32[1,1024]{1,0:T(1,128)} %bitcast.13, f32[3,192]{1,0:T(4,128)} %pos_hbm.1, f32[1,192]{1,0:T(1,128)} %bitcast.17, f32[1,192]{1,0:T(1,128)} %bitcast.18, ...), custom_call_target="tpu_custom_call" | custom-call | flops 2000000000 | bytes 2097152 | tf_op jit(solution)/shard_map/pallas_call | solution.py:547
  8.5 0.5 %collective-permute-start.1 = (bf16[192,1024]{1,0:T(8,128)(2,1)}, bf16[192,1024]{1,0:T(8,128)(2,1)S(1)}, u32[]{:S(2)}, u32[]{:S(2)}) collective-permute-start(bf16[192,1024]{1,0:T(8,128)(2,1)} %get-tuple-element.20.own_ref), channel_id=1, source_target_pairs={{0,8},{8,0},{16,24},{24,16},{1,9},{9,1},{17,25},{25,17},{2,10},{10... | collective-permute-start | bytes 1179656 | tf_op jit(solution)/shard_map/ppermute | solution.py:512
  9.0 2.6 %collective-permute-start = (bf16[192,1024]{1,0:T(8,128)(2,1)}, bf16[192,1024]{1,0:T(8,128)(2,1)S(1)}, u32[]{:S(2)}, u32[]{:S(2)}) collective-permute-start(bf16[192,1024]{1,0:T(8,128)(2,1)} %get-tuple-element.20.own_ref), channel_id=1, source_target_pairs={{0,16},{8,24},{16,0},{24,8},{1,17},{9,25},{17,1},{25,9},{2,18},{10... | collective-permute-start | bytes 1179656 | tf_op jit(solution)/shard_map/ppermute | solution.py:512
  11.5 3.0 %shard_map.168 = (bf16[1536,192]{1,0:T(8,128)(2,1)}, bf16[16,1024]{1,0:T(8,128)(2,1)}, f32[192,128]{1,0:T(8,128)}) custom-call(bf16[192,576]{1,0:T(8,128)(2,1)} %qkv_hbm.3, bf16[192,192]{1,0:T(8,128)(2,1)} %out_hbm.3, bf16[192,768]{1,0:T(8,128)(2,1)} %up_hbm.1, s32[1,512]{1,0:T(1,128)} %bitcast.14, s32[1,512]{1,0:T(1,128)} %bitcast.15, s32[1,512]{1,0:T(1,128)} %bitcast.16, ...), custom_call_target="tpu_custom_call" | custom-call | flops 2000000000 | bytes 2097152 | tf_op jit(solution)/shard_map/pallas_call | solution.py:588
  14.5 0.0 collective-permute-done.1.near_ref
  14.5 0.0 copy-done
  14.5 0.0 copy-start.2
  14.6 1.1 %copy-done.2 = bf16[1536,192]{1,0:T(8,128)(2,1)S(1)} copy-done((bf16[1536,192]{1,0:T(8,128)(2,1)S(1)}, bf16[1536,192]{1,0:T(8,128)(2,1)}, u32[]{:S(2)}) %copy-start.2) | copy-done | bytes 589848
  15.7 3.8 %shard_map.169 = (f32[8,24,8,128]{3,2,1,0:T(8,128)S(1)}, f32[8,28,8,128]{3,2,1,0:T(8,128)S(1)}) custom-call(bf16[192,1024]{1,0:T(8,128)(2,1)S(1)} %copy-done, bf16[192,1024]{1,0:T(8,128)(2,1)S(1)} %collective-permute-done.1.near_ref, bf16[1536,192]{1,0:T(8,128)(2,1)S(1)} %copy-done.2), custom_call_target="tpu_custom_call" | custom-call | flops 3000000000 | bytes 2097152 | tf_op jit(solution)/shard_map/pallas_call | solution.py:629
  19.5 1.9 %collective-permute-done.refs_0_ = bf16[192,1024]{1,0:T(8,128)(2,1)S(1)} collective-permute-done((bf16[192,1024]{1,0:T(8,128)(2,1)}, bf16[192,1024]{1,0:T(8,128)(2,1)S(1)}, u32[]{:S(2)}, u32[]{:S(2)}) %collective-permute-start) | collective-permute-done | bytes 393248 | tf_op jit(solution)/shard_map/ppermute | solution.py:512
  21.4 0.0 collective-permute-start.2
  21.5 0.0 copy-start.5
  21.5 2.0 %shard_map.170.refs_2_ = f32[8,28,8,128]{3,2,1,0:T(8,128)S(1)} custom-call(bf16[192,1024]{1,0:T(8,128)(2,1)S(1)} %collective-permute-done.refs_0_, f32[8,24,8,128]{3,2,1,0:T(8,128)S(1)} %get-tuple-element.24.refs_1_, f32[8,28,8,128]{3,2,1,0:T(8,128)S(1)} %get-tuple-element.25.refs_2_, bf16[1536,192]{1,0:T(8,128)(2,1)S(1)} %copy-done.2), custom_call_target="tpu_custom_call" | custom-call | flops 2000000000 | bytes 2097152 | tf_op jit(solution)/shard_map/pallas_call | solution.py:640
  23.5 0.0 collective-permute-done.2.refs_0_
  23.5 0.0 copy-done.1
  23.6 5.3 %shard_map.171 = (f32[192,1024]{1,0:T(8,128)}, bf16[208,128]{1,0:T(8,128)(2,1)S(1)}, bf16[208,128]{1,0:T(8,128)(2,1)S(1)}, bf16[208,128]{1,0:T(8,128)(2,1)S(1)},...) custom-call(s32[1]{0:T(128)S(6)} %copy.18.count_ref, ...), custom_call_target="tpu_custom_call" | custom-call | flops 3000000000 | bytes 2097152 | tf_op jit(solution)/shard_map/pallas_call | solution.py:649
  28.8 1.9 %collective-permute-start.6 = (bf16[208,128]{1,0:T(8,128)(2,1)S(1)}, bf16[208,128]{1,0:T(8,128)(2,1)S(1)}, u32[]{:S(2)}, u32[]{:S(2)}) collective-permute-start(bf16[208,128]{1,0:T(8,128)(2,1)S(1)} %get-tuple-element.35), channel_id=1, source_target_pairs={{0,1},{1,0},{2,3},{3,2},{4,5},{5,4},{6,7},{7,6},{8,9},{9,8},{10,11... | collective-permute-start | bytes 159752 | tf_op jit(solution)/shard_map/ppermute | solution.py:512
  30.7 1.6 %collective-permute-start.7 = (bf16[208,128]{1,0:T(8,128)(2,1)S(1)}, bf16[208,128]{1,0:T(8,128)(2,1)S(1)}, u32[]{:S(2)}, u32[]{:S(2)}) collective-permute-start(bf16[208,128]{1,0:T(8,128)(2,1)S(1)} %get-tuple-element.36), channel_id=1, source_target_pairs={{0,2},{1,3},{2,0},{3,1},{4,6},{5,7},{6,4},{7,5},{8,10},{9,11},{10,... | collective-permute-start | bytes 159752 | tf_op jit(solution)/shard_map/ppermute | solution.py:512
  32.3 0.1 collective-permute-start.8
  32.4 0.8 %collective-permute-done.6.refs_1_ = bf16[208,128]{1,0:T(8,128)(2,1)S(1)} collective-permute-done((bf16[208,128]{1,0:T(8,128)(2,1)S(1)}, bf16[208,128]{1,0:T(8,128)(2,1)S(1)}, u32[]{:S(2)}, u32[]{:S(2)}) %collective-permute-start.6) | collective-permute-done | bytes 53280 | tf_op jit(solution)/shard_map/ppermute | solution.py:512
  33.2 1.8 %collective-permute-done.7.refs_2_ = bf16[208,128]{1,0:T(8,128)(2,1)S(1)} collective-permute-done((bf16[208,128]{1,0:T(8,128)(2,1)S(1)}, bf16[208,128]{1,0:T(8,128)(2,1)S(1)}, u32[]{:S(2)}, u32[]{:S(2)}) %collective-permute-start.7) | collective-permute-done | bytes 53280 | tf_op jit(solution)/shard_map/ppermute | solution.py:512
  35.0 2.3 %collective-permute-done.8.refs_3_ = bf16[208,128]{1,0:T(8,128)(2,1)S(1)} collective-permute-done((bf16[208,128]{1,0:T(8,128)(2,1)S(1)}, bf16[208,128]{1,0:T(8,128)(2,1)S(1)}, u32[]{:S(2)}, u32[]{:S(2)}) %collective-permute-start.8) | collective-permute-done | bytes 53280 | tf_op jit(solution)/shard_map/ppermute | solution.py:512
  37.3 0.3 shard_map.172
  37.6 2.7 %collective-permute-start.9 = (bf16[192,256]{1,0:T(8,128)(2,1)S(1)}, bf16[192,256]{1,0:T(8,128)(2,1)S(1)}, u32[]{:S(2)}, u32[]{:S(2)}) collective-permute-start(bf16[192,256]{1,0:T(8,128)(2,1)S(1)} %shard_map.172), channel_id=1, source_target_pairs={{0,4},{1,5},{2,6},{3,7},{4,0},{5,1},{6,2},{7,3},{8,12},{9,13},{10,... | collective-permute-start | bytes 294920 | tf_op jit(solution)/shard_map/ppermute | solution.py:512
  40.2 0.5 %collective-permute-start.3 = (bf16[208,128]{1,0:T(8,128)(2,1)S(1)}, bf16[208,128]{1,0:T(8,128)(2,1)S(1)}, u32[]{:S(2)}, u32[]{:S(2)}) collective-permute-start(bf16[208,128]{1,0:T(8,128)(2,1)S(1)} %get-tuple-element.31), channel_id=1, source_target_pairs={{0,1},{1,0},{2,3},{3,2},{4,5},{5,4},{6,7},{7,6},{8,9},{9,8},{10,11... | collective-permute-start | bytes 159752 | tf_op jit(solution)/shard_map/ppermute | solution.py:512
  40.7 1.0 %collective-permute-start.4 = (bf16[208,128]{1,0:T(8,128)(2,1)S(1)}, bf16[208,128]{1,0:T(8,128)(2,1)S(1)}, u32[]{:S(2)}, u32[]{:S(2)}) collective-permute-start(bf16[208,128]{1,0:T(8,128)(2,1)S(1)} %get-tuple-element.32), channel_id=1, source_target_pairs={{0,2},{1,3},{2,0},{3,1},{4,6},{5,7},{6,4},{7,5},{8,10},{9,11},{10,... | collective-permute-start | bytes 159752 | tf_op jit(solution)/shard_map/ppermute | solution.py:512
  41.7 2.0 %collective-permute-start.5 = (bf16[208,128]{1,0:T(8,128)(2,1)S(1)}, bf16[208,128]{1,0:T(8,128)(2,1)S(1)}, u32[]{:S(2)}, u32[]{:S(2)}) collective-permute-start(bf16[208,128]{1,0:T(8,128)(2,1)S(1)} %get-tuple-element.33), channel_id=1, source_target_pairs={{0,3},{1,2},{2,1},{3,0},{4,7},{5,6},{6,5},{7,4},{8,11},{9,10},{10,... | collective-permute-start | bytes 159752 | tf_op jit(solution)/shard_map/ppermute | solution.py:512
  43.7 1.1 %collective-permute-done.3.refs_1_ = bf16[208,128]{1,0:T(8,128)(2,1)S(1)} collective-permute-done((bf16[208,128]{1,0:T(8,128)(2,1)S(1)}, bf16[208,128]{1,0:T(8,128)(2,1)S(1)}, u32[]{:S(2)}, u32[]{:S(2)}) %collective-permute-start.3) | collective-permute-done | bytes 53280 | tf_op jit(solution)/shard_map/ppermute | solution.py:512
  44.8 0.1 collective-permute-done.4.refs_2_
  45.0 1.8 %collective-permute-done.5.refs_3_ = bf16[208,128]{1,0:T(8,128)(2,1)S(1)} collective-permute-done((bf16[208,128]{1,0:T(8,128)(2,1)S(1)}, bf16[208,128]{1,0:T(8,128)(2,1)S(1)}, u32[]{:S(2)}, u32[]{:S(2)}) %collective-permute-start.5) | collective-permute-done | bytes 53280 | tf_op jit(solution)/shard_map/ppermute | solution.py:512
  46.8 0.0 collective-permute-done.9.refs_4_
  46.8 1.0 %shard_map.173 = f32[192,256]{1,0:T(8,128)} custom-call(bf16[208,128]{1,0:T(8,128)(2,1)S(1)} %get-tuple-element.30.refs_0_, bf16[208,128]{1,0:T(8,128)(2,1)S(1)} %collective-permute-done.3.refs_1_, bf16[208,128]{1,0:T(8,128)(2,1)S(1)} %collective-permute-done.4.refs_2_, bf16[208,128]{1,0:T(8,128)(2,1)S(1)} %collective-permute-done.5.refs_3_, ...), custom_call_target="tpu_custom_call" | custom-call | flops 200000000 | bytes 2097152 | tf_op jit(solution)/shard_map/pallas_call | solution.py:682
  (9 shorter events, 0.0 us)
Async XLA Ops:
  8.5 6.1 %collective-permute-start.1 = (bf16[192,1024]{1,0:T(8,128)(2,1)}, bf16[192,1024]{1,0:T(8,128)(2,1)S(1)}, u32[]{:S(2)}, u32[]{:S(2)}) collective-permute-start(bf16[192,1024]{1,0:T(8,128)(2,1)} %get-tuple-element.20.own_ref), channel_id=1, source_target_pairs={{0,8},{8,0},{16,24},{24,16},{1,9},{9,1},{17,25},{25,17},{2,10},{10... | collective-permute-start | bytes 1179656 | tf_op jit(solution)/shard_map/ppermute | solution.py:512
  9.0 12.5 %collective-permute-start = (bf16[192,1024]{1,0:T(8,128)(2,1)}, bf16[192,1024]{1,0:T(8,128)(2,1)S(1)}, u32[]{:S(2)}, u32[]{:S(2)}) collective-permute-start(bf16[192,1024]{1,0:T(8,128)(2,1)} %get-tuple-element.20.own_ref), channel_id=1, source_target_pairs={{0,16},{8,24},{16,0},{24,8},{1,17},{9,25},{17,1},{25,9},{2,18},{10... | collective-permute-start | bytes 1179656 | tf_op jit(solution)/shard_map/ppermute | solution.py:512
  11.5 3.0 %copy-start = (bf16[192,1024]{1,0:T(8,128)(2,1)S(1)}, bf16[192,1024]{1,0:T(8,128)(2,1)}, u32[]{:S(2)}) copy-start(bf16[192,1024]{1,0:T(8,128)(2,1)} %get-tuple-element.20.own_ref) | copy-start | bytes 1179652
  14.5 1.1 %copy-start.2 = (bf16[1536,192]{1,0:T(8,128)(2,1)S(1)}, bf16[1536,192]{1,0:T(8,128)(2,1)}, u32[]{:S(2)}) copy-start(bf16[1536,192]{1,0:T(8,128)(2,1)} %get-tuple-element.21.weights_ref.refs_3_) | copy-start | bytes 1769476
  21.4 2.1 %collective-permute-start.2 = (bf16[192,1024]{1,0:T(8,128)(2,1)S(1)}, bf16[192,1024]{1,0:T(8,128)(2,1)S(1)}, u32[]{:S(2)}, u32[]{:S(2)}) collective-permute-start(bf16[192,1024]{1,0:T(8,128)(2,1)S(1)} %collective-permute-done.refs_0_), channel_id=1, source_target_pairs={{0,8},{8,0},{16,24},{24,16},{1,9},{9,1},{17,25},{25,17},{2,10},{10... | collective-permute-start | bytes 1179656 | tf_op jit(solution)/shard_map/ppermute | solution.py:512
  21.4 2.1 %copy-start.1 = (bf16[768,192]{0,1:T(8,128)(2,1)S(1)}, bf16[768,192]{0,1:T(8,128)(2,1)}, u32[]{:S(2)}) copy-start(bf16[768,192]{0,1:T(8,128)(2,1)} %param.28) | copy-start | bytes 884740
  21.5 2.1 %copy-start.3 = (bf16[1536,192]{1,0:T(8,128)(2,1)S(1)}, bf16[1536,192]{1,0:T(8,128)(2,1)}, u32[]{:S(2)}) copy-start(bf16[1536,192]{1,0:T(8,128)(2,1)} %get-tuple-element.21.weights_ref.refs_3_) | copy-start | bytes 1769476
  21.5 2.1 %copy-start.4 = (bf16[192,1024]{1,0:T(8,128)(2,1)S(1)}, bf16[192,1024]{1,0:T(8,128)(2,1)}, u32[]{:S(2)}) copy-start(bf16[192,1024]{1,0:T(8,128)(2,1)} %get-tuple-element.26.refs_4_) | copy-start | bytes 1179652
  21.5 2.1 %copy-start.5 = (f32[192,128]{1,0:T(8,128)S(1)}, f32[192,128]{1,0:T(8,128)}, u32[]{:S(2)}) copy-start(f32[192,128]{1,0:T(8,128)} %get-tuple-element.27.refs_5_) | copy-start | bytes 294916
  21.5 2.1 %copy-start.6 = (bf16[16,1024]{1,0:T(8,128)(2,1)S(1)}, bf16[16,1024]{1,0:T(8,128)(2,1)}, u32[]{:S(2)}) copy-start(bf16[16,1024]{1,0:T(8,128)(2,1)} %get-tuple-element.28.refs_7_) | copy-start | bytes 98308
  28.8 4.4 %collective-permute-start.6 = (bf16[208,128]{1,0:T(8,128)(2,1)S(1)}, bf16[208,128]{1,0:T(8,128)(2,1)S(1)}, u32[]{:S(2)}, u32[]{:S(2)}) collective-permute-start(bf16[208,128]{1,0:T(8,128)(2,1)S(1)} %get-tuple-element.35), channel_id=1, source_target_pairs={{0,1},{1,0},{2,3},{3,2},{4,5},{5,4},{6,7},{7,6},{8,9},{9,8},{10,11... | collective-permute-start | bytes 159752 | tf_op jit(solution)/shard_map/ppermute | solution.py:512
  30.7 4.3 %collective-permute-start.7 = (bf16[208,128]{1,0:T(8,128)(2,1)S(1)}, bf16[208,128]{1,0:T(8,128)(2,1)S(1)}, u32[]{:S(2)}, u32[]{:S(2)}) collective-permute-start(bf16[208,128]{1,0:T(8,128)(2,1)S(1)} %get-tuple-element.36), channel_id=1, source_target_pairs={{0,2},{1,3},{2,0},{3,1},{4,6},{5,7},{6,4},{7,5},{8,10},{9,11},{10,... | collective-permute-start | bytes 159752 | tf_op jit(solution)/shard_map/ppermute | solution.py:512
  32.3 5.0 %collective-permute-start.8 = (bf16[208,128]{1,0:T(8,128)(2,1)S(1)}, bf16[208,128]{1,0:T(8,128)(2,1)S(1)}, u32[]{:S(2)}, u32[]{:S(2)}) collective-permute-start(bf16[208,128]{1,0:T(8,128)(2,1)S(1)} %get-tuple-element.37), channel_id=1, source_target_pairs={{0,3},{1,2},{2,1},{3,0},{4,7},{5,6},{6,5},{7,4},{8,11},{9,10},{10,... | collective-permute-start | bytes 159752 | tf_op jit(solution)/shard_map/ppermute | solution.py:512
  37.6 9.2 %collective-permute-start.9 = (bf16[192,256]{1,0:T(8,128)(2,1)S(1)}, bf16[192,256]{1,0:T(8,128)(2,1)S(1)}, u32[]{:S(2)}, u32[]{:S(2)}) collective-permute-start(bf16[192,256]{1,0:T(8,128)(2,1)S(1)} %shard_map.172), channel_id=1, source_target_pairs={{0,4},{1,5},{2,6},{3,7},{4,0},{5,1},{6,2},{7,3},{8,12},{9,13},{10,... | collective-permute-start | bytes 294920 | tf_op jit(solution)/shard_map/ppermute | solution.py:512
  40.2 4.6 %collective-permute-start.3 = (bf16[208,128]{1,0:T(8,128)(2,1)S(1)}, bf16[208,128]{1,0:T(8,128)(2,1)S(1)}, u32[]{:S(2)}, u32[]{:S(2)}) collective-permute-start(bf16[208,128]{1,0:T(8,128)(2,1)S(1)} %get-tuple-element.31), channel_id=1, source_target_pairs={{0,1},{1,0},{2,3},{3,2},{4,5},{5,4},{6,7},{7,6},{8,9},{9,8},{10,11... | collective-permute-start | bytes 159752 | tf_op jit(solution)/shard_map/ppermute | solution.py:512
  40.7 4.2 %collective-permute-start.4 = (bf16[208,128]{1,0:T(8,128)(2,1)S(1)}, bf16[208,128]{1,0:T(8,128)(2,1)S(1)}, u32[]{:S(2)}, u32[]{:S(2)}) collective-permute-start(bf16[208,128]{1,0:T(8,128)(2,1)S(1)} %get-tuple-element.32), channel_id=1, source_target_pairs={{0,2},{1,3},{2,0},{3,1},{4,6},{5,7},{6,4},{7,5},{8,10},{9,11},{10,... | collective-permute-start | bytes 159752 | tf_op jit(solution)/shard_map/ppermute | solution.py:512
  41.7 5.0 %collective-permute-start.5 = (bf16[208,128]{1,0:T(8,128)(2,1)S(1)}, bf16[208,128]{1,0:T(8,128)(2,1)S(1)}, u32[]{:S(2)}, u32[]{:S(2)}) collective-permute-start(bf16[208,128]{1,0:T(8,128)(2,1)S(1)} %get-tuple-element.33), channel_id=1, source_target_pairs={{0,3},{1,2},{2,1},{3,0},{4,7},{5,6},{6,5},{7,4},{8,11},{9,10},{10,... | collective-permute-start | bytes 159752 | tf_op jit(solution)/shard_map/ppermute | solution.py:512

commit v11 on v9

--- a/solution.py
+++ b/solution.py
@@ -13,7 +13,9 @@
 VOX_DEV = 256
 LANES = 128
 FLAG = 16384.0
+PARTS = 2
 VMEM = 64 * 1024 * 1024 - 65536
+TIGHT = VMEM - 2 * 1024 * 1024
 ROOMY = 24 * 1024 * 1024
 F32 = jnp.float32
 BF16 = jnp.bfloat16
@@ -122,9 +124,13 @@
 
 def first_kernel(
     run, count_ref, nodes_hbm, ids_hbm, pos_hbm, gain_one_hbm, gain_two_hbm, qkv_hbm, out_hbm,
-    first_hbm, sent_hbm, nodes_ref, ids_ref, pos_ref, gain_one_ref, gain_two_ref, qkv_ref, out_ref,
-    sems, qkv_s, q_s, k_s, v_s, ctx_s, n_s, first_s, sent_s, stores
+    first_hbm, *refs
 ):
+    sent_hbm, refs = refs[:PARTS], refs[PARTS:]
+    (
+        nodes_ref, ids_ref, pos_ref, gain_one_ref, gain_two_ref, qkv_ref, out_ref, sems, qkv_s, q_s,
+        k_s, v_s, ctx_s, n_s, first_s, sent_s, stores
+    ) = refs
     loads = start_all(
         [
             (nodes_hbm, nodes_ref),
@@ -142,7 +148,7 @@
     size = chans // HEADS
     per = LANES // WIN
     count = count_ref[0]
-    wait_all(loads[:5])
+    wait_all(loads)
     cols = jnp.concatenate(
         [pos_ref[...], gain_one_ref[...], gain_two_ref[...], jnp.zeros((3, chans), F32)], 0
     ).T
@@ -162,7 +168,6 @@
         start = (nodes_ref[:, at].astype(F32) + start).astype(BF16)
         nodes_ref[:, at] = start
         n_s[:, at] = norm_t(start.astype(F32), cols[:, 3:4]).astype(BF16)
-    wait_all(loads[5:])
     qkv_t = transposed(qkv_ref[...])
     out_t = transposed(out_ref[...])
     qkv_s[...] = dot(qkv_t, n_s[...]).astype(BF16)
@@ -239,10 +244,13 @@
     keep_first.start()
     inside = within(run)
     for t, block in enumerate(swap_blocks([dot(n_s[:, tile(t)], inside) for t in range(tiles)])):
-        sent_s[:, tile(t)] = block.astype(BF16)
-    send = pltpu.make_async_copy(sent_s, sent_hbm, stores.at[1])
-    send.start()
-    wait_all([keep_first, send])
+        sent_s[t * PARTS // tiles, :, tile(t % (tiles // PARTS))] = block.astype(BF16)
+    send = [
+        pltpu.make_async_copy(sent_s.at[n], sent_hbm[n], stores.at[1 + n]) for n in range(PARTS)
+    ]
+    for copy in send:
+        copy.start()
+    wait_all([keep_first] + send)
 
 
 def tables_kernel(
@@ -301,15 +309,16 @@
 
 def add_keys(blocks, kv_t, k_s, v_s, m_s):
     chans = kv_t.shape[1]
-    tiles = k_s.shape[1]
-    for n, block in enumerate(blocks):
-        block, gone = clean(block)
+    tiles = k_s.shape[1] // PARTS
+    for n, part in enumerate(blocks):
+        block, gone = clean(part[...])
         kv = dot(kv_t, block)
         mask = jnp.where(gone, -1e9, 0.0)
+        n, start = n // PARTS, n % PARTS * tiles
         for t in range(tiles):
-            k_s[n, t] = kv[:chans, tile(t)].reshape(chans // 8, 8, LANES)
-            v_s[n, t] = kv[chans:, tile(t)].reshape(chans // 8, 8, LANES)
-            m_s[n, t] = jnp.broadcast_to(mask[:, tile(t)], (8, LANES))
+            k_s[n, start + t] = kv[:chans, tile(t)].reshape(chans // 8, 8, LANES)
+            v_s[n, start + t] = kv[chans:, tile(t)].reshape(chans // 8, 8, LANES)
+            m_s[n, start + t] = jnp.broadcast_to(mask[:, tile(t)], (8, LANES))
 
 
 def attend_two(t, run, q_s, k_s, v_s, m_s, s_s, state_s, fresh):
@@ -387,15 +396,18 @@
             state_s[2 * n + m, rows8 + 2 + part] = sums[2 * m + part]
 
 
-def near_kernel(run, own_ref, near_ref, weights_ref, q_s, state_s, k_s, v_s, m_s, s_s):
-    chans, slots = own_ref.shape
-    tiles = slots // LANES
+def near_kernel(run, *refs):
+    blocks, refs = refs[: 2 * PARTS], refs[2 * PARTS :]
+    weights_ref, q_s, state_s, k_s, v_s, m_s, s_s = refs
+    chans = weights_ref.shape[1]
+    tiles = q_s.shape[0]
     scale = (chans // HEADS) ** -0.5 * LOG2E
-    own, _ = clean(own_ref[...])
-    query = dot(weights_ref[:chans, :], own) * scale
-    for t in range(tiles):
-        q_s[t] = query[:, tile(t)].reshape(chans // 8, 8, LANES)
-    add_keys([own_ref[...], near_ref[...]], weights_ref[chans : 3 * chans, :], k_s, v_s, m_s)
+    for n in range(PARTS):
+        own, _ = clean(blocks[n][...])
+        query = dot(weights_ref[:chans, :], own) * scale
+        for t in range(tiles // PARTS):
+            q_s[n * tiles // PARTS + t] = query[:, tile(t)].reshape(chans // 8, 8, LANES)
+    add_keys(blocks, weights_ref[chans : 3 * chans, :], k_s, v_s, m_s)
 
     def step(n, _):
         hold_two(n, attend_two(2 * n, run, q_s, k_s, v_s, m_s, s_s, state_s, True), state_s)
@@ -409,7 +421,7 @@
     q_s, old_s, weights_ref, state_s, k_s, v_s, m_s, s_s = refs
     chans = weights_ref.shape[1]
     kv_t = weights_ref[chans : 3 * chans, :]
-    add_keys([block[...] for block in blocks], kv_t, k_s, v_s, m_s)
+    add_keys(blocks, kv_t, k_s, v_s, m_s)
 
     def step(n, _):
         hold_two(n, attend_two(2 * n, run, q_s, k_s, v_s, m_s, s_s, old_s, False), state_s)
@@ -426,7 +438,7 @@
     chans, slots = first_s.shape
     tiles = slots // LANES
     count = count_ref[0]
-    add_keys([block[...] for block in blocks], weights_s[chans : 3 * chans], k_s, v_s, m_s)
+    add_keys(blocks, weights_s[chans : 3 * chans], k_s, v_s, m_s)
     rows8 = chans // 8
 
     def step(n, _):
@@ -537,9 +549,9 @@
     vmem = pltpu.VMEM
     dma = pltpu.SemaphoreType.DMA
 
-    first, sent = call(
+    first, *sent = call(
         functools.partial(first_kernel, run),
-        [sds((chans, slots), BF16), sds((chans, slots), BF16)],
+        [sds((chans, slots), BF16)] + [sds((chans, slots // PARTS), BF16)] * PARTS,
         [
             vmem((chans, slots), BF16),
             vmem((1, slots), jnp.int32),
@@ -556,12 +568,12 @@
             vmem((tiles, chans, LANES), BF16),
             vmem((chans, slots), BF16),
             vmem((chans, slots), BF16),
-            vmem((chans, slots), BF16),
-            dma((2,)),
+            vmem((PARTS, chans, slots // PARTS), BF16),
+            dma((1 + PARTS,)),
         ],
         2_000_000_000,
         "saaaaaaa",
-        "aa",
+        "a" * (1 + PARTS),
     )(
         node_count,
         nodes.T,
@@ -575,9 +587,9 @@
     bit = groups // 2
     mid = []
     while bit > 1:
-        mid += [turned(block, "grp", bit) for block in [sent] + mid]
+        mid += [turned(part, "grp", bit) for part in sent + mid]
         bit //= 2
-    near = turned(sent, "grp", 1)
+    near = [turned(part, "grp", 1) for part in sent]
     weights, facts, gain = call(
         functools.partial(tables_kernel, cap),
         [
@@ -598,7 +610,7 @@
         2_000_000_000,
         "aaaaaaa",
         "vvv",
-        limit=ROOMY,
+        limit=TIGHT,
     )(
         qkv_two,
         out_two,
@@ -624,16 +636,16 @@
         [sds(*q_like), sds(*state_like)],
         key_scratch(2),
         3_000_000_000,
-        "vvv",
+        "v" * (2 * PARTS + 1),
         "vv",
         limit=ROOMY,
-    )(sent, near, weights)
+    )(*sent, *near, weights)
     mid, query = lax.optimization_barrier((mid, query))
-    far = [turned(block, "grp", 1) for block in mid]
+    far = [turned(part, "grp", 1) for part in mid]
     (state,) = call(
         functools.partial(middle_kernel, run, len(mid)),
         [sds(*state_like)],
-        key_scratch(len(mid)),
+        key_scratch(len(mid) // PARTS),
         2_000_000_000,
         "v" * len(mid) + "vvv",
         "v",
@@ -643,7 +655,7 @@
         functools.partial(second_kernel, run, cap, len(far), owners),
         [sds((chans, slots), F32)] + [sds((chans + 16, cap), BF16)] * owners,
         [vmem((chans, slots), F32), dma]
-        + key_scratch(len(far))
+        + key_scratch(len(far) // PARTS)
         + [vmem(*q_like), vmem((chans, slots), BF16), vmem((chans, slots), BF16)],
         3_000_000_000,
         "s" + "v" * (len(far) + 7),

time: 46.2 us -> 46.2 us (level)
  local copies, waits for them, and re-layouts: 3.53 us -> 1.15 us
  Pallas kernels: 20.8 us -> 22.3 us
  starting transfers between devices: 14.4 us -> 15.3 us
    unnamed x20 -> x16, local copies, waits for them, and re-layouts: 3.53 us -> 1.15 us
    pallas_call x1, Pallas kernels: 1.48 us -> 2.98 us  [body(): call(functools.partial(tables_kernel, cap), [sds((4 * chans + hidden, cha...]
    ppermute x10 -> x13, starting transfers between devices: 14.4 us -> 15.3 us  [turned(): return lax.ppermute(x, axis, [(i, i ^ bit) for i in range(n)])]
    ppermute x10 -> x13, waiting for transfers between devices: 5.89 us -> 5.72 us  [turned(): return lax.ppermute(x, axis, [(i, i ^ bit) for i in range(n)])]
  transfers between devices with their start and end apart: 10 -> 13, of which waited for: 4 -> 6; matrix products, arithmetic and copies ran while one was open for 0% -> 0% of each run, Pallas kernels for 16% -> 19%
where the time goes in v11:
time: 46.2 us; the launch traced here: 46 us
  Pallas kernels  22.3 us (48%)
  starting transfers between devices  15.3 us (33%)
  waiting for transfers between devices  5.72 us (12%)
  between operations  1.44 us (3%)
  local copies, waits for them, and re-layouts  1.15 us (2%)
    ppermute x13, starting transfers between devices, turned(): return lax.ppermute(x, axis, [(i, i ^ bit) for i in range(n)])  15.3 us
    pallas_call x1, Pallas kernels, body(): call(functools.partial(first_kernel, run), [sds((chans, slots), BF16)] +...  7.18 us
    ppermute x13, waiting for transfers between devices, turned(): return lax.ppermute(x, axis, [(i, i ^ bit) for i in range(n)])  5.72 us
    pallas_call x1, Pallas kernels, body(): call(functools.partial(second_kernel, run, cap, len(far), owners), [sds((...  5.26 us
    pallas_call x1, Pallas kernels, body(): call(functools.partial(near_kernel, run), [sds(*q_like), sds(*state_like)...  3.84 us
    pallas_call x1, Pallas kernels, body(): call(functools.partial(tables_kernel, cap), [sds((4 * chans + hidden, cha...  2.98 us
    pallas_call x1, Pallas kernels, body(): call(functools.partial(middle_kernel, run, len(mid)), [sds(*state_like)],...  2.01 us
    unnamed x16, local copies, waits for them, and re-layouts  1.15 us
  transfers between devices with their start and end apart: 13, of which 6 were waited for; matrix products, arithmetic and copies ran while one was open for 0% of the time, Pallas kernels for 19%

profile of v11, /device:TPU:0, one launch (start us, length us, event | category | flops | bytes accessed | tf_op | source)
XLA Modules:
  0.0 46.0 jit_solution(16083298744670612459)
XLA Ops:
  1.3 7.2 %shard_map.167 = (bf16[192,1024]{1,0:T(8,128)(2,1)}, bf16[192,512]{1,0:T(8,128)(2,1)}, bf16[192,512]{1,0:T(8,128)(2,1)}) custom-call(s32[1]{0:T(128)S(6)} %copy.18.count_ref, bf16[192,1024]{1,0:T(8,128)(2,1)} %bitcast.12, s32[1,1024]{1,0:T(1,128)} %bitcast.13, f32[3,192]{1,0:T(4,128)} %pos_hbm.1, f32[1,192]{1,0:T(1,128)} %bitcast.17, f32[1,192]{1,0:T(1,128)} %bitcast.18, ...), custom_call_target="tpu_custom_call" | custom-call | flops 2000000000 | bytes 2097152 | tf_op jit(solution)/shard_map/pallas_call | solution.py:552
  8.5 0.5 %collective-permute-start.2 = (bf16[192,512]{1,0:T(8,128)(2,1)}, bf16[192,512]{1,0:T(8,128)(2,1)S(1)}, u32[]{:S(2)}, u32[]{:S(2)}) collective-permute-start(bf16[192,512]{1,0:T(8,128)(2,1)} %get-tuple-element.22.refs_0_), channel_id=1, source_target_pairs={{0,8},{8,0},{16,24},{24,16},{1,9},{9,1},{17,25},{25,17},{2,10},{10... | collective-permute-start | bytes 589832 | tf_op jit(solution)/shard_map/ppermute | solution.py:517
  9.0 0.1 collective-permute-start.3
  9.0 2.9 %collective-permute-start = (bf16[192,512]{1,0:T(8,128)(2,1)}, bf16[192,512]{1,0:T(8,128)(2,1)S(1)}, u32[]{:S(2)}, u32[]{:S(2)}) collective-permute-start(bf16[192,512]{1,0:T(8,128)(2,1)} %get-tuple-element.22.refs_0_), channel_id=1, source_target_pairs={{0,16},{8,24},{16,0},{24,8},{1,17},{9,25},{17,1},{25,9},{2,18},{10... | collective-permute-start | bytes 589832 | tf_op jit(solution)/shard_map/ppermute | solution.py:517
  12.0 0.0 collective-permute-start.1
  12.0 3.0 %shard_map.168 = (bf16[1536,192]{1,0:T(8,128)(2,1)}, bf16[16,1024]{1,0:T(8,128)(2,1)}, f32[192,128]{1,0:T(8,128)}) custom-call(bf16[192,576]{1,0:T(8,128)(2,1)} %qkv_hbm.3, bf16[192,192]{1,0:T(8,128)(2,1)} %out_hbm.3, bf16[192,768]{1,0:T(8,128)(2,1)} %up_hbm.1, s32[1,512]{1,0:T(1,128)} %bitcast.14, s32[1,512]{1,0:T(1,128)} %bitcast.15, s32[1,512]{1,0:T(1,128)} %bitcast.16, ...), custom_call_target="tpu_custom_call" | custom-call | flops 2000000000 | bytes 2097152 | tf_op jit(solution)/shard_map/pallas_call | solution.py:593
  15.0 0.0 collective-permute-done.2.refs_2_
  15.0 0.0 collective-permute-done.3.refs_3_
  15.0 0.0 copy-start.3
  15.0 1.1 %copy-done.3 = bf16[1536,192]{1,0:T(8,128)(2,1)S(1)} copy-done((bf16[1536,192]{1,0:T(8,128)(2,1)S(1)}, bf16[1536,192]{1,0:T(8,128)(2,1)}, u32[]{:S(2)}) %copy-start.3) | copy-done | bytes 589848
  16.2 3.8 %shard_map.169 = (f32[8,24,8,128]{3,2,1,0:T(8,128)S(1)}, f32[8,28,8,128]{3,2,1,0:T(8,128)S(1)}) custom-call(bf16[192,512]{1,0:T(8,128)(2,1)S(1)} %copy-done.2, bf16[192,512]{1,0:T(8,128)(2,1)S(1)} %copy-done.1, bf16[192,512]{1,0:T(8,128)(2,1)S(1)} %collective-permute-done.2.refs_2_, bf16[192,512]{1,0:T(8,128)(2,1)S(1)} %collective-permute-done.3.refs_3_, ...), custom_call_target="tpu_custom_call" | custom-call | flops 3000000000 | bytes 2097152 | tf_op jit(solution)/shard_map/pallas_call | solution.py:634
  20.0 0.0 collective-permute-done.refs_0_
  20.0 1.5 %collective-permute-done.1.refs_1_ = bf16[192,512]{1,0:T(8,128)(2,1)S(1)} collective-permute-done((bf16[192,512]{1,0:T(8,128)(2,1)}, bf16[192,512]{1,0:T(8,128)(2,1)S(1)}, u32[]{:S(2)}, u32[]{:S(2)}) %collective-permute-start.1) | collective-permute-done | bytes 196640 | tf_op jit(solution)/shard_map/ppermute | solution.py:517
  21.5 0.0 collective-permute-start.4
  21.5 0.5 %collective-permute-start.5 = (bf16[192,512]{1,0:T(8,128)(2,1)S(1)}, bf16[192,512]{1,0:T(8,128)(2,1)S(1)}, u32[]{:S(2)}, u32[]{:S(2)}) collective-permute-start(bf16[192,512]{1,0:T(8,128)(2,1)S(1)} %collective-permute-done.1.refs_1_), channel_id=1, source_target_pairs={{0,8},{8,0},{16,24},{24,16},{1,9},{9,1},{17,25},{25,17},{2,10},{10... | collective-permute-start | bytes 589832 | tf_op jit(solution)/shard_map/ppermute | solution.py:517
  22.1 2.0 %shard_map.170.refs_3_ = f32[8,28,8,128]{3,2,1,0:T(8,128)S(1)} custom-call(bf16[192,512]{1,0:T(8,128)(2,1)S(1)} %collective-permute-done.refs_0_, bf16[192,512]{1,0:T(8,128)(2,1)S(1)} %collective-permute-done.1.refs_1_, f32[8,24,8,128]{3,2,1,0:T(8,128)S(1)} %get-tuple-element.28.refs_2_, f32[8,28,8,128]{3,2,1,0:T(8,128)S(1)} %get-tuple-element.29.refs_3_, ...), custom_call_target="tpu_custom_call" | custom-call | flops 2000000000 | bytes 2097152 | tf_op jit(solution)/shard_map/pallas_call | solution.py:645
  24.1 0.0 collective-permute-done.4.refs_0_
  24.1 0.0 collective-permute-done.5.refs_1_
  24.1 5.3 %shard_map.171 = (f32[192,1024]{1,0:T(8,128)}, bf16[208,128]{1,0:T(8,128)(2,1)S(1)}, bf16[208,128]{1,0:T(8,128)(2,1)S(1)}, bf16[208,128]{1,0:T(8,128)(2,1)S(1)},...) custom-call(s32[1]{0:T(128)S(6)} %copy.18.count_ref, ...), custom_call_target="tpu_custom_call" | custom-call | flops 3000000000 | bytes 2097152 | tf_op jit(solution)/shard_map/pallas_call | solution.py:654
  29.4 1.9 %collective-permute-start.6 = (bf16[208,128]{1,0:T(8,128)(2,1)S(1)}, bf16[208,128]{1,0:T(8,128)(2,1)S(1)}, u32[]{:S(2)}, u32[]{:S(2)}) collective-permute-start(bf16[208,128]{1,0:T(8,128)(2,1)S(1)} %get-tuple-element.35), channel_id=1, source_target_pairs={{0,1},{1,0},{2,3},{3,2},{4,5},{5,4},{6,7},{7,6},{8,9},{9,8},{10,11... | collective-permute-start | bytes 159752 | tf_op jit(solution)/shard_map/ppermute | solution.py:517
  31.3 3.5 %collective-permute-start.7 = (bf16[208,128]{1,0:T(8,128)(2,1)S(1)}, bf16[208,128]{1,0:T(8,128)(2,1)S(1)}, u32[]{:S(2)}, u32[]{:S(2)}) collective-permute-start(bf16[208,128]{1,0:T(8,128)(2,1)S(1)} %get-tuple-element.36), channel_id=1, source_target_pairs={{0,7},{1,6},{2,5},{3,4},{4,3},{5,2},{6,1},{7,0},{8,15},{9,14},{10,... | collective-permute-start | bytes 159752 | tf_op jit(solution)/shard_map/ppermute | solution.py:517
  34.8 0.1 collective-permute-start.8
  34.9 1.9 %collective-permute-start.9 = (bf16[208,128]{1,0:T(8,128)(2,1)S(1)}, bf16[208,128]{1,0:T(8,128)(2,1)S(1)}, u32[]{:S(2)}, u32[]{:S(2)}) collective-permute-start(bf16[208,128]{1,0:T(8,128)(2,1)S(1)} %get-tuple-element.38), channel_id=1, source_target_pairs={{0,5},{1,4},{2,7},{3,6},{4,1},{5,0},{6,3},{7,2},{8,13},{9,12},{10,... | collective-permute-start | bytes 159752 | tf_op jit(solution)/shard_map/ppermute | solution.py:517
  36.8 2.1 %collective-permute-start.10 = (bf16[208,128]{1,0:T(8,128)(2,1)S(1)}, bf16[208,128]{1,0:T(8,128)(2,1)S(1)}, u32[]{:S(2)}, u32[]{:S(2)}) collective-permute-start(bf16[208,128]{1,0:T(8,128)(2,1)S(1)} %get-tuple-element.39), channel_id=1, source_target_pairs={{0,4},{1,5},{2,6},{3,7},{4,0},{5,1},{6,2},{7,3},{8,12},{9,13},{10,... | collective-permute-start | bytes 159752 | tf_op jit(solution)/shard_map/ppermute | solution.py:517
  38.9 1.2 %collective-permute-start.11 = (bf16[208,128]{1,0:T(8,128)(2,1)S(1)}, bf16[208,128]{1,0:T(8,128)(2,1)S(1)}, u32[]{:S(2)}, u32[]{:S(2)}) collective-permute-start(bf16[208,128]{1,0:T(8,128)(2,1)S(1)} %get-tuple-element.40), channel_id=1, source_target_pairs={{0,3},{1,2},{2,1},{3,0},{4,7},{5,6},{6,5},{7,4},{8,11},{9,10},{10,... | collective-permute-start | bytes 159752 | tf_op jit(solution)/shard_map/ppermute | solution.py:517
  40.2 0.6 %collective-permute-start.12 = (bf16[208,128]{1,0:T(8,128)(2,1)S(1)}, bf16[208,128]{1,0:T(8,128)(2,1)S(1)}, u32[]{:S(2)}, u32[]{:S(2)}) collective-permute-start(bf16[208,128]{1,0:T(8,128)(2,1)S(1)} %get-tuple-element.41), channel_id=1, source_target_pairs={{0,2},{1,3},{2,0},{3,1},{4,6},{5,7},{6,4},{7,5},{8,10},{9,11},{10,... | collective-permute-start | bytes 159752 | tf_op jit(solution)/shard_map/ppermute | solution.py:517
  40.7 0.1 collective-permute-done.8.refs_3_
  40.8 2.9 %collective-permute-done.9.refs_4_ = bf16[208,128]{1,0:T(8,128)(2,1)S(1)} collective-permute-done((bf16[208,128]{1,0:T(8,128)(2,1)S(1)}, bf16[208,128]{1,0:T(8,128)(2,1)S(1)}, u32[]{:S(2)}, u32[]{:S(2)}) %collective-permute-start.9) | collective-permute-done | bytes 53280 | tf_op jit(solution)/shard_map/ppermute | solution.py:517
  43.7 0.1 collective-permute-done.10.refs_5_
  43.9 1.0 %collective-permute-done.11.refs_6_ = bf16[208,128]{1,0:T(8,128)(2,1)S(1)} collective-permute-done((bf16[208,128]{1,0:T(8,128)(2,1)S(1)}, bf16[208,128]{1,0:T(8,128)(2,1)S(1)}, u32[]{:S(2)}, u32[]{:S(2)}) %collective-permute-start.11) | collective-permute-done | bytes 53280 | tf_op jit(solution)/shard_map/ppermute | solution.py:517
  44.9 0.1 collective-permute-done.12.refs_7_
  44.9 1.0 %shard_map.172 = f32[192,256]{1,0:T(8,128)} custom-call(bf16[208,128]{1,0:T(8,128)(2,1)S(1)} %get-tuple-element.34.refs_0_, bf16[208,128]{1,0:T(8,128)(2,1)S(1)} %collective-permute-done.6.refs_1_, bf16[208,128]{1,0:T(8,128)(2,1)S(1)} %collective-permute-done.7.refs_2_, bf16[208,128]{1,0:T(8,128)(2,1)S(1)} %collective-permute-done.8.refs_3_, ...), custom_call_target="tpu_custom_call" | custom-call | flops 200000000 | bytes 2097152 | tf_op jit(solution)/shard_map/pallas_call | solution.py:676
  (16 shorter events, 0.0 us)
Async XLA Ops:
  8.5 6.5 %collective-permute-start.2 = (bf16[192,512]{1,0:T(8,128)(2,1)}, bf16[192,512]{1,0:T(8,128)(2,1)S(1)}, u32[]{:S(2)}, u32[]{:S(2)}) collective-permute-start(bf16[192,512]{1,0:T(8,128)(2,1)} %get-tuple-element.22.refs_0_), channel_id=1, source_target_pairs={{0,8},{8,0},{16,24},{24,16},{1,9},{9,1},{17,25},{25,17},{2,10},{10... | collective-permute-start | bytes 589832 | tf_op jit(solution)/shard_map/ppermute | solution.py:517
  9.0 6.0 %collective-permute-start.3 = (bf16[192,512]{1,0:T(8,128)(2,1)}, bf16[192,512]{1,0:T(8,128)(2,1)S(1)}, u32[]{:S(2)}, u32[]{:S(2)}) collective-permute-start(bf16[192,512]{1,0:T(8,128)(2,1)} %get-tuple-element.23.refs_1_), channel_id=1, source_target_pairs={{0,8},{8,0},{16,24},{24,16},{1,9},{9,1},{17,25},{25,17},{2,10},{10... | collective-permute-start | bytes 589832 | tf_op jit(solution)/shard_map/ppermute | solution.py:517
  9.0 11.0 %collective-permute-start = (bf16[192,512]{1,0:T(8,128)(2,1)}, bf16[192,512]{1,0:T(8,128)(2,1)S(1)}, u32[]{:S(2)}, u32[]{:S(2)}) collective-permute-start(bf16[192,512]{1,0:T(8,128)(2,1)} %get-tuple-element.22.refs_0_), channel_id=1, source_target_pairs={{0,16},{8,24},{16,0},{24,8},{1,17},{9,25},{17,1},{25,9},{2,18},{10... | collective-permute-start | bytes 589832 | tf_op jit(solution)/shard_map/ppermute | solution.py:517
  12.0 9.6 %collective-permute-start.1 = (bf16[192,512]{1,0:T(8,128)(2,1)}, bf16[192,512]{1,0:T(8,128)(2,1)S(1)}, u32[]{:S(2)}, u32[]{:S(2)}) collective-permute-start(bf16[192,512]{1,0:T(8,128)(2,1)} %get-tuple-element.23.refs_1_), channel_id=1, source_target_pairs={{0,16},{8,24},{16,0},{24,8},{1,17},{9,25},{17,1},{25,9},{2,18},{10... | collective-permute-start | bytes 589832 | tf_op jit(solution)/shard_map/ppermute | solution.py:517
  12.0 3.0 %copy-start.1 = (bf16[192,512]{1,0:T(8,128)(2,1)S(1)}, bf16[192,512]{1,0:T(8,128)(2,1)}, u32[]{:S(2)}) copy-start(bf16[192,512]{1,0:T(8,128)(2,1)} %get-tuple-element.23.refs_1_) | copy-start | bytes 589828
  12.0 3.0 %copy-start.2 = (bf16[192,512]{1,0:T(8,128)(2,1)S(1)}, bf16[192,512]{1,0:T(8,128)(2,1)}, u32[]{:S(2)}) copy-start(bf16[192,512]{1,0:T(8,128)(2,1)} %get-tuple-element.22.refs_0_) | copy-start | bytes 589828
  15.0 1.1 %copy-start.3 = (bf16[1536,192]{1,0:T(8,128)(2,1)S(1)}, bf16[1536,192]{1,0:T(8,128)(2,1)}, u32[]{:S(2)}) copy-start(bf16[1536,192]{1,0:T(8,128)(2,1)} %get-tuple-element.24.refs_4_) | copy-start | bytes 1769476
  21.5 2.6 %collective-permute-start.4 = (bf16[192,512]{1,0:T(8,128)(2,1)S(1)}, bf16[192,512]{1,0:T(8,128)(2,1)S(1)}, u32[]{:S(2)}, u32[]{:S(2)}) collective-permute-start(bf16[192,512]{1,0:T(8,128)(2,1)S(1)} %collective-permute-done.refs_0_), channel_id=1, source_target_pairs={{0,8},{8,0},{16,24},{24,16},{1,9},{9,1},{17,25},{25,17},{2,10},{10... | collective-permute-start | bytes 589832 | tf_op jit(solution)/shard_map/ppermute | solution.py:517
  21.5 2.6 %collective-permute-start.5 = (bf16[192,512]{1,0:T(8,128)(2,1)S(1)}, bf16[192,512]{1,0:T(8,128)(2,1)S(1)}, u32[]{:S(2)}, u32[]{:S(2)}) collective-permute-start(bf16[192,512]{1,0:T(8,128)(2,1)S(1)} %collective-permute-done.1.refs_1_), channel_id=1, source_target_pairs={{0,8},{8,0},{16,24},{24,16},{1,9},{9,1},{17,25},{25,17},{2,10},{10... | collective-permute-start | bytes 589832 | tf_op jit(solution)/shard_map/ppermute | solution.py:517
  22.0 2.1 %copy-start = (bf16[768,192]{0,1:T(8,128)(2,1)S(1)}, bf16[768,192]{0,1:T(8,128)(2,1)}, u32[]{:S(2)}) copy-start(bf16[768,192]{0,1:T(8,128)(2,1)} %param.28) | copy-start | bytes 884740
  22.0 2.1 %copy-start.4 = (bf16[1536,192]{1,0:T(8,128)(2,1)S(1)}, bf16[1536,192]{1,0:T(8,128)(2,1)}, u32[]{:S(2)}) copy-start(bf16[1536,192]{1,0:T(8,128)(2,1)} %get-tuple-element.24.refs_4_) | copy-start | bytes 1769476
  22.0 2.1 %copy-start.5 = (bf16[192,1024]{1,0:T(8,128)(2,1)S(1)}, bf16[192,1024]{1,0:T(8,128)(2,1)}, u32[]{:S(2)}) copy-start(bf16[192,1024]{1,0:T(8,128)(2,1)} %get-tuple-element.30.refs_5_) | copy-start | bytes 1179652
  22.0 2.1 %copy-start.6 = (f32[192,128]{1,0:T(8,128)S(1)}, f32[192,128]{1,0:T(8,128)}, u32[]{:S(2)}) copy-start(f32[192,128]{1,0:T(8,128)} %get-tuple-element.31.refs_6_) | copy-start | bytes 294916
  22.0 2.1 %copy-start.7 = (bf16[16,1024]{1,0:T(8,128)(2,1)S(1)}, bf16[16,1024]{1,0:T(8,128)(2,1)}, u32[]{:S(2)}) copy-start(bf16[16,1024]{1,0:T(8,128)(2,1)} %get-tuple-element.32.refs_8_) | copy-start | bytes 98308
  29.4 9.5 %collective-permute-start.6 = (bf16[208,128]{1,0:T(8,128)(2,1)S(1)}, bf16[208,128]{1,0:T(8,128)(2,1)S(1)}, u32[]{:S(2)}, u32[]{:S(2)}) collective-permute-start(bf16[208,128]{1,0:T(8,128)(2,1)S(1)} %get-tuple-element.35), channel_id=1, source_target_pairs={{0,1},{1,0},{2,3},{3,2},{4,5},{5,4},{6,7},{7,6},{8,9},{9,8},{10,11... | collective-permute-start | bytes 159752 | tf_op jit(solution)/shard_map/ppermute | solution.py:517
  31.3 8.9 %collective-permute-start.7 = (bf16[208,128]{1,0:T(8,128)(2,1)S(1)}, bf16[208,128]{1,0:T(8,128)(2,1)S(1)}, u32[]{:S(2)}, u32[]{:S(2)}) collective-permute-start(bf16[208,128]{1,0:T(8,128)(2,1)S(1)} %get-tuple-element.36), channel_id=1, source_target_pairs={{0,7},{1,6},{2,5},{3,4},{4,3},{5,2},{6,1},{7,0},{8,15},{9,14},{10,... | collective-permute-start | bytes 159752 | tf_op jit(solution)/shard_map/ppermute | solution.py:517
  34.8 6.0 %collective-permute-start.8 = (bf16[208,128]{1,0:T(8,128)(2,1)S(1)}, bf16[208,128]{1,0:T(8,128)(2,1)S(1)}, u32[]{:S(2)}, u32[]{:S(2)}) collective-permute-start(bf16[208,128]{1,0:T(8,128)(2,1)S(1)} %get-tuple-element.37), channel_id=1, source_target_pairs={{0,6},{1,7},{2,4},{3,5},{4,2},{5,3},{6,0},{7,1},{8,14},{9,15},{10,... | collective-permute-start | bytes 159752 | tf_op jit(solution)/shard_map/ppermute | solution.py:517
  34.9 8.9 %collective-permute-start.9 = (bf16[208,128]{1,0:T(8,128)(2,1)S(1)}, bf16[208,128]{1,0:T(8,128)(2,1)S(1)}, u32[]{:S(2)}, u32[]{:S(2)}) collective-permute-start(bf16[208,128]{1,0:T(8,128)(2,1)S(1)} %get-tuple-element.38), channel_id=1, source_target_pairs={{0,5},{1,4},{2,7},{3,6},{4,1},{5,0},{6,3},{7,2},{8,13},{9,12},{10,... | collective-permute-start | bytes 159752 | tf_op jit(solution)/shard_map/ppermute | solution.py:517
  36.8 7.1 %collective-permute-start.10 = (bf16[208,128]{1,0:T(8,128)(2,1)S(1)}, bf16[208,128]{1,0:T(8,128)(2,1)S(1)}, u32[]{:S(2)}, u32[]{:S(2)}) collective-permute-start(bf16[208,128]{1,0:T(8,128)(2,1)S(1)} %get-tuple-element.39), channel_id=1, source_target_pairs={{0,4},{1,5},{2,6},{3,7},{4,0},{5,1},{6,2},{7,3},{8,12},{9,13},{10,... | collective-permute-start | bytes 159752 | tf_op jit(solution)/shard_map/ppermute | solution.py:517
  38.9 5.9 %collective-permute-start.11 = (bf16[208,128]{1,0:T(8,128)(2,1)S(1)}, bf16[208,128]{1,0:T(8,128)(2,1)S(1)}, u32[]{:S(2)}, u32[]{:S(2)}) collective-permute-start(bf16[208,128]{1,0:T(8,128)(2,1)S(1)} %get-tuple-element.40), channel_id=1, source_target_pairs={{0,3},{1,2},{2,1},{3,0},{4,7},{5,6},{6,5},{7,4},{8,11},{9,10},{10,... | collective-permute-start | bytes 159752 | tf_op jit(solution)/shard_map/ppermute | solution.py:517
  40.2 4.8 %collective-permute-start.12 = (bf16[208,128]{1,0:T(8,128)(2,1)S(1)}, bf16[208,128]{1,0:T(8,128)(2,1)S(1)}, u32[]{:S(2)}, u32[]{:S(2)}) collective-permute-start(bf16[208,128]{1,0:T(8,128)(2,1)S(1)} %get-tuple-element.41), channel_id=1, source_target_pairs={{0,2},{1,3},{2,0},{3,1},{4,6},{5,7},{6,4},{7,5},{8,10},{9,11},{10,... | collective-permute-start | bytes 159752 | tf_op jit(solution)/shard_map/ppermute | solution.py:517

commit v12 on v9

--- a/solution.py
+++ b/solution.py
@@ -14,6 +14,7 @@
 LANES = 128
 FLAG = 16384.0
 VMEM = 64 * 1024 * 1024 - 65536
+TIGHT = VMEM - 2 * 1024 * 1024
 ROOMY = 24 * 1024 * 1024
 F32 = jnp.float32
 BF16 = jnp.bfloat16
@@ -142,7 +143,7 @@
     size = chans // HEADS
     per = LANES // WIN
     count = count_ref[0]
-    wait_all(loads[:5])
+    wait_all(loads)
     cols = jnp.concatenate(
         [pos_ref[...], gain_one_ref[...], gain_two_ref[...], jnp.zeros((3, chans), F32)], 0
     ).T
@@ -162,7 +163,6 @@
         start = (nodes_ref[:, at].astype(F32) + start).astype(BF16)
         nodes_ref[:, at] = start
         n_s[:, at] = norm_t(start.astype(F32), cols[:, 3:4]).astype(BF16)
-    wait_all(loads[5:])
     qkv_t = transposed(qkv_ref[...])
     out_t = transposed(out_ref[...])
     qkv_s[...] = dot(qkv_t, n_s[...]).astype(BF16)
@@ -224,7 +224,7 @@
         ctx_s[t] = jnp.concatenate(parts, 0).astype(BF16)
         return 0
 
-    lax.fori_loop(0, tiles, group, 0, unroll=4)
+    lax.fori_loop(0, tiles, group, 0, unroll=8)
     ctx = jnp.concatenate([ctx_s[t] for t in range(tiles)], 1)
     moved = dot(out_t, ctx)
     for t in range(tiles):
@@ -346,7 +346,7 @@
         old = tuple(jnp.full((8, LANES), -3e38, F32) for _ in range(4))
     else:
         old = tuple(state_s[t + n, rows8 + part] for n in both for part in both)
-    tops = lax.fori_loop(0, keys, score, old, unroll=2)
+    tops = lax.fori_loop(0, keys, score, old, unroll=4)
     if fresh:
         zero = jnp.zeros((8, LANES), F32)
         sums = tuple(zero for _ in range(4))
@@ -372,7 +372,7 @@
                 accs[at_acc] = accs[at_acc] + weight[2 * n + int(i >= cut)] * row
         return tuple(sums[n] + weight[n] for n in range(4)), tuple(accs)
 
-    sums, accs = lax.fori_loop(0, keys, gather, (sums, accs), unroll=2)
+    sums, accs = lax.fori_loop(0, keys, gather, (sums, accs), unroll=4)
     return tops, sums, accs
 
 
@@ -470,8 +470,8 @@
     low, high = facts[2:3].astype(jnp.int32), facts[1:2].astype(jnp.int32)
     picked = dot(bf_s[...], place(low, high, tiles)).astype(BF16)
     for o in range(owners):
-        votes_s[o][:chans, :] = picked[:, o * cap : (o + 1) * cap]
-        votes_s[o][chans:, :] = facts_s[:, o * cap : (o + 1) * cap]
+        at = slice(o * cap, (o + 1) * cap)
+        votes_s[o][...] = jnp.concatenate([picked[:, at], facts_s[:8, at]], 0)
     keep.wait()
 
 
@@ -481,9 +481,10 @@
     cap = got[0].shape[1]
     total = jnp.zeros(out_ref.shape, F32)
     for ref in got:
-        label = ref[chans:, :].astype(F32)[0:1]
+        ballot = ref[...]
+        label = ballot[chans:].astype(F32)[0:1]
         hot = (label == iota((voxels, cap), 0).astype(F32)).astype(BF16)
-        total = total + dot_t(ref[:chans, :], hot)
+        total = total + dot_t(ballot[:chans], hot)
     out_ref[...] = total
 
 
@@ -598,7 +599,7 @@
         2_000_000_000,
         "aaaaaaa",
         "vvv",
-        limit=ROOMY,
+        limit=TIGHT,
     )(
         qkv_two,
         out_two,
@@ -641,7 +642,7 @@
     )(*mid, query, state, weights)
     features_t, *ballots = call(
         functools.partial(second_kernel, run, cap, len(far), owners),
-        [sds((chans, slots), F32)] + [sds((chans + 16, cap), BF16)] * owners,
+        [sds((chans, slots), F32)] + [sds((chans + 8, cap), BF16)] * owners,
         [vmem((chans, slots), F32), dma]
         + key_scratch(len(far))
         + [vmem(*q_like), vmem((chans, slots), BF16), vmem((chans, slots), BF16)],

time: 46.2 us -> 45.1 us (0.976)
  local copies, waits for them, and re-layouts: 3.53 us -> 1.15 us
  waiting for transfers between devices: 5.89 us -> 7.19 us
    unnamed x20 -> x14, local copies, waits for them, and re-layouts: 3.53 us -> 1.15 us
    pallas_call x1, Pallas kernels: 1.48 us -> 2.99 us  [body(): call(functools.partial(tables_kernel, cap), [sds((4 * chans + hidden, cha...]
    ppermute x10, waiting for transfers between devices: 5.89 us -> 7.19 us  [turned(): return lax.ppermute(x, axis, [(i, i ^ bit) for i in range(n)])]
    pallas_call x1, Pallas kernels: 3.83 us -> 3.17 us  [body(): call(functools.partial(near_kernel, run), [sds(*q_like), sds(*state_like)...]
  transfers between devices with their start and end apart: 10 -> 10, of which waited for: 4 -> 5; matrix products, arithmetic and copies ran while one was open for 0% -> 0% of each run, Pallas kernels for 16% -> 18%
where the time goes in v12:
time: 45.1 us; the launch traced here: 44.9 us
  Pallas kernels  20.8 us (46%)
  starting transfers between devices  14.4 us (32%)
  waiting for transfers between devices  7.19 us (16%)
  between operations  1.41 us (3%)
  local copies, waits for them, and re-layouts  1.15 us (3%)
    ppermute x10, starting transfers between devices, turned(): return lax.ppermute(x, axis, [(i, i ^ bit) for i in range(n)])  14.4 us
    ppermute x10, waiting for transfers between devices, turned(): return lax.ppermute(x, axis, [(i, i ^ bit) for i in range(n)])  7.19 us
    pallas_call x1, Pallas kernels, body(): call(functools.partial(first_kernel, run), [sds((chans, slots), BF16), sd...  6.91 us
    pallas_call x1, Pallas kernels, body(): call(functools.partial(second_kernel, run, cap, len(far), owners), [sds((...  4.97 us
    pallas_call x1, Pallas kernels, body(): call(functools.partial(near_kernel, run), [sds(*q_like), sds(*state_like)...  3.17 us
    pallas_call x1, Pallas kernels, body(): call(functools.partial(tables_kernel, cap), [sds((4 * chans + hidden, cha...  2.99 us
    pallas_call x1, Pallas kernels, body(): call(functools.partial(middle_kernel, run, len(mid)), [sds(*state_like)],...  1.71 us
    unnamed x14, local copies, waits for them, and re-layouts  1.15 us
  transfers between devices with their start and end apart: 10, of which 5 were waited for; matrix products, arithmetic and copies ran while one was open for 0% of the time, Pallas kernels for 18%

profile of v12, /device:TPU:0, one launch (start us, length us, event | category | flops | bytes accessed | tf_op | source)
XLA Modules:
  0.0 44.9 jit_solution(3479777432230613366)
XLA Ops:
  1.3 6.9 %shard_map.167 = (bf16[192,1024]{1,0:T(8,128)(2,1)}, bf16[192,1024]{1,0:T(8,128)(2,1)}) custom-call(s32[1]{0:T(128)S(6)} %copy.18.count_ref, bf16[192,1024]{1,0:T(8,128)(2,1)} %bitcast.12, s32[1,1024]{1,0:T(1,128)} %bitcast.13, f32[3,192]{1,0:T(4,128)} %pos_hbm.1, f32[1,192]{1,0:T(1,128)} %bitcast.17, f32[1,192]{1,0:T(1,128)} %bitcast.18, ...), custom_call_target="tpu_custom_call" | custom-call | flops 2000000000 | bytes 2097152 | tf_op jit(solution)/shard_map/pallas_call | solution.py:541
  8.2 0.5 %collective-permute-start.1 = (bf16[192,1024]{1,0:T(8,128)(2,1)}, bf16[192,1024]{1,0:T(8,128)(2,1)S(1)}, u32[]{:S(2)}, u32[]{:S(2)}) collective-permute-start(bf16[192,1024]{1,0:T(8,128)(2,1)} %get-tuple-element.20.own_ref), channel_id=1, source_target_pairs={{0,8},{8,0},{16,24},{24,16},{1,9},{9,1},{17,25},{25,17},{2,10},{10... | collective-permute-start | bytes 1179656 | tf_op jit(solution)/shard_map/ppermute | solution.py:506
  8.7 2.6 %collective-permute-start = (bf16[192,1024]{1,0:T(8,128)(2,1)}, bf16[192,1024]{1,0:T(8,128)(2,1)S(1)}, u32[]{:S(2)}, u32[]{:S(2)}) collective-permute-start(bf16[192,1024]{1,0:T(8,128)(2,1)} %get-tuple-element.20.own_ref), channel_id=1, source_target_pairs={{0,16},{8,24},{16,0},{24,8},{1,17},{9,25},{17,1},{25,9},{2,18},{10... | collective-permute-start | bytes 1179656 | tf_op jit(solution)/shard_map/ppermute | solution.py:506
  11.3 3.0 %shard_map.168 = (bf16[1536,192]{1,0:T(8,128)(2,1)}, bf16[16,1024]{1,0:T(8,128)(2,1)}, f32[192,128]{1,0:T(8,128)}) custom-call(bf16[192,576]{1,0:T(8,128)(2,1)} %qkv_hbm.3, bf16[192,192]{1,0:T(8,128)(2,1)} %out_hbm.3, bf16[192,768]{1,0:T(8,128)(2,1)} %up_hbm.1, s32[1,512]{1,0:T(1,128)} %bitcast.14, s32[1,512]{1,0:T(1,128)} %bitcast.15, s32[1,512]{1,0:T(1,128)} %bitcast.16, ...), custom_call_target="tpu_custom_call" | custom-call | flops 2000000000 | bytes 2097152 | tf_op jit(solution)/shard_map/pallas_call | solution.py:582
  14.3 0.0 collective-permute-done.1.near_ref
  14.3 0.0 copy-done
  14.3 0.0 copy-start.2
  14.3 1.1 %copy-done.2 = bf16[1536,192]{1,0:T(8,128)(2,1)S(1)} copy-done((bf16[1536,192]{1,0:T(8,128)(2,1)S(1)}, bf16[1536,192]{1,0:T(8,128)(2,1)}, u32[]{:S(2)}) %copy-start.2) | copy-done | bytes 589848
  15.4 3.2 %shard_map.169 = (f32[8,24,8,128]{3,2,1,0:T(8,128)S(1)}, f32[8,28,8,128]{3,2,1,0:T(8,128)S(1)}) custom-call(bf16[192,1024]{1,0:T(8,128)(2,1)S(1)} %copy-done, bf16[192,1024]{1,0:T(8,128)(2,1)S(1)} %collective-permute-done.1.near_ref, bf16[1536,192]{1,0:T(8,128)(2,1)S(1)} %copy-done.2), custom_call_target="tpu_custom_call" | custom-call | flops 3000000000 | bytes 2097152 | tf_op jit(solution)/shard_map/pallas_call | solution.py:623
  18.6 2.6 %collective-permute-done.refs_0_ = bf16[192,1024]{1,0:T(8,128)(2,1)S(1)} collective-permute-done((bf16[192,1024]{1,0:T(8,128)(2,1)}, bf16[192,1024]{1,0:T(8,128)(2,1)S(1)}, u32[]{:S(2)}, u32[]{:S(2)}) %collective-permute-start) | collective-permute-done | bytes 393248 | tf_op jit(solution)/shard_map/ppermute | solution.py:506
  21.2 0.0 collective-permute-start.2
  21.2 0.0 copy-done.3
  21.2 0.0 copy-start.4
  21.2 0.0 copy-start.5
  21.2 1.7 %shard_map.170.refs_2_ = f32[8,28,8,128]{3,2,1,0:T(8,128)S(1)} custom-call(bf16[192,1024]{1,0:T(8,128)(2,1)S(1)} %collective-permute-done.refs_0_, f32[8,24,8,128]{3,2,1,0:T(8,128)S(1)} %get-tuple-element.24.refs_1_, f32[8,28,8,128]{3,2,1,0:T(8,128)S(1)} %get-tuple-element.25.refs_2_, bf16[1536,192]{1,0:T(8,128)(2,1)S(1)} %copy-done.3), custom_call_target="tpu_custom_call" | custom-call | flops 2000000000 | bytes 2097152 | tf_op jit(solution)/shard_map/pallas_call | solution.py:634
  22.9 0.0 collective-permute-done.2.refs_0_
  23.0 5.0 %shard_map.171 = (f32[192,1024]{1,0:T(8,128)}, bf16[200,128]{1,0:T(8,128)(2,1)S(1)}, bf16[200,128]{1,0:T(8,128)(2,1)S(1)}, bf16[200,128]{1,0:T(8,128)(2,1)S(1)},...) custom-call(s32[1]{0:T(128)S(6)} %copy.18.count_ref, ...), custom_call_target="tpu_custom_call" | custom-call | flops 3000000000 | bytes 2097152 | tf_op jit(solution)/shard_map/pallas_call | solution.py:643
  28.0 1.9 %collective-permute-start.3 = (bf16[200,128]{1,0:T(8,128)(2,1)S(1)}, bf16[200,128]{1,0:T(8,128)(2,1)S(1)}, u32[]{:S(2)}, u32[]{:S(2)}) collective-permute-start(bf16[200,128]{1,0:T(8,128)(2,1)S(1)} %get-tuple-element.31), channel_id=1, source_target_pairs={{0,1},{1,0},{2,3},{3,2},{4,5},{5,4},{6,7},{7,6},{8,9},{9,8},{10,11... | collective-permute-start | bytes 153608 | tf_op jit(solution)/shard_map/ppermute | solution.py:506
  29.8 3.5 %collective-permute-start.4 = (bf16[200,128]{1,0:T(8,128)(2,1)S(1)}, bf16[200,128]{1,0:T(8,128)(2,1)S(1)}, u32[]{:S(2)}, u32[]{:S(2)}) collective-permute-start(bf16[200,128]{1,0:T(8,128)(2,1)S(1)} %get-tuple-element.32), channel_id=1, source_target_pairs={{0,7},{1,6},{2,5},{3,4},{4,3},{5,2},{6,1},{7,0},{8,15},{9,14},{10,... | collective-permute-start | bytes 153608 | tf_op jit(solution)/shard_map/ppermute | solution.py:506
  33.4 0.1 collective-permute-start.5
  33.4 1.9 %collective-permute-start.6 = (bf16[200,128]{1,0:T(8,128)(2,1)S(1)}, bf16[200,128]{1,0:T(8,128)(2,1)S(1)}, u32[]{:S(2)}, u32[]{:S(2)}) collective-permute-start(bf16[200,128]{1,0:T(8,128)(2,1)S(1)} %get-tuple-element.34), channel_id=1, source_target_pairs={{0,5},{1,4},{2,7},{3,6},{4,1},{5,0},{6,3},{7,2},{8,13},{9,12},{10,... | collective-permute-start | bytes 153608 | tf_op jit(solution)/shard_map/ppermute | solution.py:506
  35.4 2.1 %collective-permute-start.7 = (bf16[200,128]{1,0:T(8,128)(2,1)S(1)}, bf16[200,128]{1,0:T(8,128)(2,1)S(1)}, u32[]{:S(2)}, u32[]{:S(2)}) collective-permute-start(bf16[200,128]{1,0:T(8,128)(2,1)S(1)} %get-tuple-element.35), channel_id=1, source_target_pairs={{0,4},{1,5},{2,6},{3,7},{4,0},{5,1},{6,2},{7,3},{8,12},{9,13},{10,... | collective-permute-start | bytes 153608 | tf_op jit(solution)/shard_map/ppermute | solution.py:506
  37.5 0.0 collective-permute-done.3.refs_1_
  37.5 1.2 %collective-permute-start.8 = (bf16[200,128]{1,0:T(8,128)(2,1)S(1)}, bf16[200,128]{1,0:T(8,128)(2,1)S(1)}, u32[]{:S(2)}, u32[]{:S(2)}) collective-permute-start(bf16[200,128]{1,0:T(8,128)(2,1)S(1)} %get-tuple-element.36), channel_id=1, source_target_pairs={{0,3},{1,2},{2,1},{3,0},{4,7},{5,6},{6,5},{7,4},{8,11},{9,10},{10,... | collective-permute-start | bytes 153608 | tf_op jit(solution)/shard_map/ppermute | solution.py:506
  38.7 0.0 collective-permute-done.4.refs_2_
  38.7 0.6 %collective-permute-start.9 = (bf16[200,128]{1,0:T(8,128)(2,1)S(1)}, bf16[200,128]{1,0:T(8,128)(2,1)S(1)}, u32[]{:S(2)}, u32[]{:S(2)}) collective-permute-start(bf16[200,128]{1,0:T(8,128)(2,1)S(1)} %get-tuple-element.37), channel_id=1, source_target_pairs={{0,2},{1,3},{2,0},{3,1},{4,6},{5,7},{6,4},{7,5},{8,10},{9,11},{10,... | collective-permute-start | bytes 153608 | tf_op jit(solution)/shard_map/ppermute | solution.py:506
  39.3 0.2 collective-permute-done.5.refs_3_
  39.5 3.1 %collective-permute-done.6.refs_4_ = bf16[200,128]{1,0:T(8,128)(2,1)S(1)} collective-permute-done((bf16[200,128]{1,0:T(8,128)(2,1)S(1)}, bf16[200,128]{1,0:T(8,128)(2,1)S(1)}, u32[]{:S(2)}, u32[]{:S(2)}) %collective-permute-start.6) | collective-permute-done | bytes 51232 | tf_op jit(solution)/shard_map/ppermute | solution.py:506
  42.5 0.2 collective-permute-done.7.refs_5_
  42.7 1.2 %collective-permute-done.8.refs_6_ = bf16[200,128]{1,0:T(8,128)(2,1)S(1)} collective-permute-done((bf16[200,128]{1,0:T(8,128)(2,1)S(1)}, bf16[200,128]{1,0:T(8,128)(2,1)S(1)}, u32[]{:S(2)}, u32[]{:S(2)}) %collective-permute-start.8) | collective-permute-done | bytes 51232 | tf_op jit(solution)/shard_map/ppermute | solution.py:506
  43.9 0.0 collective-permute-done.9.refs_7_
  43.9 1.0 %shard_map.172 = f32[192,256]{1,0:T(8,128)} custom-call(bf16[200,128]{1,0:T(8,128)(2,1)S(1)} %get-tuple-element.30.refs_0_, bf16[200,128]{1,0:T(8,128)(2,1)S(1)} %collective-permute-done.3.refs_1_, bf16[200,128]{1,0:T(8,128)(2,1)S(1)} %collective-permute-done.4.refs_2_, bf16[200,128]{1,0:T(8,128)(2,1)S(1)} %collective-permute-done.5.refs_3_, ...), custom_call_target="tpu_custom_call" | custom-call | flops 200000000 | bytes 2097152 | tf_op jit(solution)/shard_map/pallas_call | solution.py:665
  (8 shorter events, 0.0 us)
Async XLA Ops:
  8.2 6.1 %collective-permute-start.1 = (bf16[192,1024]{1,0:T(8,128)(2,1)}, bf16[192,1024]{1,0:T(8,128)(2,1)S(1)}, u32[]{:S(2)}, u32[]{:S(2)}) collective-permute-start(bf16[192,1024]{1,0:T(8,128)(2,1)} %get-tuple-element.20.own_ref), channel_id=1, source_target_pairs={{0,8},{8,0},{16,24},{24,16},{1,9},{9,1},{17,25},{25,17},{2,10},{10... | collective-permute-start | bytes 1179656 | tf_op jit(solution)/shard_map/ppermute | solution.py:506
  8.7 12.5 %collective-permute-start = (bf16[192,1024]{1,0:T(8,128)(2,1)}, bf16[192,1024]{1,0:T(8,128)(2,1)S(1)}, u32[]{:S(2)}, u32[]{:S(2)}) collective-permute-start(bf16[192,1024]{1,0:T(8,128)(2,1)} %get-tuple-element.20.own_ref), channel_id=1, source_target_pairs={{0,16},{8,24},{16,0},{24,8},{1,17},{9,25},{17,1},{25,9},{2,18},{10... | collective-permute-start | bytes 1179656 | tf_op jit(solution)/shard_map/ppermute | solution.py:506
  11.3 3.0 %copy-start = (bf16[192,1024]{1,0:T(8,128)(2,1)S(1)}, bf16[192,1024]{1,0:T(8,128)(2,1)}, u32[]{:S(2)}) copy-start(bf16[192,1024]{1,0:T(8,128)(2,1)} %get-tuple-element.20.own_ref) | copy-start | bytes 1179652
  14.3 1.1 %copy-start.2 = (bf16[1536,192]{1,0:T(8,128)(2,1)S(1)}, bf16[1536,192]{1,0:T(8,128)(2,1)}, u32[]{:S(2)}) copy-start(bf16[1536,192]{1,0:T(8,128)(2,1)} %get-tuple-element.21.weights_ref.refs_3_) | copy-start | bytes 1769476
  15.4 5.8 %copy-start.3 = (bf16[1536,192]{1,0:T(8,128)(2,1)S(1)}, bf16[1536,192]{1,0:T(8,128)(2,1)}, u32[]{:S(2)}) copy-start(bf16[1536,192]{1,0:T(8,128)(2,1)} %get-tuple-element.21.weights_ref.refs_3_) | copy-start | bytes 1769476
  21.2 1.8 %collective-permute-start.2 = (bf16[192,1024]{1,0:T(8,128)(2,1)S(1)}, bf16[192,1024]{1,0:T(8,128)(2,1)S(1)}, u32[]{:S(2)}, u32[]{:S(2)}) collective-permute-start(bf16[192,1024]{1,0:T(8,128)(2,1)S(1)} %collective-permute-done.refs_0_), channel_id=1, source_target_pairs={{0,8},{8,0},{16,24},{24,16},{1,9},{9,1},{17,25},{25,17},{2,10},{10... | collective-permute-start | bytes 1179656 | tf_op jit(solution)/shard_map/ppermute | solution.py:506
  21.2 1.8 %copy-start.1 = (bf16[768,192]{0,1:T(8,128)(2,1)S(1)}, bf16[768,192]{0,1:T(8,128)(2,1)}, u32[]{:S(2)}) copy-start(bf16[768,192]{0,1:T(8,128)(2,1)} %param.28) | copy-start | bytes 884740
  21.2 1.8 %copy-start.4 = (bf16[192,1024]{1,0:T(8,128)(2,1)S(1)}, bf16[192,1024]{1,0:T(8,128)(2,1)}, u32[]{:S(2)}) copy-start(bf16[192,1024]{1,0:T(8,128)(2,1)} %get-tuple-element.26.refs_4_) | copy-start | bytes 1179652
  21.2 1.8 %copy-start.5 = (f32[192,128]{1,0:T(8,128)S(1)}, f32[192,128]{1,0:T(8,128)}, u32[]{:S(2)}) copy-start(f32[192,128]{1,0:T(8,128)} %get-tuple-element.27.refs_5_) | copy-start | bytes 294916
  21.2 1.8 %copy-start.6 = (bf16[16,1024]{1,0:T(8,128)(2,1)S(1)}, bf16[16,1024]{1,0:T(8,128)(2,1)}, u32[]{:S(2)}) copy-start(bf16[16,1024]{1,0:T(8,128)(2,1)} %get-tuple-element.28.refs_7_) | copy-start | bytes 98308
  28.0 9.5 %collective-permute-start.3 = (bf16[200,128]{1,0:T(8,128)(2,1)S(1)}, bf16[200,128]{1,0:T(8,128)(2,1)S(1)}, u32[]{:S(2)}, u32[]{:S(2)}) collective-permute-start(bf16[200,128]{1,0:T(8,128)(2,1)S(1)} %get-tuple-element.31), channel_id=1, source_target_pairs={{0,1},{1,0},{2,3},{3,2},{4,5},{5,4},{6,7},{7,6},{8,9},{9,8},{10,11... | collective-permute-start | bytes 153608 | tf_op jit(solution)/shard_map/ppermute | solution.py:506
  29.8 8.9 %collective-permute-start.4 = (bf16[200,128]{1,0:T(8,128)(2,1)S(1)}, bf16[200,128]{1,0:T(8,128)(2,1)S(1)}, u32[]{:S(2)}, u32[]{:S(2)}) collective-permute-start(bf16[200,128]{1,0:T(8,128)(2,1)S(1)} %get-tuple-element.32), channel_id=1, source_target_pairs={{0,7},{1,6},{2,5},{3,4},{4,3},{5,2},{6,1},{7,0},{8,15},{9,14},{10,... | collective-permute-start | bytes 153608 | tf_op jit(solution)/shard_map/ppermute | solution.py:506
  33.4 6.1 %collective-permute-start.5 = (bf16[200,128]{1,0:T(8,128)(2,1)S(1)}, bf16[200,128]{1,0:T(8,128)(2,1)S(1)}, u32[]{:S(2)}, u32[]{:S(2)}) collective-permute-start(bf16[200,128]{1,0:T(8,128)(2,1)S(1)} %get-tuple-element.33), channel_id=1, source_target_pairs={{0,6},{1,7},{2,4},{3,5},{4,2},{5,3},{6,0},{7,1},{8,14},{9,15},{10,... | collective-permute-start | bytes 153608 | tf_op jit(solution)/shard_map/ppermute | solution.py:506
  33.4 9.1 %collective-permute-start.6 = (bf16[200,128]{1,0:T(8,128)(2,1)S(1)}, bf16[200,128]{1,0:T(8,128)(2,1)S(1)}, u32[]{:S(2)}, u32[]{:S(2)}) collective-permute-start(bf16[200,128]{1,0:T(8,128)(2,1)S(1)} %get-tuple-element.34), channel_id=1, source_target_pairs={{0,5},{1,4},{2,7},{3,6},{4,1},{5,0},{6,3},{7,2},{8,13},{9,12},{10,... | collective-permute-start | bytes 153608 | tf_op jit(solution)/shard_map/ppermute | solution.py:506
  35.4 7.4 %collective-permute-start.7 = (bf16[200,128]{1,0:T(8,128)(2,1)S(1)}, bf16[200,128]{1,0:T(8,128)(2,1)S(1)}, u32[]{:S(2)}, u32[]{:S(2)}) collective-permute-start(bf16[200,128]{1,0:T(8,128)(2,1)S(1)} %get-tuple-element.35), channel_id=1, source_target_pairs={{0,4},{1,5},{2,6},{3,7},{4,0},{5,1},{6,2},{7,3},{8,12},{9,13},{10,... | collective-permute-start | bytes 153608 | tf_op jit(solution)/shard_map/ppermute | solution.py:506
  37.5 6.4 %collective-permute-start.8 = (bf16[200,128]{1,0:T(8,128)(2,1)S(1)}, bf16[200,128]{1,0:T(8,128)(2,1)S(1)}, u32[]{:S(2)}, u32[]{:S(2)}) collective-permute-start(bf16[200,128]{1,0:T(8,128)(2,1)S(1)} %get-tuple-element.36), channel_id=1, source_target_pairs={{0,3},{1,2},{2,1},{3,0},{4,7},{5,6},{6,5},{7,4},{8,11},{9,10},{10,... | collective-permute-start | bytes 153608 | tf_op jit(solution)/shard_map/ppermute | solution.py:506
  38.7 5.2 %collective-permute-start.9 = (bf16[200,128]{1,0:T(8,128)(2,1)S(1)}, bf16[200,128]{1,0:T(8,128)(2,1)S(1)}, u32[]{:S(2)}, u32[]{:S(2)}) collective-permute-start(bf16[200,128]{1,0:T(8,128)(2,1)S(1)} %get-tuple-element.37), channel_id=1, source_target_pairs={{0,2},{1,3},{2,0},{3,1},{4,6},{5,7},{6,4},{7,5},{8,10},{9,11},{10,... | collective-permute-start | bytes 153608 | tf_op jit(solution)/shard_map/ppermute | solution.py:506

commit v13 on v12

--- a/solution.py
+++ b/solution.py
@@ -346,7 +346,7 @@
         old = tuple(jnp.full((8, LANES), -3e38, F32) for _ in range(4))
     else:
         old = tuple(state_s[t + n, rows8 + part] for n in both for part in both)
-    tops = lax.fori_loop(0, keys, score, old, unroll=4)
+    tops = lax.fori_loop(0, keys, score, old, unroll=8)
     if fresh:
         zero = jnp.zeros((8, LANES), F32)
         sums = tuple(zero for _ in range(4))
@@ -372,7 +372,7 @@
                 accs[at_acc] = accs[at_acc] + weight[2 * n + int(i >= cut)] * row
         return tuple(sums[n] + weight[n] for n in range(4)), tuple(accs)
 
-    sums, accs = lax.fori_loop(0, keys, gather, (sums, accs), unroll=4)
+    sums, accs = lax.fori_loop(0, keys, gather, (sums, accs), unroll=8)
     return tops, sums, accs
 
 
@@ -421,7 +421,7 @@
 def second_kernel(run, cap, far, owners, count_ref, *refs):
     blocks, refs = refs[:far], refs[far:]
     q_s, state_s, weights_s, first_s, gain_s, down_s, facts_s, feat_hbm = refs[:8]
-    votes_s, refs = refs[8 : 8 + owners], refs[8 + owners :]
+    votes_s, refs = refs[8 : 8 + owners // 2], refs[8 + owners // 2 :]
     feat_s, store, k_s, v_s, m_s, s_s, ctx_s, bf_s, inner_s = refs
     chans, slots = first_s.shape
     tiles = slots // LANES
@@ -471,21 +471,27 @@
     picked = dot(bf_s[...], place(low, high, tiles)).astype(BF16)
     for o in range(owners):
         at = slice(o * cap, (o + 1) * cap)
-        votes_s[o][...] = jnp.concatenate([picked[:, at], facts_s[:8, at]], 0)
+        ballot = jnp.concatenate([picked[:, at], facts_s[:8, at]], 0)
+        votes_s[o % len(votes_s)][o // len(votes_s)] = ballot
     keep.wait()
 
 
 def sums_kernel(*refs):
-    got, out_ref = refs[:-1], refs[-1]
-    chans, voxels = out_ref.shape
-    cap = got[0].shape[1]
-    total = jnp.zeros(out_ref.shape, F32)
-    for ref in got:
-        ballot = ref[...]
-        label = ballot[chans:].astype(F32)[0:1]
-        hot = (label == iota((voxels, cap), 0).astype(F32)).astype(BF16)
-        total = total + dot_t(ballot[:chans], hot)
-    out_ref[...] = total
+    ballots, outs = refs[:-2], refs[-2:]
+    cap = ballots[0].shape[2]
+    for kind, out_ref in enumerate(outs):
+        chans, voxels = out_ref.shape
+        total = jnp.zeros(out_ref.shape, F32)
+        for ref in ballots:
+            ballot = ref[kind]
+            label = ballot[chans:].astype(F32)[0:1]
+            hot = (label == iota((voxels, cap), 0).astype(F32)).astype(BF16)
+            total = total + dot_t(ballot[:chans], hot)
+        out_ref[...] = total.astype(out_ref.dtype)
+
+
+def total_kernel(here_ref, there_ref, out_ref):
+    out_ref[...] = here_ref[...] + there_ref[...].astype(F32)
 
 
 def call(kernel, outs, scratch, flops, spaces, out_spaces, limit=VMEM):
@@ -642,13 +648,13 @@
     )(*mid, query, state, weights)
     features_t, *ballots = call(
         functools.partial(second_kernel, run, cap, len(far), owners),
-        [sds((chans, slots), F32)] + [sds((chans + 8, cap), BF16)] * owners,
+        [sds((chans, slots), F32)] + [sds((2, chans + 8, cap), BF16)] * (owners // 2),
         [vmem((chans, slots), F32), dma]
         + key_scratch(len(far))
         + [vmem(*q_like), vmem((chans, slots), BF16), vmem((chans, slots), BF16)],
         3_000_000_000,
         "s" + "v" * (len(far) + 7),
-        "a" + "v" * owners,
+        "a" + "v" * (owners // 2),
         limit=ROOMY,
     )(
         node_count,
@@ -661,16 +667,20 @@
         w_down.T,
         facts,
     )
-    got = [ballots[0]] + [turned(ballots[k], "tile", k) for k in [1] + list(range(owners - 1, 1, -1))]
-    (sums_t,) = call(
+    half = owners // 2
+    got = [ballots[0]] + [turned(ballots[k], "tile", k) for k in range(1, half)]
+    here, there = call(
         sums_kernel,
-        [sds((chans, VOX_DEV), F32)],
+        [sds((chans, VOX_DEV), F32), sds((chans, VOX_DEV), BF16)],
         [],
         200_000_000,
-        "v" * owners,
-        "v",
+        "v" * half,
+        "vv",
         limit=ROOMY,
     )(*got)
+    (sums_t,) = call(
+        total_kernel, [sds((chans, VOX_DEV), F32)], [], 1_000_000, "vv", "v", limit=ROOMY
+    )(here, turned(there, "tile", half))
     return (features_t.T, sums_t.T)
 
 

time: 45.1 us -> 44.5 us (0.987)
  waiting for transfers between devices: 7.19 us -> 12.5 us
  starting transfers between devices: 14.4 us -> 9.27 us
  Pallas kernels: 20.8 us -> 20 us
    ppermute x10 -> x7, waiting for transfers between devices: 7.19 us -> 12.5 us  [turned(): return lax.ppermute(x, axis, [(i, i ^ bit) for i in range(n)])]
    ppermute x10 -> x7, starting transfers between devices: 14.4 us -> 9.27 us  [turned(): return lax.ppermute(x, axis, [(i, i ^ bit) for i in range(n)])]
    pallas_call x1 -> x2, Pallas kernels: 1.05 us -> 1.07 us  [the longest x1 0.69 us: body(): call(total_kernel, [sds((chans, VOX_DEV), F32)], [], 1000000, 'vv', 'v',...]
    unnamed x14 -> x12, local copies, waits for them, and re-layouts: 1.15 us -> 1.15 us
  transfers between devices with their start and end apart: 10 -> 7, of which waited for: 5 -> 6; matrix products, arithmetic and copies ran while one was open for 0% -> 0% of each run, Pallas kernels for 18% -> 17%
where the time goes in v13:
time: 44.5 us; the launch traced here: 44.3 us
  Pallas kernels  20 us (45%)
  waiting for transfers between devices  12.5 us (28%)
  starting transfers between devices  9.27 us (21%)
  between operations  1.38 us (3%)
  local copies, waits for them, and re-layouts  1.15 us (3%)
    ppermute x7, waiting for transfers between devices, turned(): return lax.ppermute(x, axis, [(i, i ^ bit) for i in range(n)])  12.5 us
    ppermute x7, starting transfers between devices, turned(): return lax.ppermute(x, axis, [(i, i ^ bit) for i in range(n)])  9.27 us
    pallas_call x1, Pallas kernels, body(): call(functools.partial(first_kernel, run), [sds((chans, slots), BF16), sd...  6.91 us
    pallas_call x1, Pallas kernels, body(): call(functools.partial(second_kernel, run, cap, len(far), owners), [sds((...  4.65 us
    pallas_call x1, Pallas kernels, body(): call(functools.partial(tables_kernel, cap), [sds((4 * chans + hidden, cha...  2.99 us
    pallas_call x1, Pallas kernels, body(): call(functools.partial(near_kernel, run), [sds(*q_like), sds(*state_like)...  2.93 us
    pallas_call x1, Pallas kernels, body(): call(functools.partial(middle_kernel, run, len(mid)), [sds(*state_like)],...  1.41 us
    unnamed x12, local copies, waits for them, and re-layouts  1.15 us
  transfers between devices with their start and end apart: 7, of which 6 were waited for; matrix products, arithmetic and copies ran while one was open for 0% of the time, Pallas kernels for 17%

profile of v13, /device:TPU:0, one launch (start us, length us, event | category | flops | bytes accessed | tf_op | source)
XLA Modules:
  0.0 44.3 jit_solution(18077012095826720317)
XLA Ops:
  1.3 6.9 %shard_map.167 = (bf16[192,1024]{1,0:T(8,128)(2,1)}, bf16[192,1024]{1,0:T(8,128)(2,1)}) custom-call(s32[1]{0:T(128)S(6)} %copy.18.count_ref, bf16[192,1024]{1,0:T(8,128)(2,1)} %bitcast.13, s32[1,1024]{1,0:T(1,128)} %bitcast.14, f32[3,192]{1,0:T(4,128)} %pos_hbm.1, f32[1,192]{1,0:T(1,128)} %bitcast.18, f32[1,192]{1,0:T(1,128)} %bitcast.19, ...), custom_call_target="tpu_custom_call" | custom-call | flops 2000000000 | bytes 2097152 | tf_op jit(solution)/shard_map/pallas_call | solution.py:547
  8.2 0.5 %collective-permute-start.1 = (bf16[192,1024]{1,0:T(8,128)(2,1)}, bf16[192,1024]{1,0:T(8,128)(2,1)S(1)}, u32[]{:S(2)}, u32[]{:S(2)}) collective-permute-start(bf16[192,1024]{1,0:T(8,128)(2,1)} %get-tuple-element.18.own_ref), channel_id=1, source_target_pairs={{0,8},{8,0},{16,24},{24,16},{1,9},{9,1},{17,25},{25,17},{2,10},{10... | collective-permute-start | bytes 1179656 | tf_op jit(solution)/shard_map/ppermute | solution.py:512
  8.7 2.6 %collective-permute-start = (bf16[192,1024]{1,0:T(8,128)(2,1)}, bf16[192,1024]{1,0:T(8,128)(2,1)S(1)}, u32[]{:S(2)}, u32[]{:S(2)}) collective-permute-start(bf16[192,1024]{1,0:T(8,128)(2,1)} %get-tuple-element.18.own_ref), channel_id=1, source_target_pairs={{0,16},{8,24},{16,0},{24,8},{1,17},{9,25},{17,1},{25,9},{2,18},{10... | collective-permute-start | bytes 1179656 | tf_op jit(solution)/shard_map/ppermute | solution.py:512
  11.3 0.0 copy-start
  11.3 3.0 %shard_map.168 = (bf16[1536,192]{1,0:T(8,128)(2,1)}, bf16[16,1024]{1,0:T(8,128)(2,1)}, f32[192,128]{1,0:T(8,128)}) custom-call(bf16[192,576]{1,0:T(8,128)(2,1)} %qkv_hbm.3, bf16[192,192]{1,0:T(8,128)(2,1)} %out_hbm.3, bf16[192,768]{1,0:T(8,128)(2,1)} %up_hbm.1, s32[1,512]{1,0:T(1,128)} %bitcast.15, s32[1,512]{1,0:T(1,128)} %bitcast.16, s32[1,512]{1,0:T(1,128)} %bitcast.17, ...), custom_call_target="tpu_custom_call" | custom-call | flops 2000000000 | bytes 2097152 | tf_op jit(solution)/shard_map/pallas_call | solution.py:588
  14.3 0.0 collective-permute-done.1.near_ref
  14.3 0.0 copy-done
  14.3 0.0 copy-start.2
  14.3 1.1 %copy-done.2 = bf16[1536,192]{1,0:T(8,128)(2,1)S(1)} copy-done((bf16[1536,192]{1,0:T(8,128)(2,1)S(1)}, bf16[1536,192]{1,0:T(8,128)(2,1)}, u32[]{:S(2)}) %copy-start.2) | copy-done | bytes 589848
  15.4 2.9 %shard_map.169 = (f32[8,24,8,128]{3,2,1,0:T(8,128)S(1)}, f32[8,28,8,128]{3,2,1,0:T(8,128)S(1)}) custom-call(bf16[192,1024]{1,0:T(8,128)(2,1)S(1)} %copy-done, bf16[192,1024]{1,0:T(8,128)(2,1)S(1)} %collective-permute-done.1.near_ref, bf16[1536,192]{1,0:T(8,128)(2,1)S(1)} %copy-done.2), custom_call_target="tpu_custom_call" | custom-call | flops 3000000000 | bytes 2097152 | tf_op jit(solution)/shard_map/pallas_call | solution.py:629
  18.4 2.8 %collective-permute-done.refs_0_ = bf16[192,1024]{1,0:T(8,128)(2,1)S(1)} collective-permute-done((bf16[192,1024]{1,0:T(8,128)(2,1)}, bf16[192,1024]{1,0:T(8,128)(2,1)S(1)}, u32[]{:S(2)}, u32[]{:S(2)}) %collective-permute-start) | collective-permute-done | bytes 393248 | tf_op jit(solution)/shard_map/ppermute | solution.py:512
  21.2 0.0 collective-permute-start.2
  21.2 0.0 copy-start.1
  21.2 0.0 copy-start.3
  21.2 0.0 copy-start.5
  21.2 1.4 %shard_map.170.refs_2_ = f32[8,28,8,128]{3,2,1,0:T(8,128)S(1)} custom-call(bf16[192,1024]{1,0:T(8,128)(2,1)S(1)} %collective-permute-done.refs_0_, f32[8,24,8,128]{3,2,1,0:T(8,128)S(1)} %get-tuple-element.22.refs_1_, f32[8,28,8,128]{3,2,1,0:T(8,128)S(1)} %get-tuple-element.23.refs_2_, bf16[1536,192]{1,0:T(8,128)(2,1)S(1)} %copy-done.2), custom_call_target="tpu_custom_call" | custom-call | flops 2000000000 | bytes 2097152 | tf_op jit(solution)/shard_map/pallas_call | solution.py:640
  22.6 0.3 collective-permute-done.2.refs_0_
  22.9 0.0 copy-done.1
  22.9 0.0 copy-done.3
  22.9 0.0 copy-done.4
  22.9 0.0 copy-done.5
  22.9 4.6 %shard_map.171 = (f32[192,1024]{1,0:T(8,128)}, bf16[2,200,128]{2,1,0:T(8,128)(2,1)S(1)}, bf16[2,200,128]{2,1,0:T(8,128)(2,1)S(1)}, bf16[2,200,128]{2,1,0:T(8,128)(2,1)S(1)}, bf16[2,200,128]{2,1,0:T(8,128)(2,1)S(1)}) custom-call(s32[1]{0:T(128)S(6)} %copy.18.count_ref, bf16[192,1024]{1,0:T(8,128)(2,1)S(1)} %collective-permute-done.2.refs_0_, ...), custom_call_target="tpu_custom_call" | custom-call | flops 3000000000 | bytes 2097152 | tf_op jit(solution)/shard_map/pallas_call | solution.py:649
  27.6 1.9 %collective-permute-start.3 = (bf16[2,200,128]{2,1,0:T(8,128)(2,1)S(1)}, bf16[2,200,128]{2,1,0:T(8,128)(2,1)S(1)}, u32[]{:S(2)}, u32[]{:S(2)}) collective-permute-start(bf16[2,200,128]{2,1,0:T(8,128)(2,1)S(1)} %get-tuple-element.29), channel_id=1, source_target_pairs={{0,1},{1,0},{2,3},{3,2},{4,5},{5,4},{6,7},{7,6},{8,9},{9,8},{10,11... | collective-permute-start | bytes 307208 | tf_op jit(solution)/shard_map/ppermute | solution.py:512
  29.5 1.6 %collective-permute-start.4 = (bf16[2,200,128]{2,1,0:T(8,128)(2,1)S(1)}, bf16[2,200,128]{2,1,0:T(8,128)(2,1)S(1)}, u32[]{:S(2)}, u32[]{:S(2)}) collective-permute-start(bf16[2,200,128]{2,1,0:T(8,128)(2,1)S(1)} %get-tuple-element.30), channel_id=1, source_target_pairs={{0,2},{1,3},{2,0},{3,1},{4,6},{5,7},{6,4},{7,5},{8,10},{9,11},{10,... | collective-permute-start | bytes 307208 | tf_op jit(solution)/shard_map/ppermute | solution.py:512
  31.0 0.1 collective-permute-start.5
  31.1 1.6 %collective-permute-done.3.refs_1_ = bf16[2,200,128]{2,1,0:T(8,128)(2,1)S(1)} collective-permute-done((bf16[2,200,128]{2,1,0:T(8,128)(2,1)S(1)}, bf16[2,200,128]{2,1,0:T(8,128)(2,1)S(1)}, u32[]{:S(2)}, u32[]{:S(2)}) %collective-permute-start.3) | collective-permute-done | bytes 102432 | tf_op jit(solution)/shard_map/ppermute | solution.py:512
  32.8 2.4 %collective-permute-done.4.refs_2_ = bf16[2,200,128]{2,1,0:T(8,128)(2,1)S(1)} collective-permute-done((bf16[2,200,128]{2,1,0:T(8,128)(2,1)S(1)}, bf16[2,200,128]{2,1,0:T(8,128)(2,1)S(1)}, u32[]{:S(2)}, u32[]{:S(2)}) %collective-permute-start.4) | collective-permute-done | bytes 102432 | tf_op jit(solution)/shard_map/ppermute | solution.py:512
  35.2 1.4 %collective-permute-done.5.refs_3_ = bf16[2,200,128]{2,1,0:T(8,128)(2,1)S(1)} collective-permute-done((bf16[2,200,128]{2,1,0:T(8,128)(2,1)S(1)}, bf16[2,200,128]{2,1,0:T(8,128)(2,1)S(1)}, u32[]{:S(2)}, u32[]{:S(2)}) %collective-permute-start.5) | collective-permute-done | bytes 102432 | tf_op jit(solution)/shard_map/ppermute | solution.py:512
  36.6 0.4 shard_map.172
  37.0 2.6 %collective-permute-start.6 = (bf16[192,256]{1,0:T(8,128)(2,1)S(1)}, bf16[192,256]{1,0:T(8,128)(2,1)S(1)}, u32[]{:S(2)}, u32[]{:S(2)}) collective-permute-start(bf16[192,256]{1,0:T(8,128)(2,1)S(1)} %get-tuple-element.33), channel_id=1, source_target_pairs={{0,4},{1,5},{2,6},{3,7},{4,0},{5,1},{6,2},{7,3},{8,12},{9,13},{10,... | collective-permute-start | bytes 294920 | tf_op jit(solution)/shard_map/ppermute | solution.py:512
  39.6 4.0 %collective-permute-done.6.there_ref = bf16[192,256]{1,0:T(8,128)(2,1)S(1)} collective-permute-done((bf16[192,256]{1,0:T(8,128)(2,1)S(1)}, bf16[192,256]{1,0:T(8,128)(2,1)S(1)}, u32[]{:S(2)}, u32[]{:S(2)}) %collective-permute-start.6) | collective-permute-done | bytes 98336 | tf_op jit(solution)/shard_map/ppermute | solution.py:512
  43.6 0.7 %shard_map.173 = f32[192,256]{1,0:T(8,128)} custom-call(f32[192,256]{1,0:T(8,128)S(1)} %get-tuple-element.32.here_ref, bf16[192,256]{1,0:T(8,128)(2,1)S(1)} %collective-permute-done.6.there_ref), custom_call_target="tpu_custom_call" | custom-call | flops 1000000 | bytes 2097152 | tf_op jit(solution)/shard_map/pallas_call | solution.py:681
  (1 shorter events, 0.0 us)
Async XLA Ops:
  8.2 6.1 %collective-permute-start.1 = (bf16[192,1024]{1,0:T(8,128)(2,1)}, bf16[192,1024]{1,0:T(8,128)(2,1)S(1)}, u32[]{:S(2)}, u32[]{:S(2)}) collective-permute-start(bf16[192,1024]{1,0:T(8,128)(2,1)} %get-tuple-element.18.own_ref), channel_id=1, source_target_pairs={{0,8},{8,0},{16,24},{24,16},{1,9},{9,1},{17,25},{25,17},{2,10},{10... | collective-permute-start | bytes 1179656 | tf_op jit(solution)/shard_map/ppermute | solution.py:512
  8.7 12.5 %collective-permute-start = (bf16[192,1024]{1,0:T(8,128)(2,1)}, bf16[192,1024]{1,0:T(8,128)(2,1)S(1)}, u32[]{:S(2)}, u32[]{:S(2)}) collective-permute-start(bf16[192,1024]{1,0:T(8,128)(2,1)} %get-tuple-element.18.own_ref), channel_id=1, source_target_pairs={{0,16},{8,24},{16,0},{24,8},{1,17},{9,25},{17,1},{25,9},{2,18},{10... | collective-permute-start | bytes 1179656 | tf_op jit(solution)/shard_map/ppermute | solution.py:512
  11.3 3.0 %copy-start = (bf16[192,1024]{1,0:T(8,128)(2,1)S(1)}, bf16[192,1024]{1,0:T(8,128)(2,1)}, u32[]{:S(2)}) copy-start(bf16[192,1024]{1,0:T(8,128)(2,1)} %get-tuple-element.18.own_ref) | copy-start | bytes 1179652
  14.3 1.1 %copy-start.2 = (bf16[1536,192]{1,0:T(8,128)(2,1)S(1)}, bf16[1536,192]{1,0:T(8,128)(2,1)}, u32[]{:S(2)}) copy-start(bf16[1536,192]{1,0:T(8,128)(2,1)} %get-tuple-element.19.weights_ref.refs_3_) | copy-start | bytes 1769476
  21.2 1.7 %collective-permute-start.2 = (bf16[192,1024]{1,0:T(8,128)(2,1)S(1)}, bf16[192,1024]{1,0:T(8,128)(2,1)S(1)}, u32[]{:S(2)}, u32[]{:S(2)}) collective-permute-start(bf16[192,1024]{1,0:T(8,128)(2,1)S(1)} %collective-permute-done.refs_0_), channel_id=1, source_target_pairs={{0,8},{8,0},{16,24},{24,16},{1,9},{9,1},{17,25},{25,17},{2,10},{10... | collective-permute-start | bytes 1179656 | tf_op jit(solution)/shard_map/ppermute | solution.py:512
  21.2 1.7 %copy-start.1 = (bf16[768,192]{0,1:T(8,128)(2,1)S(1)}, bf16[768,192]{0,1:T(8,128)(2,1)}, u32[]{:S(2)}) copy-start(bf16[768,192]{0,1:T(8,128)(2,1)} %param.28) | copy-start | bytes 884740
  21.2 1.7 %copy-start.3 = (bf16[192,1024]{1,0:T(8,128)(2,1)S(1)}, bf16[192,1024]{1,0:T(8,128)(2,1)}, u32[]{:S(2)}) copy-start(bf16[192,1024]{1,0:T(8,128)(2,1)} %get-tuple-element.24.refs_4_) | copy-start | bytes 1179652
  21.2 1.7 %copy-start.4 = (f32[192,128]{1,0:T(8,128)S(1)}, f32[192,128]{1,0:T(8,128)}, u32[]{:S(2)}) copy-start(f32[192,128]{1,0:T(8,128)} %get-tuple-element.25.refs_5_) | copy-start | bytes 294916
  21.2 1.7 %copy-start.5 = (bf16[16,1024]{1,0:T(8,128)(2,1)S(1)}, bf16[16,1024]{1,0:T(8,128)(2,1)}, u32[]{:S(2)}) copy-start(bf16[16,1024]{1,0:T(8,128)(2,1)} %get-tuple-element.26.refs_7_) | copy-start | bytes 98308
  27.6 5.2 %collective-permute-start.3 = (bf16[2,200,128]{2,1,0:T(8,128)(2,1)S(1)}, bf16[2,200,128]{2,1,0:T(8,128)(2,1)S(1)}, u32[]{:S(2)}, u32[]{:S(2)}) collective-permute-start(bf16[2,200,128]{2,1,0:T(8,128)(2,1)S(1)} %get-tuple-element.29), channel_id=1, source_target_pairs={{0,1},{1,0},{2,3},{3,2},{4,5},{5,4},{6,7},{7,6},{8,9},{9,8},{10,11... | collective-permute-start | bytes 307208 | tf_op jit(solution)/shard_map/ppermute | solution.py:512
  29.5 5.7 %collective-permute-start.4 = (bf16[2,200,128]{2,1,0:T(8,128)(2,1)S(1)}, bf16[2,200,128]{2,1,0:T(8,128)(2,1)S(1)}, u32[]{:S(2)}, u32[]{:S(2)}) collective-permute-start(bf16[2,200,128]{2,1,0:T(8,128)(2,1)S(1)} %get-tuple-element.30), channel_id=1, source_target_pairs={{0,2},{1,3},{2,0},{3,1},{4,6},{5,7},{6,4},{7,5},{8,10},{9,11},{10,... | collective-permute-start | bytes 307208 | tf_op jit(solution)/shard_map/ppermute | solution.py:512
  31.0 5.6 %collective-permute-start.5 = (bf16[2,200,128]{2,1,0:T(8,128)(2,1)S(1)}, bf16[2,200,128]{2,1,0:T(8,128)(2,1)S(1)}, u32[]{:S(2)}, u32[]{:S(2)}) collective-permute-start(bf16[2,200,128]{2,1,0:T(8,128)(2,1)S(1)} %get-tuple-element.31), channel_id=1, source_target_pairs={{0,3},{1,2},{2,1},{3,0},{4,7},{5,6},{6,5},{7,4},{8,11},{9,10},{10,... | collective-permute-start | bytes 307208 | tf_op jit(solution)/shard_map/ppermute | solution.py:512
  37.0 6.6 %collective-permute-start.6 = (bf16[192,256]{1,0:T(8,128)(2,1)S(1)}, bf16[192,256]{1,0:T(8,128)(2,1)S(1)}, u32[]{:S(2)}, u32[]{:S(2)}) collective-permute-start(bf16[192,256]{1,0:T(8,128)(2,1)S(1)} %get-tuple-element.33), channel_id=1, source_target_pairs={{0,4},{1,5},{2,6},{3,7},{4,0},{5,1},{6,2},{7,3},{8,12},{9,13},{10,... | collective-permute-start | bytes 294920 | tf_op jit(solution)/shard_map/ppermute | solution.py:512

commit v14 on v13

--- a/solution.py
+++ b/solution.py
@@ -124,7 +124,7 @@
 def first_kernel(
     run, count_ref, nodes_hbm, ids_hbm, pos_hbm, gain_one_hbm, gain_two_hbm, qkv_hbm, out_hbm,
     first_hbm, sent_hbm, nodes_ref, ids_ref, pos_ref, gain_one_ref, gain_two_ref, qkv_ref, out_ref,
-    sems, qkv_s, q_s, k_s, v_s, ctx_s, n_s, first_s, sent_s, stores
+    sems, qkv_s, q_s, k_s, v_s, n_s, first_s, sent_s, stores
 ):
     loads = start_all(
         [
@@ -181,7 +181,7 @@
     wide_window = iota((WIN, LANES), 1) // WIN
     rank = iota((WIN, LANES), 0) + WIN * (iota((WIN, LANES), 1) // WIN)
 
-    def group(t, _):
+    def group(t):
         query = q_s[t]
         even, odd = None, None
         for w in range(per):
@@ -221,24 +221,21 @@
                 block = got[n * size : (n + 1) * size, tile(n)].reshape(-1, 8, LANES)
                 block = block * inverse[2 * m + n][None]
                 parts.append(block.reshape(size, LANES))
-        ctx_s[t] = jnp.concatenate(parts, 0).astype(BF16)
-        return 0
-
-    lax.fori_loop(0, tiles, group, 0, unroll=8)
-    ctx = jnp.concatenate([ctx_s[t] for t in range(tiles)], 1)
-    moved = dot(out_t, ctx)
+        return jnp.concatenate(parts, 0).astype(BF16)
+
+    inside = within(run)
+    placed = []
     for t in range(tiles):
         at = tile(t)
-        first = (nodes_ref[:, at].astype(F32) + moved[:, at]).astype(BF16)
+        first = (nodes_ref[:, at].astype(F32) + dot(out_t, group(t))).astype(BF16)
         first_s[:, at] = first
         normed = norm_t(first.astype(F32), cols[:, 4:5])
         kept = iota((1, LANES), 1) + t * LANES < count
         head = jnp.where((iota((16, LANES), 0) > 0) | kept, normed[:16], FLAG)
-        n_s[:, at] = jnp.concatenate([head, normed[16:]], 0).astype(BF16)
+        placed.append(dot(jnp.concatenate([head, normed[16:]], 0).astype(BF16), inside))
     keep_first = pltpu.make_async_copy(first_s, first_hbm, stores.at[0])
     keep_first.start()
-    inside = within(run)
-    for t, block in enumerate(swap_blocks([dot(n_s[:, tile(t)], inside) for t in range(tiles)])):
+    for t, block in enumerate(swap_blocks(placed)):
         sent_s[:, tile(t)] = block.astype(BF16)
     send = pltpu.make_async_copy(sent_s, sent_hbm, stores.at[1])
     send.start()
@@ -247,7 +244,7 @@
 
 def tables_kernel(
     cap, qkv_hbm, out_hbm, up_hbm, slot_hbm, owner_hbm, voxel_hbm, gain_hbm, weights_s, facts_s,
-    gain_s, qkv_ref, out_ref, up_ref, slot_ref, owner_ref, voxel_ref, gain_ref, sems
+    gain_s, hot_s, qkv_ref, out_ref, up_ref, slot_ref, owner_ref, voxel_ref, gain_ref, sems
 ):
     loads = start_all(
         [
@@ -289,7 +286,10 @@
         jnp.where(row == 1, slot // LANES, jnp.where(row == 2, slot % LANES, 1)),
     )
     listed = dot_t(facts.astype(F32).astype(BF16), member)
-    facts_s[...] = jnp.where(listed[3:4] > 0.5, listed, -1.0).astype(BF16)
+    facts = jnp.where(listed[3:4] > 0.5, listed, -1.0)
+    facts_s[...] = facts.astype(BF16)
+    low, high = facts[2:3].astype(jnp.int32), facts[1:2].astype(jnp.int32)
+    hot_s[...] = place(low, high, hot_s.shape[0] // LANES)
 
 
 def clean(block):
@@ -420,9 +420,9 @@
 
 def second_kernel(run, cap, far, owners, count_ref, *refs):
     blocks, refs = refs[:far], refs[far:]
-    q_s, state_s, weights_s, first_s, gain_s, down_s, facts_s, feat_hbm = refs[:8]
-    votes_s, refs = refs[8 : 8 + owners // 2], refs[8 + owners // 2 :]
-    feat_s, store, k_s, v_s, m_s, s_s, ctx_s, bf_s, inner_s = refs
+    q_s, state_s, weights_s, first_s, gain_s, down_s, facts_s, hot_s, feat_hbm = refs[:9]
+    votes_s, refs = refs[9 : 9 + owners // 2], refs[9 + owners // 2 :]
+    feat_s, store, k_s, v_s, m_s, s_s, ctx_s, bf_s = refs
     chans, slots = first_s.shape
     tiles = slots // LANES
     count = count_ref[0]
@@ -444,21 +444,26 @@
     ctx = dot_t(jnp.concatenate(ctx, 0).astype(BF16), within(run)).astype(BF16)
     ctx = jnp.concatenate([ctx[t * chans : (t + 1) * chans] for t in range(tiles)], 1)
     gain = gain_s[...]
-    moved = dot(weights_s[3 * chans : 4 * chans], ctx)
-    for t in range(tiles):
-        at = tile(t)
-        second = first_s[:, at].astype(F32) + moved[:, at]
-        feat_s[:, at] = second
-        inner_s[:, at] = norm_t(second, gain).astype(BF16)
     kept = iota((1, slots), 1) < count
     wide = 2 * LANES
     cuts = [slice(at, at + wide) for at in range(0, slots, wide)]
-    up_t = weights_s[4 * chans :]
-    raised = dot(up_t, inner_s[:, cuts[0]])
+    out_t, up_t = weights_s[3 * chans : 4 * chans], weights_s[4 * chans :]
+
+    def raise_chunk(at):
+        moved = dot(out_t, ctx[:, at])
+        inner = []
+        for n in range(wide // LANES):
+            lanes = slice(at.start + n * LANES, at.start + (n + 1) * LANES)
+            second = first_s[:, lanes].astype(F32) + moved[:, tile(n)]
+            feat_s[:, lanes] = second
+            inner.append(norm_t(second, gain).astype(BF16))
+        return dot(up_t, jnp.concatenate(inner, 1))
+
+    raised = raise_chunk(cuts[0])
     for n, at in enumerate(cuts):
         now = raised
         if n + 1 < len(cuts):
-            raised = dot(up_t, inner_s[:, cuts[n + 1]])
+            raised = raise_chunk(cuts[n + 1])
         hidden = gelu(now).astype(BF16)
         third = feat_s[:, at] + dot(down_s[...], hidden)
         third = jnp.where(kept[:, at], third, 0.0)
@@ -466,9 +471,7 @@
         bf_s[:, at] = third.astype(BF16)
     keep = pltpu.make_async_copy(feat_s, feat_hbm, store)
     keep.start()
-    facts = facts_s[...].astype(F32)
-    low, high = facts[2:3].astype(jnp.int32), facts[1:2].astype(jnp.int32)
-    picked = dot(bf_s[...], place(low, high, tiles)).astype(BF16)
+    picked = dot(bf_s[...], hot_s[...]).astype(BF16)
     for o in range(owners):
         at = slice(o * cap, (o + 1) * cap)
         ballot = jnp.concatenate([picked[:, at], facts_s[:8, at]], 0)
@@ -560,7 +563,6 @@
             vmem((tiles, chans, 2 * LANES), BF16),
             vmem((tiles, LANES, chans), BF16),
             vmem((tiles, chans, LANES), BF16),
-            vmem((tiles, chans, LANES), BF16),
             vmem((chans, slots), BF16),
             vmem((chans, slots), BF16),
             vmem((chans, slots), BF16),
@@ -585,12 +587,13 @@
         mid += [turned(block, "grp", bit) for block in [sent] + mid]
         bit //= 2
     near = turned(sent, "grp", 1)
-    weights, facts, gain = call(
+    weights, facts, gain, hot = call(
         functools.partial(tables_kernel, cap),
         [
             sds((4 * chans + hidden, chans), BF16),
             sds((16, codes), BF16),
             sds((chans, LANES), F32),
+            sds((slots, codes), BF16),
         ],
         [
             vmem((chans, 3 * chans), BF16),
@@ -604,7 +607,7 @@
         ],
         2_000_000_000,
         "aaaaaaa",
-        "vvv",
+        "vvvv",
         limit=TIGHT,
     )(
         qkv_two,
@@ -651,9 +654,9 @@
         [sds((chans, slots), F32)] + [sds((2, chans + 8, cap), BF16)] * (owners // 2),
         [vmem((chans, slots), F32), dma]
         + key_scratch(len(far))
-        + [vmem(*q_like), vmem((chans, slots), BF16), vmem((chans, slots), BF16)],
+        + [vmem(*q_like), vmem((chans, slots), BF16)],
         3_000_000_000,
-        "s" + "v" * (len(far) + 7),
+        "s" + "v" * (len(far) + 8),
         "a" + "v" * (owners // 2),
         limit=ROOMY,
     )(
@@ -666,6 +669,7 @@
         gain,
         w_down.T,
         facts,
+        hot,
     )
     half = owners // 2
     got = [ballots[0]] + [turned(ballots[k], "tile", k) for k in range(1, half)]

time: 44.5 us -> 47.2 us (1.061)
  Pallas kernels: 20 us -> 23.1 us
  waiting for transfers between devices: 12.5 us -> 12 us
    pallas_call x1, Pallas kernels: 6.91 us -> 8.98 us  [body(): call(functools.partial(first_kernel, run), [sds((chans, slots), BF16), sd...]
    pallas_call x1, Pallas kernels: 2.99 us -> 4 us  [body(): call(functools.partial(tables_kernel, cap), [sds((4 * chans + hidden, cha...]
    ppermute x7, waiting for transfers between devices: 12.5 us -> 12 us  [turned(): return lax.ppermute(x, axis, [(i, i ^ bit) for i in range(n)])]
    unnamed x12 -> x16, local copies, waits for them, and re-layouts: 1.15 us -> 1.16 us
  transfers between devices with their start and end apart: 7 -> 7, of which waited for: 6 -> 6; matrix products, arithmetic and copies ran while one was open for 0% -> 0% of each run, Pallas kernels for 17% -> 18%
where the time goes in v14:
time: 47.2 us; the launch traced here: 47 us
  Pallas kernels  23.1 us (49%)
  waiting for transfers between devices  12 us (25%)
  starting transfers between devices  9.29 us (20%)
  between operations  1.41 us (3%)
  local copies, waits for them, and re-layouts  1.16 us (2%)
    ppermute x7, waiting for transfers between devices, turned(): return lax.ppermute(x, axis, [(i, i ^ bit) for i in range(n)])  12 us
    ppermute x7, starting transfers between devices, turned(): return lax.ppermute(x, axis, [(i, i ^ bit) for i in range(n)])  9.29 us
    pallas_call x1, Pallas kernels, body(): call(functools.partial(first_kernel, run), [sds((chans, slots), BF16), sd...  8.98 us
    pallas_call x1, Pallas kernels, body(): call(functools.partial(second_kernel, run, cap, len(far), owners), [sds((...  4.74 us
    pallas_call x1, Pallas kernels, body(): call(functools.partial(tables_kernel, cap), [sds((4 * chans + hidden, cha...  4 us
    pallas_call x1, Pallas kernels, body(): call(functools.partial(near_kernel, run), [sds(*q_like), sds(*state_like)...  2.94 us
    pallas_call x1, Pallas kernels, body(): call(functools.partial(middle_kernel, run, len(mid)), [sds(*state_like)],...  1.42 us
    unnamed x16, local copies, waits for them, and re-layouts  1.16 us
  transfers between devices with their start and end apart: 7, of which 6 were waited for; matrix products, arithmetic and copies ran while one was open for 0% of the time, Pallas kernels for 18%

profile of v14, /device:TPU:0, one launch (start us, length us, event | category | flops | bytes accessed | tf_op | source)
XLA Modules:
  0.0 47.0 jit_solution(17724454819457790949)
XLA Ops:
  1.3 9.0 %shard_map.167 = (bf16[192,1024]{1,0:T(8,128)(2,1)}, bf16[192,1024]{1,0:T(8,128)(2,1)}) custom-call(s32[1]{0:T(128)S(6)} %copy.18.count_ref, bf16[192,1024]{1,0:T(8,128)(2,1)} %bitcast.13, s32[1,1024]{1,0:T(1,128)} %bitcast.14, f32[3,192]{1,0:T(4,128)} %pos_hbm.1, f32[1,192]{1,0:T(1,128)} %bitcast.18, f32[1,192]{1,0:T(1,128)} %bitcast.19, ...), custom_call_target="tpu_custom_call" | custom-call | flops 2000000000 | bytes 2097152 | tf_op jit(solution)/shard_map/pallas_call | solution.py:550
  10.3 0.5 %collective-permute-start.1 = (bf16[192,1024]{1,0:T(8,128)(2,1)}, bf16[192,1024]{1,0:T(8,128)(2,1)S(1)}, u32[]{:S(2)}, u32[]{:S(2)}) collective-permute-start(bf16[192,1024]{1,0:T(8,128)(2,1)} %get-tuple-element.19.own_ref), channel_id=1, source_target_pairs={{0,8},{8,0},{16,24},{24,16},{1,9},{9,1},{17,25},{25,17},{2,10},{10... | collective-permute-start | bytes 1179656 | tf_op jit(solution)/shard_map/ppermute | solution.py:515
  10.8 2.6 %collective-permute-start = (bf16[192,1024]{1,0:T(8,128)(2,1)}, bf16[192,1024]{1,0:T(8,128)(2,1)S(1)}, u32[]{:S(2)}, u32[]{:S(2)}) collective-permute-start(bf16[192,1024]{1,0:T(8,128)(2,1)} %get-tuple-element.19.own_ref), channel_id=1, source_target_pairs={{0,16},{8,24},{16,0},{24,8},{1,17},{9,25},{17,1},{25,9},{2,18},{10... | collective-permute-start | bytes 1179656 | tf_op jit(solution)/shard_map/ppermute | solution.py:515
  13.4 4.0 %shard_map.168 = (bf16[1536,192]{1,0:T(8,128)(2,1)}, bf16[16,1024]{1,0:T(8,128)(2,1)}, f32[192,128]{1,0:T(8,128)}, bf16[1024,1024]{1,0:T(8,128)(2,1)}) custom-call(bf16[192,576]{1,0:T(8,128)(2,1)} %qkv_hbm.3, bf16[192,192]{1,0:T(8,128)(2,1)} %out_hbm.3, bf16[192,768]{1,0:T(8,128)(2,1)} %up_hbm.1, s32[1,512]{1,0:T(1,128)} %bitcast.15, s32[1,512]{1,0:T(1,128)} %bitcast.16, ...), custom_call_target="tpu_custom_call" | custom-call | flops 2000000000 | bytes 2097152 | tf_op jit(solution)/shard_map/pallas_call | solution.py:590
  17.4 0.0 collective-permute-done.1.near_ref
  17.4 0.0 copy-done
  17.4 0.0 copy-start.3
  17.4 1.1 %copy-done.3 = bf16[1536,192]{1,0:T(8,128)(2,1)S(1)} copy-done((bf16[1536,192]{1,0:T(8,128)(2,1)S(1)}, bf16[1536,192]{1,0:T(8,128)(2,1)}, u32[]{:S(2)}) %copy-start.3) | copy-done | bytes 589848
  18.5 2.9 %shard_map.169 = (f32[8,24,8,128]{3,2,1,0:T(8,128)S(1)}, f32[8,28,8,128]{3,2,1,0:T(8,128)S(1)}) custom-call(bf16[192,1024]{1,0:T(8,128)(2,1)S(1)} %copy-done, bf16[192,1024]{1,0:T(8,128)(2,1)S(1)} %collective-permute-done.1.near_ref, bf16[1536,192]{1,0:T(8,128)(2,1)S(1)} %copy-done.3), custom_call_target="tpu_custom_call" | custom-call | flops 3000000000 | bytes 2097152 | tf_op jit(solution)/shard_map/pallas_call | solution.py:632
  21.5 1.8 %collective-permute-done.refs_0_ = bf16[192,1024]{1,0:T(8,128)(2,1)S(1)} collective-permute-done((bf16[192,1024]{1,0:T(8,128)(2,1)}, bf16[192,1024]{1,0:T(8,128)(2,1)S(1)}, u32[]{:S(2)}, u32[]{:S(2)}) %collective-permute-start) | collective-permute-done | bytes 393248 | tf_op jit(solution)/shard_map/ppermute | solution.py:515
  23.3 0.0 collective-permute-start.2
  23.3 0.0 copy-done.4
  23.3 0.0 copy-start.2
  23.3 0.0 copy-start.5
  23.3 0.0 copy-start.6
  23.3 0.0 copy-start.7
  23.3 1.4 %shard_map.170.refs_2_ = f32[8,28,8,128]{3,2,1,0:T(8,128)S(1)} custom-call(bf16[192,1024]{1,0:T(8,128)(2,1)S(1)} %collective-permute-done.refs_0_, f32[8,24,8,128]{3,2,1,0:T(8,128)S(1)} %get-tuple-element.23.refs_1_, f32[8,28,8,128]{3,2,1,0:T(8,128)S(1)} %get-tuple-element.24.refs_2_, bf16[1536,192]{1,0:T(8,128)(2,1)S(1)} %copy-done.4), custom_call_target="tpu_custom_call" | custom-call | flops 2000000000 | bytes 2097152 | tf_op jit(solution)/shard_map/pallas_call | solution.py:643
  24.7 0.2 collective-permute-done.2.refs_0_
  25.0 0.0 copy-done.1
  25.0 0.0 copy-done.2
  25.0 0.0 copy-done.6
  25.0 4.7 %shard_map.171 = (f32[192,1024]{1,0:T(8,128)}, bf16[2,200,128]{2,1,0:T(8,128)(2,1)S(1)}, bf16[2,200,128]{2,1,0:T(8,128)(2,1)S(1)}, bf16[2,200,128]{2,1,0:T(8,128)(2,1)S(1)}, bf16[2,200,128]{2,1,0:T(8,128)(2,1)S(1)}) custom-call(s32[1]{0:T(128)S(6)} %copy.18.count_ref, bf16[192,1024]{1,0:T(8,128)(2,1)S(1)} %collective-permute-done.2.refs_0_, ...), custom_call_target="tpu_custom_call" | custom-call | flops 3000000000 | bytes 2097152 | tf_op jit(solution)/shard_map/pallas_call | solution.py:652
  29.8 1.9 %collective-permute-start.3 = (bf16[2,200,128]{2,1,0:T(8,128)(2,1)S(1)}, bf16[2,200,128]{2,1,0:T(8,128)(2,1)S(1)}, u32[]{:S(2)}, u32[]{:S(2)}) collective-permute-start(bf16[2,200,128]{2,1,0:T(8,128)(2,1)S(1)} %get-tuple-element.31), channel_id=1, source_target_pairs={{0,1},{1,0},{2,3},{3,2},{4,5},{5,4},{6,7},{7,6},{8,9},{9,8},{10,11... | collective-permute-start | bytes 307208 | tf_op jit(solution)/shard_map/ppermute | solution.py:515
  31.6 1.6 %collective-permute-start.4 = (bf16[2,200,128]{2,1,0:T(8,128)(2,1)S(1)}, bf16[2,200,128]{2,1,0:T(8,128)(2,1)S(1)}, u32[]{:S(2)}, u32[]{:S(2)}) collective-permute-start(bf16[2,200,128]{2,1,0:T(8,128)(2,1)S(1)} %get-tuple-element.32), channel_id=1, source_target_pairs={{0,2},{1,3},{2,0},{3,1},{4,6},{5,7},{6,4},{7,5},{8,10},{9,11},{10,... | collective-permute-start | bytes 307208 | tf_op jit(solution)/shard_map/ppermute | solution.py:515
  33.2 0.1 collective-permute-start.5
  33.3 1.8 %collective-permute-done.3.refs_1_ = bf16[2,200,128]{2,1,0:T(8,128)(2,1)S(1)} collective-permute-done((bf16[2,200,128]{2,1,0:T(8,128)(2,1)S(1)}, bf16[2,200,128]{2,1,0:T(8,128)(2,1)S(1)}, u32[]{:S(2)}, u32[]{:S(2)}) %collective-permute-start.3) | collective-permute-done | bytes 102432 | tf_op jit(solution)/shard_map/ppermute | solution.py:515
  35.2 2.2 %collective-permute-done.4.refs_2_ = bf16[2,200,128]{2,1,0:T(8,128)(2,1)S(1)} collective-permute-done((bf16[2,200,128]{2,1,0:T(8,128)(2,1)S(1)}, bf16[2,200,128]{2,1,0:T(8,128)(2,1)S(1)}, u32[]{:S(2)}, u32[]{:S(2)}) %collective-permute-start.4) | collective-permute-done | bytes 102432 | tf_op jit(solution)/shard_map/ppermute | solution.py:515
  37.4 1.5 %collective-permute-done.5.refs_3_ = bf16[2,200,128]{2,1,0:T(8,128)(2,1)S(1)} collective-permute-done((bf16[2,200,128]{2,1,0:T(8,128)(2,1)S(1)}, bf16[2,200,128]{2,1,0:T(8,128)(2,1)S(1)}, u32[]{:S(2)}, u32[]{:S(2)}) %collective-permute-start.5) | collective-permute-done | bytes 102432 | tf_op jit(solution)/shard_map/ppermute | solution.py:515
  38.8 0.4 shard_map.172
  39.2 2.7 %collective-permute-start.6 = (bf16[192,256]{1,0:T(8,128)(2,1)S(1)}, bf16[192,256]{1,0:T(8,128)(2,1)S(1)}, u32[]{:S(2)}, u32[]{:S(2)}) collective-permute-start(bf16[192,256]{1,0:T(8,128)(2,1)S(1)} %get-tuple-element.35), channel_id=1, source_target_pairs={{0,4},{1,5},{2,6},{3,7},{4,0},{5,1},{6,2},{7,3},{8,12},{9,13},{10,... | collective-permute-start | bytes 294920 | tf_op jit(solution)/shard_map/ppermute | solution.py:515
  41.8 4.4 %collective-permute-done.6.there_ref = bf16[192,256]{1,0:T(8,128)(2,1)S(1)} collective-permute-done((bf16[192,256]{1,0:T(8,128)(2,1)S(1)}, bf16[192,256]{1,0:T(8,128)(2,1)S(1)}, u32[]{:S(2)}, u32[]{:S(2)}) %collective-permute-start.6) | collective-permute-done | bytes 98336 | tf_op jit(solution)/shard_map/ppermute | solution.py:515
  46.3 0.7 %shard_map.173 = f32[192,256]{1,0:T(8,128)} custom-call(f32[192,256]{1,0:T(8,128)S(1)} %get-tuple-element.34.here_ref, bf16[192,256]{1,0:T(8,128)(2,1)S(1)} %collective-permute-done.6.there_ref), custom_call_target="tpu_custom_call" | custom-call | flops 1000000 | bytes 2097152 | tf_op jit(solution)/shard_map/pallas_call | solution.py:685
  (5 shorter events, 0.0 us)
Async XLA Ops:
  10.3 7.1 %collective-permute-start.1 = (bf16[192,1024]{1,0:T(8,128)(2,1)}, bf16[192,1024]{1,0:T(8,128)(2,1)S(1)}, u32[]{:S(2)}, u32[]{:S(2)}) collective-permute-start(bf16[192,1024]{1,0:T(8,128)(2,1)} %get-tuple-element.19.own_ref), channel_id=1, source_target_pairs={{0,8},{8,0},{16,24},{24,16},{1,9},{9,1},{17,25},{25,17},{2,10},{10... | collective-permute-start | bytes 1179656 | tf_op jit(solution)/shard_map/ppermute | solution.py:515
  10.8 12.5 %collective-permute-start = (bf16[192,1024]{1,0:T(8,128)(2,1)}, bf16[192,1024]{1,0:T(8,128)(2,1)S(1)}, u32[]{:S(2)}, u32[]{:S(2)}) collective-permute-start(bf16[192,1024]{1,0:T(8,128)(2,1)} %get-tuple-element.19.own_ref), channel_id=1, source_target_pairs={{0,16},{8,24},{16,0},{24,8},{1,17},{9,25},{17,1},{25,9},{2,18},{10... | collective-permute-start | bytes 1179656 | tf_op jit(solution)/shard_map/ppermute | solution.py:515
  13.4 4.0 %copy-start = (bf16[192,1024]{1,0:T(8,128)(2,1)S(1)}, bf16[192,1024]{1,0:T(8,128)(2,1)}, u32[]{:S(2)}) copy-start(bf16[192,1024]{1,0:T(8,128)(2,1)} %get-tuple-element.19.own_ref) | copy-start | bytes 1179652
  17.4 1.1 %copy-start.3 = (bf16[1536,192]{1,0:T(8,128)(2,1)S(1)}, bf16[1536,192]{1,0:T(8,128)(2,1)}, u32[]{:S(2)}) copy-start(bf16[1536,192]{1,0:T(8,128)(2,1)} %get-tuple-element.20.weights_ref.refs_3_) | copy-start | bytes 1769476
  18.5 4.8 %copy-start.4 = (bf16[1536,192]{1,0:T(8,128)(2,1)S(1)}, bf16[1536,192]{1,0:T(8,128)(2,1)}, u32[]{:S(2)}) copy-start(bf16[1536,192]{1,0:T(8,128)(2,1)} %get-tuple-element.20.weights_ref.refs_3_) | copy-start | bytes 1769476
  23.3 1.7 %collective-permute-start.2 = (bf16[192,1024]{1,0:T(8,128)(2,1)S(1)}, bf16[192,1024]{1,0:T(8,128)(2,1)S(1)}, u32[]{:S(2)}, u32[]{:S(2)}) collective-permute-start(bf16[192,1024]{1,0:T(8,128)(2,1)S(1)} %collective-permute-done.refs_0_), channel_id=1, source_target_pairs={{0,8},{8,0},{16,24},{24,16},{1,9},{9,1},{17,25},{25,17},{2,10},{10... | collective-permute-start | bytes 1179656 | tf_op jit(solution)/shard_map/ppermute | solution.py:515
  23.3 1.7 %copy-start.1 = (bf16[768,192]{0,1:T(8,128)(2,1)S(1)}, bf16[768,192]{0,1:T(8,128)(2,1)}, u32[]{:S(2)}) copy-start(bf16[768,192]{0,1:T(8,128)(2,1)} %param.28) | copy-start | bytes 884740
  23.3 1.7 %copy-start.2 = (bf16[1024,1024]{1,0:T(8,128)(2,1)S(1)}, bf16[1024,1024]{1,0:T(8,128)(2,1)}, u32[]{:S(2)}) copy-start(bf16[1024,1024]{1,0:T(8,128)(2,1)} %get-tuple-element.28.refs_8_) | copy-start | bytes 6291460
  23.3 1.7 %copy-start.5 = (bf16[192,1024]{1,0:T(8,128)(2,1)S(1)}, bf16[192,1024]{1,0:T(8,128)(2,1)}, u32[]{:S(2)}) copy-start(bf16[192,1024]{1,0:T(8,128)(2,1)} %get-tuple-element.25.refs_4_) | copy-start | bytes 1179652
  23.3 1.7 %copy-start.6 = (f32[192,128]{1,0:T(8,128)S(1)}, f32[192,128]{1,0:T(8,128)}, u32[]{:S(2)}) copy-start(f32[192,128]{1,0:T(8,128)} %get-tuple-element.26.refs_5_) | copy-start | bytes 294916
  23.3 1.7 %copy-start.7 = (bf16[16,1024]{1,0:T(8,128)(2,1)S(1)}, bf16[16,1024]{1,0:T(8,128)(2,1)}, u32[]{:S(2)}) copy-start(bf16[16,1024]{1,0:T(8,128)(2,1)} %get-tuple-element.27.refs_7_) | copy-start | bytes 98308
  29.8 5.4 %collective-permute-start.3 = (bf16[2,200,128]{2,1,0:T(8,128)(2,1)S(1)}, bf16[2,200,128]{2,1,0:T(8,128)(2,1)S(1)}, u32[]{:S(2)}, u32[]{:S(2)}) collective-permute-start(bf16[2,200,128]{2,1,0:T(8,128)(2,1)S(1)} %get-tuple-element.31), channel_id=1, source_target_pairs={{0,1},{1,0},{2,3},{3,2},{4,5},{5,4},{6,7},{7,6},{8,9},{9,8},{10,11... | collective-permute-start | bytes 307208 | tf_op jit(solution)/shard_map/ppermute | solution.py:515
  31.6 5.7 %collective-permute-start.4 = (bf16[2,200,128]{2,1,0:T(8,128)(2,1)S(1)}, bf16[2,200,128]{2,1,0:T(8,128)(2,1)S(1)}, u32[]{:S(2)}, u32[]{:S(2)}) collective-permute-start(bf16[2,200,128]{2,1,0:T(8,128)(2,1)S(1)} %get-tuple-element.32), channel_id=1, source_target_pairs={{0,2},{1,3},{2,0},{3,1},{4,6},{5,7},{6,4},{7,5},{8,10},{9,11},{10,... | collective-permute-start | bytes 307208 | tf_op jit(solution)/shard_map/ppermute | solution.py:515
  33.2 5.6 %collective-permute-start.5 = (bf16[2,200,128]{2,1,0:T(8,128)(2,1)S(1)}, bf16[2,200,128]{2,1,0:T(8,128)(2,1)S(1)}, u32[]{:S(2)}, u32[]{:S(2)}) collective-permute-start(bf16[2,200,128]{2,1,0:T(8,128)(2,1)S(1)} %get-tuple-element.33), channel_id=1, source_target_pairs={{0,3},{1,2},{2,1},{3,0},{4,7},{5,6},{6,5},{7,4},{8,11},{9,10},{10,... | collective-permute-start | bytes 307208 | tf_op jit(solution)/shard_map/ppermute | solution.py:515
  39.2 7.1 %collective-permute-start.6 = (bf16[192,256]{1,0:T(8,128)(2,1)S(1)}, bf16[192,256]{1,0:T(8,128)(2,1)S(1)}, u32[]{:S(2)}, u32[]{:S(2)}) collective-permute-start(bf16[192,256]{1,0:T(8,128)(2,1)S(1)} %get-tuple-element.35), channel_id=1, source_target_pairs={{0,4},{1,5},{2,6},{3,7},{4,0},{5,1},{6,2},{7,3},{8,12},{9,13},{10,... | collective-permute-start | bytes 294920 | tf_op jit(solution)/shard_map/ppermute | solution.py:515

commit v15 on v13

--- a/solution.py
+++ b/solution.py
@@ -124,7 +124,7 @@
 def first_kernel(
     run, count_ref, nodes_hbm, ids_hbm, pos_hbm, gain_one_hbm, gain_two_hbm, qkv_hbm, out_hbm,
     first_hbm, sent_hbm, nodes_ref, ids_ref, pos_ref, gain_one_ref, gain_two_ref, qkv_ref, out_ref,
-    sems, qkv_s, q_s, k_s, v_s, ctx_s, n_s, first_s, sent_s, stores
+    sems, qkv_s, q_s, k_s, v_s, ctx_s, n_s, stack_s, first_s, sent_s, stores
 ):
     loads = start_all(
         [
@@ -166,15 +166,19 @@
     qkv_t = transposed(qkv_ref[...])
     out_t = transposed(out_ref[...])
     qkv_s[...] = dot(qkv_t, n_s[...]).astype(BF16)
-    side = eye(LANES)
+    side = eye(2 * LANES)
     row_head = iota((chans, LANES), 0) // size
     even_row = row_head % 2 == 0
     for t in range(tiles):
         query = qkv_s[:chans, tile(t)].astype(F32) * size**-0.5
         q_s[t, :, :LANES] = jnp.where(even_row, query, 0.0).astype(BF16)
         q_s[t, :, LANES:] = jnp.where(even_row, 0.0, query).astype(BF16)
-        k_s[t] = dot_t(side, qkv_s[chans : 2 * chans, tile(t)]).astype(BF16)
         v_s[t] = qkv_s[2 * chans :, tile(t)]
+    for t in range(0, tiles, 2):
+        keys = qkv_s[chans : 2 * chans, t * LANES : (t + 2) * LANES]
+        rows = dot_t(side, keys).astype(BF16)
+        k_s[t] = rows[:LANES]
+        k_s[t + 1] = rows[LANES:]
 
     lane_pair = iota((WIN, chans), 1) // (2 * size)
     window = iota((8, LANES), 1) // WIN
@@ -234,12 +238,13 @@
         normed = norm_t(first.astype(F32), cols[:, 4:5])
         kept = iota((1, LANES), 1) + t * LANES < count
         head = jnp.where((iota((16, LANES), 0) > 0) | kept, normed[:16], FLAG)
-        n_s[:, at] = jnp.concatenate([head, normed[16:]], 0).astype(BF16)
+        stack_s[t * chans : (t + 1) * chans] = jnp.concatenate([head, normed[16:]], 0).astype(BF16)
     keep_first = pltpu.make_async_copy(first_s, first_hbm, stores.at[0])
     keep_first.start()
-    inside = within(run)
-    for t, block in enumerate(swap_blocks([dot(n_s[:, tile(t)], inside) for t in range(tiles)])):
-        sent_s[:, tile(t)] = block.astype(BF16)
+    moved = dot(stack_s[...], within(run))
+    moved = swap_blocks([moved[t * chans : (t + 1) * chans] for t in range(tiles)])
+    for t in range(tiles):
+        sent_s[:, tile(t)] = moved[t].astype(BF16)
     send = pltpu.make_async_copy(sent_s, sent_hbm, stores.at[1])
     send.start()
     wait_all([keep_first, send])
@@ -247,7 +252,7 @@
 
 def tables_kernel(
     cap, qkv_hbm, out_hbm, up_hbm, slot_hbm, owner_hbm, voxel_hbm, gain_hbm, weights_s, facts_s,
-    gain_s, qkv_ref, out_ref, up_ref, slot_ref, owner_ref, voxel_ref, gain_ref, sems
+    gain_s, hot_s, qkv_ref, out_ref, up_ref, slot_ref, owner_ref, voxel_ref, gain_ref, sems
 ):
     loads = start_all(
         [
@@ -289,7 +294,10 @@
         jnp.where(row == 1, slot // LANES, jnp.where(row == 2, slot % LANES, 1)),
     )
     listed = dot_t(facts.astype(F32).astype(BF16), member)
-    facts_s[...] = jnp.where(listed[3:4] > 0.5, listed, -1.0).astype(BF16)
+    facts = jnp.where(listed[3:4] > 0.5, listed, -1.0)
+    facts_s[...] = facts.astype(BF16)
+    low, high = facts[2:3].astype(jnp.int32), facts[1:2].astype(jnp.int32)
+    hot_s[...] = place(low, high, hot_s.shape[0] // LANES)
 
 
 def clean(block):
@@ -420,8 +428,8 @@
 
 def second_kernel(run, cap, far, owners, count_ref, *refs):
     blocks, refs = refs[:far], refs[far:]
-    q_s, state_s, weights_s, first_s, gain_s, down_s, facts_s, feat_hbm = refs[:8]
-    votes_s, refs = refs[8 : 8 + owners // 2], refs[8 + owners // 2 :]
+    q_s, state_s, weights_s, first_s, gain_s, down_s, facts_s, hot_s, feat_hbm = refs[:9]
+    votes_s, refs = refs[9 : 9 + owners // 2], refs[9 + owners // 2 :]
     feat_s, store, k_s, v_s, m_s, s_s, ctx_s, bf_s, inner_s = refs
     chans, slots = first_s.shape
     tiles = slots // LANES
@@ -466,9 +474,7 @@
         bf_s[:, at] = third.astype(BF16)
     keep = pltpu.make_async_copy(feat_s, feat_hbm, store)
     keep.start()
-    facts = facts_s[...].astype(F32)
-    low, high = facts[2:3].astype(jnp.int32), facts[1:2].astype(jnp.int32)
-    picked = dot(bf_s[...], place(low, high, tiles)).astype(BF16)
+    picked = dot(bf_s[...], hot_s[...]).astype(BF16)
     for o in range(owners):
         at = slice(o * cap, (o + 1) * cap)
         ballot = jnp.concatenate([picked[:, at], facts_s[:8, at]], 0)
@@ -562,6 +568,7 @@
             vmem((tiles, chans, LANES), BF16),
             vmem((tiles, chans, LANES), BF16),
             vmem((chans, slots), BF16),
+            vmem((tiles * chans, LANES), BF16),
             vmem((chans, slots), BF16),
             vmem((chans, slots), BF16),
             dma((2,)),
@@ -585,12 +592,13 @@
         mid += [turned(block, "grp", bit) for block in [sent] + mid]
         bit //= 2
     near = turned(sent, "grp", 1)
-    weights, facts, gain = call(
+    weights, facts, gain, hot = call(
         functools.partial(tables_kernel, cap),
         [
             sds((4 * chans + hidden, chans), BF16),
             sds((16, codes), BF16),
             sds((chans, LANES), F32),
+            sds((slots, codes), BF16),
         ],
         [
             vmem((chans, 3 * chans), BF16),
@@ -604,7 +612,7 @@
         ],
         2_000_000_000,
         "aaaaaaa",
-        "vvv",
+        "vvvv",
         limit=TIGHT,
     )(
         qkv_two,
@@ -653,7 +661,7 @@
         + key_scratch(len(far))
         + [vmem(*q_like), vmem((chans, slots), BF16), vmem((chans, slots), BF16)],
         3_000_000_000,
-        "s" + "v" * (len(far) + 7),
+        "s" + "v" * (len(far) + 8),
         "a" + "v" * (owners // 2),
         limit=ROOMY,
     )(
@@ -666,6 +674,7 @@
         gain,
         w_down.T,
         facts,
+        hot,
     )
     half = owners // 2
     got = [ballots[0]] + [turned(ballots[k], "tile", k) for k in range(1, half)]

time: 44.5 us -> 44.9 us (level)
  Pallas kernels: 20 us -> 20.9 us
  waiting for transfers between devices: 12.5 us -> 11.9 us
    pallas_call x1, Pallas kernels: 2.99 us -> 4 us  [body(): call(functools.partial(tables_kernel, cap), [sds((4 * chans + hidden, cha...]
    ppermute x7, waiting for transfers between devices: 12.5 us -> 11.9 us  [turned(): return lax.ppermute(x, axis, [(i, i ^ bit) for i in range(n)])]
    unnamed x12 -> x16, local copies, waits for them, and re-layouts: 1.15 us -> 1.16 us
  transfers between devices with their start and end apart: 7 -> 7, of which waited for: 6 -> 6; matrix products, arithmetic and copies ran while one was open for 0% -> 0% of each run, Pallas kernels for 17% -> 19%
where the time goes in v15:
time: 44.9 us; the launch traced here: 44.7 us
  Pallas kernels  20.9 us (47%)
  waiting for transfers between devices  11.9 us (27%)
  starting transfers between devices  9.28 us (21%)
  between operations  1.41 us (3%)
  local copies, waits for them, and re-layouts  1.16 us (3%)
    ppermute x7, waiting for transfers between devices, turned(): return lax.ppermute(x, axis, [(i, i ^ bit) for i in range(n)])  11.9 us
    ppermute x7, starting transfers between devices, turned(): return lax.ppermute(x, axis, [(i, i ^ bit) for i in range(n)])  9.28 us
    pallas_call x1, Pallas kernels, body(): call(functools.partial(first_kernel, run), [sds((chans, slots), BF16), sd...  6.83 us
    pallas_call x1, Pallas kernels, body(): call(functools.partial(second_kernel, run, cap, len(far), owners), [sds((...  4.63 us
    pallas_call x1, Pallas kernels, body(): call(functools.partial(tables_kernel, cap), [sds((4 * chans + hidden, cha...  4 us
    pallas_call x1, Pallas kernels, body(): call(functools.partial(near_kernel, run), [sds(*q_like), sds(*state_like)...  2.93 us
    pallas_call x1, Pallas kernels, body(): call(functools.partial(middle_kernel, run, len(mid)), [sds(*state_like)],...  1.41 us
    unnamed x16, local copies, waits for them, and re-layouts  1.16 us
  transfers between devices with their start and end apart: 7, of which 6 were waited for; matrix products, arithmetic and copies ran while one was open for 0% of the time, Pallas kernels for 19%

profile of v15, /device:TPU:0, one launch (start us, length us, event | category | flops | bytes accessed | tf_op | source)
XLA Modules:
  0.0 44.7 jit_solution(17023421266775488628)
XLA Ops:
  1.3 6.8 %shard_map.167 = (bf16[192,1024]{1,0:T(8,128)(2,1)}, bf16[192,1024]{1,0:T(8,128)(2,1)}) custom-call(s32[1]{0:T(128)S(6)} %copy.18.count_ref, bf16[192,1024]{1,0:T(8,128)(2,1)} %bitcast.13, s32[1,1024]{1,0:T(1,128)} %bitcast.14, f32[3,192]{1,0:T(4,128)} %pos_hbm.1, f32[1,192]{1,0:T(1,128)} %bitcast.18, f32[1,192]{1,0:T(1,128)} %bitcast.19, ...), custom_call_target="tpu_custom_call" | custom-call | flops 2000000000 | bytes 2097152 | tf_op jit(solution)/shard_map/pallas_call | solution.py:553
  8.1 0.5 %collective-permute-start.1 = (bf16[192,1024]{1,0:T(8,128)(2,1)}, bf16[192,1024]{1,0:T(8,128)(2,1)S(1)}, u32[]{:S(2)}, u32[]{:S(2)}) collective-permute-start(bf16[192,1024]{1,0:T(8,128)(2,1)} %get-tuple-element.19.own_ref), channel_id=1, source_target_pairs={{0,8},{8,0},{16,24},{24,16},{1,9},{9,1},{17,25},{25,17},{2,10},{10... | collective-permute-start | bytes 1179656 | tf_op jit(solution)/shard_map/ppermute | solution.py:518
  8.6 2.6 %collective-permute-start = (bf16[192,1024]{1,0:T(8,128)(2,1)}, bf16[192,1024]{1,0:T(8,128)(2,1)S(1)}, u32[]{:S(2)}, u32[]{:S(2)}) collective-permute-start(bf16[192,1024]{1,0:T(8,128)(2,1)} %get-tuple-element.19.own_ref), channel_id=1, source_target_pairs={{0,16},{8,24},{16,0},{24,8},{1,17},{9,25},{17,1},{25,9},{2,18},{10... | collective-permute-start | bytes 1179656 | tf_op jit(solution)/shard_map/ppermute | solution.py:518
  11.2 4.0 %shard_map.168 = (bf16[1536,192]{1,0:T(8,128)(2,1)}, bf16[16,1024]{1,0:T(8,128)(2,1)}, f32[192,128]{1,0:T(8,128)}, bf16[1024,1024]{1,0:T(8,128)(2,1)}) custom-call(bf16[192,576]{1,0:T(8,128)(2,1)} %qkv_hbm.3, bf16[192,192]{1,0:T(8,128)(2,1)} %out_hbm.3, bf16[192,768]{1,0:T(8,128)(2,1)} %up_hbm.1, s32[1,512]{1,0:T(1,128)} %bitcast.15, s32[1,512]{1,0:T(1,128)} %bitcast.16, ...), custom_call_target="tpu_custom_call" | custom-call | flops 2000000000 | bytes 2097152 | tf_op jit(solution)/shard_map/pallas_call | solution.py:595
  15.2 0.0 collective-permute-done.1.near_ref
  15.2 0.0 copy-done
  15.2 0.0 copy-start.3
  15.2 1.1 %copy-done.3 = bf16[1536,192]{1,0:T(8,128)(2,1)S(1)} copy-done((bf16[1536,192]{1,0:T(8,128)(2,1)S(1)}, bf16[1536,192]{1,0:T(8,128)(2,1)}, u32[]{:S(2)}) %copy-start.3) | copy-done | bytes 589848
  16.4 2.9 %shard_map.169 = (f32[8,24,8,128]{3,2,1,0:T(8,128)S(1)}, f32[8,28,8,128]{3,2,1,0:T(8,128)S(1)}) custom-call(bf16[192,1024]{1,0:T(8,128)(2,1)S(1)} %copy-done, bf16[192,1024]{1,0:T(8,128)(2,1)S(1)} %collective-permute-done.1.near_ref, bf16[1536,192]{1,0:T(8,128)(2,1)S(1)} %copy-done.3), custom_call_target="tpu_custom_call" | custom-call | flops 3000000000 | bytes 2097152 | tf_op jit(solution)/shard_map/pallas_call | solution.py:637
  19.3 1.8 %collective-permute-done.refs_0_ = bf16[192,1024]{1,0:T(8,128)(2,1)S(1)} collective-permute-done((bf16[192,1024]{1,0:T(8,128)(2,1)}, bf16[192,1024]{1,0:T(8,128)(2,1)S(1)}, u32[]{:S(2)}, u32[]{:S(2)}) %collective-permute-start) | collective-permute-done | bytes 393248 | tf_op jit(solution)/shard_map/ppermute | solution.py:518
  21.1 0.0 collective-permute-start.2
  21.1 0.0 copy-done.4
  21.1 0.0 copy-start.2
  21.1 0.0 copy-start.5
  21.2 0.0 copy-start.6
  21.2 0.0 copy-start.7
  21.2 1.4 %shard_map.170.refs_2_ = f32[8,28,8,128]{3,2,1,0:T(8,128)S(1)} custom-call(bf16[192,1024]{1,0:T(8,128)(2,1)S(1)} %collective-permute-done.refs_0_, f32[8,24,8,128]{3,2,1,0:T(8,128)S(1)} %get-tuple-element.23.refs_1_, f32[8,28,8,128]{3,2,1,0:T(8,128)S(1)} %get-tuple-element.24.refs_2_, bf16[1536,192]{1,0:T(8,128)(2,1)S(1)} %copy-done.4), custom_call_target="tpu_custom_call" | custom-call | flops 2000000000 | bytes 2097152 | tf_op jit(solution)/shard_map/pallas_call | solution.py:648
  22.6 0.3 collective-permute-done.2.refs_0_
  22.8 0.0 copy-done.1
  22.8 0.0 copy-done.5
  22.9 0.0 copy-done.6
  22.9 4.6 %shard_map.171 = (f32[192,1024]{1,0:T(8,128)}, bf16[2,200,128]{2,1,0:T(8,128)(2,1)S(1)}, bf16[2,200,128]{2,1,0:T(8,128)(2,1)S(1)}, bf16[2,200,128]{2,1,0:T(8,128)(2,1)S(1)}, bf16[2,200,128]{2,1,0:T(8,128)(2,1)S(1)}) custom-call(s32[1]{0:T(128)S(6)} %copy.18.count_ref, bf16[192,1024]{1,0:T(8,128)(2,1)S(1)} %collective-permute-done.2.refs_0_, ...), custom_call_target="tpu_custom_call" | custom-call | flops 3000000000 | bytes 2097152 | tf_op jit(solution)/shard_map/pallas_call | solution.py:657
  27.5 1.9 %collective-permute-start.3 = (bf16[2,200,128]{2,1,0:T(8,128)(2,1)S(1)}, bf16[2,200,128]{2,1,0:T(8,128)(2,1)S(1)}, u32[]{:S(2)}, u32[]{:S(2)}) collective-permute-start(bf16[2,200,128]{2,1,0:T(8,128)(2,1)S(1)} %get-tuple-element.31), channel_id=1, source_target_pairs={{0,1},{1,0},{2,3},{3,2},{4,5},{5,4},{6,7},{7,6},{8,9},{9,8},{10,11... | collective-permute-start | bytes 307208 | tf_op jit(solution)/shard_map/ppermute | solution.py:518
  29.4 1.6 %collective-permute-start.4 = (bf16[2,200,128]{2,1,0:T(8,128)(2,1)S(1)}, bf16[2,200,128]{2,1,0:T(8,128)(2,1)S(1)}, u32[]{:S(2)}, u32[]{:S(2)}) collective-permute-start(bf16[2,200,128]{2,1,0:T(8,128)(2,1)S(1)} %get-tuple-element.32), channel_id=1, source_target_pairs={{0,2},{1,3},{2,0},{3,1},{4,6},{5,7},{6,4},{7,5},{8,10},{9,11},{10,... | collective-permute-start | bytes 307208 | tf_op jit(solution)/shard_map/ppermute | solution.py:518
  30.9 0.1 collective-permute-start.5
  31.1 1.8 %collective-permute-done.3.refs_1_ = bf16[2,200,128]{2,1,0:T(8,128)(2,1)S(1)} collective-permute-done((bf16[2,200,128]{2,1,0:T(8,128)(2,1)S(1)}, bf16[2,200,128]{2,1,0:T(8,128)(2,1)S(1)}, u32[]{:S(2)}, u32[]{:S(2)}) %collective-permute-start.3) | collective-permute-done | bytes 102432 | tf_op jit(solution)/shard_map/ppermute | solution.py:518
  32.9 2.2 %collective-permute-done.4.refs_2_ = bf16[2,200,128]{2,1,0:T(8,128)(2,1)S(1)} collective-permute-done((bf16[2,200,128]{2,1,0:T(8,128)(2,1)S(1)}, bf16[2,200,128]{2,1,0:T(8,128)(2,1)S(1)}, u32[]{:S(2)}, u32[]{:S(2)}) %collective-permute-start.4) | collective-permute-done | bytes 102432 | tf_op jit(solution)/shard_map/ppermute | solution.py:518
  35.1 1.5 %collective-permute-done.5.refs_3_ = bf16[2,200,128]{2,1,0:T(8,128)(2,1)S(1)} collective-permute-done((bf16[2,200,128]{2,1,0:T(8,128)(2,1)S(1)}, bf16[2,200,128]{2,1,0:T(8,128)(2,1)S(1)}, u32[]{:S(2)}, u32[]{:S(2)}) %collective-permute-start.5) | collective-permute-done | bytes 102432 | tf_op jit(solution)/shard_map/ppermute | solution.py:518
  36.6 0.4 shard_map.172
  36.9 2.6 %collective-permute-start.6 = (bf16[192,256]{1,0:T(8,128)(2,1)S(1)}, bf16[192,256]{1,0:T(8,128)(2,1)S(1)}, u32[]{:S(2)}, u32[]{:S(2)}) collective-permute-start(bf16[192,256]{1,0:T(8,128)(2,1)S(1)} %get-tuple-element.35), channel_id=1, source_target_pairs={{0,4},{1,5},{2,6},{3,7},{4,0},{5,1},{6,2},{7,3},{8,12},{9,13},{10,... | collective-permute-start | bytes 294920 | tf_op jit(solution)/shard_map/ppermute | solution.py:518
  39.6 4.4 %collective-permute-done.6.there_ref = bf16[192,256]{1,0:T(8,128)(2,1)S(1)} collective-permute-done((bf16[192,256]{1,0:T(8,128)(2,1)S(1)}, bf16[192,256]{1,0:T(8,128)(2,1)S(1)}, u32[]{:S(2)}, u32[]{:S(2)}) %collective-permute-start.6) | collective-permute-done | bytes 98336 | tf_op jit(solution)/shard_map/ppermute | solution.py:518
  44.0 0.7 %shard_map.173 = f32[192,256]{1,0:T(8,128)} custom-call(f32[192,256]{1,0:T(8,128)S(1)} %get-tuple-element.34.here_ref, bf16[192,256]{1,0:T(8,128)(2,1)S(1)} %collective-permute-done.6.there_ref), custom_call_target="tpu_custom_call" | custom-call | flops 1000000 | bytes 2097152 | tf_op jit(solution)/shard_map/pallas_call | solution.py:690
  (5 shorter events, 0.0 us)
Async XLA Ops:
  8.1 7.1 %collective-permute-start.1 = (bf16[192,1024]{1,0:T(8,128)(2,1)}, bf16[192,1024]{1,0:T(8,128)(2,1)S(1)}, u32[]{:S(2)}, u32[]{:S(2)}) collective-permute-start(bf16[192,1024]{1,0:T(8,128)(2,1)} %get-tuple-element.19.own_ref), channel_id=1, source_target_pairs={{0,8},{8,0},{16,24},{24,16},{1,9},{9,1},{17,25},{25,17},{2,10},{10... | collective-permute-start | bytes 1179656 | tf_op jit(solution)/shard_map/ppermute | solution.py:518
  8.6 12.5 %collective-permute-start = (bf16[192,1024]{1,0:T(8,128)(2,1)}, bf16[192,1024]{1,0:T(8,128)(2,1)S(1)}, u32[]{:S(2)}, u32[]{:S(2)}) collective-permute-start(bf16[192,1024]{1,0:T(8,128)(2,1)} %get-tuple-element.19.own_ref), channel_id=1, source_target_pairs={{0,16},{8,24},{16,0},{24,8},{1,17},{9,25},{17,1},{25,9},{2,18},{10... | collective-permute-start | bytes 1179656 | tf_op jit(solution)/shard_map/ppermute | solution.py:518
  11.2 4.0 %copy-start = (bf16[192,1024]{1,0:T(8,128)(2,1)S(1)}, bf16[192,1024]{1,0:T(8,128)(2,1)}, u32[]{:S(2)}) copy-start(bf16[192,1024]{1,0:T(8,128)(2,1)} %get-tuple-element.19.own_ref) | copy-start | bytes 1179652
  15.2 1.1 %copy-start.3 = (bf16[1536,192]{1,0:T(8,128)(2,1)S(1)}, bf16[1536,192]{1,0:T(8,128)(2,1)}, u32[]{:S(2)}) copy-start(bf16[1536,192]{1,0:T(8,128)(2,1)} %get-tuple-element.20.weights_ref.refs_3_) | copy-start | bytes 1769476
  16.4 4.8 %copy-start.4 = (bf16[1536,192]{1,0:T(8,128)(2,1)S(1)}, bf16[1536,192]{1,0:T(8,128)(2,1)}, u32[]{:S(2)}) copy-start(bf16[1536,192]{1,0:T(8,128)(2,1)} %get-tuple-element.20.weights_ref.refs_3_) | copy-start | bytes 1769476
  21.1 1.7 %collective-permute-start.2 = (bf16[192,1024]{1,0:T(8,128)(2,1)S(1)}, bf16[192,1024]{1,0:T(8,128)(2,1)S(1)}, u32[]{:S(2)}, u32[]{:S(2)}) collective-permute-start(bf16[192,1024]{1,0:T(8,128)(2,1)S(1)} %collective-permute-done.refs_0_), channel_id=1, source_target_pairs={{0,8},{8,0},{16,24},{24,16},{1,9},{9,1},{17,25},{25,17},{2,10},{10... | collective-permute-start | bytes 1179656 | tf_op jit(solution)/shard_map/ppermute | solution.py:518
  21.1 1.7 %copy-start.1 = (bf16[768,192]{0,1:T(8,128)(2,1)S(1)}, bf16[768,192]{0,1:T(8,128)(2,1)}, u32[]{:S(2)}) copy-start(bf16[768,192]{0,1:T(8,128)(2,1)} %param.28) | copy-start | bytes 884740
  21.1 1.7 %copy-start.2 = (bf16[1024,1024]{1,0:T(8,128)(2,1)S(1)}, bf16[1024,1024]{1,0:T(8,128)(2,1)}, u32[]{:S(2)}) copy-start(bf16[1024,1024]{1,0:T(8,128)(2,1)} %get-tuple-element.28.refs_8_) | copy-start | bytes 6291460
  21.1 1.7 %copy-start.5 = (bf16[192,1024]{1,0:T(8,128)(2,1)S(1)}, bf16[192,1024]{1,0:T(8,128)(2,1)}, u32[]{:S(2)}) copy-start(bf16[192,1024]{1,0:T(8,128)(2,1)} %get-tuple-element.25.refs_4_) | copy-start | bytes 1179652
  21.2 1.7 %copy-start.6 = (f32[192,128]{1,0:T(8,128)S(1)}, f32[192,128]{1,0:T(8,128)}, u32[]{:S(2)}) copy-start(f32[192,128]{1,0:T(8,128)} %get-tuple-element.26.refs_5_) | copy-start | bytes 294916
  21.2 1.7 %copy-start.7 = (bf16[16,1024]{1,0:T(8,128)(2,1)S(1)}, bf16[16,1024]{1,0:T(8,128)(2,1)}, u32[]{:S(2)}) copy-start(bf16[16,1024]{1,0:T(8,128)(2,1)} %get-tuple-element.27.refs_7_) | copy-start | bytes 98308
  27.5 5.4 %collective-permute-start.3 = (bf16[2,200,128]{2,1,0:T(8,128)(2,1)S(1)}, bf16[2,200,128]{2,1,0:T(8,128)(2,1)S(1)}, u32[]{:S(2)}, u32[]{:S(2)}) collective-permute-start(bf16[2,200,128]{2,1,0:T(8,128)(2,1)S(1)} %get-tuple-element.31), channel_id=1, source_target_pairs={{0,1},{1,0},{2,3},{3,2},{4,5},{5,4},{6,7},{7,6},{8,9},{9,8},{10,11... | collective-permute-start | bytes 307208 | tf_op jit(solution)/shard_map/ppermute | solution.py:518
  29.4 5.7 %collective-permute-start.4 = (bf16[2,200,128]{2,1,0:T(8,128)(2,1)S(1)}, bf16[2,200,128]{2,1,0:T(8,128)(2,1)S(1)}, u32[]{:S(2)}, u32[]{:S(2)}) collective-permute-start(bf16[2,200,128]{2,1,0:T(8,128)(2,1)S(1)} %get-tuple-element.32), channel_id=1, source_target_pairs={{0,2},{1,3},{2,0},{3,1},{4,6},{5,7},{6,4},{7,5},{8,10},{9,11},{10,... | collective-permute-start | bytes 307208 | tf_op jit(solution)/shard_map/ppermute | solution.py:518
  30.9 5.6 %collective-permute-start.5 = (bf16[2,200,128]{2,1,0:T(8,128)(2,1)S(1)}, bf16[2,200,128]{2,1,0:T(8,128)(2,1)S(1)}, u32[]{:S(2)}, u32[]{:S(2)}) collective-permute-start(bf16[2,200,128]{2,1,0:T(8,128)(2,1)S(1)} %get-tuple-element.33), channel_id=1, source_target_pairs={{0,3},{1,2},{2,1},{3,0},{4,7},{5,6},{6,5},{7,4},{8,11},{9,10},{10,... | collective-permute-start | bytes 307208 | tf_op jit(solution)/shard_map/ppermute | solution.py:518
  36.9 7.0 %collective-permute-start.6 = (bf16[192,256]{1,0:T(8,128)(2,1)S(1)}, bf16[192,256]{1,0:T(8,128)(2,1)S(1)}, u32[]{:S(2)}, u32[]{:S(2)}) collective-permute-start(bf16[192,256]{1,0:T(8,128)(2,1)S(1)} %get-tuple-element.35), channel_id=1, source_target_pairs={{0,4},{1,5},{2,6},{3,7},{4,0},{5,1},{6,2},{7,3},{8,12},{9,13},{10,... | collective-permute-start | bytes 294920 | tf_op jit(solution)/shard_map/ppermute | solution.py:518

commit v16 on v13

--- a/solution.py
+++ b/solution.py
@@ -451,7 +451,7 @@
         feat_s[:, at] = second
         inner_s[:, at] = norm_t(second, gain).astype(BF16)
     kept = iota((1, slots), 1) < count
-    wide = 2 * LANES
+    wide = 4 * LANES
     cuts = [slice(at, at + wide) for at in range(0, slots, wide)]
     up_t = weights_s[4 * chans :]
     raised = dot(up_t, inner_s[:, cuts[0]])
@@ -668,7 +668,7 @@
         facts,
     )
     half = owners // 2
-    got = [ballots[0]] + [turned(ballots[k], "tile", k) for k in range(1, half)]
+    got = [ballots[0]] + [turned(ballots[k], "tile", k) for k in range(half - 1, 0, -1)]
     here, there = call(
         sums_kernel,
         [sds((chans, VOX_DEV), F32), sds((chans, VOX_DEV), BF16)],

time: 44.5 us -> 44.6 us (level)
  transfers between devices with their start and end apart: 7 -> 7, of which waited for: 6 -> 5; matrix products, arithmetic and copies ran while one was open for 0% -> 0% of each run, Pallas kernels for 17% -> 17%
where the time goes in v16:
time: 44.6 us; the launch traced here: 44.4 us
  Pallas kernels  20 us (45%)
  waiting for transfers between devices  12.6 us (28%)
  starting transfers between devices  9.28 us (21%)
  between operations  1.38 us (3%)
  local copies, waits for them, and re-layouts  1.15 us (3%)
    ppermute x7, waiting for transfers between devices, turned(): return lax.ppermute(x, axis, [(i, i ^ bit) for i in range(n)])  12.6 us
    ppermute x7, starting transfers between devices, turned(): return lax.ppermute(x, axis, [(i, i ^ bit) for i in range(n)])  9.28 us
    pallas_call x1, Pallas kernels, body(): call(functools.partial(first_kernel, run), [sds((chans, slots), BF16), sd...  6.91 us
    pallas_call x1, Pallas kernels, body(): call(functools.partial(second_kernel, run, cap, len(far), owners), [sds((...  4.66 us
    pallas_call x1, Pallas kernels, body(): call(functools.partial(tables_kernel, cap), [sds((4 * chans + hidden, cha...  2.99 us
    pallas_call x1, Pallas kernels, body(): call(functools.partial(near_kernel, run), [sds(*q_like), sds(*state_like)...  2.93 us
    pallas_call x1, Pallas kernels, body(): call(functools.partial(middle_kernel, run, len(mid)), [sds(*state_like)],...  1.41 us
    unnamed x12, local copies, waits for them, and re-layouts  1.15 us
  transfers between devices with their start and end apart: 7, of which 5 were waited for; matrix products, arithmetic and copies ran while one was open for 0% of the time, Pallas kernels for 17%

profile of v16, /device:TPU:0, one launch (start us, length us, event | category | flops | bytes accessed | tf_op | source)
XLA Modules:
  0.0 44.4 jit_solution(6406548241775992743)
XLA Ops:
  1.3 6.9 %shard_map.167 = (bf16[192,1024]{1,0:T(8,128)(2,1)}, bf16[192,1024]{1,0:T(8,128)(2,1)}) custom-call(s32[1]{0:T(128)S(6)} %copy.18.count_ref, bf16[192,1024]{1,0:T(8,128)(2,1)} %bitcast.13, s32[1,1024]{1,0:T(1,128)} %bitcast.14, f32[3,192]{1,0:T(4,128)} %pos_hbm.1, f32[1,192]{1,0:T(1,128)} %bitcast.18, f32[1,192]{1,0:T(1,128)} %bitcast.19, ...), custom_call_target="tpu_custom_call" | custom-call | flops 2000000000 | bytes 2097152 | tf_op jit(solution)/shard_map/pallas_call | solution.py:547
  8.2 0.5 %collective-permute-start.1 = (bf16[192,1024]{1,0:T(8,128)(2,1)}, bf16[192,1024]{1,0:T(8,128)(2,1)S(1)}, u32[]{:S(2)}, u32[]{:S(2)}) collective-permute-start(bf16[192,1024]{1,0:T(8,128)(2,1)} %get-tuple-element.18.own_ref), channel_id=1, source_target_pairs={{0,8},{8,0},{16,24},{24,16},{1,9},{9,1},{17,25},{25,17},{2,10},{10... | collective-permute-start | bytes 1179656 | tf_op jit(solution)/shard_map/ppermute | solution.py:512
  8.7 2.6 %collective-permute-start = (bf16[192,1024]{1,0:T(8,128)(2,1)}, bf16[192,1024]{1,0:T(8,128)(2,1)S(1)}, u32[]{:S(2)}, u32[]{:S(2)}) collective-permute-start(bf16[192,1024]{1,0:T(8,128)(2,1)} %get-tuple-element.18.own_ref), channel_id=1, source_target_pairs={{0,16},{8,24},{16,0},{24,8},{1,17},{9,25},{17,1},{25,9},{2,18},{10... | collective-permute-start | bytes 1179656 | tf_op jit(solution)/shard_map/ppermute | solution.py:512
  11.3 0.0 copy-start
  11.3 3.0 %shard_map.168 = (bf16[1536,192]{1,0:T(8,128)(2,1)}, bf16[16,1024]{1,0:T(8,128)(2,1)}, f32[192,128]{1,0:T(8,128)}) custom-call(bf16[192,576]{1,0:T(8,128)(2,1)} %qkv_hbm.3, bf16[192,192]{1,0:T(8,128)(2,1)} %out_hbm.3, bf16[192,768]{1,0:T(8,128)(2,1)} %up_hbm.1, s32[1,512]{1,0:T(1,128)} %bitcast.15, s32[1,512]{1,0:T(1,128)} %bitcast.16, s32[1,512]{1,0:T(1,128)} %bitcast.17, ...), custom_call_target="tpu_custom_call" | custom-call | flops 2000000000 | bytes 2097152 | tf_op jit(solution)/shard_map/pallas_call | solution.py:588
  14.3 0.0 collective-permute-done.1.near_ref
  14.3 0.0 copy-done
  14.3 0.0 copy-start.2
  14.3 1.1 %copy-done.2 = bf16[1536,192]{1,0:T(8,128)(2,1)S(1)} copy-done((bf16[1536,192]{1,0:T(8,128)(2,1)S(1)}, bf16[1536,192]{1,0:T(8,128)(2,1)}, u32[]{:S(2)}) %copy-start.2) | copy-done | bytes 589848
  15.4 2.9 %shard_map.169 = (f32[8,24,8,128]{3,2,1,0:T(8,128)S(1)}, f32[8,28,8,128]{3,2,1,0:T(8,128)S(1)}) custom-call(bf16[192,1024]{1,0:T(8,128)(2,1)S(1)} %copy-done, bf16[192,1024]{1,0:T(8,128)(2,1)S(1)} %collective-permute-done.1.near_ref, bf16[1536,192]{1,0:T(8,128)(2,1)S(1)} %copy-done.2), custom_call_target="tpu_custom_call" | custom-call | flops 3000000000 | bytes 2097152 | tf_op jit(solution)/shard_map/pallas_call | solution.py:629
  18.4 2.8 %collective-permute-done.refs_0_ = bf16[192,1024]{1,0:T(8,128)(2,1)S(1)} collective-permute-done((bf16[192,1024]{1,0:T(8,128)(2,1)}, bf16[192,1024]{1,0:T(8,128)(2,1)S(1)}, u32[]{:S(2)}, u32[]{:S(2)}) %collective-permute-start) | collective-permute-done | bytes 393248 | tf_op jit(solution)/shard_map/ppermute | solution.py:512
  21.2 0.0 collective-permute-start.2
  21.2 0.0 copy-start.1
  21.2 0.0 copy-start.3
  21.2 0.0 copy-start.5
  21.2 1.4 %shard_map.170.refs_2_ = f32[8,28,8,128]{3,2,1,0:T(8,128)S(1)} custom-call(bf16[192,1024]{1,0:T(8,128)(2,1)S(1)} %collective-permute-done.refs_0_, f32[8,24,8,128]{3,2,1,0:T(8,128)S(1)} %get-tuple-element.22.refs_1_, f32[8,28,8,128]{3,2,1,0:T(8,128)S(1)} %get-tuple-element.23.refs_2_, bf16[1536,192]{1,0:T(8,128)(2,1)S(1)} %copy-done.2), custom_call_target="tpu_custom_call" | custom-call | flops 2000000000 | bytes 2097152 | tf_op jit(solution)/shard_map/pallas_call | solution.py:640
  22.6 0.3 collective-permute-done.2.refs_0_
  22.9 0.0 copy-done.1
  22.9 0.0 copy-done.3
  22.9 0.0 copy-done.4
  22.9 0.0 copy-done.5
  22.9 4.7 %shard_map.171 = (f32[192,1024]{1,0:T(8,128)}, bf16[2,200,128]{2,1,0:T(8,128)(2,1)S(1)}, bf16[2,200,128]{2,1,0:T(8,128)(2,1)S(1)}, bf16[2,200,128]{2,1,0:T(8,128)(2,1)S(1)}, bf16[2,200,128]{2,1,0:T(8,128)(2,1)S(1)}) custom-call(s32[1]{0:T(128)S(6)} %copy.18.count_ref, bf16[192,1024]{1,0:T(8,128)(2,1)S(1)} %collective-permute-done.2.refs_0_, ...), custom_call_target="tpu_custom_call" | custom-call | flops 3000000000 | bytes 2097152 | tf_op jit(solution)/shard_map/pallas_call | solution.py:649
  27.6 2.9 %collective-permute-start.3 = (bf16[2,200,128]{2,1,0:T(8,128)(2,1)S(1)}, bf16[2,200,128]{2,1,0:T(8,128)(2,1)S(1)}, u32[]{:S(2)}, u32[]{:S(2)}) collective-permute-start(bf16[2,200,128]{2,1,0:T(8,128)(2,1)S(1)} %get-tuple-element.29), channel_id=1, source_target_pairs={{0,3},{1,2},{2,1},{3,0},{4,7},{5,6},{6,5},{7,4},{8,11},{9,10},{10,... | collective-permute-start | bytes 307208 | tf_op jit(solution)/shard_map/ppermute | solution.py:512
  30.5 0.5 %collective-permute-start.4 = (bf16[2,200,128]{2,1,0:T(8,128)(2,1)S(1)}, bf16[2,200,128]{2,1,0:T(8,128)(2,1)S(1)}, u32[]{:S(2)}, u32[]{:S(2)}) collective-permute-start(bf16[2,200,128]{2,1,0:T(8,128)(2,1)S(1)} %get-tuple-element.30), channel_id=1, source_target_pairs={{0,2},{1,3},{2,0},{3,1},{4,6},{5,7},{6,4},{7,5},{8,10},{9,11},{10,... | collective-permute-start | bytes 307208 | tf_op jit(solution)/shard_map/ppermute | solution.py:512
  30.9 0.2 collective-permute-start.5
  31.1 3.1 %collective-permute-done.3.refs_1_ = bf16[2,200,128]{2,1,0:T(8,128)(2,1)S(1)} collective-permute-done((bf16[2,200,128]{2,1,0:T(8,128)(2,1)S(1)}, bf16[2,200,128]{2,1,0:T(8,128)(2,1)S(1)}, u32[]{:S(2)}, u32[]{:S(2)}) %collective-permute-start.3) | collective-permute-done | bytes 102432 | tf_op jit(solution)/shard_map/ppermute | solution.py:512
  34.2 1.9 %collective-permute-done.4.refs_2_ = bf16[2,200,128]{2,1,0:T(8,128)(2,1)S(1)} collective-permute-done((bf16[2,200,128]{2,1,0:T(8,128)(2,1)S(1)}, bf16[2,200,128]{2,1,0:T(8,128)(2,1)S(1)}, u32[]{:S(2)}, u32[]{:S(2)}) %collective-permute-start.4) | collective-permute-done | bytes 102432 | tf_op jit(solution)/shard_map/ppermute | solution.py:512
  36.1 0.0 collective-permute-done.5.refs_3_
  36.1 0.4 shard_map.172
  36.5 2.7 %collective-permute-start.6 = (bf16[192,256]{1,0:T(8,128)(2,1)S(1)}, bf16[192,256]{1,0:T(8,128)(2,1)S(1)}, u32[]{:S(2)}, u32[]{:S(2)}) collective-permute-start(bf16[192,256]{1,0:T(8,128)(2,1)S(1)} %get-tuple-element.33), channel_id=1, source_target_pairs={{0,4},{1,5},{2,6},{3,7},{4,0},{5,1},{6,2},{7,3},{8,12},{9,13},{10,... | collective-permute-start | bytes 294920 | tf_op jit(solution)/shard_map/ppermute | solution.py:512
  39.2 4.6 %collective-permute-done.6.there_ref = bf16[192,256]{1,0:T(8,128)(2,1)S(1)} collective-permute-done((bf16[192,256]{1,0:T(8,128)(2,1)S(1)}, bf16[192,256]{1,0:T(8,128)(2,1)S(1)}, u32[]{:S(2)}, u32[]{:S(2)}) %collective-permute-start.6) | collective-permute-done | bytes 98336 | tf_op jit(solution)/shard_map/ppermute | solution.py:512
  43.7 0.7 %shard_map.173 = f32[192,256]{1,0:T(8,128)} custom-call(f32[192,256]{1,0:T(8,128)S(1)} %get-tuple-element.32.here_ref, bf16[192,256]{1,0:T(8,128)(2,1)S(1)} %collective-permute-done.6.there_ref), custom_call_target="tpu_custom_call" | custom-call | flops 1000000 | bytes 2097152 | tf_op jit(solution)/shard_map/pallas_call | solution.py:681
  (1 shorter events, 0.0 us)
Async XLA Ops:
  8.2 6.1 %collective-permute-start.1 = (bf16[192,1024]{1,0:T(8,128)(2,1)}, bf16[192,1024]{1,0:T(8,128)(2,1)S(1)}, u32[]{:S(2)}, u32[]{:S(2)}) collective-permute-start(bf16[192,1024]{1,0:T(8,128)(2,1)} %get-tuple-element.18.own_ref), channel_id=1, source_target_pairs={{0,8},{8,0},{16,24},{24,16},{1,9},{9,1},{17,25},{25,17},{2,10},{10... | collective-permute-start | bytes 1179656 | tf_op jit(solution)/shard_map/ppermute | solution.py:512
  8.7 12.5 %collective-permute-start = (bf16[192,1024]{1,0:T(8,128)(2,1)}, bf16[192,1024]{1,0:T(8,128)(2,1)S(1)}, u32[]{:S(2)}, u32[]{:S(2)}) collective-permute-start(bf16[192,1024]{1,0:T(8,128)(2,1)} %get-tuple-element.18.own_ref), channel_id=1, source_target_pairs={{0,16},{8,24},{16,0},{24,8},{1,17},{9,25},{17,1},{25,9},{2,18},{10... | collective-permute-start | bytes 1179656 | tf_op jit(solution)/shard_map/ppermute | solution.py:512
  11.3 3.0 %copy-start = (bf16[192,1024]{1,0:T(8,128)(2,1)S(1)}, bf16[192,1024]{1,0:T(8,128)(2,1)}, u32[]{:S(2)}) copy-start(bf16[192,1024]{1,0:T(8,128)(2,1)} %get-tuple-element.18.own_ref) | copy-start | bytes 1179652
  14.3 1.1 %copy-start.2 = (bf16[1536,192]{1,0:T(8,128)(2,1)S(1)}, bf16[1536,192]{1,0:T(8,128)(2,1)}, u32[]{:S(2)}) copy-start(bf16[1536,192]{1,0:T(8,128)(2,1)} %get-tuple-element.19.weights_ref.refs_3_) | copy-start | bytes 1769476
  21.2 1.7 %collective-permute-start.2 = (bf16[192,1024]{1,0:T(8,128)(2,1)S(1)}, bf16[192,1024]{1,0:T(8,128)(2,1)S(1)}, u32[]{:S(2)}, u32[]{:S(2)}) collective-permute-start(bf16[192,1024]{1,0:T(8,128)(2,1)S(1)} %collective-permute-done.refs_0_), channel_id=1, source_target_pairs={{0,8},{8,0},{16,24},{24,16},{1,9},{9,1},{17,25},{25,17},{2,10},{10... | collective-permute-start | bytes 1179656 | tf_op jit(solution)/shard_map/ppermute | solution.py:512
  21.2 1.7 %copy-start.1 = (bf16[768,192]{0,1:T(8,128)(2,1)S(1)}, bf16[768,192]{0,1:T(8,128)(2,1)}, u32[]{:S(2)}) copy-start(bf16[768,192]{0,1:T(8,128)(2,1)} %param.28) | copy-start | bytes 884740
  21.2 1.7 %copy-start.3 = (bf16[192,1024]{1,0:T(8,128)(2,1)S(1)}, bf16[192,1024]{1,0:T(8,128)(2,1)}, u32[]{:S(2)}) copy-start(bf16[192,1024]{1,0:T(8,128)(2,1)} %get-tuple-element.24.refs_4_) | copy-start | bytes 1179652
  21.2 1.7 %copy-start.4 = (f32[192,128]{1,0:T(8,128)S(1)}, f32[192,128]{1,0:T(8,128)}, u32[]{:S(2)}) copy-start(f32[192,128]{1,0:T(8,128)} %get-tuple-element.25.refs_5_) | copy-start | bytes 294916
  21.2 1.7 %copy-start.5 = (bf16[16,1024]{1,0:T(8,128)(2,1)S(1)}, bf16[16,1024]{1,0:T(8,128)(2,1)}, u32[]{:S(2)}) copy-start(bf16[16,1024]{1,0:T(8,128)(2,1)} %get-tuple-element.26.refs_7_) | copy-start | bytes 98308
  27.6 6.7 %collective-permute-start.3 = (bf16[2,200,128]{2,1,0:T(8,128)(2,1)S(1)}, bf16[2,200,128]{2,1,0:T(8,128)(2,1)S(1)}, u32[]{:S(2)}, u32[]{:S(2)}) collective-permute-start(bf16[2,200,128]{2,1,0:T(8,128)(2,1)S(1)} %get-tuple-element.29), channel_id=1, source_target_pairs={{0,3},{1,2},{2,1},{3,0},{4,7},{5,6},{6,5},{7,4},{8,11},{9,10},{10,... | collective-permute-start | bytes 307208 | tf_op jit(solution)/shard_map/ppermute | solution.py:512
  30.5 5.7 %collective-permute-start.4 = (bf16[2,200,128]{2,1,0:T(8,128)(2,1)S(1)}, bf16[2,200,128]{2,1,0:T(8,128)(2,1)S(1)}, u32[]{:S(2)}, u32[]{:S(2)}) collective-permute-start(bf16[2,200,128]{2,1,0:T(8,128)(2,1)S(1)} %get-tuple-element.30), channel_id=1, source_target_pairs={{0,2},{1,3},{2,0},{3,1},{4,6},{5,7},{6,4},{7,5},{8,10},{9,11},{10,... | collective-permute-start | bytes 307208 | tf_op jit(solution)/shard_map/ppermute | solution.py:512
  30.9 5.2 %collective-permute-start.5 = (bf16[2,200,128]{2,1,0:T(8,128)(2,1)S(1)}, bf16[2,200,128]{2,1,0:T(8,128)(2,1)S(1)}, u32[]{:S(2)}, u32[]{:S(2)}) collective-permute-start(bf16[2,200,128]{2,1,0:T(8,128)(2,1)S(1)} %get-tuple-element.31), channel_id=1, source_target_pairs={{0,1},{1,0},{2,3},{3,2},{4,5},{5,4},{6,7},{7,6},{8,9},{9,8},{10,11... | collective-permute-start | bytes 307208 | tf_op jit(solution)/shard_map/ppermute | solution.py:512
  36.5 7.2 %collective-permute-start.6 = (bf16[192,256]{1,0:T(8,128)(2,1)S(1)}, bf16[192,256]{1,0:T(8,128)(2,1)S(1)}, u32[]{:S(2)}, u32[]{:S(2)}) collective-permute-start(bf16[192,256]{1,0:T(8,128)(2,1)S(1)} %get-tuple-element.33), channel_id=1, source_target_pairs={{0,4},{1,5},{2,6},{3,7},{4,0},{5,1},{6,2},{7,3},{8,12},{9,13},{10,... | collective-permute-start | bytes 294920 | tf_op jit(solution)/shard_map/ppermute | solution.py:512

commit v17 on v13

--- a/solution.py
+++ b/solution.py
@@ -179,6 +179,7 @@
     lane_pair = iota((WIN, chans), 1) // (2 * size)
     window = iota((8, LANES), 1) // WIN
     wide_window = iota((WIN, LANES), 1) // WIN
+    ones = jnp.ones((16, LANES), BF16)
     rank = iota((WIN, LANES), 0) + WIN * (iota((WIN, LANES), 1) // WIN)
 
     def group(t, _):
@@ -197,13 +198,12 @@
             odd = right if w == 0 else jnp.where(window[None] == w, right, odd)
         mask = jnp.where(rank + t * LANES < count, 0.0, -1e9).astype(F32)
         mask = mask.reshape(WIN // 8, 8, LANES)
-        probs, inverse = [], []
+        probs = []
         for h in range(HEADS):
             scores = (even, odd)[h % 2]
             mine = scores[h // 2 * (WIN // 8) : (h // 2 + 1) * (WIN // 8)] + mask
             top = fold8(mine, jnp.maximum)
             weight = jnp.exp(mine - top[None])
-            inverse.append(1.0 / fold8(weight, jnp.add))
             probs.append(weight.reshape(WIN, LANES).astype(BF16))
         parts = []
         for m in range(HEADS // 2):
@@ -216,10 +216,11 @@
                     )
                 )
             rows = slice(2 * m * size, 2 * (m + 1) * size)
-            got = dot(v_s[t, rows, :], jnp.concatenate(both, 1))
+            value = jnp.concatenate([v_s[t, rows, :], ones], 0)
+            got = dot(value, jnp.concatenate(both, 1))
             for n in range(2):
                 block = got[n * size : (n + 1) * size, tile(n)].reshape(-1, 8, LANES)
-                block = block * inverse[2 * m + n][None]
+                block = block * (1.0 / got[2 * size : 2 * size + 8, tile(n)])[None]
                 parts.append(block.reshape(size, LANES))
         ctx_s[t] = jnp.concatenate(parts, 0).astype(BF16)
         return 0

time: 44.5 us -> 44.4 us (level)
  no operation moved by 1% of the time
where the time goes in v17:
time: 44.4 us; the launch traced here: 44.2 us
  Pallas kernels  19.9 us (45%)
  waiting for transfers between devices  12.5 us (28%)
  starting transfers between devices  9.3 us (21%)
  between operations  1.38 us (3%)
  local copies, waits for them, and re-layouts  1.15 us (3%)
    ppermute x7, waiting for transfers between devices, turned(): return lax.ppermute(x, axis, [(i, i ^ bit) for i in range(n)])  12.5 us
    ppermute x7, starting transfers between devices, turned(): return lax.ppermute(x, axis, [(i, i ^ bit) for i in range(n)])  9.3 us
    pallas_call x1, Pallas kernels, body(): call(functools.partial(first_kernel, run), [sds((chans, slots), BF16), sd...  6.83 us
    pallas_call x1, Pallas kernels, body(): call(functools.partial(second_kernel, run, cap, len(far), owners), [sds((...  4.65 us
    pallas_call x1, Pallas kernels, body(): call(functools.partial(tables_kernel, cap), [sds((4 * chans + hidden, cha...  2.99 us
    pallas_call x1, Pallas kernels, body(): call(functools.partial(near_kernel, run), [sds(*q_like), sds(*state_like)...  2.93 us
    pallas_call x1, Pallas kernels, body(): call(functools.partial(middle_kernel, run, len(mid)), [sds(*state_like)],...  1.42 us
    unnamed x12, local copies, waits for them, and re-layouts  1.15 us
  transfers between devices with their start and end apart: 7, of which 6 were waited for; matrix products, arithmetic and copies ran while one was open for 0% of the time, Pallas kernels for 17%

profile of v17, /device:TPU:0, one launch (start us, length us, event | category | flops | bytes accessed | tf_op | source)
XLA Modules:
  0.0 44.2 jit_solution(5508016909063084161)
XLA Ops:
  1.3 6.8 %shard_map.167 = (bf16[192,1024]{1,0:T(8,128)(2,1)}, bf16[192,1024]{1,0:T(8,128)(2,1)}) custom-call(s32[1]{0:T(128)S(6)} %copy.18.count_ref, bf16[192,1024]{1,0:T(8,128)(2,1)} %bitcast.13, s32[1,1024]{1,0:T(1,128)} %bitcast.14, f32[3,192]{1,0:T(4,128)} %pos_hbm.1, f32[1,192]{1,0:T(1,128)} %bitcast.18, f32[1,192]{1,0:T(1,128)} %bitcast.19, ...), custom_call_target="tpu_custom_call" | custom-call | flops 2000000000 | bytes 2097152 | tf_op jit(solution)/shard_map/pallas_call | solution.py:548
  8.1 0.5 %collective-permute-start.1 = (bf16[192,1024]{1,0:T(8,128)(2,1)}, bf16[192,1024]{1,0:T(8,128)(2,1)S(1)}, u32[]{:S(2)}, u32[]{:S(2)}) collective-permute-start(bf16[192,1024]{1,0:T(8,128)(2,1)} %get-tuple-element.18.own_ref), channel_id=1, source_target_pairs={{0,8},{8,0},{16,24},{24,16},{1,9},{9,1},{17,25},{25,17},{2,10},{10... | collective-permute-start | bytes 1179656 | tf_op jit(solution)/shard_map/ppermute | solution.py:513
  8.6 2.6 %collective-permute-start = (bf16[192,1024]{1,0:T(8,128)(2,1)}, bf16[192,1024]{1,0:T(8,128)(2,1)S(1)}, u32[]{:S(2)}, u32[]{:S(2)}) collective-permute-start(bf16[192,1024]{1,0:T(8,128)(2,1)} %get-tuple-element.18.own_ref), channel_id=1, source_target_pairs={{0,16},{8,24},{16,0},{24,8},{1,17},{9,25},{17,1},{25,9},{2,18},{10... | collective-permute-start | bytes 1179656 | tf_op jit(solution)/shard_map/ppermute | solution.py:513
  11.2 0.0 copy-start
  11.2 3.0 %shard_map.168 = (bf16[1536,192]{1,0:T(8,128)(2,1)}, bf16[16,1024]{1,0:T(8,128)(2,1)}, f32[192,128]{1,0:T(8,128)}) custom-call(bf16[192,576]{1,0:T(8,128)(2,1)} %qkv_hbm.3, bf16[192,192]{1,0:T(8,128)(2,1)} %out_hbm.3, bf16[192,768]{1,0:T(8,128)(2,1)} %up_hbm.1, s32[1,512]{1,0:T(1,128)} %bitcast.15, s32[1,512]{1,0:T(1,128)} %bitcast.16, s32[1,512]{1,0:T(1,128)} %bitcast.17, ...), custom_call_target="tpu_custom_call" | custom-call | flops 2000000000 | bytes 2097152 | tf_op jit(solution)/shard_map/pallas_call | solution.py:589
  14.2 0.0 collective-permute-done.1.near_ref
  14.2 0.0 copy-done
  14.2 0.0 copy-start.2
  14.2 1.1 %copy-done.2 = bf16[1536,192]{1,0:T(8,128)(2,1)S(1)} copy-done((bf16[1536,192]{1,0:T(8,128)(2,1)S(1)}, bf16[1536,192]{1,0:T(8,128)(2,1)}, u32[]{:S(2)}) %copy-start.2) | copy-done | bytes 589848
  15.4 2.9 %shard_map.169 = (f32[8,24,8,128]{3,2,1,0:T(8,128)S(1)}, f32[8,28,8,128]{3,2,1,0:T(8,128)S(1)}) custom-call(bf16[192,1024]{1,0:T(8,128)(2,1)S(1)} %copy-done, bf16[192,1024]{1,0:T(8,128)(2,1)S(1)} %collective-permute-done.1.near_ref, bf16[1536,192]{1,0:T(8,128)(2,1)S(1)} %copy-done.2), custom_call_target="tpu_custom_call" | custom-call | flops 3000000000 | bytes 2097152 | tf_op jit(solution)/shard_map/pallas_call | solution.py:630
  18.3 2.8 %collective-permute-done.refs_0_ = bf16[192,1024]{1,0:T(8,128)(2,1)S(1)} collective-permute-done((bf16[192,1024]{1,0:T(8,128)(2,1)}, bf16[192,1024]{1,0:T(8,128)(2,1)S(1)}, u32[]{:S(2)}, u32[]{:S(2)}) %collective-permute-start) | collective-permute-done | bytes 393248 | tf_op jit(solution)/shard_map/ppermute | solution.py:513
  21.1 0.0 collective-permute-start.2
  21.1 0.0 copy-start.1
  21.1 0.0 copy-start.3
  21.1 0.0 copy-start.5
  21.2 1.4 %shard_map.170.refs_2_ = f32[8,28,8,128]{3,2,1,0:T(8,128)S(1)} custom-call(bf16[192,1024]{1,0:T(8,128)(2,1)S(1)} %collective-permute-done.refs_0_, f32[8,24,8,128]{3,2,1,0:T(8,128)S(1)} %get-tuple-element.22.refs_1_, f32[8,28,8,128]{3,2,1,0:T(8,128)S(1)} %get-tuple-element.23.refs_2_, bf16[1536,192]{1,0:T(8,128)(2,1)S(1)} %copy-done.2), custom_call_target="tpu_custom_call" | custom-call | flops 2000000000 | bytes 2097152 | tf_op jit(solution)/shard_map/pallas_call | solution.py:641
  22.6 0.3 collective-permute-done.2.refs_0_
  22.9 0.0 copy-done.1
  22.9 0.0 copy-done.3
  22.9 0.0 copy-done.4
  22.9 0.0 copy-done.5
  22.9 4.7 %shard_map.171 = (f32[192,1024]{1,0:T(8,128)}, bf16[2,200,128]{2,1,0:T(8,128)(2,1)S(1)}, bf16[2,200,128]{2,1,0:T(8,128)(2,1)S(1)}, bf16[2,200,128]{2,1,0:T(8,128)(2,1)S(1)}, bf16[2,200,128]{2,1,0:T(8,128)(2,1)S(1)}) custom-call(s32[1]{0:T(128)S(6)} %copy.18.count_ref, bf16[192,1024]{1,0:T(8,128)(2,1)S(1)} %collective-permute-done.2.refs_0_, ...), custom_call_target="tpu_custom_call" | custom-call | flops 3000000000 | bytes 2097152 | tf_op jit(solution)/shard_map/pallas_call | solution.py:650
  27.5 1.8 %collective-permute-start.3 = (bf16[2,200,128]{2,1,0:T(8,128)(2,1)S(1)}, bf16[2,200,128]{2,1,0:T(8,128)(2,1)S(1)}, u32[]{:S(2)}, u32[]{:S(2)}) collective-permute-start(bf16[2,200,128]{2,1,0:T(8,128)(2,1)S(1)} %get-tuple-element.29), channel_id=1, source_target_pairs={{0,1},{1,0},{2,3},{3,2},{4,5},{5,4},{6,7},{7,6},{8,9},{9,8},{10,11... | collective-permute-start | bytes 307208 | tf_op jit(solution)/shard_map/ppermute | solution.py:513
  29.4 1.6 %collective-permute-start.4 = (bf16[2,200,128]{2,1,0:T(8,128)(2,1)S(1)}, bf16[2,200,128]{2,1,0:T(8,128)(2,1)S(1)}, u32[]{:S(2)}, u32[]{:S(2)}) collective-permute-start(bf16[2,200,128]{2,1,0:T(8,128)(2,1)S(1)} %get-tuple-element.30), channel_id=1, source_target_pairs={{0,2},{1,3},{2,0},{3,1},{4,6},{5,7},{6,4},{7,5},{8,10},{9,11},{10,... | collective-permute-start | bytes 307208 | tf_op jit(solution)/shard_map/ppermute | solution.py:513
  30.9 0.1 collective-permute-start.5
  31.1 1.6 %collective-permute-done.3.refs_1_ = bf16[2,200,128]{2,1,0:T(8,128)(2,1)S(1)} collective-permute-done((bf16[2,200,128]{2,1,0:T(8,128)(2,1)S(1)}, bf16[2,200,128]{2,1,0:T(8,128)(2,1)S(1)}, u32[]{:S(2)}, u32[]{:S(2)}) %collective-permute-start.3) | collective-permute-done | bytes 102432 | tf_op jit(solution)/shard_map/ppermute | solution.py:513
  32.7 2.4 %collective-permute-done.4.refs_2_ = bf16[2,200,128]{2,1,0:T(8,128)(2,1)S(1)} collective-permute-done((bf16[2,200,128]{2,1,0:T(8,128)(2,1)S(1)}, bf16[2,200,128]{2,1,0:T(8,128)(2,1)S(1)}, u32[]{:S(2)}, u32[]{:S(2)}) %collective-permute-start.4) | collective-permute-done | bytes 102432 | tf_op jit(solution)/shard_map/ppermute | solution.py:513
  35.1 1.4 %collective-permute-done.5.refs_3_ = bf16[2,200,128]{2,1,0:T(8,128)(2,1)S(1)} collective-permute-done((bf16[2,200,128]{2,1,0:T(8,128)(2,1)S(1)}, bf16[2,200,128]{2,1,0:T(8,128)(2,1)S(1)}, u32[]{:S(2)}, u32[]{:S(2)}) %collective-permute-start.5) | collective-permute-done | bytes 102432 | tf_op jit(solution)/shard_map/ppermute | solution.py:513
  36.5 0.4 shard_map.172
  36.9 2.6 %collective-permute-start.6 = (bf16[192,256]{1,0:T(8,128)(2,1)S(1)}, bf16[192,256]{1,0:T(8,128)(2,1)S(1)}, u32[]{:S(2)}, u32[]{:S(2)}) collective-permute-start(bf16[192,256]{1,0:T(8,128)(2,1)S(1)} %get-tuple-element.33), channel_id=1, source_target_pairs={{0,4},{1,5},{2,6},{3,7},{4,0},{5,1},{6,2},{7,3},{8,12},{9,13},{10,... | collective-permute-start | bytes 294920 | tf_op jit(solution)/shard_map/ppermute | solution.py:513
  39.5 4.0 %collective-permute-done.6.there_ref = bf16[192,256]{1,0:T(8,128)(2,1)S(1)} collective-permute-done((bf16[192,256]{1,0:T(8,128)(2,1)S(1)}, bf16[192,256]{1,0:T(8,128)(2,1)S(1)}, u32[]{:S(2)}, u32[]{:S(2)}) %collective-permute-start.6) | collective-permute-done | bytes 98336 | tf_op jit(solution)/shard_map/ppermute | solution.py:513
  43.5 0.7 %shard_map.173 = f32[192,256]{1,0:T(8,128)} custom-call(f32[192,256]{1,0:T(8,128)S(1)} %get-tuple-element.32.here_ref, bf16[192,256]{1,0:T(8,128)(2,1)S(1)} %collective-permute-done.6.there_ref), custom_call_target="tpu_custom_call" | custom-call | flops 1000000 | bytes 2097152 | tf_op jit(solution)/shard_map/pallas_call | solution.py:682
  (1 shorter events, 0.0 us)
Async XLA Ops:
  8.1 6.1 %collective-permute-start.1 = (bf16[192,1024]{1,0:T(8,128)(2,1)}, bf16[192,1024]{1,0:T(8,128)(2,1)S(1)}, u32[]{:S(2)}, u32[]{:S(2)}) collective-permute-start(bf16[192,1024]{1,0:T(8,128)(2,1)} %get-tuple-element.18.own_ref), channel_id=1, source_target_pairs={{0,8},{8,0},{16,24},{24,16},{1,9},{9,1},{17,25},{25,17},{2,10},{10... | collective-permute-start | bytes 1179656 | tf_op jit(solution)/shard_map/ppermute | solution.py:513
  8.6 12.5 %collective-permute-start = (bf16[192,1024]{1,0:T(8,128)(2,1)}, bf16[192,1024]{1,0:T(8,128)(2,1)S(1)}, u32[]{:S(2)}, u32[]{:S(2)}) collective-permute-start(bf16[192,1024]{1,0:T(8,128)(2,1)} %get-tuple-element.18.own_ref), channel_id=1, source_target_pairs={{0,16},{8,24},{16,0},{24,8},{1,17},{9,25},{17,1},{25,9},{2,18},{10... | collective-permute-start | bytes 1179656 | tf_op jit(solution)/shard_map/ppermute | solution.py:513
  11.2 3.0 %copy-start = (bf16[192,1024]{1,0:T(8,128)(2,1)S(1)}, bf16[192,1024]{1,0:T(8,128)(2,1)}, u32[]{:S(2)}) copy-start(bf16[192,1024]{1,0:T(8,128)(2,1)} %get-tuple-element.18.own_ref) | copy-start | bytes 1179652
  14.2 1.1 %copy-start.2 = (bf16[1536,192]{1,0:T(8,128)(2,1)S(1)}, bf16[1536,192]{1,0:T(8,128)(2,1)}, u32[]{:S(2)}) copy-start(bf16[1536,192]{1,0:T(8,128)(2,1)} %get-tuple-element.19.weights_ref.refs_3_) | copy-start | bytes 1769476
  21.1 1.7 %collective-permute-start.2 = (bf16[192,1024]{1,0:T(8,128)(2,1)S(1)}, bf16[192,1024]{1,0:T(8,128)(2,1)S(1)}, u32[]{:S(2)}, u32[]{:S(2)}) collective-permute-start(bf16[192,1024]{1,0:T(8,128)(2,1)S(1)} %collective-permute-done.refs_0_), channel_id=1, source_target_pairs={{0,8},{8,0},{16,24},{24,16},{1,9},{9,1},{17,25},{25,17},{2,10},{10... | collective-permute-start | bytes 1179656 | tf_op jit(solution)/shard_map/ppermute | solution.py:513
  21.1 1.7 %copy-start.1 = (bf16[768,192]{0,1:T(8,128)(2,1)S(1)}, bf16[768,192]{0,1:T(8,128)(2,1)}, u32[]{:S(2)}) copy-start(bf16[768,192]{0,1:T(8,128)(2,1)} %param.28) | copy-start | bytes 884740
  21.1 1.7 %copy-start.3 = (bf16[192,1024]{1,0:T(8,128)(2,1)S(1)}, bf16[192,1024]{1,0:T(8,128)(2,1)}, u32[]{:S(2)}) copy-start(bf16[192,1024]{1,0:T(8,128)(2,1)} %get-tuple-element.24.refs_4_) | copy-start | bytes 1179652
  21.1 1.7 %copy-start.4 = (f32[192,128]{1,0:T(8,128)S(1)}, f32[192,128]{1,0:T(8,128)}, u32[]{:S(2)}) copy-start(f32[192,128]{1,0:T(8,128)} %get-tuple-element.25.refs_5_) | copy-start | bytes 294916
  21.1 1.7 %copy-start.5 = (bf16[16,1024]{1,0:T(8,128)(2,1)S(1)}, bf16[16,1024]{1,0:T(8,128)(2,1)}, u32[]{:S(2)}) copy-start(bf16[16,1024]{1,0:T(8,128)(2,1)} %get-tuple-element.26.refs_7_) | copy-start | bytes 98308
  27.5 5.1 %collective-permute-start.3 = (bf16[2,200,128]{2,1,0:T(8,128)(2,1)S(1)}, bf16[2,200,128]{2,1,0:T(8,128)(2,1)S(1)}, u32[]{:S(2)}, u32[]{:S(2)}) collective-permute-start(bf16[2,200,128]{2,1,0:T(8,128)(2,1)S(1)} %get-tuple-element.29), channel_id=1, source_target_pairs={{0,1},{1,0},{2,3},{3,2},{4,5},{5,4},{6,7},{7,6},{8,9},{9,8},{10,11... | collective-permute-start | bytes 307208 | tf_op jit(solution)/shard_map/ppermute | solution.py:513
  29.4 5.7 %collective-permute-start.4 = (bf16[2,200,128]{2,1,0:T(8,128)(2,1)S(1)}, bf16[2,200,128]{2,1,0:T(8,128)(2,1)S(1)}, u32[]{:S(2)}, u32[]{:S(2)}) collective-permute-start(bf16[2,200,128]{2,1,0:T(8,128)(2,1)S(1)} %get-tuple-element.30), channel_id=1, source_target_pairs={{0,2},{1,3},{2,0},{3,1},{4,6},{5,7},{6,4},{7,5},{8,10},{9,11},{10,... | collective-permute-start | bytes 307208 | tf_op jit(solution)/shard_map/ppermute | solution.py:513
  30.9 5.6 %collective-permute-start.5 = (bf16[2,200,128]{2,1,0:T(8,128)(2,1)S(1)}, bf16[2,200,128]{2,1,0:T(8,128)(2,1)S(1)}, u32[]{:S(2)}, u32[]{:S(2)}) collective-permute-start(bf16[2,200,128]{2,1,0:T(8,128)(2,1)S(1)} %get-tuple-element.31), channel_id=1, source_target_pairs={{0,3},{1,2},{2,1},{3,0},{4,7},{5,6},{6,5},{7,4},{8,11},{9,10},{10,... | collective-permute-start | bytes 307208 | tf_op jit(solution)/shard_map/ppermute | solution.py:513
  36.9 6.6 %collective-permute-start.6 = (bf16[192,256]{1,0:T(8,128)(2,1)S(1)}, bf16[192,256]{1,0:T(8,128)(2,1)S(1)}, u32[]{:S(2)}, u32[]{:S(2)}) collective-permute-start(bf16[192,256]{1,0:T(8,128)(2,1)S(1)} %get-tuple-element.33), channel_id=1, source_target_pairs={{0,4},{1,5},{2,6},{3,7},{4,0},{5,1},{6,2},{7,3},{8,12},{9,13},{10,... | collective-permute-start | bytes 294920 | tf_op jit(solution)/shard_map/ppermute | solution.py:513
